TPU v7x, 32 devices: a whole 2x2x4 slice. The times are simulated.
32 devices in a mesh: dp: 16 (over z, x, core), tp: 2 (over y).
Axes of the slice: x: 2, y: 2, z: 4, core: 2. Of those that a mesh axis runs over, the one named last changes fastest.
Arguments:
- tokens: bfloat16 [6144, 768], P('dp'), may hold values from -6 to 6
- lengths: int32 [16, 6], P('dp'), may hold values from 1 to 256, 384 in all within a row
- pad_mask: int32 [6144], P('dp'), may hold values 0 or 1
- w_qkv: bfloat16 [3, 768, 768], P(None, None, 'tp'), may hold values from -0.21875 to 0.21875
- b_qv: bfloat16 [2, 768], P(None, 'tp'), may hold values from -3 to 3
- w_out: bfloat16 [768, 768], P('tp'), may hold values from -0.875 to 0.875
- b_out: bfloat16 [768], replicated, may hold values from -2 to 2
- ln1_gain: bfloat16 [768], replicated, may hold values from 0.5 to 1.5
- ln1_bias: bfloat16 [768], replicated, may hold values from -2 to 2
- w_up: bfloat16 [768, 3072], P(None, 'tp'), may hold values from -0.21875 to 0.21875
- b_up: bfloat16 [3072], P('tp'), may hold values from -3 to 3
- w_down: bfloat16 [3072, 768], P('tp'), may hold values from -0.109375 to 0.109375
- b_down: bfloat16 [768], replicated, may hold values from -2 to 2
- ln2_gain: bfloat16 [768], replicated, may hold values from 0.5 to 1.5
- ln2_bias: bfloat16 [768], replicated, may hold values from -2 to 2
- cotangent: bfloat16 [6144, 768], P('dp'), may hold values from -6 to 6
Outputs:
- layer_out: bfloat16 [6144, 768], P('dp')
- d_tokens: float32 [6144, 768], P('dp')
- d_w_qkv: float32 [3, 768, 768], P(None, 'dp', 'tp')
- d_b_qv: float32 [2, 768], P(None, 'tp')
- d_w_out: float32 [768, 768], P('tp', 'dp')
- d_b_out: float32 [768], replicated
- d_ln1_gain: float32 [768], replicated
- d_ln1_bias: float32 [768], replicated
- d_w_up: float32 [768, 3072], P('dp', 'tp')
- d_b_up: float32 [3072], P('tp')
- d_w_down: float32 [3072, 768], P('tp', 'dp')
- d_b_down: float32 [768], replicated
- d_ln2_gain: float32 [768], replicated
- d_ln2_bias: float32 [768], replicated
Inputs may be any that keep to these rules, and one draw needn't show every extreme that they name: Each row holds the lengths of the 6 sequences packed in order on one index of dp; a row sums to 384, and its largest length is exactly 256.
All inputs are finite; a program needn't handle non-finite values. No bound on the sum of `pad_mask` on one device may be relied on, other than what follows from the above.
Results may differ from a plain program's by a relative error of at most 0.013.
The roundings to bfloat16 on the way count: a program that leaves them out, or rounds other values in their place, can miss the bound.
Values sent between devices are 32-bit elements; how exact they have to be, the bound alone decides.
No kernel may reach another device: no remote copies, remote signals or barrier semaphores. Data moves between devices by JAX's collectives and lax.ppermute only.
A program may use at most 128 MiB of HBM per device.

v0:
```python
import jax
import jax.numpy as jnp
from jax import lax
from jax.sharding import PartitionSpec as P

HEAD = 64


NEG_FILL = -1e30
EPS_NORM = 1e-12


def norm_rows(value, gain, bias):
    centered = value - jnp.mean(value, -1, keepdims=True)
    inverse = lax.rsqrt(jnp.mean(centered * centered, -1, keepdims=True) + EPS_NORM)
    normed = centered * inverse
    return (normed * gain + bias, normed, inverse)


def norm_back(grad, normed, inverse, gain):
    scaled = grad * gain
    return inverse * (
        scaled
        - jnp.mean(scaled, -1, keepdims=True)
        - normed * jnp.mean(scaled * normed, -1, keepdims=True)
    )


def gelu_slope(pre):
    return (
        0.5 * (1.0 + jax.scipy.special.erf(pre * 0.7071067811865476))
        + pre * jnp.exp(-0.5 * pre * pre) * 0.3989422804014327
    )


def on_device(
    tokens,
    lengths,
    pad_mask,
    w_qkv,
    b_qv,
    w_out,
    b_out,
    ln1_gain,
    ln1_bias,
    w_up,
    b_up,
    w_down,
    b_down,
    ln2_gain,
    ln2_bias,
    cotangent,
):
    rows = tokens.shape[0]
    local = w_qkv.shape[2]
    heads = local // HEAD
    block = min(rows, 512)
    count = rows // block
    scale = float(HEAD) ** (-0.5)
    places = jnp.arange(rows, dtype=jnp.int32)
    ends = jnp.cumsum(lengths[0])
    segment = jnp.sum((ends[None, :] <= places[:, None]).astype(jnp.int32), 1)
    usable = pad_mask == 1
    qv_bias = b_qv.astype(jnp.float32)
    out_bias = b_out.astype(jnp.float32)
    gain_one = ln1_gain.astype(jnp.float32)
    shift_one = ln1_bias.astype(jnp.float32)
    up_bias = b_up.astype(jnp.float32)
    down_bias = b_down.astype(jnp.float32)
    gain_two = ln2_gain.astype(jnp.float32)
    shift_two = ln2_bias.astype(jnp.float32)

    def allowed_block():
        return (segment[:, None] == segment[None, :]) & (
            usable[None, :] | (places[:, None] == places[None, :])
        )

    def forward(inputs):
        x_float = inputs.astype(jnp.float32)
        mixed = jnp.einsum("rd,tdc->trc", inputs, w_qkv, preferred_element_type=jnp.float32)
        query = ((mixed[0] + qv_bias[0]) * scale).astype(jnp.bfloat16).reshape(rows, heads, HEAD)
        keys = mixed[1].astype(jnp.bfloat16).reshape(rows, heads, HEAD)
        values = (mixed[2] + qv_bias[1]).astype(jnp.bfloat16).reshape(rows, heads, HEAD)

        def attend(index):
            scores = jnp.einsum("qhd,khd->hqk", query, keys, preferred_element_type=jnp.float32)
            scores = jnp.where(allowed_block()[None], scores, NEG_FILL)
            top = jnp.max(scores, -1, keepdims=True)
            expo = jnp.exp(scores - top)
            total = jnp.sum(expo, -1, keepdims=True)
            probs = (expo / total).astype(jnp.bfloat16)
            result = jnp.einsum("hqk,khd->qhd", probs, values, preferred_element_type=jnp.float32)
            return (
                result.reshape(block, local).astype(jnp.bfloat16),
                (top + jnp.log(total))[..., 0],
            )

        pieces, log_totals = lax.map(attend, jnp.arange(count, dtype=jnp.int32))
        context = pieces.reshape(rows, local)
        attn = lax.psum(jnp.dot(context, w_out, preferred_element_type=jnp.float32), "tp")
        hidden, normed_one, inverse_one = norm_rows(x_float + attn + out_bias, gain_one, shift_one)
        hidden_low = hidden.astype(jnp.bfloat16)
        pre = jnp.dot(hidden_low, w_up, preferred_element_type=jnp.float32) + up_bias
        act_low = jax.nn.gelu(pre, approximate=False).astype(jnp.bfloat16)
        ffn = lax.psum(jnp.dot(act_low, w_down, preferred_element_type=jnp.float32), "tp")
        result, normed_two, inverse_two = norm_rows(hidden + ffn + down_bias, gain_two, shift_two)
        state = (
            query,
            keys,
            values,
            context,
            log_totals,
            normed_one,
            inverse_one,
            hidden_low,
            pre,
            act_low,
            normed_two,
            inverse_two,
        )
        return (result.astype(jnp.bfloat16), state)

    layer_out, state = forward(tokens)
    again = lax.optimization_barrier((tokens, layer_out))[0]
    state = forward(again)[1]
    (
        query,
        keys,
        values,
        context,
        log_totals,
        normed_one,
        inverse_one,
        hidden_low,
        pre,
        act_low,
        normed_two,
        inverse_two,
    ) = state
    part = rows // lax.axis_size("tp")
    first = lax.axis_index("tp") * part

    def mine(array):
        return jnp.sum(lax.dynamic_slice_in_dim(array, first, part, 0), 0)

    upstream = cotangent.astype(jnp.float32)
    d_gain_two = mine(upstream * normed_two)
    d_shift_two = mine(upstream)
    grad_two = norm_back(upstream, normed_two, inverse_two, gain_two)
    d_down_bias = mine(grad_two)
    grad_two_low = grad_two.astype(jnp.bfloat16)
    d_w_down = jnp.dot(act_low.T, grad_two_low, preferred_element_type=jnp.float32)
    grad_act = jnp.dot(grad_two_low, w_down.T, preferred_element_type=jnp.float32)
    grad_pre = (grad_act * gelu_slope(pre)).astype(jnp.bfloat16)
    d_up_bias = jnp.sum(grad_pre.astype(jnp.float32), 0)
    d_w_up = jnp.dot(hidden_low.T, grad_pre, preferred_element_type=jnp.float32)
    grad_hidden = grad_two + lax.psum(
        jnp.dot(grad_pre, w_up.T, preferred_element_type=jnp.float32), "tp"
    )
    d_gain_one = mine(grad_hidden * normed_one)
    d_shift_one = mine(grad_hidden)
    grad_one = norm_back(grad_hidden, normed_one, inverse_one, gain_one)
    d_out_bias = mine(grad_one)
    grad_one_low = grad_one.astype(jnp.bfloat16)
    d_w_out = jnp.dot(context.T, grad_one_low, preferred_element_type=jnp.float32)
    grad_context = (
        jnp.dot(grad_one_low, w_out.T, preferred_element_type=jnp.float32)
        .astype(jnp.bfloat16)
        .reshape(rows, heads, HEAD)
    )

    def attend_back(carry, index):
        grad_keys, grad_values = carry
        scores = jnp.einsum("qhd,khd->hqk", query, keys, preferred_element_type=jnp.float32)
        scores = jnp.where(allowed_block()[None], scores, NEG_FILL)
        probs = jnp.exp(scores - log_totals[index][..., None])
        grad_probs = jnp.einsum(
            "qhd,khd->hqk", grad_context, values, preferred_element_type=jnp.float32
        )
        grad_scores = (
            probs * (grad_probs - jnp.sum(probs * grad_probs, -1, keepdims=True))
        ).astype(jnp.bfloat16)
        grad_query = jnp.einsum(
            "hqk,khd->qhd", grad_scores, keys, preferred_element_type=jnp.float32
        )
        grad_keys = grad_keys + jnp.einsum(
            "hqk,qhd->khd", grad_scores, query, preferred_element_type=jnp.float32
        )
        grad_values = grad_values + jnp.einsum(
            "hqk,qhd->khd",
            probs.astype(jnp.bfloat16),
            grad_context,
            preferred_element_type=jnp.float32,
        )
        return ((grad_keys, grad_values), grad_query)

    empty = jnp.zeros((rows, heads, HEAD), jnp.float32)
    (grad_keys, grad_values), grad_query = lax.scan(
        attend_back, (empty, empty), jnp.arange(count, dtype=jnp.int32)
    )
    query_low = grad_query.reshape(rows, local).astype(jnp.bfloat16) * scale
    stacked = jnp.stack(
        [
            query_low,
            grad_keys.reshape(rows, local).astype(jnp.bfloat16),
            grad_values.reshape(rows, local).astype(jnp.bfloat16),
        ]
    )
    d_qv_bias = jnp.stack(
        [jnp.sum(stacked[0].astype(jnp.float32), 0), jnp.sum(stacked[2].astype(jnp.float32), 0)]
    )
    d_w_qkv = jnp.einsum("rd,trc->tdc", tokens, stacked, preferred_element_type=jnp.float32)
    d_tokens = grad_one + lax.psum(
        jnp.einsum("trc,tdc->rd", stacked, w_qkv, preferred_element_type=jnp.float32), "tp"
    )
    part_qkv, part_out, part_up, part_down = (
        lax.psum_scatter(d_w_qkv, "dp", scatter_dimension=1, tiled=True),
        lax.psum_scatter(d_w_out, "dp", scatter_dimension=1, tiled=True),
        lax.psum_scatter(d_w_up, "dp", scatter_dimension=0, tiled=True),
        lax.psum_scatter(d_w_down, "dp", scatter_dimension=1, tiled=True),
    )
    sum_qv, sum_up = lax.psum((d_qv_bias, d_up_bias), "dp")
    sum_out, sum_gain_one, sum_shift_one, sum_down, sum_gain_two, sum_shift_two = lax.psum(
        (d_out_bias, d_gain_one, d_shift_one, d_down_bias, d_gain_two, d_shift_two), ("dp", "tp")
    )
    return (
        layer_out,
        d_tokens,
        part_qkv,
        sum_qv,
        part_out,
        sum_out,
        sum_gain_one,
        sum_shift_one,
        part_up,
        sum_up,
        part_down,
        sum_down,
        sum_gain_two,
        sum_shift_two,
    )


def solution(mesh):
    placed = (
        P("dp", None),
        P("dp", None),
        P("dp"),
        P(None, None, "tp"),
        P(None, "tp"),
        P("tp", None),
        P(),
        P(),
        P(),
        P(None, "tp"),
        P("tp"),
        P("tp", None),
        P(),
        P(),
        P(),
        P("dp", None),
    )
    return jax.shard_map(
        on_device,
        mesh=mesh,
        in_specs=placed,
        out_specs=(
            P("dp", None),
            P("dp", None),
            P(None, "dp", "tp"),
            P(None, "tp"),
            P("tp", "dp"),
            P(),
            P(),
            P(),
            P("dp", "tp"),
            P("tp"),
            P("tp", "dp"),
            P(),
            P(),
            P(),
        ),
        check_vma=False,
    )
```

profile of v0, /device:TPU:0, one launch (start us, length us, event | category | flops | bytes accessed | tf_op | source)
XLA Modules:
  0.0 698.8 jit_solution(4303877730345176219)
XLA Ops:
  7.2 2.9 convolution_bitcast_fusion.2
  11.8 3.0 fusion.128
  14.8 2.7 fusion.43
  20.5 44.4 %all-reduce.11.cloned.1.call-done = f32[384,768]{1,0:T(8,128)} async-done(((f32[384,768]{1,0:T(8,128)}), f32[384,768]{1,0:T(8,128)}) %all-reduce.11.cloned.1.call-update) | async-done | bytes 1179664 | tf_op jit(solution)/shard_map/psum | solution.py:100
  67.4 9.9 %fusion.46 = f32[384,768]{1,0:T(8,128)} fusion(bf16[1536,768]{1,0:T(8,128)(2,1)} %param.27, bf16[768,1536]{1,0:T(8,128)(2,1)S(1)} %copy-done, f32[1536]{0:T(1024)} %convert_element_type.201, f32[768]{0:T(1024)S(1)} %convert_element_type.199, f32[768]{0:T(1024)S(1)} %convert_element_type.198, f32[384]{0:T(512)} %add_rsqrt_fusion.3, ...), kind=kOutput, calls=%fused_computation.95 | convolution fusion | flops 1853227008 | bytes 7686144 | tf_op jit(solution)/shard_map/dot_general | solution.py:105
  80.8 39.6 %all-reduce.13.cloned.1.call-done = f32[384,768]{1,0:T(8,128)} async-done(((f32[384,768]{1,0:T(8,128)}), f32[384,768]{1,0:T(8,128)}) %all-reduce.13.cloned.1.call-update) | async-done | bytes 1179664 | tf_op jit(solution)/shard_map/psum | solution.py:105
  120.4 2.2 fusion.125
  131.2 43.0 %all-reduce.15.cloned.1.call-done = f32[384,768]{1,0:T(8,128)} async-done(((f32[384,768]{1,0:T(8,128)}), f32[384,768]{1,0:T(8,128)}) %all-reduce.15.cloned.1.call-update) | async-done | bytes 1179664 | tf_op jit(solution)/shard_map/psum | solution.py:100
  178.1 7.0 fusion.11
  186.1 2.1 fusion.131
  188.3 43.0 %all-reduce.17.cloned.1.call-done = f32[384,768]{1,0:T(8,128)} async-done(((f32[384,768]{1,0:T(8,128)}), f32[384,768]{1,0:T(8,128)}) %all-reduce.17.cloned.1.call-update) | async-done | bytes 1179664 | tf_op jit(solution)/shard_map/psum | solution.py:105
  236.1 2.3 convert_reduce_fusion
  239.4 2.2 fusion.132
  243.2 41.5 %all-reduce.19.cloned.1.call-done = f32[384,768]{1,0:T(8,128)} async-done(((f32[384,768]{1,0:T(8,128)}), f32[384,768]{1,0:T(8,128)}) %all-reduce.19.cloned.1.call-update) | async-done | bytes 1179664 | tf_op jit(solution)/shard_map/psum | solution.py:157
  284.7 2.0 multiply_reduce_fusion.7
  289.7 2.3 convert_reduce_fusion.1
  297.0 1.8 copy.64
  298.8 1.9 copy.62
  302.6 3.9 convolution_bitcast_fusion.3
  306.5 4.2 convolution_bitcast_fusion
  310.7 6.3 copy.66
  317.1 3.0 fusion.69
  320.1 4.9 fusion.76
  325.2 5.2 fusion.72
  330.4 2.2 convert_element_type.217
  341.2 40.9 %all-reduce.1 = (f32[768]{0:T(1024)}, f32[768]{0:T(1024)}, f32[768]{0:T(1024)}, f32[768]{0:T(1024)}, f32[768]{0:T(1024)}, /*index=5*/f32[768]{0:T(1024)}) all-reduce(f32[768]{0:T(1024)S(1)} %dynamic-slice_reduce_fusion.1, f32[768]{0:T(1024)} %get-tuple-element.150, ...), channel_id=1, replica_groups=mesh['dp'=16,'tp'=2] {'dp','tp'}, use_global_device_ids=true, to_apply=%region_31.32 | all-reduce | flops 4608 | bytes 36864 | tf_op jit(solution)/shard_map/psum | solution.py:223
  382.8 61.0 %all-reduce.2 = (f32[2,384]{1,0:T(2,128)}, f32[1536]{0:T(1024)}) all-reduce(f32[2,384]{1,0:T(2,128)S(1)} %pad_maximum_fusion.3, f32[1536]{0:T(1024)} %get-tuple-element.185), channel_id=1, replica_groups=mesh['dp'=16,'tp'=2] {'dp'}, use_global_device_ids=true, to_apply=%region_28.29 | all-reduce | flops 2304 | bytes 18432 | tf_op jit(solution)/shard_map/psum | solution.py:222
  443.8 2.8 add.256
  446.6 24.9 %all-reduce.23.cloned.1.call-done = f32[3,768,384]{2,0,1:T(4,128)} async-done(((f32[3,768,384]{2,0,1:T(4,128)}), f32[3,768,384]{2,0,1:T(4,128)}) %all-reduce.23.cloned.1.call-update) | async-done | bytes 3538960
  473.3 60.3 %reduce-scatter.4.cloned.1.call-done = f32[384,48]{0,1:T(8,128)} async-done(((f32[384,768]{0,1:T(8,128)}), f32[384,48]{0,1:T(8,128)}) %reduce-scatter.4.cloned.1.call-update) | async-done | bytes 73744 | tf_op jit(solution)/shard_map/reduce_scatter | solution.py:218
  533.5 79.0 %reduce-scatter.6.cloned.1.call-done = f32[48,1536]{1,0:T(8,128)} async-done(((f32[768,1536]{1,0:T(8,128)}), f32[48,1536]{1,0:T(8,128)}) %reduce-scatter.6.cloned.1.call-update) | async-done | bytes 294928 | tf_op jit(solution)/shard_map/reduce_scatter | solution.py:219
  612.6 79.4 %reduce-scatter.8.cloned.1.call-done = f32[1536,48]{0,1:T(8,128)} async-done(((f32[1536,768]{0,1:T(8,128)}), f32[1536,48]{0,1:T(8,128)}) %reduce-scatter.8.cloned.1.call-update) | async-done | bytes 294928 | tf_op jit(solution)/shard_map/reduce_scatter | solution.py:220
  (188 shorter events, 51.6 us)
Async XLA Ops:
  7.2 60.2 %copy-start = (bf16[768,1536]{1,0:T(8,128)(2,1)S(1)}, bf16[768,1536]{1,0:T(8,128)(2,1)}, u32[]{:S(2)}) copy-start(bf16[768,1536]{1,0:T(8,128)(2,1)} %param.25) | copy-start | bytes 7077892
  7.2 57.7 %all-reduce.11.cloned.1.call-start = ((), (), s32[]{:S(2)}) async-start(), calls=%async_computation.3 | async-start | bytes 2359296 | tf_op jit(solution)/shard_map/psum | solution.py:100
  11.5 3.3 copy-start.35
  11.6 3.2 copy-start.28
  11.7 3.0 copy-start.15
  14.8 2.8 copy-start.13
  17.5 2.4 copy-start.40
  17.5 47.3 %copy-start.3 = (bf16[384,768]{1,0:T(8,128)(2,1)S(1)}, bf16[384,768]{1,0:T(8,128)(2,1)}, u32[]{:S(2)}) copy-start(bf16[384,768]{1,0:T(8,128)(2,1)} %param.16) | copy-start | bytes 1769476
  19.1 101.3 %all-reduce.13.cloned.1.call-start = ((), (), s32[]{:S(2)}) async-start(), calls=%async_computation.4 | async-start | bytes 2359296 | tf_op jit(solution)/shard_map/psum | solution.py:105
  66.5 10.8 %copy-start.32 = (f32[384]{0:T(512)}, f32[384]{0:T(512)S(1)}, u32[]{:S(2)}) copy-start(f32[384]{0:T(512)S(1)} %broadcast_multiply_fusion.7) | copy-start | bytes 4612
  77.4 96.9 %all-reduce.15.cloned.1.call-start = ((), (), s32[]{:S(2)}) async-start(), calls=%async_computation.5 | async-start | bytes 2359296 | tf_op jit(solution)/shard_map/psum | solution.py:100
  120.4 2.5 copy-start.38
  125.4 2.3 copy-start.21
  131.2 100.1 %all-reduce.17.cloned.1.call-start = ((), (), s32[]{:S(2)}) async-start(), calls=%async_computation.6 | async-start | bytes 2359296 | tf_op jit(solution)/shard_map/psum | solution.py:105
  175.9 2.2 copy-start.39
  178.1 8.0 %copy-start.45 = (bf16[1536,768]{1,0:T(8,128)(2,1)S(1)}, bf16[1536,768]{1,0:T(8,128)(2,1)}, u32[]{:S(2)}) copy-start(bf16[1536,768]{1,0:T(8,128)(2,1)} %param.27) | copy-start | bytes 7077892
  186.1 45.2 %copy-start.31 = (f32[768]{0:T(1024)S(1)}, f32[768]{0:T(1024)}, u32[]{:S(2)}) copy-start(f32[768]{0:T(1024)} %convert_element_type.203) | copy-start | bytes 9220
  188.2 96.5 %all-reduce.19.cloned.1.call-start = ((), (), s32[]{:S(2)}) async-start(), calls=%async_computation.7 | async-start | bytes 2359296 | tf_op jit(solution)/shard_map/psum | solution.py:157
  233.2 2.8 copy-start.50
  235.0 3.4 copy-start.5
  241.6 202.2 %all-reduce.21.cloned.1.call-start = ((), (), s32[]{:S(2)}) async-start(), calls=%async_computation.8 | async-start | bytes 2359296 | tf_op jit(solution)/shard_map/psum | solution.py:213
  243.2 43.5 %copy-start.34 = (f32[384]{0:T(512)S(1)}, f32[384]{0:T(512)}, u32[]{:S(2)}) copy-start(f32[384]{0:T(512)} %copy-done.33) | copy-start | bytes 4612
  286.7 3.0 copy-start.2
  286.7 3.0 copy-start.17
  286.7 3.0 copy-start.26
  288.6 3.3 copy-start.22
  288.6 3.3 copy-start.37
  306.4 165.1 %all-reduce.23.cloned.1.call-start = ((), (), s32[]{:S(2)}) async-start(), calls=%async_computation.12 | async-start | bytes 9437184
  317.0 216.5 %reduce-scatter.4.cloned.1.call-start = ((), (), s32[]{:S(2)}) async-start(), calls=%async_computation.9 | async-start | bytes 1253376 | tf_op jit(solution)/shard_map/reduce_scatter | solution.py:218
  320.1 292.5 %reduce-scatter.6.cloned.1.call-start = ((), (), s32[]{:S(2)}) async-start(), calls=%async_computation.10 | async-start | bytes 5013504 | tf_op jit(solution)/shard_map/reduce_scatter | solution.py:219
  325.1 366.9 %reduce-scatter.8.cloned.1.call-start = ((), (), s32[]{:S(2)}) async-start(), calls=%async_computation.11 | async-start | bytes 5013504 | tf_op jit(solution)/shard_map/reduce_scatter | solution.py:220
  330.3 2.2 copy-start.49
  (29 other events, 38.0 us)
Sparse Core Ops, SparseCore 0:
  19.2 45.5 all-reduce.10
  77.5 42.8 all-reduce.12
  131.3 42.8 all-reduce.14
  188.3 42.8 all-reduce.16
  241.7 42.8 all-reduce.18
  306.6 43.1 all-reduce.20
  353.4 118.1 all-reduce.22
  475.7 57.7 reduce-scatter.3
  538.0 74.5 reduce-scatter.5
  617.3 74.5 reduce-scatter.7
where the time goes:
time: 700 us; the launch traced here: 699 us
  waiting for transfers between devices  455 us (65%)
  blocking collectives  102 us (15%)
  matrix products  66 us (9%)
  other arithmetic  33.1 us (5%)
  local copies, waits for them, and re-layouts  26.3 us (4%)
  between operations  15.5 us (2%)
    psum x2, waiting for transfers between devices, forward(): lax.psum(jnp.dot(context, w_out, preferred_element_type=jnp.float32), 'tp')  87.4 us
    psum x2, waiting for transfers between devices, forward(): lax.psum(jnp.dot(act_low, w_down, preferred_element_type=jnp.float32), 'tp')  82.6 us
    reduce_scatter x1, waiting for transfers between devices, on_device(): lax.psum_scatter(d_w_down, 'dp', scatter_dimension=1, tiled=True)  79.4 us
    reduce_scatter x1, waiting for transfers between devices, on_device(): lax.psum_scatter(d_w_up, 'dp', scatter_dimension=0, tiled=True)  79 us
    psum x1, blocking collectives, on_device(): sum_qv, sum_up = lax.psum((d_qv_bias, d_up_bias), 'dp')  61 us
    reduce_scatter x1, waiting for transfers between devices, on_device(): lax.psum_scatter(d_w_out, 'dp', scatter_dimension=1, tiled=True)  60.3 us
    psum x1, waiting for transfers between devices, on_device(): lax.psum(jnp.dot(grad_pre, w_up.T, preferred_element_type=jnp.float32), '...  41.5 us
    psum x1, blocking collectives, on_device(): lax.psum((d_out_bias, d_gain_one, d_shift_one, d_down_bias, d_gain_two, d...  40.9 us
  transfers between devices with their start and end apart: 10, of which 9 were waited for; matrix products, arithmetic and copies ran while one was open for 6% of the time, Pallas kernels for 0%

commit v1 on v0

v1 whole, which is shorter than its diff:
```python
import functools

import jax
import jax.numpy as jnp
from jax import lax
from jax.experimental import pallas as pl
from jax.experimental.pallas import tpu as pltpu
from jax.sharding import PartitionSpec as P

HEAD = 64
NEG_FILL = -1e30
EPS_NORM = 1e-12
LANES = 128
F32 = jnp.float32
LOW = jnp.bfloat16
MIB = 1 << 20


def dot(a, b):
    return lax.dot_general(a, b, (((1,), (0,)), ((), ())), preferred_element_type=F32)


def dot_nt(a, b):
    return lax.dot_general(a, b, (((1,), (1,)), ((), ())), preferred_element_type=F32)


def whole(shape):
    return pl.BlockSpec(shape, lambda *_: (0,) * len(shape))


def params(limit=48):
    return pltpu.CompilerParams(vmem_limit_bytes=limit * MIB)


def cost(flops, moved, special=0):
    return pl.CostEstimate(flops=int(flops), bytes_accessed=int(moved), transcendentals=int(special))


def key_mask(lengths_ref, pad_ref, rows):
    seqs = lengths_ref.shape[1]
    key_at = lax.broadcasted_iota(jnp.int32, (rows, LANES), 0)
    query_at = lax.broadcasted_iota(jnp.int32, (8, rows), 1)
    key_seg = jnp.zeros((rows, LANES), jnp.int32)
    query_seg = jnp.zeros((8, rows), jnp.int32)
    end = jnp.int32(0)
    for i in range(seqs):
        end = end + lengths_ref[0, i]
        key_seg = key_seg + (key_at >= end).astype(jnp.int32)
        query_seg = query_seg + (query_at >= end).astype(jnp.int32)
    pad = jnp.broadcast_to(pad_ref[...].astype(F32), (LANES, rows)).T
    pieces = []
    for j in range(rows // LANES):
        span = slice(j * LANES, (j + 1) * LANES)
        same = key_seg == query_seg[0:1, span]
        usable = (pad == 1.0) | (key_at == query_at[0:1, span])
        pieces.append(jnp.where(same & usable, 0.0, NEG_FILL))
    return jnp.concatenate(pieces, 1)


def halves():
    lane = lax.broadcasted_iota(jnp.int32, (1, LANES), 1)
    left = (lane < HEAD).astype(F32)
    return left.astype(LOW), (1.0 - left).astype(LOW)


def attend(x_ref, w_ref, b_ref, lengths_ref, pad_ref, q_ref, k_ref, v_ref, ctx_ref, wide_ref, lse_ref):
    rows = x_ref.shape[0]
    local = w_ref.shape[2]
    scale = float(HEAD) ** (-0.5)
    x = x_ref[...]
    q_ref[...] = ((dot(x, w_ref[0]) + b_ref[0:1, :].astype(F32)) * scale).astype(LOW)
    k_ref[...] = dot(x, w_ref[1]).astype(LOW)
    v_ref[...] = (dot(x, w_ref[2]) + b_ref[1:2, :].astype(F32)).astype(LOW)
    bias = key_mask(lengths_ref, pad_ref, rows)
    sides = halves()
    for pair in range(local // LANES):
        span = slice(pair * LANES, (pair + 1) * LANES)
        query = q_ref[:, span]
        keys = k_ref[:, span]
        flipped = v_ref[:, span].T
        parts = []
        for side in range(2):
            scores = dot_nt(keys * sides[side], query) + bias
            top = jnp.max(scores, 0, keepdims=True)
            expo = jnp.exp(scores - top)
            total = jnp.sum(expo, 0, keepdims=True)
            probs = (expo * (1.0 / total)).astype(LOW)
            parts.append(dot(flipped[side * HEAD : (side + 1) * HEAD], probs))
            head = 2 * pair + side
            lse_ref[head : head + 1, :] = top + jnp.log(total)
        context = jnp.concatenate(parts, 0).T.astype(LOW)
        ctx_ref[:, span] = context
        wide_ref[:, span] = context.astype(F32)


def norm_rows(value):
    centered = value - jnp.mean(value, -1, keepdims=True)
    inverse = lax.rsqrt(jnp.mean(centered * centered, -1, keepdims=True) + EPS_NORM)
    return centered * inverse, inverse


def norm_back(grad, normed, inverse, gain):
    scaled = grad * gain
    return inverse * (
        scaled
        - jnp.mean(scaled, -1, keepdims=True)
        - normed * jnp.mean(scaled * normed, -1, keepdims=True)
    )


def row(ref):
    return ref[...].astype(F32)


def feed(
    core_ref, x_ref, own_ref, far_ref, w_own_ref, w_near_ref, w_far_ref, b_out_ref, gain_ref, shift_ref,
    w_up_ref, b_up_ref, w_down_ref,
    normed_ref, inverse_ref, low_ref, act_ref, slope_ref, part_ref,
    w_full, ctx_full, low_scr,
):
    step = pl.program_id(0)

    @pl.when(step == 0)
    def _():
        half = w_near_ref.shape[0]
        local = own_ref.shape[1]
        mine, side = core_ref[0], core_ref[1]
        here = pl.multiple_of(side * local, LANES)
        there = pl.multiple_of((1 - side) * local, LANES)
        near = pl.multiple_of(there + mine * half, 16)
        far = pl.multiple_of(there + (1 - mine) * half, 16)
        w_full[pl.ds(here, local), :] = w_own_ref[...]
        w_full[pl.ds(near, half), :] = w_near_ref[...].astype(LOW)
        w_full[pl.ds(far, half), :] = w_far_ref[...].astype(LOW)
        ctx_full[:, pl.ds(here, local)] = own_ref[...]
        ctx_full[:, pl.ds(there, local)] = far_ref[...].astype(LOW)
        attn = dot(ctx_full[...], w_full[...])
        normed, inverse = norm_rows(x_ref[...].astype(F32) + attn + row(b_out_ref))
        normed_ref[...] = normed
        inverse_ref[...] = jnp.broadcast_to(inverse, inverse_ref.shape)
        low = (normed * row(gain_ref) + row(shift_ref)).astype(LOW)
        low_ref[...] = low
        low_scr[...] = low

    pre = dot(low_scr[...], w_up_ref[...]) + row(b_up_ref)
    share = 0.5 * (1.0 + lax.erf(pre * 0.7071067811865476))
    act = (pre * share).astype(LOW)
    act_ref[...] = act
    slope_ref[...] = share + pre * jnp.exp(-0.5 * pre * pre) * 0.3989422804014327
    added = dot(act, w_down_ref[...])

    @pl.when(step == 0)
    def _():
        part_ref[...] = added

    @pl.when(step > 0)
    def _():
        part_ref[...] += added


def feed_back(
    own_ref, far_ref, normed_ref, gain1_ref, shift1_ref, b_down_ref, gain_ref, shift_ref, up_ref,
    slope_ref, w_up_ref, w_down_ref,
    out_ref, grad_ref, low_ref, pre_ref, part_ref, sums_ref, b_up_ref,
    low_scr,
):
    step = pl.program_id(0)

    @pl.when(step == 0)
    def _():
        hidden = normed_ref[...] * row(gain1_ref) + row(shift1_ref)
        normed, inverse = norm_rows(hidden + (own_ref[...] + far_ref[...]) + row(b_down_ref))
        gain = row(gain_ref)
        out_ref[...] = (normed * gain + row(shift_ref)).astype(LOW)
        upstream = up_ref[...].astype(F32)
        grad = norm_back(upstream, normed, inverse, gain)
        grad_ref[...] = grad
        low = grad.astype(LOW)
        low_ref[...] = low
        low_scr[...] = low
        sums_ref[0:1, :] = jnp.sum(upstream * normed, 0, keepdims=True)
        sums_ref[1:2, :] = jnp.sum(upstream, 0, keepdims=True)
        sums_ref[2:3, :] = jnp.sum(grad, 0, keepdims=True)
        sums_ref[3:8, :] = jnp.zeros((5, sums_ref.shape[1]), F32)

    pre = (dot_nt(low_scr[...], w_down_ref[...]) * slope_ref[...]).astype(LOW)
    pre_ref[...] = pre
    b_up_ref[...] = jnp.broadcast_to(jnp.sum(pre.astype(F32), 0, keepdims=True), b_up_ref.shape)
    added = dot_nt(pre, w_up_ref[...])

    @pl.when(step == 0)
    def _():
        part_ref[...] = added

    @pl.when(step > 0)
    def _():
        part_ref[...] += added


def attend_back(blocks, *refs):
    count = len(blocks)
    take = iter(refs)
    dr2, own, far, normed, inverse, sums2, up2 = ([next(take) for _ in range(count)] for _ in range(7))
    gain_ref, w_ref, q_ref, k_ref, v_ref, ctx_ref, lse_ref, lengths_ref, pad_ref = (next(take) for _ in range(9))
    dr1_ref, low_ref, e_ref, bias_ref = (next(take) for _ in range(4))
    rows = dr1_ref.shape[0]
    local = q_ref.shape[1]
    width = dr1_ref.shape[1]
    scale = float(HEAD) ** (-0.5)
    gain = row(gain_ref)
    totals = [jnp.zeros((1, width), F32)] * 3
    start = 0
    for i, size in enumerate(blocks):
        grad = dr2[i][...] + (own[i][...] + far[i][...])
        norm = normed[i][...]
        totals[0] = totals[0] + jnp.sum(grad * norm, 0, keepdims=True)
        totals[1] = totals[1] + jnp.sum(grad, 0, keepdims=True)
        dr1 = norm_back(grad, norm, inverse[i][:, 0:1], gain)
        totals[2] = totals[2] + jnp.sum(dr1, 0, keepdims=True)
        dr1_ref[start : start + size, :] = dr1
        low_ref[start : start + size, :] = dr1.astype(LOW)
        start += size
    bias_ref[...] = jnp.zeros(bias_ref.shape, F32)
    twos = sums2[0][...]
    ups = up2[0][0:1, :]
    for i in range(1, count):
        twos = twos + sums2[i][...]
        ups = ups + up2[i][0:1, :]
    bias_ref[0:3, 0:width] = twos[0:3]
    for i in range(3):
        bias_ref[3 + i : 4 + i, 0:width] = totals[i]
    wide_up = ups.shape[1]
    bias_ref[6:7, 0:wide_up] = ups
    d_ctx = dot_nt(low_ref[...], w_ref[...]).astype(LOW)
    mask = key_mask(lengths_ref, pad_ref, rows)
    sides = halves()
    for pair in range(local // LANES):
        span = slice(pair * LANES, (pair + 1) * LANES)
        query = q_ref[:, span]
        keys = k_ref[:, span]
        values = v_ref[:, span]
        grads = d_ctx[:, span]
        flipped = keys.T
        d_q = []
        d_k = jnp.zeros((rows, LANES), F32)
        d_v = jnp.zeros((rows, LANES), F32)
        for side in range(2):
            head = 2 * pair + side
            scores = dot_nt(keys * sides[side], query) + mask
            probs = jnp.exp(scores - lse_ref[head : head + 1, :])
            d_p = dot_nt(values * sides[side], grads)
            mixed = jnp.sum(probs * d_p, 0, keepdims=True)
            d_s = (probs * (d_p - mixed)).astype(LOW)
            d_k = d_k + dot(d_s, query * sides[side])
            d_v = d_v + dot(probs.astype(LOW), grads * sides[side])
            d_q.append(dot(flipped[side * HEAD : (side + 1) * HEAD], d_s))
        d_query = jnp.concatenate(d_q, 0).T.astype(LOW).astype(F32) * scale
        d_k = d_k.astype(LOW)
        d_v = d_v.astype(LOW)
        at = pair * LANES
        e_ref[:, at : at + LANES] = d_query.astype(LOW)
        e_ref[:, local + at : local + at + LANES] = d_k
        e_ref[:, 2 * local + at : 2 * local + at + LANES] = d_v
        bias_ref[7:8, at : at + LANES] = jnp.sum(d_query, 0, keepdims=True)
        bias_ref[7:8, local + at : local + at + LANES] = jnp.sum(d_v.astype(F32), 0, keepdims=True)
    e_ref[:, 3 * local : 4 * local] = ctx_ref[...]


def place_blocks(me, source, target, order, size):
    for i, block in enumerate(order):
        at = pl.multiple_of((me ^ block) * size, size)
        target[i * size : (i + 1) * size, :] = source[pl.ds(at, size), :]


def outer(order, size, splits, last, me_ref, *refs):
    lefts = refs[: len(splits)]
    extra, rest = (refs[len(splits)], refs[len(splits) + 1 :]) if last else (None, refs[len(splits) :])
    rights = rest[: len(splits)]
    send_ref, keep_ref, flipped, placed = rest[len(splits) :]
    step = pl.program_id(0)

    def place(index, source):
        if order is None:
            placed[index] = source
        else:
            flipped[...] = source
            place_blocks(me_ref[0], flipped, placed.at[index], order, size)

    @pl.when(step == 0)
    def _():
        place(0, jnp.concatenate([ref[...].T for ref in lefts], 1))
        if last:
            place(1, extra[...].T)

    if last:
        left = placed[jnp.where(step == pl.num_programs(0) - 1, 1, 0)]
    else:
        left = placed[0]
    right = jnp.concatenate([ref[...] for ref in rights], 0)
    half = send_ref.shape[0]
    send_ref[...] = dot(left[0:half], right)
    keep_ref[...] = dot(left[half:], right)


def back_tokens(e_ref, w_ref, out_ref):
    local = w_ref.shape[2]
    out_ref[...] = (
        dot_nt(e_ref[:, 0:local], w_ref[0])
        + dot_nt(e_ref[:, local : 2 * local], w_ref[1])
        + dot_nt(e_ref[:, 2 * local : 3 * local], w_ref[2])
    )


def on_device(
    tokens, lengths, pad_mask, w_qkv, b_qv, w_out, b_out, ln1_gain, ln1_bias,
    w_up, b_up, w_down, b_down, ln2_gain, ln2_bias, cotangent,
):
    rows, width = tokens.shape
    local = w_qkv.shape[2]
    heads = local // HEAD
    hidden = w_up.shape[1]
    ranks = lax.axis_size("dp")
    me = lax.axis_index("dp").astype(jnp.int32)
    me_arr = me.reshape(1)
    core_arr = jnp.stack([me % 2, lax.axis_index("tp").astype(jnp.int32)])
    size = width // ranks
    blocks = [LANES, rows - LANES] if rows > LANES else [rows]
    lse_rows = -(-heads // 8) * 8

    def swap_tp(array):
        pairs = [(i, i ^ 1) for i in range(lax.axis_size("tp"))]
        return lax.ppermute(array, "tp", pairs)

    def swap_dp(array, bits):
        return lax.ppermute(array, "dp", [(i, i ^ bits) for i in range(ranks)])

    def as_row(vector):
        return vector.reshape(1, -1)

    stages = []
    done = 1
    while done < ranks:
        ways = 2 if done < 4 else min(4, ranks // done)
        stages.append((done, ways))
        done *= ways
    order = [0]
    for step, ways in reversed(stages):
        order = [i * step + rest for i in range(ways) for rest in order]
    order = [p for p in order if p % 2 == 1] + [p for p in order if p % 2 == 0]
    fused = size % 16 == 0

    smem = pl.BlockSpec(memory_space=pltpu.SMEM)
    pad_row = as_row(pad_mask)

    low_rows = jax.ShapeDtypeStruct((rows, local), LOW)
    query, keys, values, context, context_wide, lse = pl.pallas_call(
        attend,
        out_shape=(
            low_rows, low_rows, low_rows, low_rows,
            jax.ShapeDtypeStruct((rows, local), F32),
            jax.ShapeDtypeStruct((lse_rows, rows), F32),
        ),
        in_specs=[pl.BlockSpec(memory_space=pltpu.VMEM)] * 3 + [smem, pl.BlockSpec(memory_space=pltpu.VMEM)],
        compiler_params=params(),
        cost_estimate=cost(2 * rows * width * 3 * local + 4 * rows * rows * local * 2, 6 * MIB, heads * rows * rows),
        name="attend",
    )(tokens, w_qkv, b_qv, lengths, pad_row)

    half = w_out.shape[0] // 2
    w_piece = lax.dynamic_slice_in_dim(w_out, (me % 2) * half, half, 0).astype(F32)
    w_near = swap_tp(w_piece)
    w_far = swap_dp(w_near, 1)
    context_far = swap_tp(context_wide)

    tile = min(hidden, 512)
    tiles = hidden // tile
    saved = []
    start = 0
    for block in blocks:
        index = start // block if start % block == 0 else None
        begin = start

        def cut(array):
            return lax.slice_in_dim(array, begin, begin + block, axis=0)

        own = jax.ShapeDtypeStruct
        outs = pl.pallas_call(
            feed,
            grid=(tiles,),
            out_shape=(
                own((block, width), F32), own((block, LANES), F32), own((block, width), LOW),
                own((block, hidden), LOW), own((block, hidden), F32), own((block, width), F32),
            ),
            in_specs=[
                smem, whole((block, width)), whole((block, local)), whole((block, local)),
                whole((local, width)), whole((half, width)), whole((half, width)),
                whole((1, width)), whole((1, width)), whole((1, width)),
                pl.BlockSpec((width, tile), lambda f: (0, f)),
                pl.BlockSpec((1, tile), lambda f: (0, f)),
                pl.BlockSpec((tile, width), lambda f: (f, 0)),
            ],
            out_specs=(
                whole((block, width)), whole((block, LANES)), whole((block, width)),
                pl.BlockSpec((block, tile), lambda f: (0, f)),
                pl.BlockSpec((block, tile), lambda f: (0, f)),
                whole((block, width)),
            ),
            scratch_shapes=[
                pltpu.VMEM((2 * local, width), LOW),
                pltpu.VMEM((block, 2 * local), LOW),
                pltpu.VMEM((block, width), LOW),
            ],
            compiler_params=params(),
            cost_estimate=cost(4 * block * width * (hidden + local), 8 * MIB, 2 * block * hidden),
            name="feed",
        )(
            core_arr, cut(tokens), cut(context), cut(context_far), w_out, w_near, w_far,
            as_row(b_out), as_row(ln1_gain), as_row(ln1_bias), w_up, as_row(b_up), w_down,
        )
        saved.append(outs + (swap_tp(outs[5]),))
        start += block

    back = []
    start = 0
    for block, (normed, inverse, low, act, slope, part, far) in zip(blocks, saved):
        own = jax.ShapeDtypeStruct
        outs = pl.pallas_call(
            feed_back,
            grid=(tiles,),
            out_shape=(
                own((block, width), LOW), own((block, width), F32), own((block, width), LOW),
                own((block, hidden), LOW), own((block, width), F32), own((8, width), F32), own((8, hidden), F32),
            ),
            in_specs=[whole((block, width))] * 3 + [whole((1, width))] * 5 + [
                whole((block, width)),
                pl.BlockSpec((block, tile), lambda f: (0, f)),
                pl.BlockSpec((width, tile), lambda f: (0, f)),
                pl.BlockSpec((tile, width), lambda f: (f, 0)),
            ],
            out_specs=(
                whole((block, width)), whole((block, width)), whole((block, width)),
                pl.BlockSpec((block, tile), lambda f: (0, f)),
                whole((block, width)), whole((8, width)),
                pl.BlockSpec((8, tile), lambda f: (0, f)),
            ),
            scratch_shapes=[pltpu.VMEM((block, width), LOW)],
            compiler_params=params(),
            cost_estimate=cost(4 * block * width * hidden, 8 * MIB),
            name="feed_back",
        )(
            part, far, normed, as_row(ln1_gain), as_row(ln1_bias), as_row(b_down), as_row(ln2_gain), as_row(ln2_bias),
            lax.slice_in_dim(cotangent, start, start + block, axis=0), slope, w_up, w_down,
        )
        back.append(outs + (swap_tp(outs[4]),))
        start += block

    layer_out = jnp.concatenate([outs[0] for outs in back], 0)

    def gradient(lefts, rights, splits, columns, step, extra=None):
        last = extra is not None
        halved = jax.ShapeDtypeStruct((width // 2, columns), F32)
        send, keep = pl.pallas_call(
            functools.partial(outer, order if fused else None, size, splits, last),
            grid=(columns // step,),
            out_shape=(halved, halved),
            in_specs=[smem]
            + [whole((split, width)) for split in splits]
            + ([whole((rows, width))] if last else [])
            + [pl.BlockSpec((split, step), lambda n: (0, n)) for split in splits],
            out_specs=(pl.BlockSpec((width // 2, step), lambda n: (0, n)),) * 2,
            scratch_shapes=[pltpu.VMEM((width, rows), LOW), pltpu.VMEM((2 if last else 1, width, rows), LOW)],
            compiler_params=params(),
            cost_estimate=cost(2 * rows * width * columns, 8 * MIB),
            name="outer",
        )(me_arr, *lefts, *([extra] if last else []), *rights)
        if not fused:
            full = jnp.concatenate([send, keep], 0).reshape(ranks, size, columns)
            full = jnp.take(full, jnp.array(order, jnp.int32) ^ me, axis=0).reshape(width, columns)
            send, keep = full[: width // 2], full[width // 2 :]
        return send, keep

    def scatter(send, keep):
        held = [keep, swap_dp(send, 1)]
        for step, ways in stages[1:]:
            share = held[0].shape[0] // ways
            came = []
            for way in range(1, ways):
                out = functools.reduce(jnp.add, [a[way * share : (way + 1) * share] for a in held])
                came.append(swap_dp(out, way * step))
            held = [a[:share] for a in held]
            if ways == 4:
                held = [functools.reduce(jnp.add, held) + came[0], came[1] + came[2]]
            else:
                held = held + came
        return functools.reduce(jnp.add, held)

    def total(array):
        for step, ways in stages:
            came = [swap_dp(array, way * step) for way in range(1, ways)]
            if ways == 4:
                array = (array + came[0]) + (came[1] + came[2])
            else:
                array = array + came[0]
        return array

    down = scatter(*gradient([o[2] for o in back], [s[3] for s in saved], blocks, hidden, tile))
    up = scatter(*gradient([s[2] for s in saved], [o[3] for o in back], blocks, hidden, tile))

    vmem = pl.BlockSpec(memory_space=pltpu.VMEM)
    wide = max(width, hidden, 2 * local)
    dr1, dr1_low, e, bias = pl.pallas_call(
        functools.partial(attend_back, blocks),
        out_shape=(
            jax.ShapeDtypeStruct((rows, width), F32), jax.ShapeDtypeStruct((rows, width), LOW),
            jax.ShapeDtypeStruct((rows, 4 * local), LOW), jax.ShapeDtypeStruct((8, wide), F32),
        ),
        in_specs=[vmem] * (7 * len(blocks) + 7) + [smem, vmem],
        compiler_params=params(),
        cost_estimate=cost(2 * rows * width * local + 10 * rows * rows * local * 2, 8 * MIB, heads * rows * rows),
        name="attend_back",
    )(
        *[o[1] for o in back], *[o[4] for o in back], *[o[7] for o in back],
        *[s[0] for s in saved], *[s[1] for s in saved], *[o[5] for o in back], *[o[6] for o in back],
        as_row(ln1_gain), w_out, query, keys, values, context, lse, lengths, pad_row,
    )
    bias = total(bias)
    mixed = scatter(*gradient([tokens], [e], [rows], 4 * local, local, dr1_low))
    part = pl.pallas_call(
        back_tokens,
        out_shape=jax.ShapeDtypeStruct((rows, width), F32),
        in_specs=[vmem] * 2,
        compiler_params=params(),
        cost_estimate=cost(6 * rows * width * local, 5 * MIB),
        name="back_tokens",
    )(e, w_qkv)
    d_tokens = dr1 + (part + swap_tp(part))
    d_w_qkv = mixed[:, : 3 * local].reshape(size, 3, local).transpose(1, 0, 2)
    return (
        layer_out,
        d_tokens,
        d_w_qkv,
        bias[7, : 2 * local].reshape(2, local),
        mixed[:, 3 * local :].T,
        bias[5, :width],
        bias[3, :width],
        bias[4, :width],
        up,
        bias[6, :hidden],
        down.T,
        bias[2, :width],
        bias[0, :width],
        bias[1, :width],
    )


def solution(mesh):
    placed = (
        P("dp", None), P("dp", None), P("dp"), P(None, None, "tp"), P(None, "tp"), P("tp", None),
        P(), P(), P(), P(None, "tp"), P("tp"), P("tp", None), P(), P(), P(), P("dp", None),
    )
    return jax.shard_map(
        on_device,
        mesh=mesh,
        in_specs=placed,
        out_specs=(
            P("dp", None), P("dp", None), P(None, "dp", "tp"), P(None, "tp"), P("tp", "dp"), P(), P(), P(),
            P("dp", "tp"), P("tp"), P("tp", "dp"), P(), P(), P(),
        ),
        check_vma=False,
    )
```

time: 700 us -> 248 us (0.35)
  waiting for transfers between devices: 455 us -> 136 us
  blocking collectives: 102 us -> 0 us
  matrix products: 66 us -> 0 us
  Pallas kernels: 0 us -> 46.2 us
  starting transfers between devices: 0.82 us -> 31.4 us
  other arithmetic: 33.1 us -> 17.8 us
  between operations: 15.5 us -> 1.04 us
  local copies, waits for them, and re-layouts: 26.3 us -> 15.3 us
    reduce_scatter x3 -> x0, waiting for transfers between devices: 219 us -> none  [the longest x1 79.4 us: on_device(): lax.psum_scatter(d_w_down, 'dp', scatter_dimension=1, tiled=True)]
    psum x6 -> x0, waiting for transfers between devices: 211 us -> none  [the longest x2 87.4 us: forward(): lax.psum(jnp.dot(context, w_out, preferred_element_type=jnp.float32), 'tp')]
    ppermute x0 -> x28, waiting for transfers between devices: none -> 136 us  [the longest x7 74.4 us: swap_tp(): return lax.ppermute(array, 'tp', pairs)]
    psum x2 -> x0, blocking collectives: 102 us -> none  [the longest x1 61 us: on_device(): sum_qv, sum_up = lax.psum((d_qv_bias, d_up_bias), 'dp')]
    dot_general x22 -> x0, matrix products: 63 us -> none  [the longest x2 12 us: forward(): jnp.dot(act_low, w_down, preferred_element_type=jnp.float32)]
    pallas_call x0 -> x10, Pallas kernels: none -> 46.2 us  [the longest x2 11.4 us: on_device(): pl.pallas_call(feed, grid=(tiles,), out_shape=(own((block, width), F32),...]
    ppermute x0 -> x28, starting transfers between devices: none -> 31.4 us  [the longest x21 22.5 us: swap_dp(): return lax.ppermute(array, 'dp', [(i, i ^ bits) for i in range(ranks)])]
    unnamed x11 -> x0, waiting for transfers between devices: 25.1 us -> none
  transfers between devices with their start and end apart: 10 -> 28, of which waited for: 9 -> 13; matrix products, arithmetic and copies ran while one was open for 6% -> 8% of each run, Pallas kernels for 0% -> 12%
where the time goes in v1:
time: 248 us
  waiting for transfers between devices  136 us (55%)
  Pallas kernels  46.2 us (19%)
  starting transfers between devices  31.4 us (13%)
  other arithmetic  17.8 us (7%)
  local copies, waits for them, and re-layouts  15.3 us (6%)
    ppermute x7, waiting for transfers between devices, swap_tp(): return lax.ppermute(array, 'tp', pairs)  74.4 us
    ppermute x21, waiting for transfers between devices, swap_dp(): return lax.ppermute(array, 'dp', [(i, i ^ bits) for i in range(ranks)])  61.4 us
    ppermute x21, starting transfers between devices, swap_dp(): return lax.ppermute(array, 'dp', [(i, i ^ bits) for i in range(ranks)])  22.5 us
    pallas_call x2, Pallas kernels, on_device(): pl.pallas_call(feed, grid=(tiles,), out_shape=(own((block, width), F32),...  11.4 us
    pallas_call x3, Pallas kernels, gradient(): pl.pallas_call(functools.partial(outer, order if fused else None, size, s...  11.3 us
    pallas_call x2, Pallas kernels, on_device(): pl.pallas_call(feed_back, grid=(tiles,), out_shape=(own((block, width), L...  10.1 us
    unnamed x69, local copies, waits for them, and re-layouts  9.94 us
    ppermute x7, starting transfers between devices, swap_tp(): return lax.ppermute(array, 'tp', pairs)  8.92 us
  transfers between devices with their start and end apart: 28, of which 13 were waited for; matrix products, arithmetic and copies ran while one was open for 8% of the time, Pallas kernels for 12%

profile of v1, /device:TPU:0, one launch (start us, length us, event | category | flops | bytes accessed | tf_op | source)
XLA Modules:
  0.0 247.6 jit_solution(16579786819020815573)
XLA Ops:
  1.7 3.0 %collective-permute-start.1 = (f32[192,768]{1,0:T(8,128)S(1)}, f32[192,768]{1,0:T(8,128)S(1)}, u32[]{:S(2)}, u32[]{:S(2)}) collective-permute-start(f32[192,768]{1,0:T(8,128)S(1)} %dynamic-slice_convert_fusion), channel_id=1, source_target_pairs={{0,1},{1,0},{2,3},{3,2},{4,5},{5,4},{6,7},{7,6},{8,9},{9,8},{10,11... | collective-permute-start | bytes 1769480 | tf_op jit(solution)/shard_map/ppermute | solution.py:332
  9.3 5.2 %attend.1 = (bf16[384,384]{1,0:T(8,128)(2,1)S(1)}, bf16[384,384]{1,0:T(8,128)(2,1)S(1)}, bf16[384,384]{1,0:T(8,128)(2,1)S(1)}, bf16[384,384]{1,0:T(8,128)(2,1)S(...) custom-call(bf16[384,768]{1,0:T(8,128)(2,1)S(1)} %copy-done.6, bf16[3,768,384]{2,1,0:T(8,128)(2,1)S(1)} %copy-done.3, ...), custom_call_target="tpu_custom_call" | custom-call | flops 1132462080 | bytes 6291456 | tf_op jit(solution)/shard_map/attend/pallas_call | solution.py:356
  16.0 2.5 collective-permute-done.1.w_near_ref
  18.7 12.4 %collective-permute-done = f32[384,384]{1,0:T(8,128)} collective-permute-done((f32[384,384]{1,0:T(8,128)}, f32[384,384]{1,0:T(8,128)}, u32[]{:S(2)}, u32[]{:S(2)}) %collective-permute-start) | collective-permute-done | bytes 589856 | tf_op jit(solution)/shard_map/ppermute | solution.py:332
  32.1 6.5 %feed.3 = (f32[256,768]{1,0:T(8,128)S(1)}, f32[256,128]{1,0:T(8,128)S(1)}, bf16[256,768]{1,0:T(8,128)(2,1)S(1)}, bf16[256,1536]{1,0:T(8,128)(2,1)S(1)}, f32[256,1536]{1,0:T(8,128)}, /*index=5*/f32[256,768]{1,0:T(8,128)S(1)}) custom-call(s32[2]{0:T(128)S(1)} %pad_add_fusion.core_ref, bf16[256,768]{1,0:T(8,128)(2,1)S(1)} %slice.214.x_ref, ...), custom_call_target="tpu_custom_call" | custom-call | flops 1509949440 | bytes 8388608 | tf_op jit(solution)/shard_map/feed/pallas_call | solution.py:387
  42.0 4.8 %feed.2 = (f32[128,768]{1,0:T(8,128)S(1)}, f32[128,128]{1,0:T(8,128)S(1)}, bf16[128,768]{1,0:T(8,128)(2,1)S(1)}, bf16[128,1536]{1,0:T(8,128)(2,1)S(1)}, f32[128,1536]{1,0:T(8,128)S(1)}, /*index=5*/f32[128,768]{1,0:T(8,128)S(1)}) custom-call(s32[2]{0:T(128)S(1)} %pad_add_fusion.core_ref, bf16[128,768]{1,0:T(8,128)(2,1)S(1)} %slice.210.x_ref, ...), custom_call_target="tpu_custom_call" | custom-call | flops 754974720 | bytes 8388608 | tf_op jit(solution)/shard_map/feed/pallas_call | solution.py:387
  47.7 18.4 %collective-permute-done.3.far_ref = f32[128,768]{1,0:T(8,128)S(1)} collective-permute-done((f32[128,768]{1,0:T(8,128)S(1)}, f32[128,768]{1,0:T(8,128)S(1)}, u32[]{:S(2)}, u32[]{:S(2)}) %collective-permute-start.3) | collective-permute-done | bytes 393248 | tf_op jit(solution)/shard_map/ppermute | solution.py:332
  66.1 4.4 %feed_back.2 = (bf16[128,768]{1,0:T(8,128)(2,1)S(1)}, f32[128,768]{1,0:T(8,128)S(1)}, bf16[128,768]{1,0:T(8,128)(2,1)S(1)}, bf16[128,1536]{1,0:T(8,128)(2,1)S(1)...) custom-call(f32[128,768]{1,0:T(8,128)S(1)} %get-tuple-element.58.own_ref, ...), custom_call_target="tpu_custom_call" | custom-call | flops 603979776 | bytes 8388608 | tf_op jit(solution)/shard_map/feed_back/pallas_call | solution.py:427
  71.3 5.7 %feed_back.3 = (bf16[256,768]{1,0:T(8,128)(2,1)S(1)}, f32[256,768]{1,0:T(8,128)S(1)}, bf16[256,768]{1,0:T(8,128)(2,1)S(1)}, bf16[256,1536]{1,0:T(8,128)(2,1)S(1)...) custom-call(f32[256,768]{1,0:T(8,128)S(1)} %get-tuple-element.62.own_ref, ...), custom_call_target="tpu_custom_call" | custom-call | flops 1207959552 | bytes 8388608 | tf_op jit(solution)/shard_map/feed_back/pallas_call | solution.py:427
  77.0 3.5 %outer.5 = (f32[384,1536]{1,0:T(8,128)}, f32[384,1536]{1,0:T(8,128)}) custom-call(s32[1]{0:T(128)} %bitcast.2.me_ref, bf16[128,768]{1,0:T(8,128)(2,1)S(1)} %get-tuple-element.92.refs_0_, bf16[256,768]{1,0:T(8,128)(2,1)S(1)} %get-tuple-element.93.refs_1_, bf16[128,1536]{1,0:T(8,128)(2,1)S(1)} %copy-done.17, bf16[256,1536]{1,0:T(8,128)(2,1)S(1)} %copy-done.15), custom_call_target="tpu_custom_call" | custom-call | flops 905969664 | bytes 8388608 | tf_op jit(solution)/shard_map/outer/pallas_call | solution.py:462
  80.5 1.7 collective-permute-start.6
  82.2 3.6 %outer.4 = (f32[384,1536]{1,0:T(8,128)}, f32[384,1536]{1,0:T(8,128)}) custom-call(s32[1]{0:T(128)} %bitcast.2.me_ref, bf16[128,768]{1,0:T(8,128)(2,1)S(1)} %get-tuple-element.86.refs_0_, bf16[256,768]{1,0:T(8,128)(2,1)S(1)} %get-tuple-element.87.refs_1_, bf16[128,1536]{1,0:T(8,128)(2,1)S(1)} %copy-done.19, bf16[256,1536]{1,0:T(8,128)(2,1)S(1)} %get-tuple-element.89.refs_3_), custom_call_target="tpu_custom_call" | custom-call | flops 905969664 | bytes 8388608 | tf_op jit(solution)/shard_map/outer/pallas_call | solution.py:462
  86.4 22.5 %collective-permute-done.5.refs_4_ = f32[128,768]{1,0:T(8,128)S(1)} collective-permute-done((f32[128,768]{1,0:T(8,128)S(1)}, f32[128,768]{1,0:T(8,128)S(1)}, u32[]{:S(2)}, u32[]{:S(2)}) %collective-permute-start.5) | collective-permute-done | bytes 393248 | tf_op jit(solution)/shard_map/ppermute | solution.py:332
  109.8 7.2 %attend_back.1 = (f32[384,768]{1,0:T(8,128)}, bf16[384,768]{1,0:T(8,128)(2,1)S(1)}, bf16[384,1536]{1,0:T(8,128)(2,1)}, f32[8,1536]{1,0:T(8,128)S(1)}) custom-call(f32[128,768]{1,0:T(8,128)S(1)} %get-tuple-element.66.refs_0_, f32[256,768]{1,0:T(8,128)S(1)} %get-tuple-element.67.refs_1_, f32[128,768]{1,0:T(8,128)S(1)} %get-tuple-element.68.refs_2_, ...), custom_call_target="tpu_custom_call" | custom-call | flops 1358954496 | bytes 8388608 | tf_op jit(solution)/shard_map/attend_back/pallas_call | solution.py:511
  118.2 1.8 collective-permute-start.14
  121.3 4.1 %outer.3 = (f32[384,1536]{1,0:T(8,128)}, f32[384,1536]{1,0:T(8,128)}) custom-call(s32[1]{0:T(128)} %bitcast.2.me_ref, bf16[384,768]{1,0:T(8,128)(2,1)S(1)} %copy-done.7, bf16[384,768]{1,0:T(8,128)(2,1)S(1)} %get-tuple-element.82.refs_1_, bf16[384,1536]{1,0:T(8,128)(2,1)S(1)} %copy-done.5), custom_call_target="tpu_custom_call" | custom-call | flops 905969664 | bytes 8388608 | tf_op jit(solution)/shard_map/outer/pallas_call | solution.py:462
  125.4 3.7 %collective-permute-start.17 = (f32[8,1536]{1,0:T(8,128)S(1)}, f32[8,1536]{1,0:T(8,128)S(1)}, u32[]{:S(2)}, u32[]{:S(2)}) collective-permute-start(f32[8,1536]{1,0:T(8,128)S(1)} %add.154), channel_id=1, source_target_pairs={{0,24},{2,26},{4,28},{6,30},{8,16},{10,18},{12,20},{14,22},{16,8},... | collective-permute-start | bytes 147464 | tf_op jit(solution)/shard_map/ppermute | solution.py:335
  144.0 18.7 %collective-permute-done.7 = f32[384,768]{1,0:T(8,128)} collective-permute-done((f32[384,768]{1,0:T(8,128)S(1)}, f32[384,768]{1,0:T(8,128)}, u32[]{:S(2)}, u32[]{:S(2)}) %collective-permute-start.7) | collective-permute-done | bytes 1179680 | tf_op jit(solution)/shard_map/ppermute | solution.py:332
  162.6 2.7 %add_add_fusion = f32[384,768]{1,0:T(8,128)} fusion(f32[384,768]{1,0:T(8,128)S(1)} %copy-done.24, f32[384,768]{1,0:T(8,128)S(1)} %back_tokens.1, f32[384,768]{1,0:T(8,128)} %collective-permute-done.7), kind=kLoop, calls=%fused_computation.3 | loop fusion | flops 589824 | bytes 4718592 | tf_op jit(solution)/shard_map/add | solution.py:536
  167.3 1.9 collective-permute-done.24
  170.6 2.7 %collective-permute-start.27 = (f32[48,1536]{1,0:T(8,128)S(1)}, f32[48,1536]{1,0:T(8,128)S(1)}, u32[]{:S(2)}, u32[]{:S(2)}) collective-permute-start(f32[48,1536]{1,0:T(8,128)S(1)} %get-tuple-element.119), channel_id=1, source_target_pairs={{0,24},{2,26},{4,28},{6,30},{8,16},{10,18},{12,20},{14,22},{16,8},... | collective-permute-start | bytes 884744 | tf_op jit(solution)/shard_map/ppermute | solution.py:335
  173.2 1.8 collective-permute-start.25
  175.0 19.5 %collective-permute-done.19 = f32[192,1536]{1,0:T(8,128)S(1)} collective-permute-done((f32[192,1536]{1,0:T(8,128)S(1)}, f32[192,1536]{1,0:T(8,128)S(1)}, u32[]{:S(2)}, u32[]{:S(2)}) %collective-permute-start.19) | collective-permute-done | bytes 1179680 | tf_op jit(solution)/shard_map/ppermute | solution.py:335
  195.8 2.7 %collective-permute-start.22 = (f32[48,1536]{1,0:T(8,128)S(1)}, f32[48,1536]{1,0:T(8,128)S(1)}, u32[]{:S(2)}, u32[]{:S(2)}) collective-permute-start(f32[48,1536]{1,0:T(8,128)S(1)} %get-tuple-element.122), channel_id=1, source_target_pairs={{0,24},{2,26},{4,28},{6,30},{8,16},{10,18},{12,20},{14,22},{16,8},... | collective-permute-start | bytes 884744 | tf_op jit(solution)/shard_map/ppermute | solution.py:335
  198.5 1.8 collective-permute-start.20
  200.3 1.8 fusion.2
  202.1 15.9 %collective-permute-done.9 = f32[192,1536]{1,0:T(8,128)S(1)} collective-permute-done((f32[192,1536]{1,0:T(8,128)S(1)}, f32[192,1536]{1,0:T(8,128)S(1)}, u32[]{:S(2)}, u32[]{:S(2)}) %collective-permute-start.9) | collective-permute-done | bytes 1179680 | tf_op jit(solution)/shard_map/ppermute | solution.py:335
  219.4 2.5 %collective-permute-start.12 = (f32[48,1536]{1,0:T(8,128)S(1)}, f32[48,1536]{1,0:T(8,128)S(1)}, u32[]{:S(2)}, u32[]{:S(2)}) collective-permute-start(f32[48,1536]{1,0:T(8,128)S(1)} %get-tuple-element.125), channel_id=1, source_target_pairs={{0,24},{2,26},{4,28},{6,30},{8,16},{10,18},{12,20},{14,22},{16,8},... | collective-permute-start | bytes 884744 | tf_op jit(solution)/shard_map/ppermute | solution.py:335
  221.9 1.9 collective-permute-start.10
  223.8 1.8 fusion.4
  225.6 5.7 %collective-permute-done.12 = f32[48,1536]{1,0:T(8,128)S(1)} collective-permute-done((f32[48,1536]{1,0:T(8,128)S(1)}, f32[48,1536]{1,0:T(8,128)S(1)}, u32[]{:S(2)}, u32[]{:S(2)}) %collective-permute-start.12) | collective-permute-done | bytes 294944 | tf_op jit(solution)/shard_map/ppermute | solution.py:335
  231.3 13.8 %collective-permute-done.11 = f32[48,1536]{1,0:T(8,128)S(1)} collective-permute-done((f32[48,1536]{1,0:T(8,128)S(1)}, f32[48,1536]{1,0:T(8,128)S(1)}, u32[]{:S(2)}, u32[]{:S(2)}) %collective-permute-start.11) | collective-permute-done | bytes 294944 | tf_op jit(solution)/shard_map/ppermute | solution.py:335
  (141 shorter events, 40.5 us)
Async XLA Ops:
  1.7 16.8 %collective-permute-start.1 = (f32[192,768]{1,0:T(8,128)S(1)}, f32[192,768]{1,0:T(8,128)S(1)}, u32[]{:S(2)}, u32[]{:S(2)}) collective-permute-start(f32[192,768]{1,0:T(8,128)S(1)} %dynamic-slice_convert_fusion), channel_id=1, source_target_pairs={{0,1},{1,0},{2,3},{3,2},{4,5},{5,4},{6,7},{7,6},{8,9},{9,8},{10,11... | collective-permute-start | bytes 1769480 | tf_op jit(solution)/shard_map/ppermute | solution.py:332
  16.0 15.1 %collective-permute-start = (f32[384,384]{1,0:T(8,128)}, f32[384,384]{1,0:T(8,128)}, u32[]{:S(2)}, u32[]{:S(2)}) collective-permute-start(f32[384,384]{1,0:T(8,128)} %get-tuple-element.57), channel_id=1, source_target_pairs={{0,1},{1,0},{2,3},{3,2},{4,5},{5,4},{6,7},{7,6},{8,9},{9,8},{10,11... | collective-permute-start | bytes 1769480 | tf_op jit(solution)/shard_map/ppermute | solution.py:332
  18.4 13.7 %collective-permute-start.2 = (f32[192,768]{1,0:T(8,128)S(1)}, f32[192,768]{1,0:T(8,128)S(1)}, u32[]{:S(2)}, u32[]{:S(2)}) collective-permute-start(f32[192,768]{1,0:T(8,128)S(1)} %collective-permute-done.1.w_near_ref), channel_id=1, source_target_pairs={{0,2},{2,0},{4,6},{6,4},{8,10},{10,8},{12,14},{14,12},{16,18},{18,... | collective-permute-start | bytes 1769480 | tf_op jit(solution)/shard_map/ppermute | solution.py:335
  39.5 31.7 %copy-start.2 = (f32[256,768]{1,0:T(8,128)}, f32[256,768]{1,0:T(8,128)S(1)}, u32[]{:S(2)}) copy-start(f32[256,768]{1,0:T(8,128)S(1)} %get-tuple-element.63.normed_ref.refs_7_) | copy-start | bytes 2359300
  39.5 31.7 %collective-permute-start.4 = (f32[256,768]{1,0:T(8,128)S(1)}, f32[256,768]{1,0:T(8,128)S(1)}, u32[]{:S(2)}, u32[]{:S(2)}) collective-permute-start(f32[256,768]{1,0:T(8,128)S(1)} %get-tuple-element.62.own_ref), channel_id=1, source_target_pairs={{0,1},{1,0},{2,3},{3,2},{4,5},{5,4},{6,7},{7,6},{8,9},{9,8},{10,11... | collective-permute-start | bytes 2359304 | tf_op jit(solution)/shard_map/ppermute | solution.py:332
  46.9 19.2 %collective-permute-start.3 = (f32[128,768]{1,0:T(8,128)S(1)}, f32[128,768]{1,0:T(8,128)S(1)}, u32[]{:S(2)}, u32[]{:S(2)}) collective-permute-start(f32[128,768]{1,0:T(8,128)S(1)} %get-tuple-element.58.own_ref), channel_id=1, source_target_pairs={{0,1},{1,0},{2,3},{3,2},{4,5},{5,4},{6,7},{7,6},{8,9},{9,8},{10,11... | collective-permute-start | bytes 1179656 | tf_op jit(solution)/shard_map/ppermute | solution.py:332
  80.5 58.2 %collective-permute-start.23 = (f32[384,1536]{1,0:T(8,128)}, f32[384,1536]{1,0:T(8,128)}, u32[]{:S(2)}, u32[]{:S(2)}) collective-permute-start(f32[384,1536]{1,0:T(8,128)} %get-tuple-element.97), channel_id=1, source_target_pairs={{0,2},{2,0},{4,6},{6,4},{8,10},{10,8},{12,14},{14,12},{16,18},{18,... | collective-permute-start | bytes 7077896 | tf_op jit(solution)/shard_map/ppermute | solution.py:335
  80.5 28.4 %collective-permute-start.6 = (f32[256,768]{1,0:T(8,128)S(1)}, f32[256,768]{1,0:T(8,128)S(1)}, u32[]{:S(2)}, u32[]{:S(2)}) collective-permute-start(f32[256,768]{1,0:T(8,128)S(1)} %get-tuple-element.69.refs_3_), channel_id=1, source_target_pairs={{0,1},{1,0},{2,3},{3,2},{4,5},{5,4},{6,7},{7,6},{8,9},{9,8},{10,11... | collective-permute-start | bytes 2359304 | tf_op jit(solution)/shard_map/ppermute | solution.py:332
  82.2 27.5 %copy-start.9 = (bf16[384,384]{1,0:T(8,128)(2,1)S(1)}, bf16[384,384]{1,0:T(8,128)(2,1)}, u32[]{:S(2)}) copy-start(bf16[384,384]{1,0:T(8,128)(2,1)} %copy-done.8) | copy-start | bytes 884740
  82.2 27.5 %copy-start.11 = (bf16[384,384]{1,0:T(8,128)(2,1)S(1)}, bf16[384,384]{1,0:T(8,128)(2,1)}, u32[]{:S(2)}) copy-start(bf16[384,384]{1,0:T(8,128)(2,1)} %copy-done.10) | copy-start | bytes 884740
  82.2 27.5 %copy-start.13 = (s32[1,6]{1,0:T(1,128)S(1)}, s32[1,6]{1,0:T(1,128)}, u32[]{:S(2)}) copy-start(s32[1,6]{1,0:T(1,128)} %refs_21_.1) | copy-start | bytes 76
  85.9 55.0 %collective-permute-start.18 = (f32[384,1536]{1,0:T(8,128)}, f32[384,1536]{1,0:T(8,128)}, u32[]{:S(2)}, u32[]{:S(2)}) collective-permute-start(f32[384,1536]{1,0:T(8,128)} %get-tuple-element.91), channel_id=1, source_target_pairs={{0,2},{2,0},{4,6},{6,4},{8,10},{10,8},{12,14},{14,12},{16,18},{18,... | collective-permute-start | bytes 7077896 | tf_op jit(solution)/shard_map/ppermute | solution.py:335
  86.1 22.7 %collective-permute-start.5 = (f32[128,768]{1,0:T(8,128)S(1)}, f32[128,768]{1,0:T(8,128)S(1)}, u32[]{:S(2)}, u32[]{:S(2)}) collective-permute-start(f32[128,768]{1,0:T(8,128)S(1)} %get-tuple-element.68.refs_2_), channel_id=1, source_target_pairs={{0,1},{1,0},{2,3},{3,2},{4,5},{5,4},{6,7},{7,6},{8,9},{9,8},{10,11... | collective-permute-start | bytes 1179656 | tf_op jit(solution)/shard_map/ppermute | solution.py:332
  117.0 1.2 collective-permute-start.13
  118.2 7.2 %collective-permute-start.14 = (f32[8,1536]{1,0:T(8,128)S(1)}, f32[8,1536]{1,0:T(8,128)S(1)}, u32[]{:S(2)}, u32[]{:S(2)}) collective-permute-start(f32[8,1536]{1,0:T(8,128)S(1)} %add.153), channel_id=1, source_target_pairs={{0,4},{2,6},{4,0},{6,2},{8,12},{10,14},{12,8},{14,10},{16,20},{18,... | collective-permute-start | bytes 147464 | tf_op jit(solution)/shard_map/ppermute | solution.py:335
  125.4 39.9 %collective-permute-start.8 = (f32[384,1536]{1,0:T(8,128)}, f32[384,1536]{1,0:T(8,128)}, u32[]{:S(2)}, u32[]{:S(2)}) collective-permute-start(f32[384,1536]{1,0:T(8,128)} %get-tuple-element.84), channel_id=1, source_target_pairs={{0,2},{2,0},{4,6},{6,4},{8,10},{10,8},{12,14},{14,12},{16,18},{18,... | collective-permute-start | bytes 7077896 | tf_op jit(solution)/shard_map/ppermute | solution.py:335
  125.4 6.2 %collective-permute-start.17 = (f32[8,1536]{1,0:T(8,128)S(1)}, f32[8,1536]{1,0:T(8,128)S(1)}, u32[]{:S(2)}, u32[]{:S(2)}) collective-permute-start(f32[8,1536]{1,0:T(8,128)S(1)} %add.154), channel_id=1, source_target_pairs={{0,24},{2,26},{4,28},{6,30},{8,16},{10,18},{12,20},{14,22},{16,8},... | collective-permute-start | bytes 147464 | tf_op jit(solution)/shard_map/ppermute | solution.py:335
  129.9 5.1 %collective-permute-start.16 = (f32[8,1536]{1,0:T(8,128)S(1)}, f32[8,1536]{1,0:T(8,128)S(1)}, u32[]{:S(2)}, u32[]{:S(2)}) collective-permute-start(f32[8,1536]{1,0:T(8,128)S(1)} %add.154), channel_id=1, source_target_pairs={{0,16},{2,18},{4,20},{6,22},{8,24},{10,26},{12,28},{14,30},{16,0},... | collective-permute-start | bytes 147464 | tf_op jit(solution)/shard_map/ppermute | solution.py:335
  131.6 5.2 %collective-permute-start.15 = (f32[8,1536]{1,0:T(8,128)S(1)}, f32[8,1536]{1,0:T(8,128)S(1)}, u32[]{:S(2)}, u32[]{:S(2)}) collective-permute-start(f32[8,1536]{1,0:T(8,128)S(1)} %add.154), channel_id=1, source_target_pairs={{0,8},{2,10},{4,12},{6,14},{8,0},{10,2},{12,4},{14,6},{16,24},{18,... | collective-permute-start | bytes 147464 | tf_op jit(solution)/shard_map/ppermute | solution.py:335
  135.1 27.5 %collective-permute-start.7 = (f32[384,768]{1,0:T(8,128)S(1)}, f32[384,768]{1,0:T(8,128)}, u32[]{:S(2)}, u32[]{:S(2)}) collective-permute-start(f32[384,768]{1,0:T(8,128)S(1)} %back_tokens.1), channel_id=1, source_target_pairs={{0,1},{1,0},{2,3},{3,2},{4,5},{5,4},{6,7},{7,6},{8,9},{9,8},{10,11... | collective-permute-start | bytes 3538952 | tf_op jit(solution)/shard_map/ppermute | solution.py:332
  140.3 29.0 %collective-permute-start.24 = (f32[192,1536]{1,0:T(8,128)S(1)}, f32[192,1536]{1,0:T(8,128)S(1)}, u32[]{:S(2)}, u32[]{:S(2)}) collective-permute-start(f32[192,1536]{1,0:T(8,128)S(1)} %slice_add_fusion), channel_id=1, source_target_pairs={{0,4},{2,6},{4,0},{6,2},{8,12},{10,14},{12,8},{14,10},{16,20},{18,... | collective-permute-start | bytes 3538952 | tf_op jit(solution)/shard_map/ppermute | solution.py:335
  142.4 52.1 %collective-permute-start.19 = (f32[192,1536]{1,0:T(8,128)S(1)}, f32[192,1536]{1,0:T(8,128)S(1)}, u32[]{:S(2)}, u32[]{:S(2)}) collective-permute-start(f32[192,1536]{1,0:T(8,128)S(1)} %slice_add_fusion.1), channel_id=1, source_target_pairs={{0,4},{2,6},{4,0},{6,2},{8,12},{10,14},{12,8},{14,10},{16,20},{18,... | collective-permute-start | bytes 3538952 | tf_op jit(solution)/shard_map/ppermute | solution.py:335
  166.7 51.3 %collective-permute-start.9 = (f32[192,1536]{1,0:T(8,128)S(1)}, f32[192,1536]{1,0:T(8,128)S(1)}, u32[]{:S(2)}, u32[]{:S(2)}) collective-permute-start(f32[192,1536]{1,0:T(8,128)S(1)} %slice_add_fusion.2), channel_id=1, source_target_pairs={{0,4},{2,6},{4,0},{6,2},{8,12},{10,14},{12,8},{14,10},{16,20},{18,... | collective-permute-start | bytes 3538952 | tf_op jit(solution)/shard_map/ppermute | solution.py:335
  170.6 28.0 %collective-permute-start.27 = (f32[48,1536]{1,0:T(8,128)S(1)}, f32[48,1536]{1,0:T(8,128)S(1)}, u32[]{:S(2)}, u32[]{:S(2)}) collective-permute-start(f32[48,1536]{1,0:T(8,128)S(1)} %get-tuple-element.119), channel_id=1, source_target_pairs={{0,24},{2,26},{4,28},{6,30},{8,16},{10,18},{12,20},{14,22},{16,8},... | collective-permute-start | bytes 884744 | tf_op jit(solution)/shard_map/ppermute | solution.py:335
  173.2 25.3 %collective-permute-start.26 = (f32[48,1536]{1,0:T(8,128)S(1)}, f32[48,1536]{1,0:T(8,128)S(1)}, u32[]{:S(2)}, u32[]{:S(2)}) collective-permute-start(f32[48,1536]{1,0:T(8,128)S(1)} %get-tuple-element.120), channel_id=1, source_target_pairs={{0,16},{2,18},{4,20},{6,22},{8,24},{10,26},{12,28},{14,30},{16,0},... | collective-permute-start | bytes 884744 | tf_op jit(solution)/shard_map/ppermute | solution.py:335
  173.2 27.1 %collective-permute-start.25 = (f32[48,1536]{1,0:T(8,128)S(1)}, f32[48,1536]{1,0:T(8,128)S(1)}, u32[]{:S(2)}, u32[]{:S(2)}) collective-permute-start(f32[48,1536]{1,0:T(8,128)S(1)} %get-tuple-element.121), channel_id=1, source_target_pairs={{0,8},{2,10},{4,12},{6,14},{8,0},{10,2},{12,4},{14,6},{16,24},{18,... | collective-permute-start | bytes 884744 | tf_op jit(solution)/shard_map/ppermute | solution.py:335
  195.8 26.1 %collective-permute-start.22 = (f32[48,1536]{1,0:T(8,128)S(1)}, f32[48,1536]{1,0:T(8,128)S(1)}, u32[]{:S(2)}, u32[]{:S(2)}) collective-permute-start(f32[48,1536]{1,0:T(8,128)S(1)} %get-tuple-element.122), channel_id=1, source_target_pairs={{0,24},{2,26},{4,28},{6,30},{8,16},{10,18},{12,20},{14,22},{16,8},... | collective-permute-start | bytes 884744 | tf_op jit(solution)/shard_map/ppermute | solution.py:335
  198.5 25.3 %collective-permute-start.21 = (f32[48,1536]{1,0:T(8,128)S(1)}, f32[48,1536]{1,0:T(8,128)S(1)}, u32[]{:S(2)}, u32[]{:S(2)}) collective-permute-start(f32[48,1536]{1,0:T(8,128)S(1)} %get-tuple-element.123), channel_id=1, source_target_pairs={{0,16},{2,18},{4,20},{6,22},{8,24},{10,26},{12,28},{14,30},{16,0},... | collective-permute-start | bytes 884744 | tf_op jit(solution)/shard_map/ppermute | solution.py:335
  198.5 25.3 %collective-permute-start.20 = (f32[48,1536]{1,0:T(8,128)S(1)}, f32[48,1536]{1,0:T(8,128)S(1)}, u32[]{:S(2)}, u32[]{:S(2)}) collective-permute-start(f32[48,1536]{1,0:T(8,128)S(1)} %get-tuple-element.124), channel_id=1, source_target_pairs={{0,8},{2,10},{4,12},{6,14},{8,0},{10,2},{12,4},{14,6},{16,24},{18,... | collective-permute-start | bytes 884744 | tf_op jit(solution)/shard_map/ppermute | solution.py:335
  219.4 11.9 %collective-permute-start.12 = (f32[48,1536]{1,0:T(8,128)S(1)}, f32[48,1536]{1,0:T(8,128)S(1)}, u32[]{:S(2)}, u32[]{:S(2)}) collective-permute-start(f32[48,1536]{1,0:T(8,128)S(1)} %get-tuple-element.125), channel_id=1, source_target_pairs={{0,24},{2,26},{4,28},{6,30},{8,16},{10,18},{12,20},{14,22},{16,8},... | collective-permute-start | bytes 884744 | tf_op jit(solution)/shard_map/ppermute | solution.py:335
  221.9 23.2 %collective-permute-start.11 = (f32[48,1536]{1,0:T(8,128)S(1)}, f32[48,1536]{1,0:T(8,128)S(1)}, u32[]{:S(2)}, u32[]{:S(2)}) collective-permute-start(f32[48,1536]{1,0:T(8,128)S(1)} %get-tuple-element.126), channel_id=1, source_target_pairs={{0,16},{2,18},{4,20},{6,22},{8,24},{10,26},{12,28},{14,30},{16,0},... | collective-permute-start | bytes 884744 | tf_op jit(solution)/shard_map/ppermute | solution.py:335
  221.9 23.2 %collective-permute-start.10 = (f32[48,1536]{1,0:T(8,128)S(1)}, f32[48,1536]{1,0:T(8,128)S(1)}, u32[]{:S(2)}, u32[]{:S(2)}) collective-permute-start(f32[48,1536]{1,0:T(8,128)S(1)} %get-tuple-element.127), channel_id=1, source_target_pairs={{0,8},{2,10},{4,12},{6,14},{8,0},{10,2},{12,4},{14,6},{16,24},{18,... | collective-permute-start | bytes 884744 | tf_op jit(solution)/shard_map/ppermute | solution.py:335
  (30 other events, 189.9 us)

commit v2 on v1

v2 whole, which is shorter than its diff:
```python
import functools

import jax
import jax.numpy as jnp
from jax import lax
from jax.experimental import pallas as pl
from jax.experimental.pallas import tpu as pltpu
from jax.sharding import PartitionSpec as P

HEAD = 64
NEG_FILL = -1e30
EPS_NORM = 1e-12
LANES = 128
F32 = jnp.float32
LOW = jnp.bfloat16
MIB = 1 << 20


def dot(a, b):
    return lax.dot_general(a, b, (((1,), (0,)), ((), ())), preferred_element_type=F32)


def dot_nt(a, b):
    return lax.dot_general(a, b, (((1,), (1,)), ((), ())), preferred_element_type=F32)


def whole(shape):
    return pl.BlockSpec(shape, lambda *_: (0,) * len(shape))


def params(limit=24):
    return pltpu.CompilerParams(vmem_limit_bytes=limit * MIB)


def cost(micros):
    return pl.CostEstimate(flops=int(micros * 1e9), bytes_accessed=int(micros * 3e6), transcendentals=0)


def key_mask(lengths_ref, pad_ref, rows):
    seqs = lengths_ref.shape[1]
    key_at = lax.broadcasted_iota(jnp.int32, (rows, LANES), 0)
    query_at = lax.broadcasted_iota(jnp.int32, (8, rows), 1)
    key_seg = jnp.zeros((rows, LANES), jnp.int32)
    query_seg = jnp.zeros((8, rows), jnp.int32)
    end = jnp.int32(0)
    for i in range(seqs):
        end = end + lengths_ref[0, i]
        key_seg = key_seg + (key_at >= end).astype(jnp.int32)
        query_seg = query_seg + (query_at >= end).astype(jnp.int32)
    pad = jnp.broadcast_to(pad_ref[...].astype(F32), (LANES, rows)).T
    pieces = []
    for j in range(rows // LANES):
        span = slice(j * LANES, (j + 1) * LANES)
        same = key_seg == query_seg[0:1, span]
        usable = (pad == 1.0) | (key_at == query_at[0:1, span])
        pieces.append(jnp.where(same & usable, 0.0, NEG_FILL))
    return jnp.concatenate(pieces, 1)


def halves():
    lane = lax.broadcasted_iota(jnp.int32, (1, LANES), 1)
    left = (lane < HEAD).astype(F32)
    return left.astype(LOW), (1.0 - left).astype(LOW)


def project(place_ref, x_ref, w_ref, b_ref, w_out_ref, qkv_ref, piece_ref):
    local = w_ref.shape[2]
    scale = float(HEAD) ** (-0.5)
    part = piece_ref.shape[0]
    piece_ref[...] = w_out_ref[pl.ds(pl.multiple_of(place_ref[0] * part, 16), part), :].astype(F32)
    x = x_ref[...]
    qkv_ref[:, 0:local] = ((dot(x, w_ref[0]) + b_ref[0:1, :].astype(F32)) * scale).astype(LOW)
    qkv_ref[:, local : 2 * local] = dot(x, w_ref[1]).astype(LOW)
    qkv_ref[:, 2 * local :] = (dot(x, w_ref[2]) + b_ref[1:2, :].astype(F32)).astype(LOW)


def attend(blocks, qkv_ref, lengths_ref, pad_ref, ctx_ref, lse_ref, *wide_refs):
    rows = qkv_ref.shape[0]
    local = ctx_ref.shape[1]
    bias = key_mask(lengths_ref, pad_ref, rows)
    sides = halves()
    for pair in range(local // LANES):
        at = pair * LANES
        span = slice(at, at + LANES)
        query = qkv_ref[:, span]
        keys = qkv_ref[:, local + at : local + at + LANES]
        flipped = qkv_ref[:, 2 * local + at : 2 * local + at + LANES].T
        parts = []
        for side in range(2):
            scores = dot_nt(keys * sides[side], query) + bias
            top = jnp.max(scores, 0, keepdims=True)
            expo = jnp.exp(scores - top)
            total = jnp.sum(expo, 0, keepdims=True)
            probs = (expo * (1.0 / total)).astype(LOW)
            parts.append(dot(flipped[side * HEAD : (side + 1) * HEAD], probs))
            head = 2 * pair + side
            lse_ref[head : head + 1, :] = top + jnp.log(total)
        context = jnp.concatenate(parts, 0).T.astype(LOW)
        ctx_ref[:, span] = context
        start = 0
        for wide_ref, size in zip(wide_refs, blocks):
            wide_ref[:, span] = context[start : start + size].astype(F32)
            start += size


def norm_rows(value):
    centered = value - jnp.mean(value, -1, keepdims=True)
    inverse = lax.rsqrt(jnp.mean(centered * centered, -1, keepdims=True) + EPS_NORM)
    return centered * inverse, inverse


def norm_back(grad, normed, inverse, gain):
    scaled = grad * gain
    return inverse * (
        scaled
        - jnp.mean(scaled, -1, keepdims=True)
        - normed * jnp.mean(scaled * normed, -1, keepdims=True)
    )


def row(ref):
    return ref[...].astype(F32)


def feed(
    taken, place_ref, x_ref, own_ref, far_ref, w_own_ref, w_a_ref, w_b_ref, w_c_ref, w_d_ref,
    vec_ref, w_up_ref, b_up_ref, w_down_ref,
    normed_ref, inverse_ref, low_ref, act_ref, slope_ref, part_ref,
    w_full, ctx_full, low_scr,
):
    step = pl.program_id(0)

    @pl.when(step == 0)
    def _():
        part = w_a_ref.shape[0]
        local = own_ref.shape[1]
        mine, side = place_ref[0], place_ref[1]
        here = pl.multiple_of(side * local, LANES)
        there = pl.multiple_of((1 - side) * local, LANES)
        w_full[pl.ds(here, local), :] = w_own_ref[...]
        for bits, ref in ((0, w_a_ref), (2, w_b_ref), (1, w_c_ref), (3, w_d_ref)):
            at = pl.multiple_of(there + (mine ^ bits) * part, 16)
            w_full[pl.ds(at, part), :] = ref[...].astype(LOW)
        ctx_full[:, pl.ds(here, local)] = own_ref[taken, :]
        ctx_full[:, pl.ds(there, local)] = far_ref[...].astype(LOW)
        attn = dot(ctx_full[...], w_full[...])
        normed, inverse = norm_rows(x_ref[taken, :].astype(F32) + attn + vec_ref[0:1, :])
        normed_ref[...] = normed
        inverse_ref[...] = jnp.broadcast_to(inverse, inverse_ref.shape)
        low = (normed * vec_ref[1:2, :] + vec_ref[2:3, :]).astype(LOW)
        low_ref[...] = low
        low_scr[...] = low

    pre = dot(low_scr[...], w_up_ref[...]) + row(b_up_ref)
    share = 0.5 * (1.0 + lax.erf(pre * 0.7071067811865476))
    act = (pre * share).astype(LOW)
    act_ref[...] = act
    slope_ref[...] = share + pre * jnp.exp(-0.5 * pre * pre) * 0.3989422804014327
    added = dot(act, w_down_ref[...])

    @pl.when(step == 0)
    def _():
        part_ref[...] = added

    @pl.when(step > 0)
    def _():
        part_ref[...] += added


def feed_back(
    taken, own_ref, far_ref, normed_ref, vec_ref, up_ref,
    slope_ref, w_up_ref, w_down_ref,
    out_ref, grad_ref, low_ref, pre_ref, part_ref, sums_ref, b_up_ref,
    low_scr,
):
    step = pl.program_id(0)

    @pl.when(step == 0)
    def _():
        hidden = normed_ref[...] * vec_ref[1:2, :] + vec_ref[2:3, :]
        normed, inverse = norm_rows(hidden + (own_ref[...] + far_ref[...]) + vec_ref[3:4, :])
        gain = vec_ref[4:5, :]
        out_ref[...] = (normed * gain + vec_ref[5:6, :]).astype(LOW)
        upstream = up_ref[taken, :].astype(F32)
        grad = norm_back(upstream, normed, inverse, gain)
        grad_ref[...] = grad
        low = grad.astype(LOW)
        low_ref[...] = low
        low_scr[...] = low
        sums_ref[0:1, :] = jnp.sum(upstream * normed, 0, keepdims=True)
        sums_ref[1:2, :] = jnp.sum(upstream, 0, keepdims=True)
        sums_ref[2:3, :] = jnp.sum(grad, 0, keepdims=True)
        sums_ref[3:8, :] = jnp.zeros((5, sums_ref.shape[1]), F32)

    pre = (dot_nt(low_scr[...], w_down_ref[...]) * slope_ref[...]).astype(LOW)
    pre_ref[...] = pre
    b_up_ref[...] = jnp.broadcast_to(jnp.sum(pre.astype(F32), 0, keepdims=True), b_up_ref.shape)
    added = dot_nt(pre, w_up_ref[...])

    @pl.when(step == 0)
    def _():
        part_ref[...] = added

    @pl.when(step > 0)
    def _():
        part_ref[...] += added


def norm_one_back(blocks, *refs):
    count = len(blocks)
    take = iter(refs)
    dr2, own, far, normed, inverse, sums2, up2 = ([next(take) for _ in range(count)] for _ in range(7))
    vec_ref = next(take)
    dr1_ref, low_ref, bias_ref = (next(take) for _ in range(3))
    width = dr1_ref.shape[1]
    gain = vec_ref[1:2, :]
    totals = [jnp.zeros((1, width), F32)] * 3
    start = 0
    for i, size in enumerate(blocks):
        grad = dr2[i][...] + (own[i][...] + far[i][...])
        norm = normed[i][...]
        totals[0] = totals[0] + jnp.sum(grad * norm, 0, keepdims=True)
        totals[1] = totals[1] + jnp.sum(grad, 0, keepdims=True)
        dr1 = norm_back(grad, norm, inverse[i][:, 0:1], gain)
        totals[2] = totals[2] + jnp.sum(dr1, 0, keepdims=True)
        dr1_ref[start : start + size, :] = dr1
        low_ref[start : start + size, :] = dr1.astype(LOW)
        start += size
    bias_ref[...] = jnp.zeros(bias_ref.shape, F32)
    twos = sums2[0][...]
    ups = up2[0][0:1, :]
    for i in range(1, count):
        twos = twos + sums2[i][...]
        ups = ups + up2[i][0:1, :]
    bias_ref[0:3, 0:width] = twos[0:3]
    for i in range(3):
        bias_ref[3 + i : 4 + i, 0:width] = totals[i]
    bias_ref[6:7, 0 : ups.shape[1]] = ups


def attend_back(low_ref, w_ref, qkv_ref, ctx_ref, lse_ref, lengths_ref, pad_ref, so_far_ref, e_ref, bias_ref):
    rows = qkv_ref.shape[0]
    local = ctx_ref.shape[1]
    scale = float(HEAD) ** (-0.5)
    bias_ref[...] = so_far_ref[...]
    d_ctx = dot_nt(low_ref[...], w_ref[...]).astype(LOW)
    mask = key_mask(lengths_ref, pad_ref, rows)
    sides = halves()
    for pair in range(local // LANES):
        at = pair * LANES
        span = slice(at, at + LANES)
        query = qkv_ref[:, span]
        keys = qkv_ref[:, local + at : local + at + LANES]
        values = qkv_ref[:, 2 * local + at : 2 * local + at + LANES]
        grads = d_ctx[:, span]
        flipped = keys.T
        d_q = []
        d_k = jnp.zeros((rows, LANES), F32)
        d_v = jnp.zeros((rows, LANES), F32)
        for side in range(2):
            head = 2 * pair + side
            scores = dot_nt(keys * sides[side], query) + mask
            probs = jnp.exp(scores - lse_ref[head : head + 1, :])
            d_p = dot_nt(values * sides[side], grads)
            mixed = jnp.sum(probs * d_p, 0, keepdims=True)
            d_s = (probs * (d_p - mixed)).astype(LOW)
            d_k = d_k + dot(d_s, query * sides[side])
            d_v = d_v + dot(probs.astype(LOW), grads * sides[side])
            d_q.append(dot(flipped[side * HEAD : (side + 1) * HEAD], d_s))
        d_query = jnp.concatenate(d_q, 0).T.astype(LOW).astype(F32) * scale
        d_k = d_k.astype(LOW)
        d_v = d_v.astype(LOW)
        e_ref[:, at : at + LANES] = d_query.astype(LOW)
        e_ref[:, local + at : local + at + LANES] = d_k
        e_ref[:, 2 * local + at : 2 * local + at + LANES] = d_v
        bias_ref[7:8, at : at + LANES] = jnp.sum(d_query, 0, keepdims=True)
        bias_ref[7:8, local + at : local + at + LANES] = jnp.sum(d_v.astype(F32), 0, keepdims=True)
    e_ref[:, 3 * local : 4 * local] = ctx_ref[...]


def place_blocks(me, source, target, order, size):
    for i, block in enumerate(order):
        at = pl.multiple_of((me ^ block) * size, size)
        target[i * size : (i + 1) * size, :] = source[pl.ds(at, size), :]


def outer(order, size, splits, kinds, place_ref, *refs):
    count = len(splits)
    sides = max(kinds) + 1
    lefts = [refs[i * count : (i + 1) * count] for i in range(sides)]
    rights = refs[sides * count : (sides + 1) * count]
    high_ref, low_ref, keep_ref, flipped, placed = refs[-5:]
    step = pl.program_id(0)

    @pl.when(step == 0)
    def _():
        for index, group in enumerate(lefts):
            source = jnp.concatenate([ref[...] for ref in group], 0).T
            if order is None:
                placed[index] = source
            else:
                flipped[...] = source
                place_blocks(place_ref[2], flipped, placed.at[index], order, size)

    left = placed[0]
    if sides > 1:
        change = kinds.index(1)
        left = placed[jnp.where(step >= change, 1, 0)]
    right = jnp.concatenate([ref[...] for ref in rights], 0)
    part = high_ref.shape[0]
    low_ref[...] = dot(left[0:part], right)
    high_ref[...] = dot(left[part : 2 * part], right)
    keep_ref[...] = dot(left[2 * part :], right)


def fold(*refs):
    value = refs[0][...]
    for ref in refs[1:-1]:
        value = value + ref[...]
    refs[-1][...] = value


def back_tokens(e_ref, w_ref, out_ref):
    local = w_ref.shape[2]
    out_ref[...] = (
        dot_nt(e_ref[:, 0:local], w_ref[0])
        + dot_nt(e_ref[:, local : 2 * local], w_ref[1])
        + dot_nt(e_ref[:, 2 * local : 3 * local], w_ref[2])
    )


def join(dr1_ref, own_ref, far_ref, out_ref):
    out_ref[...] = dr1_ref[...] + (own_ref[...] + far_ref[...])


def spread(local, *refs):
    qkv_ref, out_ref = refs[-2:]
    value = refs[0][...]
    for ref in refs[1:-2]:
        value = value + ref[...]
    for i in range(3):
        qkv_ref[i] = value[:, i * local : (i + 1) * local]
    out_ref[...] = value[:, 3 * local :]


def chained(kernel, inputs, outputs):
    def body(*refs):
        refs[1 + inputs + outputs][...] = jnp.zeros((8, LANES), F32)
        kernel(*refs[1 : 1 + inputs + outputs], *refs[2 + inputs + outputs :])

    return body


def on_device(
    tokens, lengths, pad_mask, w_qkv, b_qv, w_out, b_out, ln1_gain, ln1_bias,
    w_up, b_up, w_down, b_down, ln2_gain, ln2_bias, cotangent,
):
    rows, width = tokens.shape
    local = w_qkv.shape[2]
    heads = local // HEAD
    hidden = w_up.shape[1]
    ranks = lax.axis_size("dp")
    me = lax.axis_index("dp").astype(jnp.int32)
    place_arr = jnp.stack([me % 4, lax.axis_index("tp").astype(jnp.int32), me])
    size = width // ranks
    blocks = [rows // 2] * 2 if rows % 32 == 0 else [rows]
    starts = [sum(blocks[:i]) for i in range(len(blocks))]
    lse_rows = -(-heads // 8) * 8
    shape = jax.ShapeDtypeStruct
    smem = pl.BlockSpec(memory_space=pltpu.SMEM)
    loose = pl.BlockSpec(memory_space=pl.ANY)
    mark = [None]

    def call(kernel, name, micros, operands, in_specs, out_shape, out_specs, grid=(1,), scratch=()):
        before = mark[0] if mark[0] is not None else operands[0]
        *outs, mark[0] = pl.pallas_call(
            chained(kernel, len(operands), len(out_shape)),
            grid=grid,
            out_shape=tuple(out_shape) + (shape((8, LANES), F32),),
            in_specs=[loose] + list(in_specs),
            out_specs=tuple(out_specs) + (whole((8, LANES)),),
            scratch_shapes=list(scratch),
            compiler_params=params(),
            cost_estimate=cost(micros),
            name=name,
        )(before, *operands)
        return outs

    def full(*arrays):
        return [whole(array.shape) for array in arrays]

    def swap_tp(array):
        pairs = [(i, i ^ 1) for i in range(lax.axis_size("tp"))]
        return lax.ppermute(array, "tp", pairs)

    def swap_dp(array, bits):
        return lax.ppermute(array, "dp", [(i, i ^ bits) for i in range(ranks)])

    stages = []
    while 1 << len(stages) < ranks:
        stages.append(1 << len(stages))
    order = [0]
    for bit in reversed(stages):
        order = order + [bit + rest for rest in order]
    order = order[ranks // 2 :] + order[: ranks // 2]
    fused = size % 16 == 0
    pad_row = pad_mask.reshape(1, rows)
    zero = jnp.zeros((width,), LOW)
    vectors = jnp.stack([b_out, ln1_gain, ln1_bias, b_down, ln2_gain, ln2_bias, zero, zero]).astype(F32)
    b_up_row = b_up.reshape(1, hidden)

    part = w_out.shape[0] // 4
    outs = [shape((rows, 3 * local), LOW), shape((part, width), F32)]
    qkv, piece = call(
        project, "project", 2, [place_arr, tokens, w_qkv, b_qv, w_out],
        [smem] + full(tokens, w_qkv, b_qv, w_out), outs, full(*outs),
    )
    w_a = swap_tp(piece)
    outs = [shape((rows, local), LOW), shape((lse_rows, rows), F32)] + [shape((block, local), F32) for block in blocks]
    context, lse, *wides = call(
        functools.partial(attend, blocks), "attend", 4, [qkv, lengths, pad_row],
        full(qkv) + [smem] + full(pad_row), outs, full(*outs),
    )
    fars = [swap_tp(wide) for wide in wides]
    w_b = swap_dp(w_a, 2)
    w_c, w_d = swap_dp(w_a, 1), swap_dp(w_b, 1)

    tile = min(hidden, 512)
    tiles = hidden // tile

    def columns(height, step):
        return pl.BlockSpec((height, step), lambda f: (0, f))

    down_spec = pl.BlockSpec((tile, width), lambda f: (f, 0))
    saved = []
    for begin, block, far in zip(starts, blocks, fars):
        outs = [
            shape((block, width), F32), shape((block, LANES), F32), shape((block, width), LOW),
            shape((block, hidden), LOW), shape((block, hidden), F32), shape((block, width), F32),
        ]
        outs = call(
            functools.partial(feed, slice(begin, begin + block)), "feed", 5,
            [place_arr, tokens, context, far, w_out, w_a, w_b, w_c, w_d, vectors, w_up, b_up_row, w_down],
            [smem] + full(tokens, context, far, w_out, w_a, w_b, w_c, w_d, vectors)
            + [columns(width, tile), columns(1, tile), down_spec],
            outs,
            full(*outs[:3]) + [columns(block, tile), columns(block, tile), whole((block, width))],
            grid=(tiles,),
            scratch=[
                pltpu.VMEM((2 * local, width), LOW),
                pltpu.VMEM((block, 2 * local), LOW),
                pltpu.VMEM((block, width), LOW),
            ],
        )
        saved.append(outs + [swap_tp(outs[5])])

    back = []
    for begin, block, (normed, inverse, low, act, slope, own, far) in zip(starts, blocks, saved):
        outs = [
            shape((block, width), LOW), shape((block, width), F32), shape((block, width), LOW),
            shape((block, hidden), LOW), shape((block, width), F32), shape((8, width), F32), shape((8, hidden), F32),
        ]
        outs = call(
            functools.partial(feed_back, slice(begin, begin + block)), "feed_back", 5,
            [own, far, normed, vectors, cotangent, slope, w_up, w_down],
            full(own, far, normed, vectors, cotangent) + [columns(block, tile), columns(width, tile), down_spec],
            outs,
            full(*outs[:3]) + [columns(block, tile)] + full(*outs[4:6]) + [columns(8, tile)],
            grid=(tiles,),
            scratch=[pltpu.VMEM((block, width), LOW)],
        )
        back.append(outs + [swap_tp(outs[4])])

    layer_out = jnp.concatenate([outs[0] for outs in back], 0)

    def gradient(lefts, rights, splits, kinds, step):
        wide = step * len(kinds)
        sides = max(kinds) + 1
        outs = [shape((width // 4, wide), F32), shape((width // 4, wide), F32), shape((width // 2, wide), F32)]
        high, low, keep = call(
            functools.partial(outer, order if fused else None, size, splits, kinds), "outer", 3,
            [place_arr, *lefts, *rights],
            [smem] + full(*lefts) + [columns(split, step) for split in splits],
            outs,
            [columns(width // 4, step), columns(width // 4, step), columns(width // 2, step)],
            grid=(len(kinds),),
            scratch=[pltpu.VMEM((width, rows), LOW), pltpu.VMEM((sides, width, rows), LOW)],
        )
        if not fused:
            every = jnp.concatenate([low, high, keep], 0).reshape(ranks, size, wide)
            every = jnp.take(every, jnp.array(order, jnp.int32) ^ me, axis=0).reshape(width, wide)
            low, high, keep = every[: width // 4], every[width // 4 : width // 2], every[width // 2 :]
        return high, low, keep

    def pick(held, begin, end):
        return [(array, first) for array, first in held if first <= begin and end <= first + array.shape[0]]

    def add(held, begin, end):
        wide = held[0][0].shape[1]
        inside = pick(held, begin, end)
        if not fused:
            return functools.reduce(jnp.add, [array[begin - first : end - first] for array, first in inside])

        def at(first):
            return pl.BlockSpec((size, wide), lambda n: (n + (begin - first) // size, 0))

        return call(
            fold, "fold", 1, [array for array, _ in inside], [at(first) for _, first in inside],
            [shape((end - begin, wide), F32)], [pl.BlockSpec((size, wide), lambda n: (n, 0))],
            grid=((end - begin) // size,),
        )[0]

    class Chunk:
        def __init__(self, high, low, keep):
            self.held = [(keep, 0), (swap_dp(high, stages[0]), width // 4), (swap_dp(low, stages[0]), 0)]
            self.stage = 0

        def high(self):
            self.stage += 1
            half = self.half = width // (4 << (self.stage - 1))
            if half > size:
                out = add(self.held, half + half // 2, 2 * half)
                self.came = [(swap_dp(out, stages[self.stage]), half // 2)]
            else:
                out = add(self.held, half, 2 * half)
                self.held = self.held + [(swap_dp(out, stages[self.stage]), 0)]

        def low(self):
            out = add(self.held, self.half, self.half + self.half // 2)
            self.held = self.held + self.came + [(swap_dp(out, stages[self.stage]), 0)]

        def rest(self):
            while self.stage < len(stages) - 1:
                self.high()
                if self.half > size:
                    self.low()
            return [(array, first) for array, first in self.held if first == 0]

    down = Chunk(*gradient([o[2] for o in back], [s[3] for s in saved], blocks, [0] * tiles, tile))
    up = Chunk(*gradient([s[2] for s in saved], [o[3] for o in back], blocks, [0] * tiles, tile))
    down.high()
    down.low()
    down.high()
    wide = max(width, hidden, 2 * local)
    outs = [shape((rows, width), F32), shape((rows, width), LOW), shape((8, wide), F32)]
    operands = [array for i in (1, 4, 7) for array in [o[i] for o in back]]
    operands += [array for i in (0, 1) for array in [s[i] for s in saved]]
    operands += [array for i in (5, 6) for array in [o[i] for o in back]] + [vectors]
    dr1, dr1_low, bias = call(
        functools.partial(norm_one_back, blocks), "norm_one_back", 2, operands, full(*operands), outs, full(*outs)
    )
    up.high()
    up.low()
    down.low()
    down.high()
    outs = [shape((rows, 4 * local), LOW), shape((8, wide), F32)]
    e, bias = call(
        attend_back, "attend_back", 6, [dr1_low, w_out, qkv, context, lse, lengths, pad_row, bias],
        full(dr1_low, w_out, qkv, context, lse) + [smem] + full(pad_row, bias), outs, full(*outs),
    )
    mixed = Chunk(*gradient([tokens, dr1_low], [e], [rows], [0, 0, 0, 1], local))

    def bias_step(bit):
        far = swap_dp(bias, bit)
        return call(fold, "fold", 1, [bias, far], full(bias, far), [shape(bias.shape, F32)], full(bias))[0]

    up.high()
    mixed.high()
    mixed.low()
    bias = bias_step(stages[0])
    outs = [shape((rows, width), F32)]
    (partial,) = call(back_tokens, "back_tokens", 2, [e, w_qkv], full(e, w_qkv), outs, full(*outs))
    partial_far = swap_tp(partial)
    up.low()
    bias = bias_step(stages[1])
    up.high()
    mixed.high()
    bias = bias_step(stages[2])
    outs = [shape((rows, width), F32)]
    third = pl.BlockSpec((blocks[0], width), lambda n: (n, 0))
    (d_tokens,) = call(
        join, "join", 2, [dr1, partial, partial_far], [third] * 3, outs, [third], grid=(rows // blocks[0],)
    )
    mixed.low()
    mixed.high()
    for bit in stages[3:]:
        bias = bias_step(bit)
    down, up, mixed = (chunk.rest() for chunk in (down, up, mixed))

    def finish(held):
        return functools.reduce(jnp.add, [array[:size] for array, _ in held])

    if fused:
        outs = [shape((3, size, local), F32), shape((size, local), F32)]
        block = pl.BlockSpec((size, 4 * local), lambda n: (0, 0))
        d_w_qkv, d_w_out = call(
            functools.partial(spread, local), "spread", 1, [array for array, _ in mixed],
            [block] * len(mixed), outs, full(*outs),
        )
    else:
        last = finish(mixed)
        d_w_qkv = last[:, : 3 * local].reshape(size, 3, local).transpose(1, 0, 2)
        d_w_out = last[:, 3 * local :]
    return (
        layer_out,
        d_tokens,
        d_w_qkv,
        bias[7, : 2 * local].reshape(2, local),
        d_w_out.T,
        bias[5, :width],
        bias[3, :width],
        bias[4, :width],
        finish(up),
        bias[6, :hidden],
        finish(down).T,
        bias[2, :width],
        bias[0, :width],
        bias[1, :width],
    )


def solution(mesh):
    placed = (
        P("dp", None), P("dp", None), P("dp"), P(None, None, "tp"), P(None, "tp"), P("tp", None),
        P(), P(), P(), P(None, "tp"), P("tp"), P("tp", None), P(), P(), P(), P("dp", None),
    )
    return jax.shard_map(
        on_device,
        mesh=mesh,
        in_specs=placed,
        out_specs=(
            P("dp", None), P("dp", None), P(None, "dp", "tp"), P(None, "tp"), P("tp", "dp"), P(), P(), P(),
            P("dp", "tp"), P("tp"), P("tp", "dp"), P(), P(), P(),
        ),
        check_vma=False,
    )
```

time: 248 us -> 197 us (0.79)
  waiting for transfers between devices: 136 us -> 92 us
  other arithmetic: 17.8 us -> 2.54 us
  starting transfers between devices: 31.4 us -> 38.1 us
  Pallas kernels: 46.2 us -> 41.7 us
  local copies, waits for them, and re-layouts: 15.3 us -> 19.1 us
    ppermute x7 -> x8, waiting for transfers between devices: 74.4 us -> 42.5 us  [swap_tp(): return lax.ppermute(array, 'tp', pairs)]
    add x12 -> x1, other arithmetic: 14.1 us -> 0.79 us  [finish(): return functools.reduce(jnp.add, [array[:size] for array, _ in held])]
    ppermute x21 -> x28, waiting for transfers between devices: 61.4 us -> 49.5 us  [swap_dp(): return lax.ppermute(array, 'dp', [(i, i ^ bits) for i in range(ranks)])]
    unnamed x69 -> x62, local copies, waits for them, and re-layouts: 9.94 us -> 16.4 us
    pallas_call x10 -> x33, Pallas kernels: 46.2 us -> 41.7 us  [call(): pl.pallas_call(chained(kernel, len(operands), len(out_shape)), grid=grid,...]
    ppermute x21 -> x28, starting transfers between devices: 22.5 us -> 26.3 us  [swap_dp(): return lax.ppermute(array, 'dp', [(i, i ^ bits) for i in range(ranks)])]
    ppermute x7 -> x8, starting transfers between devices: 8.92 us -> 11.7 us  [swap_tp(): return lax.ppermute(array, 'tp', pairs)]
  transfers between devices with their start and end apart: 28 -> 36, of which waited for: 13 -> 16; matrix products, arithmetic and copies ran while one was open for 8% -> 3% of each run, Pallas kernels for 12% -> 16%
where the time goes in v2:
time: 197 us; the launch traced here: 195 us
  waiting for transfers between devices  92 us (47%)
  Pallas kernels  41.7 us (21%)
  starting transfers between devices  38.1 us (19%)
  local copies, waits for them, and re-layouts  19.1 us (10%)
  other arithmetic  2.54 us (1%)
    ppermute x28, waiting for transfers between devices, swap_dp(): return lax.ppermute(array, 'dp', [(i, i ^ bits) for i in range(ranks)])  49.5 us
    ppermute x8, waiting for transfers between devices, swap_tp(): return lax.ppermute(array, 'tp', pairs)  42.5 us
    pallas_call x33, Pallas kernels, call(): pl.pallas_call(chained(kernel, len(operands), len(out_shape)), grid=grid,...  41.7 us
    ppermute x28, starting transfers between devices, swap_dp(): return lax.ppermute(array, 'dp', [(i, i ^ bits) for i in range(ranks)])  26.3 us
    unnamed x62, local copies, waits for them, and re-layouts  16.4 us
    ppermute x8, starting transfers between devices, swap_tp(): return lax.ppermute(array, 'tp', pairs)  11.7 us
  transfers between devices with their start and end apart: 36, of which 16 were waited for; matrix products, arithmetic and copies ran while one was open for 3% of the time, Pallas kernels for 16%

profile of v2, /device:TPU:0, one launch (start us, length us, event | category | flops | bytes accessed | tf_op | source)
XLA Modules:
  0.0 194.6 jit_solution(17354537573534608434)
XLA Ops:
  6.7 3.0 %collective-permute-start.1 = (f32[96,768]{1,0:T(8,128)S(1)}, f32[96,768]{1,0:T(8,128)S(1)}, u32[]{:S(2)}, u32[]{:S(2)}) collective-permute-start(f32[96,768]{1,0:T(8,128)S(1)} %get-tuple-element.120), channel_id=1, source_target_pairs={{0,1},{1,0},{2,3},{3,2},{4,5},{5,4},{6,7},{7,6},{8,9},{9,8},{10,11... | collective-permute-start | bytes 884744 | tf_op jit(solution)/shard_map/ppermute | solution.py:394
  9.7 7.0 %collective-permute-done.1.refs_6_ = f32[96,768]{1,0:T(8,128)S(1)} collective-permute-done((f32[96,768]{1,0:T(8,128)S(1)}, f32[96,768]{1,0:T(8,128)S(1)}, u32[]{:S(2)}, u32[]{:S(2)}) %collective-permute-start.1) | collective-permute-done | bytes 294944 | tf_op jit(solution)/shard_map/ppermute | solution.py:394
  16.7 1.7 collective-permute-start.2
  18.5 3.5 %attend.1 = (bf16[384,384]{1,0:T(8,128)(2,1)S(1)}, f32[8,384]{1,0:T(8,128)S(1)}, f32[192,384]{1,0:T(8,128)S(1)}, f32[192,384]{1,0:T(8,128)S(1)}, f32[8,128]{1,0:T(8,128)S(1)}) custom-call(f32[8,128]{1,0:T(8,128)S(1)} %get-tuple-element.115.refs_0_, bf16[384,1152]{1,0:T(8,128)(2,1)S(1)} %get-tuple-element.116.refs_1_.refs_3_, s32[1,6]{1,0:T(1,128)S(1)} %copy-done.17, ...), custom_call_target="tpu_custom_call" | custom-call | flops 4000000000 | bytes 12000000 | tf_op jit(solution)/shard_map/attend/pallas_call | solution.py:376
  26.5 6.0 %collective-permute-done.refs_4_ = f32[192,384]{1,0:T(8,128)S(1)} collective-permute-done((f32[192,384]{1,0:T(8,128)S(1)}, f32[192,384]{1,0:T(8,128)S(1)}, u32[]{:S(2)}, u32[]{:S(2)}) %collective-permute-start) | collective-permute-done | bytes 294944 | tf_op jit(solution)/shard_map/ppermute | solution.py:394
  33.3 1.8 copy-done.3
  38.6 3.8 %feed.2 = (f32[192,768]{1,0:T(8,128)S(1)}, f32[192,128]{1,0:T(8,128)S(1)}, bf16[192,768]{1,0:T(8,128)(2,1)S(1)}, bf16[192,1536]{1,0:T(8,128)(2,1)S(1)}, f32[192,...) custom-call(f32[8,128]{1,0:T(8,128)S(1)} %get-tuple-element.117.refs_0_, ...), custom_call_target="tpu_custom_call" | custom-call | flops 5000000000 | bytes 15000000 | tf_op jit(solution)/shard_map/feed/pallas_call | solution.py:376
  42.4 1.7 collective-permute-start.6
  45.1 4.2 %feed.3 = (f32[192,768]{1,0:T(8,128)S(1)}, f32[192,128]{1,0:T(8,128)S(1)}, bf16[192,768]{1,0:T(8,128)(2,1)S(1)}, bf16[192,1536]{1,0:T(8,128)(2,1)S(1)}, f32[192,...) custom-call(f32[8,128]{1,0:T(8,128)S(1)} %get-tuple-element.121.refs_0_, ...), custom_call_target="tpu_custom_call" | custom-call | flops 5000000000 | bytes 15000000 | tf_op jit(solution)/shard_map/feed/pallas_call | solution.py:376
  49.8 8.9 %collective-permute-done.6.refs_2_ = f32[192,768]{1,0:T(8,128)S(1)} collective-permute-done((f32[192,768]{1,0:T(8,128)S(1)}, f32[192,768]{1,0:T(8,128)S(1)}, u32[]{:S(2)}, u32[]{:S(2)}) %collective-permute-start.6) | collective-permute-done | bytes 589856 | tf_op jit(solution)/shard_map/ppermute | solution.py:394
  58.7 3.4 %feed_back.2 = (bf16[192,768]{1,0:T(8,128)(2,1)S(1)}, f32[192,768]{1,0:T(8,128)S(1)}, bf16[192,768]{1,0:T(8,128)(2,1)S(1)}, bf16[192,1536]{1,0:T(8,128)(2,1)S(1)...) custom-call(f32[8,128]{1,0:T(8,128)S(1)} %get-tuple-element.123.refs_0_, ...), custom_call_target="tpu_custom_call" | custom-call | flops 5000000000 | bytes 15000000 | tf_op jit(solution)/shard_map/feed_back/pallas_call | solution.py:376
  62.1 3.8 %collective-permute-done.7.refs_2_ = f32[192,768]{1,0:T(8,128)S(1)} collective-permute-done((f32[192,768]{1,0:T(8,128)S(1)}, f32[192,768]{1,0:T(8,128)S(1)}, u32[]{:S(2)}, u32[]{:S(2)}) %collective-permute-start.7) | collective-permute-done | bytes 589856 | tf_op jit(solution)/shard_map/ppermute | solution.py:394
  65.9 3.3 %feed_back.3 = (bf16[192,768]{1,0:T(8,128)(2,1)S(1)}, f32[192,768]{1,0:T(8,128)S(1)}, bf16[192,768]{1,0:T(8,128)(2,1)S(1)}, bf16[192,1536]{1,0:T(8,128)(2,1)S(1)...) custom-call(f32[8,128]{1,0:T(8,128)S(1)} %get-tuple-element.128.refs_0_, ...), custom_call_target="tpu_custom_call" | custom-call | flops 5000000000 | bytes 15000000 | tf_op jit(solution)/shard_map/feed_back/pallas_call | solution.py:376
  69.2 2.9 %outer.3 = (f32[192,1536]{1,0:T(8,128)S(1)}, f32[192,1536]{1,0:T(8,128)S(1)}, f32[384,1536]{1,0:T(8,128)S(1)}, f32[8,128]{1,0:T(8,128)S(1)}) custom-call(f32[8,128]{1,0:T(8,128)S(1)} %get-tuple-element.133.refs_0_, s32[3]{0:T(128)S(1)} %pad_add_fusion.refs_0_.refs_1_, bf16[192,768]{1,0:T(8,128)(2,1)S(1)} %get-tuple-element.134.refs_2_, ...), custom_call_target="tpu_custom_call" | custom-call | flops 3000000000 | bytes 9000000 | tf_op jit(solution)/shard_map/outer/pallas_call | solution.py:376
  72.8 2.9 %outer.4 = (f32[192,1536]{1,0:T(8,128)S(1)}, f32[192,1536]{1,0:T(8,128)S(1)}, f32[384,1536]{1,0:T(8,128)S(1)}, f32[8,128]{1,0:T(8,128)S(1)}) custom-call(f32[8,128]{1,0:T(8,128)S(1)} %get-tuple-element.138.refs_0_, s32[3]{0:T(128)S(1)} %pad_add_fusion.refs_0_.refs_1_, bf16[192,768]{1,0:T(8,128)(2,1)S(1)} %get-tuple-element.139.refs_2_, ...), custom_call_target="tpu_custom_call" | custom-call | flops 3000000000 | bytes 9000000 | tf_op jit(solution)/shard_map/outer/pallas_call | solution.py:376
  80.3 11.9 %collective-permute-done.10.refs_3_ = f32[96,1536]{1,0:T(8,128)S(1)} collective-permute-done((f32[96,1536]{1,0:T(8,128)S(1)}, f32[96,1536]{1,0:T(8,128)S(1)}, u32[]{:S(2)}, u32[]{:S(2)}) %collective-permute-start.10) | collective-permute-done | bytes 589856 | tf_op jit(solution)/shard_map/ppermute | solution.py:397
  94.3 10.7 %collective-permute-done.12.refs_6_ = f32[192,768]{1,0:T(8,128)S(1)} collective-permute-done((f32[192,768]{1,0:T(8,128)S(1)}, f32[192,768]{1,0:T(8,128)S(1)}, u32[]{:S(2)}, u32[]{:S(2)}) %collective-permute-start.12) | collective-permute-done | bytes 589856 | tf_op jit(solution)/shard_map/ppermute | solution.py:394
  107.6 4.6 %attend_back.1 = (bf16[384,1536]{1,0:T(8,128)(2,1)S(1)}, f32[8,1536]{1,0:T(8,128)S(1)}, f32[8,128]{1,0:T(8,128)S(1)}) custom-call(f32[8,128]{1,0:T(8,128)S(1)} %get-tuple-element.169.refs_0_, bf16[384,768]{1,0:T(8,128)(2,1)S(1)} %get-tuple-element.170.refs_1_.refs_3_, bf16[384,768]{1,0:T(8,128)(2,1)S(1)} %copy-done.9, bf16[384,1152]{1,0:T(8,128)(2,1)S(1)} %copy-done.19, ...), custom_call_target="tpu_custom_call" | custom-call | flops 6000000000 | bytes 18000000 | tf_op jit(solution)/shard_map/attend_back/pallas_call | solution.py:376
  112.2 3.6 %outer.5 = (f32[192,1536]{1,0:T(8,128)S(1)}, f32[192,1536]{1,0:T(8,128)S(1)}, f32[384,1536]{1,0:T(8,128)S(1)}, f32[8,128]{1,0:T(8,128)S(1)}) custom-call(f32[8,128]{1,0:T(8,128)S(1)} %get-tuple-element.173.refs_0_, s32[3]{0:T(128)S(1)} %pad_add_fusion.refs_0_.refs_1_, bf16[384,768]{1,0:T(8,128)(2,1)S(1)} %copy-done.11, ...), custom_call_target="tpu_custom_call" | custom-call | flops 3000000000 | bytes 9000000 | tf_op jit(solution)/shard_map/outer/pallas_call | solution.py:376
  120.0 12.1 %collective-permute-done.17.refs_3_ = f32[96,1536]{1,0:T(8,128)S(1)} collective-permute-done((f32[96,1536]{1,0:T(8,128)S(1)}, f32[96,1536]{1,0:T(8,128)S(1)}, u32[]{:S(2)}, u32[]{:S(2)}) %collective-permute-start.17) | collective-permute-done | bytes 589856 | tf_op jit(solution)/shard_map/ppermute | solution.py:397
  132.1 2.2 %collective-permute-start.35 = (f32[48,1536]{1,0:T(8,128)S(1)}, f32[48,1536]{1,0:T(8,128)S(1)}, u32[]{:S(2)}, u32[]{:S(2)}) collective-permute-start(f32[48,1536]{1,0:T(8,128)S(1)} %get-tuple-element.215), channel_id=1, source_target_pairs={{0,16},{2,18},{4,20},{6,22},{8,24},{10,26},{12,28},{14,30},{16,0},... | collective-permute-start | bytes 884744 | tf_op jit(solution)/shard_map/ppermute | solution.py:397
  140.4 4.9 %collective-permute-done.20.refs_2_ = f32[8,1536]{1,0:T(8,128)S(1)} collective-permute-done((f32[8,1536]{1,0:T(8,128)S(1)}, f32[8,1536]{1,0:T(8,128)S(1)}, u32[]{:S(2)}, u32[]{:S(2)}) %collective-permute-start.20) | collective-permute-done | bytes 49184 | tf_op jit(solution)/shard_map/ppermute | solution.py:397
  150.5 1.8 collective-permute-start.33
  153.1 5.3 %collective-permute-done.32 = f32[48,1536]{1,0:T(8,128)S(1)} collective-permute-done((f32[48,1536]{1,0:T(8,128)S(1)}, f32[48,1536]{1,0:T(8,128)S(1)}, u32[]{:S(2)}, u32[]{:S(2)}) %collective-permute-start.32) | collective-permute-done | bytes 294944 | tf_op jit(solution)/shard_map/ppermute | solution.py:397
  158.4 2.1 %collective-permute-start.27 = (f32[96,1536]{1,0:T(8,128)S(1)}, f32[96,1536]{1,0:T(8,128)S(1)}, u32[]{:S(2)}, u32[]{:S(2)}) collective-permute-start(f32[96,1536]{1,0:T(8,128)S(1)} %get-tuple-element.202), channel_id=1, source_target_pairs={{0,4},{2,6},{4,0},{6,2},{8,12},{10,14},{12,8},{14,10},{16,20},{18,... | collective-permute-start | bytes 1769480 | tf_op jit(solution)/shard_map/ppermute | solution.py:397
  160.5 5.1 %collective-permute-done.33 = f32[48,1536]{1,0:T(8,128)S(1)} collective-permute-done((f32[48,1536]{1,0:T(8,128)S(1)}, f32[48,1536]{1,0:T(8,128)S(1)}, u32[]{:S(2)}, u32[]{:S(2)}) %collective-permute-start.33) | collective-permute-done | bytes 294944 | tf_op jit(solution)/shard_map/ppermute | solution.py:397
  166.4 2.1 %collective-permute-start.28 = (f32[48,1536]{1,0:T(8,128)S(1)}, f32[48,1536]{1,0:T(8,128)S(1)}, u32[]{:S(2)}, u32[]{:S(2)}) collective-permute-start(f32[48,1536]{1,0:T(8,128)S(1)} %get-tuple-element.203), channel_id=1, source_target_pairs={{0,8},{2,10},{4,12},{6,14},{8,0},{10,2},{12,4},{14,6},{16,24},{18,... | collective-permute-start | bytes 884744 | tf_op jit(solution)/shard_map/ppermute | solution.py:397
  168.5 1.7 collective-permute-done.25.refs_2_
  170.9 5.2 %collective-permute-done.26.refs_3_ = f32[384,768]{1,0:T(8,128)S(1)} collective-permute-done((f32[384,768]{1,0:T(8,128)S(1)}, f32[384,768]{1,0:T(8,128)S(1)}, u32[]{:S(2)}, u32[]{:S(2)}) %collective-permute-start.26) | collective-permute-done | bytes 1179680 | tf_op jit(solution)/shard_map/ppermute | solution.py:394
  179.3 2.6 %collective-permute-start.31 = (f32[48,1536]{1,0:T(8,128)}, f32[48,1536]{1,0:T(8,128)}, u32[]{:S(2)}, u32[]{:S(2)}) collective-permute-start(f32[48,1536]{1,0:T(8,128)} %get-tuple-element.208), channel_id=1, source_target_pairs={{0,16},{2,18},{4,20},{6,22},{8,24},{10,26},{12,28},{14,30},{16,0},... | collective-permute-start | bytes 884744 | tf_op jit(solution)/shard_map/ppermute | solution.py:397
  185.2 6.5 %collective-permute-done.30.refs_4_ = f32[48,1536]{1,0:T(8,128)} collective-permute-done((f32[48,1536]{1,0:T(8,128)}, f32[48,1536]{1,0:T(8,128)}, u32[]{:S(2)}, u32[]{:S(2)}) %collective-permute-start.30) | collective-permute-done | bytes 294944 | tf_op jit(solution)/shard_map/ppermute | solution.py:397
  192.7 1.8 spread.1
  (153 shorter events, 51.3 us)
Async XLA Ops:
  6.7 10.0 %collective-permute-start.1 = (f32[96,768]{1,0:T(8,128)S(1)}, f32[96,768]{1,0:T(8,128)S(1)}, u32[]{:S(2)}, u32[]{:S(2)}) collective-permute-start(f32[96,768]{1,0:T(8,128)S(1)} %get-tuple-element.120), channel_id=1, source_target_pairs={{0,1},{1,0},{2,3},{3,2},{4,5},{5,4},{6,7},{7,6},{8,9},{9,8},{10,11... | collective-permute-start | bytes 884744 | tf_op jit(solution)/shard_map/ppermute | solution.py:394
  16.7 8.2 %collective-permute-start.2 = (f32[96,768]{1,0:T(8,128)S(1)}, f32[96,768]{1,0:T(8,128)S(1)}, u32[]{:S(2)}, u32[]{:S(2)}) collective-permute-start(f32[96,768]{1,0:T(8,128)S(1)} %collective-permute-done.1.refs_6_), channel_id=1, source_target_pairs={{0,4},{2,6},{4,0},{6,2},{8,12},{10,14},{12,8},{14,10},{16,20},{18,... | collective-permute-start | bytes 884744 | tf_op jit(solution)/shard_map/ppermute | solution.py:397
  22.7 9.8 %collective-permute-start = (f32[192,384]{1,0:T(8,128)S(1)}, f32[192,384]{1,0:T(8,128)S(1)}, u32[]{:S(2)}, u32[]{:S(2)}) collective-permute-start(f32[192,384]{1,0:T(8,128)S(1)} %get-tuple-element.119), channel_id=1, source_target_pairs={{0,1},{1,0},{2,3},{3,2},{4,5},{5,4},{6,7},{7,6},{8,9},{9,8},{10,11... | collective-permute-start | bytes 884744 | tf_op jit(solution)/shard_map/ppermute | solution.py:394
  24.2 9.0 %collective-permute-start.3 = (f32[96,768]{1,0:T(8,128)S(1)}, f32[96,768]{1,0:T(8,128)S(1)}, u32[]{:S(2)}, u32[]{:S(2)}) collective-permute-start(f32[96,768]{1,0:T(8,128)S(1)} %collective-permute-done.1.refs_6_), channel_id=1, source_target_pairs={{0,2},{2,0},{4,6},{6,4},{8,10},{10,8},{12,14},{14,12},{16,18},{18,... | collective-permute-start | bytes 884744 | tf_op jit(solution)/shard_map/ppermute | solution.py:397
  24.9 8.3 %collective-permute-start.4 = (f32[96,768]{1,0:T(8,128)S(1)}, f32[96,768]{1,0:T(8,128)S(1)}, u32[]{:S(2)}, u32[]{:S(2)}) collective-permute-start(f32[96,768]{1,0:T(8,128)S(1)} %collective-permute-done.2.refs_7_), channel_id=1, source_target_pairs={{0,2},{2,0},{4,6},{6,4},{8,10},{10,8},{12,14},{14,12},{16,18},{18,... | collective-permute-start | bytes 884744 | tf_op jit(solution)/shard_map/ppermute | solution.py:397
  24.9 19.2 %collective-permute-start.5 = (f32[192,384]{1,0:T(8,128)S(1)}, f32[192,384]{1,0:T(8,128)}, u32[]{:S(2)}, u32[]{:S(2)}) collective-permute-start(f32[192,384]{1,0:T(8,128)S(1)} %get-tuple-element.122), channel_id=1, source_target_pairs={{0,1},{1,0},{2,3},{3,2},{4,5},{5,4},{6,7},{7,6},{8,9},{9,8},{10,11... | collective-permute-start | bytes 884744 | tf_op jit(solution)/shard_map/ppermute | solution.py:394
  42.4 16.3 %collective-permute-start.6 = (f32[192,768]{1,0:T(8,128)S(1)}, f32[192,768]{1,0:T(8,128)S(1)}, u32[]{:S(2)}, u32[]{:S(2)}) collective-permute-start(f32[192,768]{1,0:T(8,128)S(1)} %get-tuple-element.124.refs_1_), channel_id=1, source_target_pairs={{0,1},{1,0},{2,3},{3,2},{4,5},{5,4},{6,7},{7,6},{8,9},{9,8},{10,11... | collective-permute-start | bytes 1769480 | tf_op jit(solution)/shard_map/ppermute | solution.py:394
  49.3 16.5 %collective-permute-start.7 = (f32[192,768]{1,0:T(8,128)S(1)}, f32[192,768]{1,0:T(8,128)S(1)}, u32[]{:S(2)}, u32[]{:S(2)}) collective-permute-start(f32[192,768]{1,0:T(8,128)S(1)} %get-tuple-element.129.refs_1_), channel_id=1, source_target_pairs={{0,1},{1,0},{2,3},{3,2},{4,5},{5,4},{6,7},{7,6},{8,9},{9,8},{10,11... | collective-permute-start | bytes 1769480 | tf_op jit(solution)/shard_map/ppermute | solution.py:394
  75.7 30.2 %collective-permute-start.13 = (f32[192,1536]{1,0:T(8,128)S(1)}, f32[192,1536]{1,0:T(8,128)S(1)}, u32[]{:S(2)}, u32[]{:S(2)}) collective-permute-start(f32[192,1536]{1,0:T(8,128)S(1)} %get-tuple-element.163), channel_id=1, source_target_pairs={{0,2},{2,0},{4,6},{6,4},{8,10},{10,8},{12,14},{14,12},{16,18},{18,... | collective-permute-start | bytes 3538952 | tf_op jit(solution)/shard_map/ppermute | solution.py:397
  76.0 16.2 %collective-permute-start.10 = (f32[96,1536]{1,0:T(8,128)S(1)}, f32[96,1536]{1,0:T(8,128)S(1)}, u32[]{:S(2)}, u32[]{:S(2)}) collective-permute-start(f32[96,1536]{1,0:T(8,128)S(1)} %get-tuple-element.149), channel_id=1, source_target_pairs={{0,4},{2,6},{4,0},{6,2},{8,12},{10,14},{12,8},{14,10},{16,20},{18,... | collective-permute-start | bytes 1769480 | tf_op jit(solution)/shard_map/ppermute | solution.py:397
  77.0 16.2 %collective-permute-start.11 = (f32[192,768]{1,0:T(8,128)S(1)}, f32[192,768]{1,0:T(8,128)S(1)}, u32[]{:S(2)}, u32[]{:S(2)}) collective-permute-start(f32[192,768]{1,0:T(8,128)S(1)} %get-tuple-element.153.refs_3_), channel_id=1, source_target_pairs={{0,1},{1,0},{2,3},{3,2},{4,5},{5,4},{6,7},{7,6},{8,9},{9,8},{10,11... | collective-permute-start | bytes 1769480 | tf_op jit(solution)/shard_map/ppermute | solution.py:394
  78.1 26.9 %collective-permute-start.12 = (f32[192,768]{1,0:T(8,128)S(1)}, f32[192,768]{1,0:T(8,128)S(1)}, u32[]{:S(2)}, u32[]{:S(2)}) collective-permute-start(f32[192,768]{1,0:T(8,128)S(1)} %get-tuple-element.154.refs_4_), channel_id=1, source_target_pairs={{0,1},{1,0},{2,3},{3,2},{4,5},{5,4},{6,7},{7,6},{8,9},{9,8},{10,11... | collective-permute-start | bytes 1769480 | tf_op jit(solution)/shard_map/ppermute | solution.py:394
  79.1 27.3 %collective-permute-start.14 = (f32[96,1536]{1,0:T(8,128)S(1)}, f32[96,1536]{1,0:T(8,128)S(1)}, u32[]{:S(2)}, u32[]{:S(2)}) collective-permute-start(f32[96,1536]{1,0:T(8,128)S(1)} %get-tuple-element.167), channel_id=1, source_target_pairs={{0,4},{2,6},{4,0},{6,2},{8,12},{10,14},{12,8},{14,10},{16,20},{18,... | collective-permute-start | bytes 1769480 | tf_op jit(solution)/shard_map/ppermute | solution.py:397
  92.2 27.8 %collective-permute-start.16 = (f32[192,1536]{1,0:T(8,128)S(1)}, f32[192,1536]{1,0:T(8,128)S(1)}, u32[]{:S(2)}, u32[]{:S(2)}) collective-permute-start(f32[192,1536]{1,0:T(8,128)S(1)} %get-tuple-element.176), channel_id=1, source_target_pairs={{0,2},{2,0},{4,6},{6,4},{8,10},{10,8},{12,14},{14,12},{16,18},{18,... | collective-permute-start | bytes 3538952 | tf_op jit(solution)/shard_map/ppermute | solution.py:397
  93.1 13.3 %collective-permute-start.15 = (f32[48,1536]{1,0:T(8,128)S(1)}, f32[48,1536]{1,0:T(8,128)S(1)}, u32[]{:S(2)}, u32[]{:S(2)}) collective-permute-start(f32[48,1536]{1,0:T(8,128)S(1)} %get-tuple-element.168), channel_id=1, source_target_pairs={{0,8},{2,10},{4,12},{6,14},{8,0},{10,2},{12,4},{14,6},{16,24},{18,... | collective-permute-start | bytes 884744 | tf_op jit(solution)/shard_map/ppermute | solution.py:397
  115.8 18.5 %collective-permute-start.18 = (f32[192,1536]{1,0:T(8,128)S(1)}, f32[192,1536]{1,0:T(8,128)S(1)}, u32[]{:S(2)}, u32[]{:S(2)}) collective-permute-start(f32[192,1536]{1,0:T(8,128)S(1)} %get-tuple-element.180), channel_id=1, source_target_pairs={{0,2},{2,0},{4,6},{6,4},{8,10},{10,8},{12,14},{14,12},{16,18},{18,... | collective-permute-start | bytes 3538952 | tf_op jit(solution)/shard_map/ppermute | solution.py:397
  115.9 16.2 %collective-permute-start.17 = (f32[96,1536]{1,0:T(8,128)S(1)}, f32[96,1536]{1,0:T(8,128)S(1)}, u32[]{:S(2)}, u32[]{:S(2)}) collective-permute-start(f32[96,1536]{1,0:T(8,128)S(1)} %get-tuple-element.177), channel_id=1, source_target_pairs={{0,4},{2,6},{4,0},{6,2},{8,12},{10,14},{12,8},{14,10},{16,20},{18,... | collective-permute-start | bytes 1769480 | tf_op jit(solution)/shard_map/ppermute | solution.py:397
  117.9 31.1 %collective-permute-start.34 = (f32[48,1536]{1,0:T(8,128)S(1)}, f32[48,1536]{1,0:T(8,128)S(1)}, u32[]{:S(2)}, u32[]{:S(2)}) collective-permute-start(f32[48,1536]{1,0:T(8,128)S(1)} %get-tuple-element.214), channel_id=1, source_target_pairs={{0,8},{2,10},{4,12},{6,14},{8,0},{10,2},{12,4},{14,6},{16,24},{18,... | collective-permute-start | bytes 884744 | tf_op jit(solution)/shard_map/ppermute | solution.py:397
  119.5 25.9 %collective-permute-start.21 = (f32[96,1536]{1,0:T(8,128)S(1)}, f32[96,1536]{1,0:T(8,128)S(1)}, u32[]{:S(2)}, u32[]{:S(2)}) collective-permute-start(f32[96,1536]{1,0:T(8,128)S(1)} %get-tuple-element.189), channel_id=1, source_target_pairs={{0,4},{2,6},{4,0},{6,2},{8,12},{10,14},{12,8},{14,10},{16,20},{18,... | collective-permute-start | bytes 1769480 | tf_op jit(solution)/shard_map/ppermute | solution.py:397
  120.0 16.2 %collective-permute-start.19 = (f32[8,1536]{1,0:T(8,128)S(1)}, f32[8,1536]{1,0:T(8,128)S(1)}, u32[]{:S(2)}, u32[]{:S(2)}) collective-permute-start(f32[8,1536]{1,0:T(8,128)S(1)} %get-tuple-element.183.refs_1_), channel_id=1, source_target_pairs={{0,2},{2,0},{4,6},{6,4},{8,10},{10,8},{12,14},{14,12},{16,18},{18,... | collective-permute-start | bytes 147464 | tf_op jit(solution)/shard_map/ppermute | solution.py:397
  132.1 18.5 %collective-permute-start.35 = (f32[48,1536]{1,0:T(8,128)S(1)}, f32[48,1536]{1,0:T(8,128)S(1)}, u32[]{:S(2)}, u32[]{:S(2)}) collective-permute-start(f32[48,1536]{1,0:T(8,128)S(1)} %get-tuple-element.215), channel_id=1, source_target_pairs={{0,16},{2,18},{4,20},{6,22},{8,24},{10,26},{12,28},{14,30},{16,0},... | collective-permute-start | bytes 884744 | tf_op jit(solution)/shard_map/ppermute | solution.py:397
  134.3 13.5 %collective-permute-start.22 = (f32[48,1536]{1,0:T(8,128)S(1)}, f32[48,1536]{1,0:T(8,128)S(1)}, u32[]{:S(2)}, u32[]{:S(2)}) collective-permute-start(f32[48,1536]{1,0:T(8,128)S(1)} %get-tuple-element.190), channel_id=1, source_target_pairs={{0,8},{2,10},{4,12},{6,14},{8,0},{10,2},{12,4},{14,6},{16,24},{18,... | collective-permute-start | bytes 884744 | tf_op jit(solution)/shard_map/ppermute | solution.py:397
  145.3 21.0 %collective-permute-start.23 = (f32[192,1536]{1,0:T(8,128)S(1)}, f32[192,1536]{1,0:T(8,128)S(1)}, u32[]{:S(2)}, u32[]{:S(2)}) collective-permute-start(f32[192,1536]{1,0:T(8,128)S(1)} %get-tuple-element.192), channel_id=1, source_target_pairs={{0,2},{2,0},{4,6},{6,4},{8,10},{10,8},{12,14},{14,12},{16,18},{18,... | collective-permute-start | bytes 3538952 | tf_op jit(solution)/shard_map/ppermute | solution.py:397
  145.3 13.1 %collective-permute-start.32 = (f32[48,1536]{1,0:T(8,128)S(1)}, f32[48,1536]{1,0:T(8,128)S(1)}, u32[]{:S(2)}, u32[]{:S(2)}) collective-permute-start(f32[48,1536]{1,0:T(8,128)S(1)} %get-tuple-element.212), channel_id=1, source_target_pairs={{0,8},{2,10},{4,12},{6,14},{8,0},{10,2},{12,4},{14,6},{16,24},{18,... | collective-permute-start | bytes 884744 | tf_op jit(solution)/shard_map/ppermute | solution.py:397
  147.8 18.5 %collective-permute-start.24 = (f32[96,1536]{1,0:T(8,128)S(1)}, f32[96,1536]{1,0:T(8,128)S(1)}, u32[]{:S(2)}, u32[]{:S(2)}) collective-permute-start(f32[96,1536]{1,0:T(8,128)S(1)} %get-tuple-element.193), channel_id=1, source_target_pairs={{0,4},{2,6},{4,0},{6,2},{8,12},{10,14},{12,8},{14,10},{16,20},{18,... | collective-permute-start | bytes 1769480 | tf_op jit(solution)/shard_map/ppermute | solution.py:397
  149.0 27.1 %collective-permute-start.26 = (f32[384,768]{1,0:T(8,128)S(1)}, f32[384,768]{1,0:T(8,128)S(1)}, u32[]{:S(2)}, u32[]{:S(2)}) collective-permute-start(f32[384,768]{1,0:T(8,128)S(1)} %get-tuple-element.198.refs_2_), channel_id=1, source_target_pairs={{0,1},{1,0},{2,3},{3,2},{4,5},{5,4},{6,7},{7,6},{8,9},{9,8},{10,11... | collective-permute-start | bytes 3538952 | tf_op jit(solution)/shard_map/ppermute | solution.py:394
  150.5 15.0 %collective-permute-start.33 = (f32[48,1536]{1,0:T(8,128)S(1)}, f32[48,1536]{1,0:T(8,128)S(1)}, u32[]{:S(2)}, u32[]{:S(2)}) collective-permute-start(f32[48,1536]{1,0:T(8,128)S(1)} %get-tuple-element.213), channel_id=1, source_target_pairs={{0,16},{2,18},{4,20},{6,22},{8,24},{10,26},{12,28},{14,30},{16,0},... | collective-permute-start | bytes 884744 | tf_op jit(solution)/shard_map/ppermute | solution.py:397
  158.4 20.0 %collective-permute-start.27 = (f32[96,1536]{1,0:T(8,128)S(1)}, f32[96,1536]{1,0:T(8,128)S(1)}, u32[]{:S(2)}, u32[]{:S(2)}) collective-permute-start(f32[96,1536]{1,0:T(8,128)S(1)} %get-tuple-element.202), channel_id=1, source_target_pairs={{0,4},{2,6},{4,0},{6,2},{8,12},{10,14},{12,8},{14,10},{16,20},{18,... | collective-permute-start | bytes 1769480 | tf_op jit(solution)/shard_map/ppermute | solution.py:397
  166.4 12.0 %collective-permute-start.28 = (f32[48,1536]{1,0:T(8,128)S(1)}, f32[48,1536]{1,0:T(8,128)S(1)}, u32[]{:S(2)}, u32[]{:S(2)}) collective-permute-start(f32[48,1536]{1,0:T(8,128)S(1)} %get-tuple-element.203), channel_id=1, source_target_pairs={{0,8},{2,10},{4,12},{6,14},{8,0},{10,2},{12,4},{14,6},{16,24},{18,... | collective-permute-start | bytes 884744 | tf_op jit(solution)/shard_map/ppermute | solution.py:397
  170.3 11.6 %collective-permute-start.29 = (f32[8,1536]{1,0:T(8,128)S(1)}, f32[8,1536]{1,0:T(8,128)S(1)}, u32[]{:S(2)}, u32[]{:S(2)}) collective-permute-start(f32[8,1536]{1,0:T(8,128)S(1)} %get-tuple-element.205.refs_1_), channel_id=1, source_target_pairs={{0,16},{2,18},{4,20},{6,22},{8,24},{10,26},{12,28},{14,30},{16,0},... | collective-permute-start | bytes 147464 | tf_op jit(solution)/shard_map/ppermute | solution.py:397
  177.9 13.7 %collective-permute-start.30 = (f32[48,1536]{1,0:T(8,128)}, f32[48,1536]{1,0:T(8,128)}, u32[]{:S(2)}, u32[]{:S(2)}) collective-permute-start(f32[48,1536]{1,0:T(8,128)} %get-tuple-element.207), channel_id=1, source_target_pairs={{0,8},{2,10},{4,12},{6,14},{8,0},{10,2},{12,4},{14,6},{16,24},{18,... | collective-permute-start | bytes 884744 | tf_op jit(solution)/shard_map/ppermute | solution.py:397
  179.3 12.4 %collective-permute-start.31 = (f32[48,1536]{1,0:T(8,128)}, f32[48,1536]{1,0:T(8,128)}, u32[]{:S(2)}, u32[]{:S(2)}) collective-permute-start(f32[48,1536]{1,0:T(8,128)} %get-tuple-element.208), channel_id=1, source_target_pairs={{0,16},{2,18},{4,20},{6,22},{8,24},{10,26},{12,28},{14,30},{16,0},... | collective-permute-start | bytes 884744 | tf_op jit(solution)/shard_map/ppermute | solution.py:397
  (35 other events, 185.9 us)

commit v3 on v2

v3 whole, which is shorter than its diff:
```python
import functools

import jax
import jax.numpy as jnp
from jax import lax
from jax.experimental import pallas as pl
from jax.experimental.pallas import tpu as pltpu
from jax.sharding import PartitionSpec as P

HEAD = 64
NEG_FILL = -1e30
EPS_NORM = 1e-12
LANES = 128
F32 = jnp.float32
LOW = jnp.bfloat16
MIB = 1 << 20


def dot(a, b):
    return lax.dot_general(a, b, (((1,), (0,)), ((), ())), preferred_element_type=F32)


def dot_nt(a, b):
    return lax.dot_general(a, b, (((1,), (1,)), ((), ())), preferred_element_type=F32)


def whole(shape):
    return pl.BlockSpec(shape, lambda *_: (0,) * len(shape))


def params(limit):
    return pltpu.CompilerParams(vmem_limit_bytes=limit * MIB)


def cost(flops):
    return pl.CostEstimate(flops=flops, bytes_accessed=10**6, transcendentals=0)


def key_mask(lengths_ref, pad_ref, rows):
    seqs = lengths_ref.shape[1]
    key_at = lax.broadcasted_iota(jnp.int32, (rows, LANES), 0)
    query_at = lax.broadcasted_iota(jnp.int32, (8, rows), 1)
    key_seg = jnp.zeros((rows, LANES), jnp.int32)
    query_seg = jnp.zeros((8, rows), jnp.int32)
    end = jnp.int32(0)
    for i in range(seqs):
        end = end + lengths_ref[0, i]
        key_seg = key_seg + (key_at >= end).astype(jnp.int32)
        query_seg = query_seg + (query_at >= end).astype(jnp.int32)
    pad = jnp.broadcast_to(pad_ref[...].astype(F32).reshape(1, rows), (LANES, rows)).T
    pieces = []
    for j in range(rows // LANES):
        span = slice(j * LANES, (j + 1) * LANES)
        same = key_seg == query_seg[0:1, span]
        usable = (pad == 1.0) | (key_at == query_at[0:1, span])
        pieces.append(jnp.where(same & usable, 0.0, NEG_FILL))
    return jnp.concatenate(pieces, 1)


def halves():
    lane = lax.broadcasted_iota(jnp.int32, (1, LANES), 1)
    left = (lane < HEAD).astype(F32)
    return left.astype(LOW), (1.0 - left).astype(LOW)


def fetch(sources, targets, sems):
    copies = [pltpu.make_async_copy(source, target, sems.at[i]) for i, (source, target) in enumerate(zip(sources, targets))]
    for copy in copies:
        copy.start()
    return copies


def attend(
    blocks, x_hbm, w_hbm, b_ref, lengths_ref, pad_ref, qkv_hbm, ctx_hbm, lse_ref, *rest
):
    wide_refs, (x_ref, w_ref, qkv_ref, ctx_ref, sems) = rest[:-5], rest[-5:]
    rows = x_ref.shape[0]
    local = w_ref.shape[2]
    scale = float(HEAD) ** (-0.5)
    came = fetch([x_hbm] + [w_hbm.at[i] for i in range(3)], [x_ref] + [w_ref.at[i] for i in range(3)], sems)
    bias = key_mask(lengths_ref, pad_ref, rows)
    sides = halves()
    came[0].wait()
    x = x_ref[...]
    came[1].wait()
    qkv_ref[:, 0:local] = ((dot(x, w_ref[0]) + b_ref[0:1, :].astype(F32)) * scale).astype(LOW)
    came[2].wait()
    qkv_ref[:, local : 2 * local] = dot(x, w_ref[1]).astype(LOW)
    came[3].wait()
    qkv_ref[:, 2 * local :] = (dot(x, w_ref[2]) + b_ref[1:2, :].astype(F32)).astype(LOW)
    saved = pltpu.make_async_copy(qkv_ref, qkv_hbm, sems.at[4])
    saved.start()
    for pair in range(local // LANES):
        at = pair * LANES
        span = slice(at, at + LANES)
        query = qkv_ref[:, span]
        keys = qkv_ref[:, local + at : local + at + LANES]
        flipped = qkv_ref[:, 2 * local + at : 2 * local + at + LANES].T
        parts = []
        for side in range(2):
            scores = dot_nt(keys * sides[side], query) + bias
            top = jnp.max(scores, 0, keepdims=True)
            expo = jnp.exp(scores - top)
            total = jnp.sum(expo, 0, keepdims=True)
            probs = (expo * (1.0 / total)).astype(LOW)
            parts.append(dot(flipped[side * HEAD : (side + 1) * HEAD], probs))
            head = 2 * pair + side
            lse_ref[head : head + 1, :] = top + jnp.log(total)
        context = jnp.concatenate(parts, 0).T.astype(LOW)
        ctx_ref[:, span] = context
        start = 0
        for wide_ref, size in zip(wide_refs, blocks):
            wide_ref[:, span] = context[start : start + size].astype(F32)
            start += size
    kept = pltpu.make_async_copy(ctx_ref, ctx_hbm, sems.at[5])
    kept.start()
    saved.wait()
    kept.wait()


def relay(in_ref, *refs):
    vectors = refs[:6]
    out_ref, vec_ref = refs[-2:]
    out_ref[...] = in_ref[...]
    vec_ref[...] = jnp.zeros(vec_ref.shape, F32)
    for i, ref in enumerate(vectors):
        vec_ref[i : i + 1, :] = ref[...].astype(F32).reshape(1, -1)


def norm_rows(value):
    centered = value - jnp.mean(value, -1, keepdims=True)
    inverse = lax.rsqrt(jnp.mean(centered * centered, -1, keepdims=True) + EPS_NORM)
    return centered * inverse, inverse


def norm_back(grad, normed, inverse, gain):
    scaled = grad * gain
    return inverse * (
        scaled
        - jnp.mean(scaled, -1, keepdims=True)
        - normed * jnp.mean(scaled * normed, -1, keepdims=True)
    )


def row(ref):
    return ref[...].astype(F32)


def feed(taken, tile, far_parts, place_ref, x_hbm, own_hbm, far_hbm, w_own_hbm, w_near_hbm, *refs):
    w_fars, refs = refs[:far_parts], refs[far_parts:]
    vec_ref, b_up_ref, w_up, w_down, normed_ref, inverse_ref, low_ref, act_ref, slope_ref, part_ref = refs[:10]
    x_ref, far_ref, w_far, w_full, ctx_full, sems = refs[10:]
    local = own_hbm.shape[1]
    half = w_near_hbm.shape[0]
    piece = half // far_parts
    hidden = w_up.shape[1]
    core, side = place_ref[0], place_ref[1]
    here = pl.multiple_of(side * local, LANES)
    there = pl.multiple_of((1 - side) * local, LANES)
    spans = [slice(at, at + tile) for at in range(0, hidden, tile)]
    sources = [w_own_hbm, own_hbm.at[taken], far_hbm, x_hbm.at[taken], w_near_hbm] + list(w_fars)
    targets = [w_full.at[pl.ds(here, local)], ctx_full.at[:, pl.ds(here, local)], far_ref, x_ref, w_far.at[0]]
    targets += [w_far.at[1, i * piece : (i + 1) * piece] for i in range(far_parts)]
    for copy in fetch(sources, targets, sems):
        copy.wait()
    for i in range(2):
        at = pl.multiple_of(there + (core ^ i) * half, 16)
        w_full[pl.ds(at, half), :] = w_far[i].astype(LOW)
    ctx_full[:, pl.ds(there, local)] = far_ref[...].astype(LOW)
    attn = dot(ctx_full[...], w_full[...])
    normed, inverse = norm_rows(x_ref[...].astype(F32) + attn + vec_ref[0:1, :])
    normed_ref[...] = normed
    inverse_ref[...] = jnp.broadcast_to(inverse, inverse_ref.shape)
    low = (normed * vec_ref[1:2, :] + vec_ref[2:3, :]).astype(LOW)
    low_ref[...] = low
    b_up = b_up_ref[...].astype(F32).reshape(1, -1)
    for i, span in enumerate(spans):
        pre = dot(low, w_up[:, span]) + b_up[:, span]
        share = 0.5 * (1.0 + lax.erf(pre * 0.7071067811865476))
        act = (pre * share).astype(LOW)
        act_ref[:, span] = act
        slope_ref[:, span] = share + pre * jnp.exp(-0.5 * pre * pre) * 0.3989422804014327
        added = dot(act, w_down[span, :])
        if i == 0:
            part_ref[...] = added
        else:
            part_ref[...] += added


def feed_back(
    taken, tile, own_ref, far_ref, normed_ref, vec_ref, slope_ref, up_hbm, w_up, w_down,
    out_ref, grad_ref, low_ref, pre_ref, part_ref, sums_ref, b_up_ref,
    up_ref, sems,
):
    hidden = w_up.shape[1]
    spans = [slice(at, at + tile) for at in range(0, hidden, tile)]
    came = fetch([up_hbm.at[taken]], [up_ref], sems)
    hidden_rows = normed_ref[...] * vec_ref[1:2, :] + vec_ref[2:3, :]
    normed, inverse = norm_rows(hidden_rows + (own_ref[...] + far_ref[...]) + vec_ref[3:4, :])
    gain = vec_ref[4:5, :]
    out_ref[...] = (normed * gain + vec_ref[5:6, :]).astype(LOW)
    came[0].wait()
    upstream = up_ref[...].astype(F32)
    grad = norm_back(upstream, normed, inverse, gain)
    grad_ref[...] = grad
    low = grad.astype(LOW)
    low_ref[...] = low
    sums_ref[0:1, :] = jnp.sum(upstream * normed, 0, keepdims=True)
    sums_ref[1:2, :] = jnp.sum(upstream, 0, keepdims=True)
    sums_ref[2:3, :] = jnp.sum(grad, 0, keepdims=True)
    sums_ref[3:8, :] = jnp.zeros((5, sums_ref.shape[1]), F32)
    for i, span in enumerate(spans):
        pre = (dot_nt(low, w_down[span, :]) * slope_ref[:, span]).astype(LOW)
        pre_ref[:, span] = pre
        b_up_ref[:, span] = jnp.broadcast_to(jnp.sum(pre.astype(F32), 0, keepdims=True), (8, tile))
        added = dot_nt(pre, w_up[:, span])
        if i == 0:
            part_ref[...] = added
        else:
            part_ref[...] += added


def norm_one_back(own_dr2, own_ref, far_ref, normed_ref, inverse_ref, sums_ref, b_up_ref, vec_ref, *refs):
    before, (dr1_ref, low_ref, bias_ref) = refs[:-3], refs[-3:]
    width = dr1_ref.shape[1]
    grad = own_dr2[...] + (own_ref[...] + far_ref[...])
    norm = normed_ref[...]
    dr1 = norm_back(grad, norm, inverse_ref[:, 0:1], vec_ref[1:2, :])
    dr1_ref[...] = dr1
    low_ref[...] = dr1.astype(LOW)
    bias_ref[...] = before[0][...] if before else jnp.zeros(bias_ref.shape, F32)
    bias_ref[0:3, 0:width] += sums_ref[0:3]
    for i, value in enumerate((grad * norm, grad, dr1)):
        bias_ref[3 + i : 4 + i, 0:width] += jnp.sum(value, 0, keepdims=True)
    bias_ref[6:7, 0 : b_up_ref.shape[1]] += b_up_ref[0:1, :]


def attend_back(
    count, *refs,
):
    attend_back_body(refs[:count], *refs[count:])


def attend_back_body(
    low_refs, w_hbm, qkv_hbm, ctx_hbm, lse_ref, lengths_ref, pad_ref, so_far_ref, e_ref, bias_ref,
    w_ref, qkv_ref, sems,
):
    rows, local = ctx_hbm.shape
    came = fetch([w_hbm, qkv_hbm, ctx_hbm], [w_ref, qkv_ref, e_ref.at[:, 3 * local : 4 * local]], sems)
    scale = float(HEAD) ** (-0.5)
    bias_ref[...] = so_far_ref[...]
    mask = key_mask(lengths_ref, pad_ref, rows)
    sides = halves()
    came[0].wait()
    d_ctx = dot_nt(jnp.concatenate([ref[...] for ref in low_refs], 0), w_ref[...]).astype(LOW)
    came[1].wait()
    for pair in range(local // LANES):
        at = pair * LANES
        span = slice(at, at + LANES)
        query = qkv_ref[:, span]
        keys = qkv_ref[:, local + at : local + at + LANES]
        values = qkv_ref[:, 2 * local + at : 2 * local + at + LANES]
        grads = d_ctx[:, span]
        flipped = keys.T
        d_q = []
        d_k = jnp.zeros((rows, LANES), F32)
        d_v = jnp.zeros((rows, LANES), F32)
        for side in range(2):
            head = 2 * pair + side
            scores = dot_nt(keys * sides[side], query) + mask
            probs = jnp.exp(scores - lse_ref[head : head + 1, :])
            d_p = dot_nt(values * sides[side], grads)
            mixed = jnp.sum(probs * d_p, 0, keepdims=True)
            d_s = (probs * (d_p - mixed)).astype(LOW)
            d_k = d_k + dot(d_s, query * sides[side])
            d_v = d_v + dot(probs.astype(LOW), grads * sides[side])
            d_q.append(dot(flipped[side * HEAD : (side + 1) * HEAD], d_s))
        d_query = jnp.concatenate(d_q, 0).T.astype(LOW).astype(F32) * scale
        d_k = d_k.astype(LOW)
        d_v = d_v.astype(LOW)
        e_ref[:, at : at + LANES] = d_query.astype(LOW)
        e_ref[:, local + at : local + at + LANES] = d_k
        e_ref[:, 2 * local + at : 2 * local + at + LANES] = d_v
        bias_ref[7:8, at : at + LANES] = jnp.sum(d_query, 0, keepdims=True)
        bias_ref[7:8, local + at : local + at + LANES] = jnp.sum(d_v.astype(F32), 0, keepdims=True)
    came[2].wait()


def place_blocks(me, source, target, order, size):
    for i, block in enumerate(order):
        at = pl.multiple_of((me ^ block) * size, size)
        target[i * size : (i + 1) * size, :] = source[pl.ds(at, size), :]


def outer(order, size, splits, kinds, more, place_ref, *refs):
    count = len(splits)
    sides = max(kinds) + 1
    lefts = [refs[:count]] + ([refs[count : count + more]] if more else [])
    rights = refs[count + more : 2 * count + more]
    *sent_refs, keep_ref, flipped, placed = refs[2 * count + more :]
    step = pl.program_id(0)

    @pl.when(step == 0)
    def _():
        for index, group in enumerate(lefts):
            source = jnp.concatenate([ref[...] for ref in group], 0).T
            if order is None:
                placed[index] = source
            else:
                flipped[...] = source
                place_blocks(place_ref[2], flipped, placed.at[index], order, size)

    left = placed[0]
    if sides > 1:
        change = kinds.index(1)
        left = placed[jnp.where(step >= change, 1, 0)]
    right = jnp.concatenate([ref[...] for ref in rights], 0)
    half = keep_ref.shape[0]
    part = half // len(sent_refs)
    for i, ref in enumerate(sent_refs):
        ref[...] = dot(left[i * part : (i + 1) * part], right)
    keep_ref[...] = dot(left[half:], right)


def fold(*refs):
    value = refs[0][...]
    for ref in refs[1:-1]:
        value = value + ref[...]
    refs[-1][...] = value


def fold_blocks(size, counts, *refs):
    out_ref = refs[-1]
    at = 0
    for i, count in enumerate(counts):
        value = refs[at][...]
        for ref in refs[at + 1 : at + count]:
            value = value + ref[...]
        out_ref[i * size : (i + 1) * size, :] = value
        at += count


def back_tokens(e_ref, w_hbm, out_ref, w_ref, sems):
    local = w_ref.shape[2]
    came = fetch([w_hbm.at[i] for i in range(3)], [w_ref.at[i] for i in range(3)], sems)
    for i in range(3):
        came[i].wait()
        added = dot_nt(e_ref[:, i * local : (i + 1) * local], w_ref[i])
        if i == 0:
            out_ref[...] = added
        else:
            out_ref[...] += added


def join(own_ref, far_ref, *refs):
    out_ref, start = refs[-1], 0
    for ref in refs[:-1]:
        span = slice(start, start + ref.shape[0])
        out_ref[span, :] = ref[...] + (own_ref[span, :] + far_ref[span, :])
        start += ref.shape[0]


def spread(local, *refs):
    count = len(refs) - 4
    parts, (qkv_ref, out_ref) = refs[:count], refs[count : count + 2]
    held, sems = refs[-2:]
    size = out_ref.shape[0]
    came = fetch([part.at[0:size] for part in parts], [held.at[i] for i in range(count)], sems)
    for copy in came:
        copy.wait()
    value = held[0]
    for i in range(1, count):
        value = value + held[i]
    for i in range(3):
        qkv_ref[i] = value[:, i * local : (i + 1) * local]
    out_ref[...] = value[:, 3 * local :]


def chained(kernel, inputs, outputs):
    def body(*refs):
        refs[1 + inputs + outputs][...] = jnp.zeros((8, LANES), F32)
        kernel(*refs[1 : 1 + inputs + outputs], *refs[2 + inputs + outputs :])

    return body


def on_device(
    tokens, lengths, pad_mask, w_qkv, b_qv, w_out, b_out, ln1_gain, ln1_bias,
    w_up, b_up, w_down, b_down, ln2_gain, ln2_bias, cotangent,
):
    rows, width = tokens.shape
    local = w_qkv.shape[2]
    heads = local // HEAD
    hidden = w_up.shape[1]
    ranks = lax.axis_size("dp")
    me = lax.axis_index("dp").astype(jnp.int32)
    place_arr = jnp.stack([me % 2, lax.axis_index("tp").astype(jnp.int32), me])
    size = width // ranks
    blocks = [rows // 2] * 2 if rows % 32 == 0 else [rows]
    starts = [sum(blocks[:i]) for i in range(len(blocks))]
    lse_rows = -(-heads // 8) * 8
    shape = jax.ShapeDtypeStruct
    smem = pl.BlockSpec(memory_space=pltpu.SMEM)
    loose = pl.BlockSpec(memory_space=pl.ANY)
    far_off = pl.BlockSpec(memory_space=pltpu.HBM)
    dma = pltpu.SemaphoreType.DMA
    mark = [None]

    def call(kernel, name, operands, in_specs, out_shape, out_specs, grid=(1,), scratch=(), limit=24, flops=10**10):
        before = mark[0] if mark[0] is not None else operands[0]
        *outs, mark[0] = pl.pallas_call(
            chained(kernel, len(operands), len(out_shape)),
            grid=grid,
            out_shape=tuple(out_shape) + (shape((8, LANES), F32),),
            in_specs=[loose] + list(in_specs),
            out_specs=tuple(out_specs) + (whole((8, LANES)),),
            scratch_shapes=list(scratch),
            compiler_params=params(limit),
            cost_estimate=cost(flops),
            name=name,
        )(before, *operands)
        return outs

    def full(*arrays):
        return [whole(array.shape) for array in arrays]

    def swap_tp(array):
        pairs = [(i, i ^ 1) for i in range(lax.axis_size("tp"))]
        return lax.ppermute(array, "tp", pairs)

    def swap_dp(array, bits):
        return lax.ppermute(array, "dp", [(i, i ^ bits) for i in range(ranks)])

    stages = []
    while 1 << len(stages) < ranks:
        stages.append(1 << len(stages))
    order = [0]
    for bit in reversed(stages):
        order = order + [bit + rest for rest in order]
    order = order[ranks // 2 :] + order[: ranks // 2]
    fused = size % 16 == 0
    pad_row = pad_mask
    half = w_out.shape[0] // 2
    w_near = swap_tp(lax.dynamic_slice_in_dim(w_out, (me % 2) * half, half, 0).astype(F32))
    outs = [shape((rows, 3 * local), LOW), shape((rows, local), LOW), shape((lse_rows, rows), F32)]
    outs += [shape((block, local), F32) for block in blocks]
    qkv, context, lse, *wides = call(
        functools.partial(attend, blocks), "attend", [tokens, w_qkv, b_qv, lengths, pad_row],
        [far_off] * 2 + full(b_qv) + [smem] + full(pad_row), outs, [far_off] * 2 + full(*outs[2:]),
        scratch=[
            pltpu.VMEM((rows, width), LOW),
            pltpu.VMEM((3, width, local), LOW),
            pltpu.VMEM((rows, 3 * local), LOW),
            pltpu.VMEM((rows, local), LOW),
            dma((6,)),
        ],
        limit=56,
    )
    fars = [swap_tp(wide) for wide in wides]
    near = pl.BlockSpec(memory_space=pltpu.VMEM)
    params_of = [b_out, ln1_gain, ln1_bias, b_down, ln2_gain, ln2_bias]
    outs = [shape(w_near.shape, F32), shape((8, width), F32)]
    w_near, vectors = call(
        relay, "relay", [w_near, *params_of, w_up, w_down],
        full(w_near, *params_of) + [near, near], outs, full(*outs),
    )
    far_parts = 3 if half % 48 == 0 else 1
    piece = half // far_parts
    w_fars = [swap_dp(w_near[i * piece : (i + 1) * piece], 1) for i in range(far_parts)]

    tile = min(hidden, 512)
    tiles = hidden // tile

    def columns(height, step):
        return pl.BlockSpec((height, step), lambda f: (0, f))

    saved = []
    for begin, block, far in zip(starts, blocks, fars):
        outs = [
            shape((block, width), F32), shape((block, LANES), F32), shape((block, width), LOW),
            shape((block, hidden), LOW), shape((block, hidden), F32), shape((block, width), F32),
        ]
        outs = call(
            functools.partial(feed, slice(begin, begin + block), tile, far_parts), "feed",
            [place_arr, tokens, context, far, w_out, w_near, *w_fars, vectors, b_up, w_up, w_down],
            [smem] + [far_off] * (5 + far_parts) + full(vectors, b_up) + [near] * 2,
            outs, full(*outs),
            scratch=[
                pltpu.VMEM((block, width), LOW),
                pltpu.VMEM((block, local), F32),
                pltpu.VMEM((2, half, width), F32),
                pltpu.VMEM((2 * local, width), LOW),
                pltpu.VMEM((block, 2 * local), LOW),
                dma((5 + far_parts,)),
            ],
        )
        saved.append(outs + [swap_tp(outs[5])])

    back = []
    for begin, block, (normed, inverse, low, act, slope, own, far) in zip(starts, blocks, saved):
        outs = [
            shape((block, width), LOW), shape((block, width), F32), shape((block, width), LOW),
            shape((block, hidden), LOW), shape((block, width), F32), shape((8, width), F32), shape((8, hidden), F32),
        ]
        outs = call(
            functools.partial(feed_back, slice(begin, begin + block), tile), "feed_back",
            [own, far, normed, vectors, slope, cotangent, w_up, w_down],
            full(own, far, normed, vectors, slope) + [far_off] + [near] * 2,
            outs, full(*outs),
            scratch=[pltpu.VMEM((block, width), LOW), dma((1,))],
        )
        back.append(outs + [swap_tp(outs[4])])

    layer_out = jnp.concatenate([outs[0] for outs in back], 0)

    def gradient(lefts, rights, splits, kinds, step, parts):
        wide = step * len(kinds)
        sides = max(kinds) + 1
        outs = [shape((width // 2 // parts, wide), F32)] * parts + [shape((width // 2, wide), F32)]
        outs = call(
            functools.partial(outer, order if fused else None, size, splits, kinds, len(lefts) - len(splits)), "outer",
            [place_arr, *lefts, *rights],
            [smem] + full(*lefts) + [columns(split, step) for split in splits],
            outs, [columns(out.shape[0], step) for out in outs],
            grid=(len(kinds),),
            scratch=[pltpu.VMEM((width, rows), LOW), pltpu.VMEM((sides, width, rows), LOW)],
        )
        if not fused:
            every = jnp.concatenate(outs, 0).reshape(ranks, size, wide)
            every = jnp.take(every, jnp.array(order, jnp.int32) ^ me, axis=0).reshape(width, wide)
            outs = [every[: width // 2], every[width // 2 :]]
        return outs

    def pick(held, begin, end):
        return [(array, first) for array, first in held if first <= begin and end <= first + array.shape[0]]

    def add(held, begin, end):
        wide = held[0][0].shape[1]
        if not fused:
            parts = []
            for row in range(begin, end, size):
                parts.append(functools.reduce(jnp.add, [a[row - f : row - f + size] for a, f in pick(held, row, row + size)]))
            return jnp.concatenate(parts, 0)
        operands, specs, counts = [], [], []
        for row in range(begin, end, size):
            inside = pick(held, row, row + size)
            counts.append(len(inside))
            for array, first in inside:
                operands.append(array)
                specs.append(pl.BlockSpec((size, wide), functools.partial(lambda index, n: (index, 0), (row - first) // size)))
        outs = [shape((end - begin, wide), F32)]
        return call(functools.partial(fold_blocks, size, counts), "fold", operands, specs, outs, full(*outs))[0]

    class Chunk:
        def __init__(self, outs):
            self.held, first = [(outs[-1], 0)], 0
            for out in outs[:-1]:
                self.held.append((swap_dp(out, stages[0]), first))
                first += out.shape[0]
            self.stage = 0

        def step(self):
            self.stage += 1
            half = width // (4 << (self.stage - 1))
            out = add(self.held, half, 2 * half)
            self.held = self.held + [(swap_dp(out, stages[self.stage]), 0)]

        def high(self):
            self.stage += 1
            half = self.half = width // (4 << (self.stage - 1))
            if half == size:
                self.stage -= 1
                self.step()
            else:
                out = add(self.held, half + half // 2, 2 * half)
                self.came = [(swap_dp(out, stages[self.stage]), half // 2)]

        def low(self):
            out = add(self.held, self.half, self.half + self.half // 2)
            self.held = self.held + self.came + [(swap_dp(out, stages[self.stage]), 0)]

        def last(self):
            self.rest()
            return add(self.held, 0, size)

        def rest(self):
            while self.stage < len(stages) - 1:
                self.step()
            return [(array, first) for array, first in self.held if first == 0]

    down = Chunk(gradient([o[2] for o in back], [s[3] for s in saved], blocks, [0] * tiles, tile, 1))
    wide = max(width, hidden, 2 * local)

    def first_norm(i):
        outs = [shape((blocks[i], width), F32), shape((blocks[i], width), LOW), shape((8, wide), F32)]
        operands = [back[i][1], back[i][4], back[i][7], saved[i][0], saved[i][1], back[i][5], back[i][6], vectors]
        operands += [norms[-1][2]] if norms else []
        norms.append(call(norm_one_back, "norm_one_back", operands, full(*operands), outs, full(*outs), flops=2 * 10**10 if i == 0 else 10**10))

    norms = []
    first_norm(0)
    down.step()
    first_norm(1)
    up = Chunk(gradient([s[2] for s in saved], [o[3] for o in back], blocks, [0] * tiles, tile, 1))
    dr1s, lows = [n[0] for n in norms], [n[1] for n in norms]
    outs = [shape((rows, 4 * local), LOW), shape((8, wide), F32)]
    operands = lows + [w_out, qkv, context, lse, lengths, pad_row, norms[-1][2]]
    e, bias = call(
        functools.partial(attend_back, len(lows)), "attend_back", operands,
        full(*lows) + [far_off] * 3 + full(lse) + [smem] + full(pad_row, norms[-1][2]), outs, full(*outs),
        scratch=[pltpu.VMEM((local, width), LOW), pltpu.VMEM((rows, 3 * local), LOW), dma((3,))],
    )
    mixed = Chunk(gradient([tokens] + lows, [e], [rows], [0, 0, 0, 1], local, 2))

    def bias_step(bit):
        far = swap_dp(bias, bit)
        return call(fold, "fold", [bias, far], full(bias, far), [shape(bias.shape, F32)], full(bias))[0]

    down.step()
    up.step()
    outs = [shape((rows, width), F32)]
    (partial,) = call(
        back_tokens, "back_tokens", [e, w_qkv], full(e) + [far_off], outs, full(*outs),
        scratch=[pltpu.VMEM((3, width, local), LOW), dma((3,))],
    )
    partial_far = swap_tp(partial)
    down.step()
    up.step()
    mixed.high()
    mixed.low()
    bias = bias_step(stages[0])
    down = down.last()
    up.step()
    mixed.high()
    mixed.low()
    bias = bias_step(stages[1])
    up = up.last()
    mixed.high()
    bias = bias_step(stages[2])
    mixed = mixed.rest()
    for bit in stages[3:]:
        bias = bias_step(bit)
    (d_tokens,) = call(
        join, "join", [partial, partial_far] + dr1s, full(partial, partial_far, *dr1s), outs, full(*outs)
    )

    def finish(held):
        return functools.reduce(jnp.add, [array[:size] for array, _ in held])

    if fused:
        outs = [shape((3, size, local), F32), shape((size, local), F32)]
        d_w_qkv, d_w_out = call(
            functools.partial(spread, local), "spread", [array for array, _ in mixed],
            [far_off] * len(mixed), outs, full(*outs),
            scratch=[pltpu.VMEM((len(mixed), size, 4 * local), F32), dma((len(mixed),))],
        )
    else:
        last = finish(mixed)
        d_w_qkv = last[:, : 3 * local].reshape(size, 3, local).transpose(1, 0, 2)
        d_w_out = last[:, 3 * local :]
    return (
        layer_out,
        d_tokens,
        d_w_qkv,
        bias[7, : 2 * local].reshape(2, local),
        d_w_out.T,
        bias[5, :width],
        bias[3, :width],
        bias[4, :width],
        up,
        bias[6, :hidden],
        down.T,
        bias[2, :width],
        bias[0, :width],
        bias[1, :width],
    )


def solution(mesh):
    placed = (
        P("dp", None), P("dp", None), P("dp"), P(None, None, "tp"), P(None, "tp"), P("tp", None),
        P(), P(), P(), P(None, "tp"), P("tp"), P("tp", None), P(), P(), P(), P("dp", None),
    )
    return jax.shard_map(
        on_device,
        mesh=mesh,
        in_specs=placed,
        out_specs=(
            P("dp", None), P("dp", None), P(None, "dp", "tp"), P(None, "tp"), P("tp", "dp"), P(), P(), P(),
            P("dp", "tp"), P("tp"), P("tp", "dp"), P(), P(), P(),
        ),
        check_vma=False,
    )
```

time: 197 us -> 181 us (0.919)
  local copies, waits for them, and re-layouts: 19.1 us -> 10.1 us
  waiting for transfers between devices: 92 us -> 85.5 us
  Pallas kernels: 41.7 us -> 44.2 us
    unnamed x62 -> x54, local copies, waits for them, and re-layouts: 16.4 us -> 7.48 us
    ppermute x8, waiting for transfers between devices: 42.5 us -> 38.9 us  [swap_tp(): return lax.ppermute(array, 'tp', pairs)]
    ppermute x28 -> x22, waiting for transfers between devices: 49.5 us -> 46.7 us  [swap_dp(): return lax.ppermute(array, 'dp', [(i, i ^ bits) for i in range(ranks)])]
    pallas_call x33 -> x32, Pallas kernels: 41.7 us -> 44.2 us  [call(): pl.pallas_call(chained(kernel, len(operands), len(out_shape)), grid=grid,...]
    ppermute x28 -> x22, starting transfers between devices: 26.3 us -> 24.3 us  [swap_dp(): return lax.ppermute(array, 'dp', [(i, i ^ bits) for i in range(ranks)])]
  transfers between devices with their start and end apart: 36 -> 30, of which waited for: 16 -> 16; matrix products, arithmetic and copies ran while one was open for 3% -> 2% of each run, Pallas kernels for 16% -> 24%
where the time goes in v3:
time: 181 us; the launch traced here: 180 us
  waiting for transfers between devices  85.5 us (47%)
  Pallas kernels  44.2 us (24%)
  starting transfers between devices  37.3 us (21%)
  local copies, waits for them, and re-layouts  10.1 us (6%)
  other arithmetic  1.94 us (1%)
    ppermute x22, waiting for transfers between devices, swap_dp(): return lax.ppermute(array, 'dp', [(i, i ^ bits) for i in range(ranks)])  46.7 us
    pallas_call x32, Pallas kernels, call(): pl.pallas_call(chained(kernel, len(operands), len(out_shape)), grid=grid,...  44.2 us
    ppermute x8, waiting for transfers between devices, swap_tp(): return lax.ppermute(array, 'tp', pairs)  38.9 us
    ppermute x22, starting transfers between devices, swap_dp(): return lax.ppermute(array, 'dp', [(i, i ^ bits) for i in range(ranks)])  24.3 us
    ppermute x8, starting transfers between devices, swap_tp(): return lax.ppermute(array, 'tp', pairs)  13 us
    unnamed x54, local copies, waits for them, and re-layouts  7.48 us
  transfers between devices with their start and end apart: 30, of which 16 were waited for; matrix products, arithmetic and copies ran while one was open for 2% of the time, Pallas kernels for 24%

profile of v3, /device:TPU:0, one launch (start us, length us, event | category | flops | bytes accessed | tf_op | source)
XLA Modules:
  0.0 180.5 jit_solution(8345874537374685913)
XLA Ops:
  1.8 3.0 %collective-permute-start = (f32[192,768]{1,0:T(8,128)S(1)}, f32[192,768]{1,0:T(8,128)S(1)}, u32[]{:S(2)}, u32[]{:S(2)}) collective-permute-start(f32[192,768]{1,0:T(8,128)S(1)} %dynamic-slice_convert_fusion), channel_id=1, source_target_pairs={{0,1},{1,0},{2,3},{3,2},{4,5},{5,4},{6,7},{7,6},{8,9},{9,8},{10,11... | collective-permute-start | bytes 1769480 | tf_op jit(solution)/shard_map/ppermute | solution.py:429
  4.8 7.7 %attend.1 = (bf16[384,1152]{1,0:T(8,128)(2,1)}, bf16[384,384]{1,0:T(8,128)(2,1)}, f32[8,384]{1,0:T(8,128)}, f32[192,384]{1,0:T(8,128)}, f32[192,384]{1,0:T(8,128)}, /*index=5*/f32[8,128]{1,0:T(8,128)}) custom-call(bf16[384,768]{1,0:T(8,128)(2,1)} %refs_2_.10, bf16[384,768]{1,0:T(8,128)(2,1)} %refs_2_.10, bf16[3,768,384]{2,1,0:T(8,128)(2,1)} %refs_2_.11, ...), custom_call_target="tpu_custom_call" | custom-call | flops 10000000000 | bytes 1000000 | tf_op jit(solution)/shard_map/attend/pallas_call | solution.py:411
  13.1 5.8 %collective-permute-done.refs_1_ = f32[192,768]{1,0:T(8,128)S(1)} collective-permute-done((f32[192,768]{1,0:T(8,128)S(1)}, f32[192,768]{1,0:T(8,128)S(1)}, u32[]{:S(2)}, u32[]{:S(2)}) %collective-permute-start) | collective-permute-done | bytes 589856 | tf_op jit(solution)/shard_map/ppermute | solution.py:429
  21.7 2.1 %collective-permute-start.5 = (f32[192,384]{1,0:T(8,128)}, f32[192,384]{1,0:T(8,128)}, u32[]{:S(2)}, u32[]{:S(2)}) collective-permute-start(f32[192,384]{1,0:T(8,128)} %get-tuple-element.121), channel_id=1, source_target_pairs={{0,1},{1,0},{2,3},{3,2},{4,5},{5,4},{6,7},{7,6},{8,9},{9,8},{10,11... | collective-permute-start | bytes 884744 | tf_op jit(solution)/shard_map/ppermute | solution.py:429
  29.0 4.6 %feed.2 = (f32[192,768]{1,0:T(8,128)S(1)}, f32[192,128]{1,0:T(8,128)S(1)}, bf16[192,768]{1,0:T(8,128)(2,1)S(1)}, bf16[192,1536]{1,0:T(8,128)(2,1)S(1)}, f32[192,...) custom-call(f32[8,128]{1,0:T(8,128)S(1)} %get-tuple-element.115.refs_0_, s32[3]{0:T(128)S(1)} %pad_add_fusion.refs_1_, ...), custom_call_target="tpu_custom_call" | custom-call | flops 10000000000 | bytes 1000000 | tf_op jit(solution)/shard_map/feed/pallas_call | solution.py:411
  33.7 1.8 collective-permute-start.6
  35.5 4.5 %feed.3 = (f32[192,768]{1,0:T(8,128)S(1)}, f32[192,128]{1,0:T(8,128)S(1)}, bf16[192,768]{1,0:T(8,128)(2,1)S(1)}, bf16[192,1536]{1,0:T(8,128)(2,1)S(1)}, f32[192,...) custom-call(f32[8,128]{1,0:T(8,128)S(1)} %get-tuple-element.120.refs_0_, s32[3]{0:T(128)S(1)} %pad_add_fusion.refs_1_, ...), custom_call_target="tpu_custom_call" | custom-call | flops 10000000000 | bytes 1000000 | tf_op jit(solution)/shard_map/feed/pallas_call | solution.py:411
  40.3 9.7 %collective-permute-done.6.refs_2_ = f32[192,768]{1,0:T(8,128)S(1)} collective-permute-done((f32[192,768]{1,0:T(8,128)S(1)}, f32[192,768]{1,0:T(8,128)S(1)}, u32[]{:S(2)}, u32[]{:S(2)}) %collective-permute-start.6) | collective-permute-done | bytes 589856 | tf_op jit(solution)/shard_map/ppermute | solution.py:429
  50.0 2.4 %feed_back.2 = (bf16[192,768]{1,0:T(8,128)(2,1)S(1)}, f32[192,768]{1,0:T(8,128)S(1)}, bf16[192,768]{1,0:T(8,128)(2,1)S(1)}, bf16[192,1536]{1,0:T(8,128)(2,1)S(1)...) custom-call(f32[8,128]{1,0:T(8,128)S(1)} %get-tuple-element.122.refs_0_, ...), custom_call_target="tpu_custom_call" | custom-call | flops 10000000000 | bytes 1000000 | tf_op jit(solution)/shard_map/feed_back/pallas_call | solution.py:411
  52.4 1.8 collective-permute-start.8
  54.2 8.5 %collective-permute-done.7.refs_2_ = f32[192,768]{1,0:T(8,128)S(1)} collective-permute-done((f32[192,768]{1,0:T(8,128)S(1)}, f32[192,768]{1,0:T(8,128)S(1)}, u32[]{:S(2)}, u32[]{:S(2)}) %collective-permute-start.7) | collective-permute-done | bytes 589856 | tf_op jit(solution)/shard_map/ppermute | solution.py:429
  62.6 2.4 %feed_back.3 = (bf16[192,768]{1,0:T(8,128)(2,1)S(1)}, f32[192,768]{1,0:T(8,128)S(1)}, bf16[192,768]{1,0:T(8,128)(2,1)S(1)}, bf16[192,1536]{1,0:T(8,128)(2,1)S(1)...) custom-call(f32[8,128]{1,0:T(8,128)S(1)} %get-tuple-element.127.refs_0_, ...), custom_call_target="tpu_custom_call" | custom-call | flops 10000000000 | bytes 1000000 | tf_op jit(solution)/shard_map/feed_back/pallas_call | solution.py:411
  65.0 2.9 %outer.3 = (f32[384,1536]{1,0:T(8,128)S(1)}, f32[384,1536]{1,0:T(8,128)S(1)}, f32[8,128]{1,0:T(8,128)S(1)}) custom-call(f32[8,128]{1,0:T(8,128)S(1)} %get-tuple-element.132.refs_0_, s32[3]{0:T(128)S(1)} %pad_add_fusion.refs_1_, bf16[192,768]{1,0:T(8,128)(2,1)S(1)} %get-tuple-element.133.refs_2_, bf16[192,768]{1,0:T(8,128)(2,1)S(1)} %get-tuple-element.134.refs_3_, ...), custom_call_target="tpu_custom_call" | custom-call | flops 10000000000 | bytes 1000000 | tf_op jit(solution)/shard_map/outer/pallas_call | solution.py:411
  68.0 1.8 collective-permute-start.10
  69.8 5.4 %collective-permute-done.8.refs_3_ = f32[192,768]{1,0:T(8,128)S(1)} collective-permute-done((f32[192,768]{1,0:T(8,128)S(1)}, f32[192,768]{1,0:T(8,128)S(1)}, u32[]{:S(2)}, u32[]{:S(2)}) %collective-permute-start.8) | collective-permute-done | bytes 589856 | tf_op jit(solution)/shard_map/ppermute | solution.py:429
  75.9 1.8 collective-permute-start.11
  77.7 8.7 %collective-permute-done.10.refs_3_ = f32[192,768]{1,0:T(8,128)S(1)} collective-permute-done((f32[192,768]{1,0:T(8,128)S(1)}, f32[192,768]{1,0:T(8,128)S(1)}, u32[]{:S(2)}, u32[]{:S(2)}) %collective-permute-start.10) | collective-permute-done | bytes 589856 | tf_op jit(solution)/shard_map/ppermute | solution.py:429
  86.9 2.9 %outer.4 = (f32[384,1536]{1,0:T(8,128)S(1)}, f32[384,1536]{1,0:T(8,128)S(1)}, f32[8,128]{1,0:T(8,128)S(1)}) custom-call(f32[8,128]{1,0:T(8,128)S(1)} %get-tuple-element.153.refs_0_, s32[3]{0:T(128)S(1)} %pad_add_fusion.refs_1_, bf16[192,768]{1,0:T(8,128)(2,1)S(1)} %get-tuple-element.154.refs_2_, bf16[192,768]{1,0:T(8,128)(2,1)S(1)} %get-tuple-element.155.refs_3_, ...), custom_call_target="tpu_custom_call" | custom-call | flops 10000000000 | bytes 1000000 | tf_op jit(solution)/shard_map/outer/pallas_call | solution.py:411
  90.0 5.4 %attend_back.1 = (bf16[384,1536]{1,0:T(8,128)(2,1)S(1)}, f32[8,1536]{1,0:T(8,128)S(1)}, f32[8,128]{1,0:T(8,128)S(1)}) custom-call(f32[8,128]{1,0:T(8,128)S(1)} %get-tuple-element.158.refs_0_, bf16[192,768]{1,0:T(8,128)(2,1)S(1)} %get-tuple-element.159.refs_1_.refs_3_, bf16[192,768]{1,0:T(8,128)(2,1)S(1)} %get-tuple-element.160.refs_2_.refs_4_, ...), custom_call_target="tpu_custom_call" | custom-call | flops 10000000000 | bytes 1000000 | tf_op jit(solution)/shard_map/attend_back/pallas_call | solution.py:411
  95.4 3.6 %outer.5 = (f32[192,1536]{1,0:T(8,128)S(1)}, f32[192,1536]{1,0:T(8,128)S(1)}, f32[384,1536]{1,0:T(8,128)S(1)}, f32[8,128]{1,0:T(8,128)S(1)}) custom-call(f32[8,128]{1,0:T(8,128)S(1)} %get-tuple-element.164.refs_0_, s32[3]{0:T(128)S(1)} %pad_add_fusion.refs_1_, bf16[384,768]{1,0:T(8,128)(2,1)S(1)} %copy-done.7, ...), custom_call_target="tpu_custom_call" | custom-call | flops 10000000000 | bytes 1000000 | tf_op jit(solution)/shard_map/outer/pallas_call | solution.py:411
  101.0 1.8 %collective-permute-start.13 = (f32[96,1536]{1,0:T(8,128)S(1)}, f32[96,1536]{1,0:T(8,128)S(1)}, u32[]{:S(2)}, u32[]{:S(2)}) collective-permute-start(f32[96,1536]{1,0:T(8,128)S(1)} %get-tuple-element.173), channel_id=1, source_target_pairs={{0,8},{2,10},{4,12},{6,14},{8,0},{10,2},{12,4},{14,6},{16,24},{18,... | collective-permute-start | bytes 1769480 | tf_op jit(solution)/shard_map/ppermute | solution.py:432
  104.6 2.0 %back_tokens.1 = (f32[384,768]{1,0:T(8,128)S(1)}, f32[8,128]{1,0:T(8,128)S(1)}) custom-call(f32[8,128]{1,0:T(8,128)S(1)} %get-tuple-element.171.refs_0_, bf16[384,1536]{1,0:T(8,128)(2,1)S(1)} %get-tuple-element.165.refs_5_.refs_1_, bf16[3,768,384]{2,1,0:T(8,128)(2,1)S(1)} %copy-done.4), custom_call_target="tpu_custom_call" | custom-call | flops 10000000000 | bytes 1000000 | tf_op jit(solution)/shard_map/back_tokens/pallas_call | solution.py:411
  106.5 9.0 %collective-permute-done.13.refs_4_ = f32[96,1536]{1,0:T(8,128)S(1)} collective-permute-done((f32[96,1536]{1,0:T(8,128)S(1)}, f32[96,1536]{1,0:T(8,128)S(1)}, u32[]{:S(2)}, u32[]{:S(2)}) %collective-permute-start.13) | collective-permute-done | bytes 589856 | tf_op jit(solution)/shard_map/ppermute | solution.py:432
  115.7 2.8 %collective-permute-start.17 = (f32[48,1536]{1,0:T(8,128)S(1)}, f32[48,1536]{1,0:T(8,128)S(1)}, u32[]{:S(2)}, u32[]{:S(2)}) collective-permute-start(f32[48,1536]{1,0:T(8,128)S(1)} %get-tuple-element.183), channel_id=1, source_target_pairs={{0,16},{2,18},{4,20},{6,22},{8,24},{10,26},{12,28},{14,30},{16,0},... | collective-permute-start | bytes 884744 | tf_op jit(solution)/shard_map/ppermute | solution.py:432
  118.5 11.4 %collective-permute-done.14.refs_3_.refs_6_ = f32[192,1536]{1,0:T(8,128)S(1)} collective-permute-done((f32[192,1536]{1,0:T(8,128)S(1)}, f32[192,1536]{1,0:T(8,128)S(1)}, u32[]{:S(2)}, u32[]{:S(2)}) %collective-permute-start.14) | collective-permute-done | bytes 1179680 | tf_op jit(solution)/shard_map/ppermute | solution.py:432
  135.1 9.3 %collective-permute-done.18.refs_4_ = f32[96,1536]{1,0:T(8,128)S(1)} collective-permute-done((f32[96,1536]{1,0:T(8,128)S(1)}, f32[96,1536]{1,0:T(8,128)S(1)}, u32[]{:S(2)}, u32[]{:S(2)}) %collective-permute-start.18) | collective-permute-done | bytes 589856 | tf_op jit(solution)/shard_map/ppermute | solution.py:432
  146.0 4.0 %collective-permute-start.22 = (f32[48,1536]{1,0:T(8,128)S(1)}, f32[48,1536]{1,0:T(8,128)S(1)}, u32[]{:S(2)}, u32[]{:S(2)}) collective-permute-start(f32[48,1536]{1,0:T(8,128)S(1)} %get-tuple-element.193), channel_id=1, source_target_pairs={{0,16},{2,18},{4,20},{6,22},{8,24},{10,26},{12,28},{14,30},{16,0},... | collective-permute-start | bytes 884744 | tf_op jit(solution)/shard_map/ppermute | solution.py:432
  150.3 2.1 %collective-permute-start.25 = (f32[8,1536]{1,0:T(8,128)S(1)}, f32[8,1536]{1,0:T(8,128)S(1)}, u32[]{:S(2)}, u32[]{:S(2)}) collective-permute-start(f32[8,1536]{1,0:T(8,128)S(1)} %get-tuple-element.198.refs_1_), channel_id=1, source_target_pairs={{0,8},{2,10},{4,12},{6,14},{8,0},{10,2},{12,4},{14,6},{16,24},{18,... | collective-permute-start | bytes 147464 | tf_op jit(solution)/shard_map/ppermute | solution.py:432
  152.4 6.4 %collective-permute-done.22.refs_5_ = f32[48,1536]{1,0:T(8,128)S(1)} collective-permute-done((f32[48,1536]{1,0:T(8,128)S(1)}, f32[48,1536]{1,0:T(8,128)S(1)}, u32[]{:S(2)}, u32[]{:S(2)}) %collective-permute-start.22) | collective-permute-done | bytes 294944 | tf_op jit(solution)/shard_map/ppermute | solution.py:432
  163.8 2.1 %collective-permute-start.29 = (f32[48,1536]{1,0:T(8,128)S(1)}, f32[48,1536]{1,0:T(8,128)S(1)}, u32[]{:S(2)}, u32[]{:S(2)}) collective-permute-start(f32[48,1536]{1,0:T(8,128)S(1)} %get-tuple-element.208), channel_id=1, source_target_pairs={{0,16},{2,18},{4,20},{6,22},{8,24},{10,26},{12,28},{14,30},{16,0},... | collective-permute-start | bytes 884744 | tf_op jit(solution)/shard_map/ppermute | solution.py:432
  170.0 4.3 %collective-permute-done.28.refs_4_ = f32[48,1536]{1,0:T(8,128)S(1)} collective-permute-done((f32[48,1536]{1,0:T(8,128)S(1)}, f32[48,1536]{1,0:T(8,128)S(1)}, u32[]{:S(2)}, u32[]{:S(2)}) %collective-permute-start.28) | collective-permute-done | bytes 294944 | tf_op jit(solution)/shard_map/ppermute | solution.py:432
  174.3 3.2 %collective-permute-done.29.refs_5_ = f32[48,1536]{1,0:T(8,128)S(1)} collective-permute-done((f32[48,1536]{1,0:T(8,128)S(1)}, f32[48,1536]{1,0:T(8,128)S(1)}, u32[]{:S(2)}, u32[]{:S(2)}) %collective-permute-start.29) | collective-permute-done | bytes 294944 | tf_op jit(solution)/shard_map/ppermute | solution.py:432
  (121 shorter events, 33.8 us)
Async XLA Ops:
  1.7 17.3 %copy-start.1 = (bf16[768,1536]{1,0:T(8,128)(2,1)S(1)}, bf16[768,1536]{1,0:T(8,128)(2,1)}, u32[]{:S(2)}) copy-start(bf16[768,1536]{1,0:T(8,128)(2,1)} %refs_7_.6) | copy-start | bytes 7077892
  1.8 17.2 %collective-permute-start = (f32[192,768]{1,0:T(8,128)S(1)}, f32[192,768]{1,0:T(8,128)S(1)}, u32[]{:S(2)}, u32[]{:S(2)}) collective-permute-start(f32[192,768]{1,0:T(8,128)S(1)} %dynamic-slice_convert_fusion), channel_id=1, source_target_pairs={{0,1},{1,0},{2,3},{3,2},{4,5},{5,4},{6,7},{7,6},{8,9},{9,8},{10,11... | collective-permute-start | bytes 1769480 | tf_op jit(solution)/shard_map/ppermute | solution.py:429
  12.5 12.0 %collective-permute-start.1 = (f32[192,384]{1,0:T(8,128)}, f32[192,384]{1,0:T(8,128)}, u32[]{:S(2)}, u32[]{:S(2)}) collective-permute-start(f32[192,384]{1,0:T(8,128)} %get-tuple-element.117), channel_id=1, source_target_pairs={{0,1},{1,0},{2,3},{3,2},{4,5},{5,4},{6,7},{7,6},{8,9},{9,8},{10,11... | collective-permute-start | bytes 884744 | tf_op jit(solution)/shard_map/ppermute | solution.py:429
  21.2 3.4 %collective-permute-start.2 = (f32[64,768]{1,0:T(8,128)}, f32[64,768]{1,0:T(8,128)}, u32[]{:S(2)}, u32[]{:S(2)}) collective-permute-start(f32[64,768]{1,0:T(8,128)} %get-tuple-element.223), channel_id=1, source_target_pairs={{0,2},{2,0},{4,6},{6,4},{8,10},{10,8},{12,14},{14,12},{16,18},{18,... | collective-permute-start | bytes 589832 | tf_op jit(solution)/shard_map/ppermute | solution.py:432
  21.2 3.4 %collective-permute-start.3 = (f32[64,768]{1,0:T(8,128)}, f32[64,768]{1,0:T(8,128)}, u32[]{:S(2)}, u32[]{:S(2)}) collective-permute-start(f32[64,768]{1,0:T(8,128)} %get-tuple-element.222), channel_id=1, source_target_pairs={{0,2},{2,0},{4,6},{6,4},{8,10},{10,8},{12,14},{14,12},{16,18},{18,... | collective-permute-start | bytes 589832 | tf_op jit(solution)/shard_map/ppermute | solution.py:432
  21.7 2.9 %collective-permute-start.4 = (f32[64,768]{1,0:T(8,128)}, f32[64,768]{1,0:T(8,128)}, u32[]{:S(2)}, u32[]{:S(2)}) collective-permute-start(f32[64,768]{1,0:T(8,128)} %get-tuple-element.221), channel_id=1, source_target_pairs={{0,2},{2,0},{4,6},{6,4},{8,10},{10,8},{12,14},{14,12},{16,18},{18,... | collective-permute-start | bytes 589832 | tf_op jit(solution)/shard_map/ppermute | solution.py:432
  21.7 13.8 %collective-permute-start.5 = (f32[192,384]{1,0:T(8,128)}, f32[192,384]{1,0:T(8,128)}, u32[]{:S(2)}, u32[]{:S(2)}) collective-permute-start(f32[192,384]{1,0:T(8,128)} %get-tuple-element.121), channel_id=1, source_target_pairs={{0,1},{1,0},{2,3},{3,2},{4,5},{5,4},{6,7},{7,6},{8,9},{9,8},{10,11... | collective-permute-start | bytes 884744 | tf_op jit(solution)/shard_map/ppermute | solution.py:429
  33.7 16.3 %collective-permute-start.6 = (f32[192,768]{1,0:T(8,128)S(1)}, f32[192,768]{1,0:T(8,128)S(1)}, u32[]{:S(2)}, u32[]{:S(2)}) collective-permute-start(f32[192,768]{1,0:T(8,128)S(1)} %get-tuple-element.123.refs_1_), channel_id=1, source_target_pairs={{0,1},{1,0},{2,3},{3,2},{4,5},{5,4},{6,7},{7,6},{8,9},{9,8},{10,11... | collective-permute-start | bytes 1769480 | tf_op jit(solution)/shard_map/ppermute | solution.py:429
  39.9 22.7 %collective-permute-start.7 = (f32[192,768]{1,0:T(8,128)S(1)}, f32[192,768]{1,0:T(8,128)S(1)}, u32[]{:S(2)}, u32[]{:S(2)}) collective-permute-start(f32[192,768]{1,0:T(8,128)S(1)} %get-tuple-element.128.refs_1_), channel_id=1, source_target_pairs={{0,1},{1,0},{2,3},{3,2},{4,5},{5,4},{6,7},{7,6},{8,9},{9,8},{10,11... | collective-permute-start | bytes 1769480 | tf_op jit(solution)/shard_map/ppermute | solution.py:429
  52.4 22.9 %collective-permute-start.8 = (f32[192,768]{1,0:T(8,128)S(1)}, f32[192,768]{1,0:T(8,128)S(1)}, u32[]{:S(2)}, u32[]{:S(2)}) collective-permute-start(f32[192,768]{1,0:T(8,128)S(1)} %get-tuple-element.139.refs_2_), channel_id=1, source_target_pairs={{0,1},{1,0},{2,3},{3,2},{4,5},{5,4},{6,7},{7,6},{8,9},{9,8},{10,11... | collective-permute-start | bytes 1769480 | tf_op jit(solution)/shard_map/ppermute | solution.py:429
  68.0 7.8 %collective-permute-start.9 = (f32[384,1536]{1,0:T(8,128)S(1)}, f32[384,1536]{1,0:T(8,128)S(1)}, u32[]{:S(2)}, u32[]{:S(2)}) collective-permute-start(f32[384,1536]{1,0:T(8,128)S(1)} %get-tuple-element.145), channel_id=1, source_target_pairs={{0,2},{2,0},{4,6},{6,4},{8,10},{10,8},{12,14},{14,12},{16,18},{18,... | collective-permute-start | bytes 7077896 | tf_op jit(solution)/shard_map/ppermute | solution.py:432
  68.0 18.4 %collective-permute-start.10 = (f32[192,768]{1,0:T(8,128)S(1)}, f32[192,768]{1,0:T(8,128)S(1)}, u32[]{:S(2)}, u32[]{:S(2)}) collective-permute-start(f32[192,768]{1,0:T(8,128)S(1)} %get-tuple-element.148.refs_2_), channel_id=1, source_target_pairs={{0,1},{1,0},{2,3},{3,2},{4,5},{5,4},{6,7},{7,6},{8,9},{9,8},{10,11... | collective-permute-start | bytes 1769480 | tf_op jit(solution)/shard_map/ppermute | solution.py:429
  75.9 25.1 %collective-permute-start.11 = (f32[192,1536]{1,0:T(8,128)S(1)}, f32[192,1536]{1,0:T(8,128)S(1)}, u32[]{:S(2)}, u32[]{:S(2)}) collective-permute-start(f32[192,1536]{1,0:T(8,128)S(1)} %get-tuple-element.167), channel_id=1, source_target_pairs={{0,4},{2,6},{4,0},{6,2},{8,12},{10,14},{12,8},{14,10},{16,20},{18,... | collective-permute-start | bytes 3538952 | tf_op jit(solution)/shard_map/ppermute | solution.py:432
  89.9 13.0 %collective-permute-start.12 = (f32[384,1536]{1,0:T(8,128)S(1)}, f32[384,1536]{1,0:T(8,128)S(1)}, u32[]{:S(2)}, u32[]{:S(2)}) collective-permute-start(f32[384,1536]{1,0:T(8,128)S(1)} %get-tuple-element.170), channel_id=1, source_target_pairs={{0,2},{2,0},{4,6},{6,4},{8,10},{10,8},{12,14},{14,12},{16,18},{18,... | collective-permute-start | bytes 7077896 | tf_op jit(solution)/shard_map/ppermute | solution.py:432
  99.0 61.3 %copy-start.17 = (f32[384,1536]{1,0:T(8,128)}, f32[384,1536]{1,0:T(8,128)S(1)}, u32[]{:S(2)}) copy-start(f32[384,1536]{1,0:T(8,128)S(1)} %get-tuple-element.177.refs_1_.refs_3_) | copy-start | bytes 7077892
  99.0 32.5 %collective-permute-start.15 = (f32[192,1536]{1,0:T(8,128)S(1)}, f32[192,1536]{1,0:T(8,128)S(1)}, u32[]{:S(2)}, u32[]{:S(2)}) collective-permute-start(f32[192,1536]{1,0:T(8,128)S(1)} %get-tuple-element.178), channel_id=1, source_target_pairs={{0,2},{2,0},{4,6},{6,4},{8,10},{10,8},{12,14},{14,12},{16,18},{18,... | collective-permute-start | bytes 3538952 | tf_op jit(solution)/shard_map/ppermute | solution.py:432
  99.5 32.6 %collective-permute-start.16 = (f32[8,1536]{1,0:T(8,128)S(1)}, f32[8,1536]{1,0:T(8,128)S(1)}, u32[]{:S(2)}, u32[]{:S(2)}) collective-permute-start(f32[8,1536]{1,0:T(8,128)S(1)} %get-tuple-element.181.refs_1_), channel_id=1, source_target_pairs={{0,2},{2,0},{4,6},{6,4},{8,10},{10,8},{12,14},{14,12},{16,18},{18,... | collective-permute-start | bytes 147464 | tf_op jit(solution)/shard_map/ppermute | solution.py:432
  99.6 46.4 %collective-permute-start.19 = (f32[192,1536]{1,0:T(8,128)S(1)}, f32[192,1536]{1,0:T(8,128)S(1)}, u32[]{:S(2)}, u32[]{:S(2)}) collective-permute-start(f32[192,1536]{1,0:T(8,128)S(1)} %get-tuple-element.187), channel_id=1, source_target_pairs={{0,2},{2,0},{4,6},{6,4},{8,10},{10,8},{12,14},{14,12},{16,18},{18,... | collective-permute-start | bytes 3538952 | tf_op jit(solution)/shard_map/ppermute | solution.py:432
  101.0 14.5 %collective-permute-start.13 = (f32[96,1536]{1,0:T(8,128)S(1)}, f32[96,1536]{1,0:T(8,128)S(1)}, u32[]{:S(2)}, u32[]{:S(2)}) collective-permute-start(f32[96,1536]{1,0:T(8,128)S(1)} %get-tuple-element.173), channel_id=1, source_target_pairs={{0,8},{2,10},{4,12},{6,14},{8,0},{10,2},{12,4},{14,6},{16,24},{18,... | collective-permute-start | bytes 1769480 | tf_op jit(solution)/shard_map/ppermute | solution.py:432
  103.0 26.9 %collective-permute-start.14 = (f32[192,1536]{1,0:T(8,128)S(1)}, f32[192,1536]{1,0:T(8,128)S(1)}, u32[]{:S(2)}, u32[]{:S(2)}) collective-permute-start(f32[192,1536]{1,0:T(8,128)S(1)} %get-tuple-element.175), channel_id=1, source_target_pairs={{0,4},{2,6},{4,0},{6,2},{8,12},{10,14},{12,8},{14,10},{16,20},{18,... | collective-permute-start | bytes 3538952 | tf_op jit(solution)/shard_map/ppermute | solution.py:432
  115.7 18.1 %collective-permute-start.17 = (f32[48,1536]{1,0:T(8,128)S(1)}, f32[48,1536]{1,0:T(8,128)S(1)}, u32[]{:S(2)}, u32[]{:S(2)}) collective-permute-start(f32[48,1536]{1,0:T(8,128)S(1)} %get-tuple-element.183), channel_id=1, source_target_pairs={{0,16},{2,18},{4,20},{6,22},{8,24},{10,26},{12,28},{14,30},{16,0},... | collective-permute-start | bytes 884744 | tf_op jit(solution)/shard_map/ppermute | solution.py:432
  129.9 37.0 %collective-permute-start.27 = (f32[384,768]{1,0:T(8,128)S(1)}, f32[384,768]{1,0:T(8,128)S(1)}, u32[]{:S(2)}, u32[]{:S(2)}) collective-permute-start(f32[384,768]{1,0:T(8,128)S(1)} %get-tuple-element.202.refs_1_), channel_id=1, source_target_pairs={{0,1},{1,0},{2,3},{3,2},{4,5},{5,4},{6,7},{7,6},{8,9},{9,8},{10,11... | collective-permute-start | bytes 3538952 | tf_op jit(solution)/shard_map/ppermute | solution.py:429
  131.5 13.0 %collective-permute-start.18 = (f32[96,1536]{1,0:T(8,128)S(1)}, f32[96,1536]{1,0:T(8,128)S(1)}, u32[]{:S(2)}, u32[]{:S(2)}) collective-permute-start(f32[96,1536]{1,0:T(8,128)S(1)} %get-tuple-element.185), channel_id=1, source_target_pairs={{0,8},{2,10},{4,12},{6,14},{8,0},{10,2},{12,4},{14,6},{16,24},{18,... | collective-permute-start | bytes 1769480 | tf_op jit(solution)/shard_map/ppermute | solution.py:432
  132.1 18.0 %collective-permute-start.20 = (f32[96,1536]{1,0:T(8,128)S(1)}, f32[96,1536]{1,0:T(8,128)S(1)}, u32[]{:S(2)}, u32[]{:S(2)}) collective-permute-start(f32[96,1536]{1,0:T(8,128)S(1)} %get-tuple-element.188), channel_id=1, source_target_pairs={{0,4},{2,6},{4,0},{6,2},{8,12},{10,14},{12,8},{14,10},{16,20},{18,... | collective-permute-start | bytes 1769480 | tf_op jit(solution)/shard_map/ppermute | solution.py:432
  133.7 16.6 %collective-permute-start.21 = (f32[8,1536]{1,0:T(8,128)S(1)}, f32[8,1536]{1,0:T(8,128)S(1)}, u32[]{:S(2)}, u32[]{:S(2)}) collective-permute-start(f32[8,1536]{1,0:T(8,128)S(1)} %get-tuple-element.191.refs_1_), channel_id=1, source_target_pairs={{0,4},{2,6},{4,0},{6,2},{8,12},{10,14},{12,8},{14,10},{16,20},{18,... | collective-permute-start | bytes 147464 | tf_op jit(solution)/shard_map/ppermute | solution.py:432
  144.5 15.1 %collective-permute-start.23 = (f32[96,1536]{1,0:T(8,128)S(1)}, f32[96,1536]{1,0:T(8,128)S(1)}, u32[]{:S(2)}, u32[]{:S(2)}) collective-permute-start(f32[96,1536]{1,0:T(8,128)S(1)} %get-tuple-element.195), channel_id=1, source_target_pairs={{0,4},{2,6},{4,0},{6,2},{8,12},{10,14},{12,8},{14,10},{16,20},{18,... | collective-permute-start | bytes 1769480 | tf_op jit(solution)/shard_map/ppermute | solution.py:432
  146.0 12.8 %collective-permute-start.22 = (f32[48,1536]{1,0:T(8,128)S(1)}, f32[48,1536]{1,0:T(8,128)S(1)}, u32[]{:S(2)}, u32[]{:S(2)}) collective-permute-start(f32[48,1536]{1,0:T(8,128)S(1)} %get-tuple-element.193), channel_id=1, source_target_pairs={{0,16},{2,18},{4,20},{6,22},{8,24},{10,26},{12,28},{14,30},{16,0},... | collective-permute-start | bytes 884744 | tf_op jit(solution)/shard_map/ppermute | solution.py:432
  150.2 10.1 %collective-permute-start.24 = (f32[48,1536]{1,0:T(8,128)S(1)}, f32[48,1536]{1,0:T(8,128)S(1)}, u32[]{:S(2)}, u32[]{:S(2)}) collective-permute-start(f32[48,1536]{1,0:T(8,128)S(1)} %get-tuple-element.196), channel_id=1, source_target_pairs={{0,8},{2,10},{4,12},{6,14},{8,0},{10,2},{12,4},{14,6},{16,24},{18,... | collective-permute-start | bytes 884744 | tf_op jit(solution)/shard_map/ppermute | solution.py:432
  150.3 10.5 %collective-permute-start.25 = (f32[8,1536]{1,0:T(8,128)S(1)}, f32[8,1536]{1,0:T(8,128)S(1)}, u32[]{:S(2)}, u32[]{:S(2)}) collective-permute-start(f32[8,1536]{1,0:T(8,128)S(1)} %get-tuple-element.198.refs_1_), channel_id=1, source_target_pairs={{0,8},{2,10},{4,12},{6,14},{8,0},{10,2},{12,4},{14,6},{16,24},{18,... | collective-permute-start | bytes 147464 | tf_op jit(solution)/shard_map/ppermute | solution.py:432
  160.8 6.0 %collective-permute-start.26 = (f32[8,1536]{1,0:T(8,128)S(1)}, f32[8,1536]{1,0:T(8,128)S(1)}, u32[]{:S(2)}, u32[]{:S(2)}) collective-permute-start(f32[8,1536]{1,0:T(8,128)S(1)} %get-tuple-element.200.refs_1_), channel_id=1, source_target_pairs={{0,16},{2,18},{4,20},{6,22},{8,24},{10,26},{12,28},{14,30},{16,0},... | collective-permute-start | bytes 147464 | tf_op jit(solution)/shard_map/ppermute | solution.py:432
  162.2 12.0 %collective-permute-start.28 = (f32[48,1536]{1,0:T(8,128)S(1)}, f32[48,1536]{1,0:T(8,128)S(1)}, u32[]{:S(2)}, u32[]{:S(2)}) collective-permute-start(f32[48,1536]{1,0:T(8,128)S(1)} %get-tuple-element.207), channel_id=1, source_target_pairs={{0,8},{2,10},{4,12},{6,14},{8,0},{10,2},{12,4},{14,6},{16,24},{18,... | collective-permute-start | bytes 884744 | tf_op jit(solution)/shard_map/ppermute | solution.py:432
  163.8 13.7 %collective-permute-start.29 = (f32[48,1536]{1,0:T(8,128)S(1)}, f32[48,1536]{1,0:T(8,128)S(1)}, u32[]{:S(2)}, u32[]{:S(2)}) collective-permute-start(f32[48,1536]{1,0:T(8,128)S(1)} %get-tuple-element.208), channel_id=1, source_target_pairs={{0,16},{2,18},{4,20},{6,22},{8,24},{10,26},{12,28},{14,30},{16,0},... | collective-permute-start | bytes 884744 | tf_op jit(solution)/shard_map/ppermute | solution.py:432
  (25 other events, 183.9 us)

commit v4 on v3

--- a/solution.py
+++ b/solution.py
@@ -146,10 +146,10 @@
     return ref[...].astype(F32)
 
 
-def feed(taken, tile, far_parts, place_ref, x_hbm, own_hbm, far_hbm, w_own_hbm, w_near_hbm, *refs):
+def feed(taken, tile, far_parts, streamed, place_ref, x_hbm, own_hbm, far_hbm, w_own_hbm, w_near_hbm, *refs):
     w_fars, refs = refs[:far_parts], refs[far_parts:]
-    vec_ref, b_up_ref, w_up, w_down, normed_ref, inverse_ref, low_ref, act_ref, slope_ref, part_ref = refs[:10]
-    x_ref, far_ref, w_far, w_full, ctx_full, sems = refs[10:]
+    vec_hbm, b_up_ref, w_up, w_down, normed_ref, inverse_ref, low_ref, act_ref, slope_ref, part_ref = refs[:10]
+    x_ref, far_ref, vec_ref, w_far, w_full, ctx_full, sems = refs[10:17]
     local = own_hbm.shape[1]
     half = w_near_hbm.shape[0]
     piece = half // far_parts
@@ -158,10 +158,18 @@
     here = pl.multiple_of(side * local, LANES)
     there = pl.multiple_of((1 - side) * local, LANES)
     spans = [slice(at, at + tile) for at in range(0, hidden, tile)]
-    sources = [w_own_hbm, own_hbm.at[taken], far_hbm, x_hbm.at[taken], w_near_hbm] + list(w_fars)
-    targets = [w_full.at[pl.ds(here, local)], ctx_full.at[:, pl.ds(here, local)], far_ref, x_ref, w_far.at[0]]
-    targets += [w_far.at[1, i * piece : (i + 1) * piece] for i in range(far_parts)]
-    for copy in fetch(sources, targets, sems):
+    sources = [w_near_hbm] + list(w_fars) + [w_own_hbm, own_hbm.at[taken], far_hbm, x_hbm.at[taken], vec_hbm]
+    targets = [w_far.at[0]] + [w_far.at[1, i * piece : (i + 1) * piece] for i in range(far_parts)]
+    targets += [w_full.at[pl.ds(here, local)], ctx_full.at[:, pl.ds(here, local)], far_ref, x_ref, vec_ref]
+    needed = len(sources)
+    if streamed:
+        w_up_vmem, w_down_vmem = refs[17:]
+        for span in spans:
+            sources += [w_up.at[:, span], w_down.at[span]]
+            targets += [w_up_vmem.at[:, span], w_down_vmem.at[span]]
+        w_up, w_down = w_up_vmem, w_down_vmem
+    came = fetch(sources, targets, sems)
+    for copy in came[:needed]:
         copy.wait()
     for i in range(2):
         at = pl.multiple_of(there + (core ^ i) * half, 16)
@@ -175,11 +183,15 @@
     low_ref[...] = low
     b_up = b_up_ref[...].astype(F32).reshape(1, -1)
     for i, span in enumerate(spans):
+        if streamed:
+            came[needed + 2 * i].wait()
         pre = dot(low, w_up[:, span]) + b_up[:, span]
         share = 0.5 * (1.0 + lax.erf(pre * 0.7071067811865476))
         act = (pre * share).astype(LOW)
         act_ref[:, span] = act
         slope_ref[:, span] = share + pre * jnp.exp(-0.5 * pre * pre) * 0.3989422804014327
+        if streamed:
+            came[needed + 2 * i + 1].wait()
         added = dot(act, w_down[span, :])
         if i == 0:
             part_ref[...] = added
@@ -188,13 +200,14 @@
 
 
 def feed_back(
-    taken, tile, own_ref, far_ref, normed_ref, vec_ref, slope_ref, up_hbm, w_up, w_down,
+    taken, tile, own_ref, far_ref, normed_ref, slope_ref, vec_hbm, up_hbm, w_up, w_down,
     out_ref, grad_ref, low_ref, pre_ref, part_ref, sums_ref, b_up_ref,
-    up_ref, sems,
+    vec_ref, up_ref, sems,
 ):
     hidden = w_up.shape[1]
     spans = [slice(at, at + tile) for at in range(0, hidden, tile)]
-    came = fetch([up_hbm.at[taken]], [up_ref], sems)
+    came = fetch([up_hbm.at[taken], vec_hbm], [up_ref, vec_ref], sems)
+    came[1].wait()
     hidden_rows = normed_ref[...] * vec_ref[1:2, :] + vec_ref[2:3, :]
     normed, inverse = norm_rows(hidden_rows + (own_ref[...] + far_ref[...]) + vec_ref[3:4, :])
     gain = vec_ref[4:5, :]
@@ -292,12 +305,13 @@
         target[i * size : (i + 1) * size, :] = source[pl.ds(at, size), :]
 
 
-def outer(order, size, splits, kinds, more, place_ref, *refs):
+def outer(order, size, splits, kinds, more, rides, place_ref, *refs):
     count = len(splits)
     sides = max(kinds) + 1
     lefts = [refs[:count]] + ([refs[count : count + more]] if more else [])
     rights = refs[count + more : 2 * count + more]
-    *sent_refs, keep_ref, flipped, placed = refs[2 * count + more :]
+    rider = refs[2 * count + more] if rides else None
+    *sent_refs, keep_ref, flipped, placed = refs[2 * count + more + rides :]
     step = pl.program_id(0)
 
     @pl.when(step == 0)
@@ -315,11 +329,14 @@
         change = kinds.index(1)
         left = placed[jnp.where(step >= change, 1, 0)]
     right = jnp.concatenate([ref[...] for ref in rights], 0)
-    half = keep_ref.shape[0]
+    half = left.shape[0] // 2
     part = half // len(sent_refs)
     for i, ref in enumerate(sent_refs):
-        ref[...] = dot(left[i * part : (i + 1) * part], right)
-    keep_ref[...] = dot(left[half:], right)
+        ref[0:part, :] = dot(left[i * part : (i + 1) * part], right)
+    keep_ref[0:half, :] = dot(left[half:], right)
+    if rides:
+        sent_refs[-1][part:, :] = rider[...]
+        keep_ref[half:, :] = rider[...]
 
 
 def fold(*refs):
@@ -329,15 +346,17 @@
     refs[-1][...] = value
 
 
-def fold_blocks(size, counts, *refs):
+def fold_blocks(counts, *refs):
     out_ref = refs[-1]
-    at = 0
-    for i, count in enumerate(counts):
+    at = start = 0
+    for count in counts:
         value = refs[at][...]
         for ref in refs[at + 1 : at + count]:
             value = value + ref[...]
-        out_ref[i * size : (i + 1) * size, :] = value
+        end = start + value.shape[0]
+        out_ref[start:end, :] = value
         at += count
+        start = end
 
 
 def back_tokens(e_ref, w_hbm, out_ref, w_ref, sems):
@@ -361,16 +380,10 @@
 
 
 def spread(local, *refs):
-    count = len(refs) - 4
-    parts, (qkv_ref, out_ref) = refs[:count], refs[count : count + 2]
-    held, sems = refs[-2:]
-    size = out_ref.shape[0]
-    came = fetch([part.at[0:size] for part in parts], [held.at[i] for i in range(count)], sems)
-    for copy in came:
-        copy.wait()
-    value = held[0]
-    for i in range(1, count):
-        value = value + held[i]
+    qkv_ref, out_ref = refs[-2:]
+    value = refs[0][...]
+    for ref in refs[1:-2]:
+        value = value + ref[...]
     for i in range(3):
         qkv_ref[i] = value[:, i * local : (i + 1) * local]
     out_ref[...] = value[:, 3 * local :]
@@ -405,9 +418,14 @@
     far_off = pl.BlockSpec(memory_space=pltpu.HBM)
     dma = pltpu.SemaphoreType.DMA
     mark = [None]
-
-    def call(kernel, name, operands, in_specs, out_shape, out_specs, grid=(1,), scratch=(), limit=24, flops=10**10):
+    pace = [10**10]
+
+    def call(kernel, name, operands, in_specs, out_shape, out_specs, grid=(1,), scratch=(), limit=24, flops=None):
         before = mark[0] if mark[0] is not None else operands[0]
+        operands = [
+            pltpu.with_memory_space_constraint(operand, pltpu.HBM) if spec is far_off else operand
+            for operand, spec in zip(operands, in_specs)
+        ]
         *outs, mark[0] = pl.pallas_call(
             chained(kernel, len(operands), len(out_shape)),
             grid=grid,
@@ -416,7 +434,7 @@
             out_specs=tuple(out_specs) + (whole((8, LANES)),),
             scratch_shapes=list(scratch),
             compiler_params=params(limit),
-            cost_estimate=cost(flops),
+            cost_estimate=cost(pace[0] if flops is None else flops),
             name=name,
         )(before, *operands)
         return outs
@@ -461,8 +479,7 @@
     params_of = [b_out, ln1_gain, ln1_bias, b_down, ln2_gain, ln2_bias]
     outs = [shape(w_near.shape, F32), shape((8, width), F32)]
     w_near, vectors = call(
-        relay, "relay", [w_near, *params_of, w_up, w_down],
-        full(w_near, *params_of) + [near, near], outs, full(*outs),
+        relay, "relay", [w_near, *params_of], full(w_near, *params_of), outs, full(*outs)
     )
     far_parts = 3 if half % 48 == 0 else 1
     piece = half // far_parts
@@ -481,18 +498,20 @@
             shape((block, hidden), LOW), shape((block, hidden), F32), shape((block, width), F32),
         ]
         outs = call(
-            functools.partial(feed, slice(begin, begin + block), tile, far_parts), "feed",
+            functools.partial(feed, slice(begin, begin + block), tile, far_parts, begin == 0), "feed",
             [place_arr, tokens, context, far, w_out, w_near, *w_fars, vectors, b_up, w_up, w_down],
-            [smem] + [far_off] * (5 + far_parts) + full(vectors, b_up) + [near] * 2,
+            [smem] + [far_off] * (6 + far_parts) + full(b_up) + [far_off if begin == 0 else near] * 2,
             outs, full(*outs),
             scratch=[
                 pltpu.VMEM((block, width), LOW),
                 pltpu.VMEM((block, local), F32),
+                pltpu.VMEM((8, width), F32),
                 pltpu.VMEM((2, half, width), F32),
                 pltpu.VMEM((2 * local, width), LOW),
                 pltpu.VMEM((block, 2 * local), LOW),
-                dma((5 + far_parts,)),
-            ],
+                dma((6 + far_parts + 2 * tiles,)),
+            ]
+            + ([pltpu.VMEM((width, hidden), LOW), pltpu.VMEM((hidden, width), LOW)] if begin == 0 else []),
         )
         saved.append(outs + [swap_tp(outs[5])])
 
@@ -504,104 +523,134 @@
         ]
         outs = call(
             functools.partial(feed_back, slice(begin, begin + block), tile), "feed_back",
-            [own, far, normed, vectors, slope, cotangent, w_up, w_down],
-            full(own, far, normed, vectors, slope) + [far_off] + [near] * 2,
+            [own, far, normed, slope, vectors, cotangent, w_up, w_down],
+            full(own, far, normed, slope) + [far_off] * 2 + [near] * 2,
             outs, full(*outs),
-            scratch=[pltpu.VMEM((block, width), LOW), dma((1,))],
+            scratch=[pltpu.VMEM((8, width), F32), pltpu.VMEM((block, width), LOW), dma((2,))],
         )
         back.append(outs + [swap_tp(outs[4])])
 
     layer_out = jnp.concatenate([outs[0] for outs in back], 0)
 
-    def gradient(lefts, rights, splits, kinds, step, parts):
+    def gradient(lefts, rights, splits, kinds, step, rider=None):
         wide = step * len(kinds)
         sides = max(kinds) + 1
-        outs = [shape((width // 2 // parts, wide), F32)] * parts + [shape((width // 2, wide), F32)]
+        riders = [] if rider is None else [rider]
+        outs = [shape((width // 2 + 8 * len(riders), wide), F32)] * 2
         outs = call(
-            functools.partial(outer, order if fused else None, size, splits, kinds, len(lefts) - len(splits)), "outer",
-            [place_arr, *lefts, *rights],
-            [smem] + full(*lefts) + [columns(split, step) for split in splits],
+            functools.partial(
+                outer, order if fused else None, size, splits, kinds, len(lefts) - len(splits), len(riders)
+            ),
+            "outer", [place_arr, *lefts, *rights, *riders],
+            [smem] + full(*lefts) + [columns(split, step) for split in splits] + [columns(8, step) for _ in riders],
             outs, [columns(out.shape[0], step) for out in outs],
             grid=(len(kinds),),
             scratch=[pltpu.VMEM((width, rows), LOW), pltpu.VMEM((sides, width, rows), LOW)],
         )
         if not fused:
-            every = jnp.concatenate(outs, 0).reshape(ranks, size, wide)
+            every = jnp.concatenate([out[: width // 2] for out in outs], 0).reshape(ranks, size, wide)
             every = jnp.take(every, jnp.array(order, jnp.int32) ^ me, axis=0).reshape(width, wide)
             outs = [every[: width // 2], every[width // 2 :]]
+            outs = [jnp.concatenate([out] + riders, 0) for out in outs]
         return outs
 
     def pick(held, begin, end):
         return [(array, first) for array, first in held if first <= begin and end <= first + array.shape[0]]
 
-    def add(held, begin, end):
+    def add(held, begin, end, flops=None, extra=()):
         wide = held[0][0].shape[1]
         if not fused:
             parts = []
             for row in range(begin, end, size):
                 parts.append(functools.reduce(jnp.add, [a[row - f : row - f + size] for a, f in pick(held, row, row + size)]))
+            if extra:
+                parts.append(functools.reduce(jnp.add, [a[row : row + 8] for a, row in extra]))
             return jnp.concatenate(parts, 0)
         operands, specs, counts = [], [], []
+
+        def take(array, row, height):
+            operands.append(array)
+            specs.append(pl.BlockSpec((height, wide), functools.partial(lambda index, n: (index, 0), row // height)))
+
         for row in range(begin, end, size):
             inside = pick(held, row, row + size)
             counts.append(len(inside))
             for array, first in inside:
-                operands.append(array)
-                specs.append(pl.BlockSpec((size, wide), functools.partial(lambda index, n: (index, 0), (row - first) // size)))
-        outs = [shape((end - begin, wide), F32)]
-        return call(functools.partial(fold_blocks, size, counts), "fold", operands, specs, outs, full(*outs))[0]
+                take(array, row - first, size)
+        if extra:
+            counts.append(len(extra))
+            for array, row in extra:
+                take(array, row, 8)
+        outs = [shape((end - begin + (8 if extra else 0), wide), F32)]
+        return call(functools.partial(fold_blocks, counts), "fold", operands, specs, outs, full(*outs), flops=flops)[0]
+
+    def add_extra(extra):
+        if not fused:
+            return functools.reduce(jnp.add, [a[row : row + 8] for a, row in extra])
+        wide = extra[0][0].shape[1]
+        specs = [pl.BlockSpec((8, wide), functools.partial(lambda index, n: (index, 0), row // 8)) for _, row in extra]
+        outs = [shape((8, wide), F32)]
+        return call(fold, "fold", [array for array, _ in extra], specs, outs, full(*outs))[0]
 
     class Chunk:
-        def __init__(self, outs):
-            self.held, first = [(outs[-1], 0)], 0
-            for out in outs[:-1]:
-                self.held.append((swap_dp(out, stages[0]), first))
-                first += out.shape[0]
+        def __init__(self, outs, rides=False):
+            sent, keep = outs
+            came = swap_dp(sent, stages[0])
+            self.held = [(keep, 0), (came, 0)]
+            self.extra = [(keep, width // 2), (came, width // 2)] if rides else []
             self.stage = 0
 
-        def step(self):
+        def send(self, begin, end, flops, rides):
+            rides = rides and self.extra and self.stage < len(stages) - 1
+            came = swap_dp(add(self.held, begin, end, flops, self.extra if rides else ()), stages[self.stage])
+            if rides:
+                self.extra = self.extra + [(came, end - begin)]
+            return came
+
+        def step(self, flops=None):
             self.stage += 1
             half = width // (4 << (self.stage - 1))
-            out = add(self.held, half, 2 * half)
-            self.held = self.held + [(swap_dp(out, stages[self.stage]), 0)]
-
-        def high(self):
-            self.stage += 1
-            half = self.half = width // (4 << (self.stage - 1))
+            self.held = self.held + [(self.send(half, 2 * half, flops, True), 0)]
+
+        def high(self, flops=None):
+            half = self.half = width // (4 << self.stage)
             if half == size:
-                self.stage -= 1
-                self.step()
+                self.step(flops)
             else:
-                out = add(self.held, half + half // 2, 2 * half)
-                self.came = [(swap_dp(out, stages[self.stage]), half // 2)]
-
-        def low(self):
-            out = add(self.held, self.half, self.half + self.half // 2)
-            self.held = self.held + self.came + [(swap_dp(out, stages[self.stage]), 0)]
-
-        def last(self):
+                self.stage += 1
+                self.came = [(self.send(half + half // 2, 2 * half, flops, True), half // 2)]
+
+        def low(self, flops=None):
+            part = self.send(self.half, self.half + self.half // 2, flops, False)
+            self.held = self.held + self.came + [(part, 0)]
+
+        def all_but_last(self):
+            self.held = [(add(self.held[:-1], 0, size), 0), self.held[-1]]
+
+        def last(self, flops=None):
             self.rest()
-            return add(self.held, 0, size)
+            return add(self.held, 0, size, flops)
 
         def rest(self):
             while self.stage < len(stages) - 1:
                 self.step()
             return [(array, first) for array, first in self.held if first == 0]
 
-    down = Chunk(gradient([o[2] for o in back], [s[3] for s in saved], blocks, [0] * tiles, tile, 1))
-    wide = max(width, hidden, 2 * local)
+    down = Chunk(gradient([o[2] for o in back], [s[3] for s in saved], blocks, [0] * tiles, tile))
+    wide = 4 * local
 
     def first_norm(i):
         outs = [shape((blocks[i], width), F32), shape((blocks[i], width), LOW), shape((8, wide), F32)]
         operands = [back[i][1], back[i][4], back[i][7], saved[i][0], saved[i][1], back[i][5], back[i][6], vectors]
         operands += [norms[-1][2]] if norms else []
-        norms.append(call(norm_one_back, "norm_one_back", operands, full(*operands), outs, full(*outs), flops=2 * 10**10 if i == 0 else 10**10))
+        norms.append(call(norm_one_back, "norm_one_back", operands, full(*operands), outs, full(*outs), flops=2 * 10**10 if i == 0 else None))
 
     norms = []
     first_norm(0)
-    down.step()
+    down.high()
+    down.low()
     first_norm(1)
-    up = Chunk(gradient([s[2] for s in saved], [o[3] for o in back], blocks, [0] * tiles, tile, 1))
+    up = Chunk(gradient([s[2] for s in saved], [o[3] for o in back], blocks, [0] * tiles, tile))
     dr1s, lows = [n[0] for n in norms], [n[1] for n in norms]
     outs = [shape((rows, 4 * local), LOW), shape((8, wide), F32)]
     operands = lows + [w_out, qkv, context, lse, lengths, pad_row, norms[-1][2]]
@@ -610,39 +659,40 @@
         full(*lows) + [far_off] * 3 + full(lse) + [smem] + full(pad_row, norms[-1][2]), outs, full(*outs),
         scratch=[pltpu.VMEM((local, width), LOW), pltpu.VMEM((rows, 3 * local), LOW), dma((3,))],
     )
-    mixed = Chunk(gradient([tokens] + lows, [e], [rows], [0, 0, 0, 1], local, 2))
-
-    def bias_step(bit):
-        far = swap_dp(bias, bit)
-        return call(fold, "fold", [bias, far], full(bias, far), [shape(bias.shape, F32)], full(bias))[0]
-
-    down.step()
-    up.step()
+    down.step(2 * 10**10)
+    up.high()
+    up.low()
+    mixed = Chunk(rides=True, outs=gradient([tokens] + lows, [e], [rows], [0, 0, 0, 1], local, bias))
+
     outs = [shape((rows, width), F32)]
     (partial,) = call(
         back_tokens, "back_tokens", [e, w_qkv], full(e) + [far_off], outs, full(*outs),
         scratch=[pltpu.VMEM((3, width, local), LOW), dma((3,))],
     )
+    pace[0] = 10**9
     partial_far = swap_tp(partial)
+    pace[0] = 10**9
     down.step()
+    up.step(2 * 10**10)
+    mixed.high()
+    mixed.low()
+    down = down.last(5 * 10**9)
     up.step()
     mixed.high()
     mixed.low()
-    bias = bias_step(stages[0])
-    down = down.last()
-    up.step()
-    mixed.high()
-    mixed.low()
-    bias = bias_step(stages[1])
     up = up.last()
-    mixed.high()
-    bias = bias_step(stages[2])
-    mixed = mixed.rest()
-    for bit in stages[3:]:
-        bias = bias_step(bit)
+    while mixed.stage < len(stages) - 1:
+        mixed.high()
+        if mixed.half > size:
+            mixed.low()
+    bias = add_extra(mixed.extra)
+    bias_far = swap_dp(bias, stages[-1])
+    mixed.all_but_last()
     (d_tokens,) = call(
         join, "join", [partial, partial_far] + dr1s, full(partial, partial_far, *dr1s), outs, full(*outs)
     )
+    (bias,) = call(fold, "fold", [bias, bias_far], full(bias, bias_far), [shape(bias.shape, F32)], full(bias))
+    mixed = mixed.rest()
 
     def finish(held):
         return functools.reduce(jnp.add, [array[:size] for array, _ in held])
@@ -651,8 +701,7 @@
         outs = [shape((3, size, local), F32), shape((size, local), F32)]
         d_w_qkv, d_w_out = call(
             functools.partial(spread, local), "spread", [array for array, _ in mixed],
-            [far_off] * len(mixed), outs, full(*outs),
-            scratch=[pltpu.VMEM((len(mixed), size, 4 * local), F32), dma((len(mixed),))],
+            [pl.BlockSpec((size, 4 * local), lambda n: (0, 0))] * len(mixed), outs, full(*outs),
         )
     else:
         last = finish(mixed)

time: 181 us -> 177 us (0.978)
  starting transfers between devices: 37.3 us -> 32.9 us
  local copies, waits for them, and re-layouts: 10.1 us -> 5.83 us
  Pallas kernels: 44.2 us -> 47.9 us
    ppermute x22 -> x20, starting transfers between devices: 24.3 us -> 20.4 us  [swap_dp(): return lax.ppermute(array, 'dp', [(i, i ^ bits) for i in range(ranks)])]
    pallas_call x32 -> x33, Pallas kernels: 44.2 us -> 47.9 us  [call(): pl.pallas_call(chained(kernel, len(operands), len(out_shape)), grid=grid,...]
    unnamed x54 -> x46, local copies, waits for them, and re-layouts: 7.48 us -> 3.94 us
    ppermute x22 -> x20, waiting for transfers between devices: 46.7 us -> 48.9 us  [swap_dp(): return lax.ppermute(array, 'dp', [(i, i ^ bits) for i in range(ranks)])]
  transfers between devices with their start and end apart: 30 -> 28, of which waited for: 16 -> 17; matrix products, arithmetic and copies ran while one was open for 2% -> 2% of each run, Pallas kernels for 24% -> 27%
where the time goes in v4:
time: 177 us; the launch traced here: 176 us
  waiting for transfers between devices  86.6 us (49%)
  Pallas kernels  47.9 us (27%)
  starting transfers between devices  32.9 us (19%)
  local copies, waits for them, and re-layouts  5.83 us (3%)
  other arithmetic  1.93 us (1%)
    ppermute x20, waiting for transfers between devices, swap_dp(): return lax.ppermute(array, 'dp', [(i, i ^ bits) for i in range(ranks)])  48.9 us
    pallas_call x33, Pallas kernels, call(): pl.pallas_call(chained(kernel, len(operands), len(out_shape)), grid=grid,...  47.9 us
    ppermute x8, waiting for transfers between devices, swap_tp(): return lax.ppermute(array, 'tp', pairs)  37.6 us
    ppermute x20, starting transfers between devices, swap_dp(): return lax.ppermute(array, 'dp', [(i, i ^ bits) for i in range(ranks)])  20.4 us
    ppermute x8, starting transfers between devices, swap_tp(): return lax.ppermute(array, 'tp', pairs)  12.5 us
    unnamed x46, local copies, waits for them, and re-layouts  3.94 us
  transfers between devices with their start and end apart: 28, of which 17 were waited for; matrix products, arithmetic and copies ran while one was open for 2% of the time, Pallas kernels for 27%

profile of v4, /device:TPU:0, one launch (start us, length us, event | category | flops | bytes accessed | tf_op | source)
XLA Modules:
  0.0 176.2 jit_solution(13009569776353080223)
XLA Ops:
  1.7 3.0 %collective-permute-start = (f32[192,768]{1,0:T(8,128)S(1)}, f32[192,768]{1,0:T(8,128)S(1)}, u32[]{:S(2)}, u32[]{:S(2)}) collective-permute-start(f32[192,768]{1,0:T(8,128)S(1)} %dynamic-slice_convert_fusion), channel_id=1, source_target_pairs={{0,1},{1,0},{2,3},{3,2},{4,5},{5,4},{6,7},{7,6},{8,9},{9,8},{10,11... | collective-permute-start | bytes 1769480 | tf_op jit(solution)/shard_map/ppermute | solution.py:447
  4.8 7.7 %attend.1 = (bf16[384,1152]{1,0:T(8,128)(2,1)}, bf16[384,384]{1,0:T(8,128)(2,1)}, f32[8,384]{1,0:T(8,128)}, f32[192,384]{1,0:T(8,128)}, f32[192,384]{1,0:T(8,128)}, /*index=5*/f32[8,128]{1,0:T(8,128)}) custom-call(bf16[384,768]{1,0:T(8,128)(2,1)} %refs_2_.10, bf16[384,768]{1,0:T(8,128)(2,1)} %refs_2_.10, bf16[3,768,384]{2,1,0:T(8,128)(2,1)} %refs_2_.11, ...), custom_call_target="tpu_custom_call" | custom-call | flops 10000000000 | bytes 1000000 | tf_op jit(solution)/shard_map/attend/pallas_call | solution.py:429
  12.6 6.3 %collective-permute-done.refs_1_ = f32[192,768]{1,0:T(8,128)S(1)} collective-permute-done((f32[192,768]{1,0:T(8,128)S(1)}, f32[192,768]{1,0:T(8,128)S(1)}, u32[]{:S(2)}, u32[]{:S(2)}) %collective-permute-start) | collective-permute-done | bytes 589856 | tf_op jit(solution)/shard_map/ppermute | solution.py:447
  21.0 2.1 %collective-permute-start.5 = (f32[192,384]{1,0:T(8,128)S(1)}, f32[192,384]{1,0:T(8,128)S(1)}, u32[]{:S(2)}, u32[]{:S(2)}) collective-permute-start(f32[192,384]{1,0:T(8,128)S(1)} %copy-done.17), channel_id=1, source_target_pairs={{0,1},{1,0},{2,3},{3,2},{4,5},{5,4},{6,7},{7,6},{8,9},{9,8},{10,11... | collective-permute-start | bytes 884744 | tf_op jit(solution)/shard_map/ppermute | solution.py:447
  25.3 5.7 %feed.2 = (f32[192,768]{1,0:T(8,128)S(1)}, f32[192,128]{1,0:T(8,128)S(1)}, bf16[192,768]{1,0:T(8,128)(2,1)S(1)}, bf16[192,1536]{1,0:T(8,128)(2,1)S(1)}, f32[192,...) custom-call(f32[8,128]{1,0:T(8,128)S(1)} %get-tuple-element.116.refs_0_, s32[3]{0:T(128)S(1)} %pad_add_fusion.refs_1_, ...), custom_call_target="tpu_custom_call" | custom-call | flops 10000000000 | bytes 1000000 | tf_op jit(solution)/shard_map/feed/pallas_call | solution.py:429
  31.0 1.8 %collective-permute-start.6 = (f32[192,768]{1,0:T(8,128)S(1)}, f32[192,768]{1,0:T(8,128)S(1)}, u32[]{:S(2)}, u32[]{:S(2)}) collective-permute-start(f32[192,768]{1,0:T(8,128)S(1)} %get-tuple-element.124.refs_1_), channel_id=1, source_target_pairs={{0,1},{1,0},{2,3},{3,2},{4,5},{5,4},{6,7},{7,6},{8,9},{9,8},{10,11... | collective-permute-start | bytes 1769480 | tf_op jit(solution)/shard_map/ppermute | solution.py:447
  33.6 4.7 %feed.3 = (f32[192,768]{1,0:T(8,128)S(1)}, f32[192,128]{1,0:T(8,128)S(1)}, bf16[192,768]{1,0:T(8,128)(2,1)S(1)}, bf16[192,1536]{1,0:T(8,128)(2,1)S(1)}, f32[192,...) custom-call(f32[8,128]{1,0:T(8,128)S(1)} %get-tuple-element.121.refs_0_, s32[3]{0:T(128)S(1)} %pad_add_fusion.refs_1_, ...), custom_call_target="tpu_custom_call" | custom-call | flops 10000000000 | bytes 1000000 | tf_op jit(solution)/shard_map/feed/pallas_call | solution.py:429
  38.6 8.8 %collective-permute-done.6.refs_2_ = f32[192,768]{1,0:T(8,128)S(1)} collective-permute-done((f32[192,768]{1,0:T(8,128)S(1)}, f32[192,768]{1,0:T(8,128)S(1)}, u32[]{:S(2)}, u32[]{:S(2)}) %collective-permute-start.6) | collective-permute-done | bytes 589856 | tf_op jit(solution)/shard_map/ppermute | solution.py:447
  47.4 3.2 %feed_back.2 = (bf16[192,768]{1,0:T(8,128)(2,1)S(1)}, f32[192,768]{1,0:T(8,128)S(1)}, bf16[192,768]{1,0:T(8,128)(2,1)S(1)}, bf16[192,1536]{1,0:T(8,128)(2,1)S(1)...) custom-call(f32[8,128]{1,0:T(8,128)S(1)} %get-tuple-element.123.refs_0_, ...), custom_call_target="tpu_custom_call" | custom-call | flops 10000000000 | bytes 1000000 | tf_op jit(solution)/shard_map/feed_back/pallas_call | solution.py:429
  52.3 7.7 %collective-permute-done.7.refs_2_ = f32[192,768]{1,0:T(8,128)S(1)} collective-permute-done((f32[192,768]{1,0:T(8,128)S(1)}, f32[192,768]{1,0:T(8,128)S(1)}, u32[]{:S(2)}, u32[]{:S(2)}) %collective-permute-start.7) | collective-permute-done | bytes 589856 | tf_op jit(solution)/shard_map/ppermute | solution.py:447
  60.0 3.2 %feed_back.3 = (bf16[192,768]{1,0:T(8,128)(2,1)S(1)}, f32[192,768]{1,0:T(8,128)S(1)}, bf16[192,768]{1,0:T(8,128)(2,1)S(1)}, bf16[192,1536]{1,0:T(8,128)(2,1)S(1)...) custom-call(f32[8,128]{1,0:T(8,128)S(1)} %get-tuple-element.128.refs_0_, ...), custom_call_target="tpu_custom_call" | custom-call | flops 10000000000 | bytes 1000000 | tf_op jit(solution)/shard_map/feed_back/pallas_call | solution.py:429
  63.2 3.1 %outer.3 = (f32[384,1536]{1,0:T(8,128)S(1)}, f32[384,1536]{1,0:T(8,128)S(1)}, f32[8,128]{1,0:T(8,128)S(1)}) custom-call(f32[8,128]{1,0:T(8,128)S(1)} %get-tuple-element.133.refs_0_, s32[3]{0:T(128)S(1)} %pad_add_fusion.refs_1_, bf16[192,768]{1,0:T(8,128)(2,1)S(1)} %get-tuple-element.134.refs_2_, bf16[192,768]{1,0:T(8,128)(2,1)S(1)} %get-tuple-element.135.refs_3_, ...), custom_call_target="tpu_custom_call" | custom-call | flops 10000000000 | bytes 1000000 | tf_op jit(solution)/shard_map/outer/pallas_call | solution.py:429
  66.4 1.8 %collective-permute-start.10 = (f32[192,768]{1,0:T(8,128)S(1)}, f32[192,768]{1,0:T(8,128)S(1)}, u32[]{:S(2)}, u32[]{:S(2)}) collective-permute-start(f32[192,768]{1,0:T(8,128)S(1)} %get-tuple-element.150.refs_2_), channel_id=1, source_target_pairs={{0,1},{1,0},{2,3},{3,2},{4,5},{5,4},{6,7},{7,6},{8,9},{9,8},{10,11... | collective-permute-start | bytes 1769480 | tf_op jit(solution)/shard_map/ppermute | solution.py:447
  68.2 4.0 %collective-permute-done.8.refs_3_ = f32[192,768]{1,0:T(8,128)S(1)} collective-permute-done((f32[192,768]{1,0:T(8,128)S(1)}, f32[192,768]{1,0:T(8,128)S(1)}, u32[]{:S(2)}, u32[]{:S(2)}) %collective-permute-start.8) | collective-permute-done | bytes 589856 | tf_op jit(solution)/shard_map/ppermute | solution.py:447
  74.0 9.6 %collective-permute-done.10.refs_3_ = f32[192,768]{1,0:T(8,128)S(1)} collective-permute-done((f32[192,768]{1,0:T(8,128)S(1)}, f32[192,768]{1,0:T(8,128)S(1)}, u32[]{:S(2)}, u32[]{:S(2)}) %collective-permute-start.10) | collective-permute-done | bytes 589856 | tf_op jit(solution)/shard_map/ppermute | solution.py:447
  84.0 2.9 %outer.4 = (f32[384,1536]{1,0:T(8,128)S(1)}, f32[384,1536]{1,0:T(8,128)S(1)}, f32[8,128]{1,0:T(8,128)S(1)}) custom-call(f32[8,128]{1,0:T(8,128)S(1)} %get-tuple-element.155.refs_0_, s32[3]{0:T(128)S(1)} %pad_add_fusion.refs_1_, bf16[192,768]{1,0:T(8,128)(2,1)S(1)} %get-tuple-element.156.refs_2_, bf16[192,768]{1,0:T(8,128)(2,1)S(1)} %get-tuple-element.157.refs_3_, ...), custom_call_target="tpu_custom_call" | custom-call | flops 10000000000 | bytes 1000000 | tf_op jit(solution)/shard_map/outer/pallas_call | solution.py:429
  88.5 5.7 %attend_back.1 = (bf16[384,1536]{1,0:T(8,128)(2,1)S(1)}, f32[8,1536]{1,0:T(8,128)S(1)}, f32[8,128]{1,0:T(8,128)S(1)}) custom-call(f32[8,128]{1,0:T(8,128)S(1)} %get-tuple-element.160.refs_0_, bf16[192,768]{1,0:T(8,128)(2,1)S(1)} %get-tuple-element.161.refs_1_.refs_3_, bf16[192,768]{1,0:T(8,128)(2,1)S(1)} %get-tuple-element.162.refs_2_.refs_4_, ...), custom_call_target="tpu_custom_call" | custom-call | flops 10000000000 | bytes 1000000 | tf_op jit(solution)/shard_map/attend_back/pallas_call | solution.py:429
  97.7 3.6 %outer.5 = (f32[392,1536]{1,0:T(8,128)S(1)}, f32[392,1536]{1,0:T(8,128)S(1)}, f32[8,128]{1,0:T(8,128)S(1)}) custom-call(f32[8,128]{1,0:T(8,128)S(1)} %get-tuple-element.172.refs_0_, s32[3]{0:T(128)S(1)} %pad_add_fusion.refs_1_, bf16[384,768]{1,0:T(8,128)(2,1)S(1)} %copy-done.3, bf16[192,768]{1,0:T(8,128)(2,1)S(1)} %get-tuple-element.161.refs_1_.refs_3_, ...), custom_call_target="tpu_custom_call" | custom-call | flops 10000000000 | bytes 1000000 | tf_op jit(solution)/shard_map/outer/pallas_call | solution.py:429
  101.3 2.7 %back_tokens.1 = (f32[384,768]{1,0:T(8,128)S(1)}, f32[8,128]{1,0:T(8,128)S(1)}) custom-call(f32[8,128]{1,0:T(8,128)S(1)} %get-tuple-element.175.refs_0_, bf16[384,1536]{1,0:T(8,128)(2,1)S(1)} %get-tuple-element.173.refs_5_.refs_1_, bf16[3,768,384]{2,1,0:T(8,128)(2,1)} %refs_2_.11), custom_call_target="tpu_custom_call" | custom-call | flops 10000000000 | bytes 1000000 | tf_op jit(solution)/shard_map/back_tokens/pallas_call | solution.py:429
  104.0 5.7 %collective-permute-done.14.refs_4_ = f32[96,1536]{1,0:T(8,128)S(1)} collective-permute-done((f32[96,1536]{1,0:T(8,128)S(1)}, f32[96,1536]{1,0:T(8,128)S(1)}, u32[]{:S(2)}, u32[]{:S(2)}) %collective-permute-start.14) | collective-permute-done | bytes 589856 | tf_op jit(solution)/shard_map/ppermute | solution.py:450
  109.8 2.6 %collective-permute-start.17 = (f32[48,1536]{1,0:T(8,128)S(1)}, f32[48,1536]{1,0:T(8,128)S(1)}, u32[]{:S(2)}, u32[]{:S(2)}) collective-permute-start(f32[48,1536]{1,0:T(8,128)S(1)} %get-tuple-element.186), channel_id=1, source_target_pairs={{0,16},{2,18},{4,20},{6,22},{8,24},{10,26},{12,28},{14,30},{16,0},... | collective-permute-start | bytes 884744 | tf_op jit(solution)/shard_map/ppermute | solution.py:450
  119.2 6.3 %collective-permute-done.17.refs_5_ = f32[48,1536]{1,0:T(8,128)S(1)} collective-permute-done((f32[48,1536]{1,0:T(8,128)S(1)}, f32[48,1536]{1,0:T(8,128)S(1)}, u32[]{:S(2)}, u32[]{:S(2)}) %collective-permute-start.17) | collective-permute-done | bytes 294944 | tf_op jit(solution)/shard_map/ppermute | solution.py:450
  126.9 1.8 %collective-permute-done.18.refs_3_ = f32[96,1536]{1,0:T(8,128)S(1)} collective-permute-done((f32[96,1536]{1,0:T(8,128)S(1)}, f32[96,1536]{1,0:T(8,128)S(1)}, u32[]{:S(2)}, u32[]{:S(2)}) %collective-permute-start.18) | collective-permute-done | bytes 589856 | tf_op jit(solution)/shard_map/ppermute | solution.py:450
  128.8 6.9 %collective-permute-done.19.refs_4_ = f32[96,1536]{1,0:T(8,128)S(1)} collective-permute-done((f32[96,1536]{1,0:T(8,128)S(1)}, f32[96,1536]{1,0:T(8,128)S(1)}, u32[]{:S(2)}, u32[]{:S(2)}) %collective-permute-start.19) | collective-permute-done | bytes 589856 | tf_op jit(solution)/shard_map/ppermute | solution.py:450
  135.8 2.6 %collective-permute-start.21 = (f32[48,1536]{1,0:T(8,128)S(1)}, f32[48,1536]{1,0:T(8,128)S(1)}, u32[]{:S(2)}, u32[]{:S(2)}) collective-permute-start(f32[48,1536]{1,0:T(8,128)S(1)} %get-tuple-element.194), channel_id=1, source_target_pairs={{0,16},{2,18},{4,20},{6,22},{8,24},{10,26},{12,28},{14,30},{16,0},... | collective-permute-start | bytes 884744 | tf_op jit(solution)/shard_map/ppermute | solution.py:450
  138.4 4.1 %collective-permute-done.20.refs_3_.refs_6_ = f32[104,1536]{1,0:T(8,128)S(1)} collective-permute-done((f32[104,1536]{1,0:T(8,128)S(1)}, f32[104,1536]{1,0:T(8,128)S(1)}, u32[]{:S(2)}, u32[]{:S(2)}) %collective-permute-start.20) | collective-permute-done | bytes 639008 | tf_op jit(solution)/shard_map/ppermute | solution.py:450
  145.6 5.6 %collective-permute-done.21.refs_5_ = f32[48,1536]{1,0:T(8,128)S(1)} collective-permute-done((f32[48,1536]{1,0:T(8,128)S(1)}, f32[48,1536]{1,0:T(8,128)S(1)}, u32[]{:S(2)}, u32[]{:S(2)}) %collective-permute-start.21) | collective-permute-done | bytes 294944 | tf_op jit(solution)/shard_map/ppermute | solution.py:450
  152.0 2.4 %collective-permute-done.22.refs_3_ = f32[96,1536]{1,0:T(8,128)S(1)} collective-permute-done((f32[96,1536]{1,0:T(8,128)S(1)}, f32[96,1536]{1,0:T(8,128)S(1)}, u32[]{:S(2)}, u32[]{:S(2)}) %collective-permute-start.22) | collective-permute-done | bytes 589856 | tf_op jit(solution)/shard_map/ppermute | solution.py:450
  154.4 3.5 %collective-permute-done.23.refs_4_ = f32[56,1536]{1,0:T(8,128)S(1)} collective-permute-done((f32[56,1536]{1,0:T(8,128)S(1)}, f32[56,1536]{1,0:T(8,128)S(1)}, u32[]{:S(2)}, u32[]{:S(2)}) %collective-permute-start.23) | collective-permute-done | bytes 344096 | tf_op jit(solution)/shard_map/ppermute | solution.py:450
  158.0 2.3 %collective-permute-start.26 = (f32[8,1536]{1,0:T(8,128)S(1)}, f32[8,1536]{1,0:T(8,128)S(1)}, u32[]{:S(2)}, u32[]{:S(2)}) collective-permute-start(f32[8,1536]{1,0:T(8,128)S(1)} %get-tuple-element.207.refs_1_), channel_id=1, source_target_pairs={{0,16},{2,18},{4,20},{6,22},{8,24},{10,26},{12,28},{14,30},{16,0},... | collective-permute-start | bytes 147464 | tf_op jit(solution)/shard_map/ppermute | solution.py:450
  161.0 3.4 %collective-permute-done.24.refs_4_ = f32[48,1536]{1,0:T(8,128)S(1)} collective-permute-done((f32[48,1536]{1,0:T(8,128)S(1)}, f32[48,1536]{1,0:T(8,128)S(1)}, u32[]{:S(2)}, u32[]{:S(2)}) %collective-permute-start.24) | collective-permute-done | bytes 294944 | tf_op jit(solution)/shard_map/ppermute | solution.py:450
  167.6 7.9 %collective-permute-done.27.refs_2_ = f32[48,1536]{1,0:T(8,128)S(1)} collective-permute-done((f32[48,1536]{1,0:T(8,128)S(1)}, f32[48,1536]{1,0:T(8,128)S(1)}, u32[]{:S(2)}, u32[]{:S(2)}) %collective-permute-start.27) | collective-permute-done | bytes 294944 | tf_op jit(solution)/shard_map/ppermute | solution.py:450
  (110 shorter events, 32.6 us)
Async XLA Ops:
  1.7 17.3 %copy-start.5 = (bf16[768]{0:T(1024)(128)(2,1)S(1)}, bf16[768]{0:T(1024)(128)(2,1)}, u32[]{:S(2)}) copy-start(bf16[768]{0:T(1024)(128)(2,1)} %refs_2_.7) | copy-start | bytes 4612
  1.7 17.3 %copy-start.6 = (bf16[768]{0:T(1024)(128)(2,1)S(1)}, bf16[768]{0:T(1024)(128)(2,1)}, u32[]{:S(2)}) copy-start(bf16[768]{0:T(1024)(128)(2,1)} %refs_3_.4) | copy-start | bytes 4612
  1.7 17.2 %copy-start.7 = (bf16[768]{0:T(1024)(128)(2,1)S(1)}, bf16[768]{0:T(1024)(128)(2,1)}, u32[]{:S(2)}) copy-start(bf16[768]{0:T(1024)(128)(2,1)} %refs_4_.3) | copy-start | bytes 4612
  1.7 17.2 %copy-start.8 = (bf16[768]{0:T(1024)(128)(2,1)S(1)}, bf16[768]{0:T(1024)(128)(2,1)}, u32[]{:S(2)}) copy-start(bf16[768]{0:T(1024)(128)(2,1)} %refs_5_.5) | copy-start | bytes 4612
  1.7 17.2 %collective-permute-start = (f32[192,768]{1,0:T(8,128)S(1)}, f32[192,768]{1,0:T(8,128)S(1)}, u32[]{:S(2)}, u32[]{:S(2)}) collective-permute-start(f32[192,768]{1,0:T(8,128)S(1)} %dynamic-slice_convert_fusion), channel_id=1, source_target_pairs={{0,1},{1,0},{2,3},{3,2},{4,5},{5,4},{6,7},{7,6},{8,9},{9,8},{10,11... | collective-permute-start | bytes 1769480 | tf_op jit(solution)/shard_map/ppermute | solution.py:447
  12.5 11.9 %collective-permute-start.1 = (f32[192,384]{1,0:T(8,128)}, f32[192,384]{1,0:T(8,128)S(1)}, u32[]{:S(2)}, u32[]{:S(2)}) collective-permute-start(f32[192,384]{1,0:T(8,128)} %get-tuple-element.118), channel_id=1, source_target_pairs={{0,1},{1,0},{2,3},{3,2},{4,5},{5,4},{6,7},{7,6},{8,9},{9,8},{10,11... | collective-permute-start | bytes 884744 | tf_op jit(solution)/shard_map/ppermute | solution.py:447
  20.4 4.0 %collective-permute-start.2 = (f32[64,768]{1,0:T(8,128)S(1)}, f32[64,768]{1,0:T(8,128)S(1)}, u32[]{:S(2)}, u32[]{:S(2)}) collective-permute-start(f32[64,768]{1,0:T(8,128)S(1)} %get-tuple-element.225), channel_id=1, source_target_pairs={{0,2},{2,0},{4,6},{6,4},{8,10},{10,8},{12,14},{14,12},{16,18},{18,... | collective-permute-start | bytes 589832 | tf_op jit(solution)/shard_map/ppermute | solution.py:450
  20.5 4.0 %collective-permute-start.3 = (f32[64,768]{1,0:T(8,128)S(1)}, f32[64,768]{1,0:T(8,128)S(1)}, u32[]{:S(2)}, u32[]{:S(2)}) collective-permute-start(f32[64,768]{1,0:T(8,128)S(1)} %get-tuple-element.224), channel_id=1, source_target_pairs={{0,2},{2,0},{4,6},{6,4},{8,10},{10,8},{12,14},{14,12},{16,18},{18,... | collective-permute-start | bytes 589832 | tf_op jit(solution)/shard_map/ppermute | solution.py:450
  21.0 3.5 %collective-permute-start.4 = (f32[64,768]{1,0:T(8,128)S(1)}, f32[64,768]{1,0:T(8,128)S(1)}, u32[]{:S(2)}, u32[]{:S(2)}) collective-permute-start(f32[64,768]{1,0:T(8,128)S(1)} %get-tuple-element.223), channel_id=1, source_target_pairs={{0,2},{2,0},{4,6},{6,4},{8,10},{10,8},{12,14},{14,12},{16,18},{18,... | collective-permute-start | bytes 589832 | tf_op jit(solution)/shard_map/ppermute | solution.py:450
  21.0 11.8 %collective-permute-start.5 = (f32[192,384]{1,0:T(8,128)S(1)}, f32[192,384]{1,0:T(8,128)S(1)}, u32[]{:S(2)}, u32[]{:S(2)}) collective-permute-start(f32[192,384]{1,0:T(8,128)S(1)} %copy-done.17), channel_id=1, source_target_pairs={{0,1},{1,0},{2,3},{3,2},{4,5},{5,4},{6,7},{7,6},{8,9},{9,8},{10,11... | collective-permute-start | bytes 884744 | tf_op jit(solution)/shard_map/ppermute | solution.py:447
  31.0 16.3 %collective-permute-start.6 = (f32[192,768]{1,0:T(8,128)S(1)}, f32[192,768]{1,0:T(8,128)S(1)}, u32[]{:S(2)}, u32[]{:S(2)}) collective-permute-start(f32[192,768]{1,0:T(8,128)S(1)} %get-tuple-element.124.refs_1_), channel_id=1, source_target_pairs={{0,1},{1,0},{2,3},{3,2},{4,5},{5,4},{6,7},{7,6},{8,9},{9,8},{10,11... | collective-permute-start | bytes 1769480 | tf_op jit(solution)/shard_map/ppermute | solution.py:447
  38.2 21.8 %collective-permute-start.7 = (f32[192,768]{1,0:T(8,128)S(1)}, f32[192,768]{1,0:T(8,128)S(1)}, u32[]{:S(2)}, u32[]{:S(2)}) collective-permute-start(f32[192,768]{1,0:T(8,128)S(1)} %get-tuple-element.129.refs_1_), channel_id=1, source_target_pairs={{0,1},{1,0},{2,3},{3,2},{4,5},{5,4},{6,7},{7,6},{8,9},{9,8},{10,11... | collective-permute-start | bytes 1769480 | tf_op jit(solution)/shard_map/ppermute | solution.py:447
  50.5 21.7 %collective-permute-start.8 = (f32[192,768]{1,0:T(8,128)S(1)}, f32[192,768]{1,0:T(8,128)S(1)}, u32[]{:S(2)}, u32[]{:S(2)}) collective-permute-start(f32[192,768]{1,0:T(8,128)S(1)} %get-tuple-element.140.refs_2_), channel_id=1, source_target_pairs={{0,1},{1,0},{2,3},{3,2},{4,5},{5,4},{6,7},{7,6},{8,9},{9,8},{10,11... | collective-permute-start | bytes 1769480 | tf_op jit(solution)/shard_map/ppermute | solution.py:447
  66.3 6.4 %collective-permute-start.9 = (f32[384,1536]{1,0:T(8,128)S(1)}, f32[384,1536]{1,0:T(8,128)S(1)}, u32[]{:S(2)}, u32[]{:S(2)}) collective-permute-start(f32[384,1536]{1,0:T(8,128)S(1)} %get-tuple-element.146), channel_id=1, source_target_pairs={{0,2},{2,0},{4,6},{6,4},{8,10},{10,8},{12,14},{14,12},{16,18},{18,... | collective-permute-start | bytes 7077896 | tf_op jit(solution)/shard_map/ppermute | solution.py:450
  66.4 17.1 %collective-permute-start.10 = (f32[192,768]{1,0:T(8,128)S(1)}, f32[192,768]{1,0:T(8,128)S(1)}, u32[]{:S(2)}, u32[]{:S(2)}) collective-permute-start(f32[192,768]{1,0:T(8,128)S(1)} %get-tuple-element.150.refs_2_), channel_id=1, source_target_pairs={{0,1},{1,0},{2,3},{3,2},{4,5},{5,4},{6,7},{7,6},{8,9},{9,8},{10,11... | collective-permute-start | bytes 1769480 | tf_op jit(solution)/shard_map/ppermute | solution.py:447
  72.8 21.5 %collective-permute-start.11 = (f32[96,1536]{1,0:T(8,128)S(1)}, f32[96,1536]{1,0:T(8,128)S(1)}, u32[]{:S(2)}, u32[]{:S(2)}) collective-permute-start(f32[96,1536]{1,0:T(8,128)S(1)} %get-tuple-element.167), channel_id=1, source_target_pairs={{0,4},{2,6},{4,0},{6,2},{8,12},{10,14},{12,8},{14,10},{16,20},{18,... | collective-permute-start | bytes 1769480 | tf_op jit(solution)/shard_map/ppermute | solution.py:450
  87.0 9.0 %collective-permute-start.12 = (f32[384,1536]{1,0:T(8,128)S(1)}, f32[384,1536]{1,0:T(8,128)S(1)}, u32[]{:S(2)}, u32[]{:S(2)}) collective-permute-start(f32[384,1536]{1,0:T(8,128)S(1)} %get-tuple-element.170), channel_id=1, source_target_pairs={{0,2},{2,0},{4,6},{6,4},{8,10},{10,8},{12,14},{14,12},{16,18},{18,... | collective-permute-start | bytes 7077896 | tf_op jit(solution)/shard_map/ppermute | solution.py:450
  87.1 17.0 %collective-permute-start.13 = (f32[96,1536]{1,0:T(8,128)S(1)}, f32[96,1536]{1,0:T(8,128)S(1)}, u32[]{:S(2)}, u32[]{:S(2)}) collective-permute-start(f32[96,1536]{1,0:T(8,128)S(1)} %get-tuple-element.177), channel_id=1, source_target_pairs={{0,4},{2,6},{4,0},{6,2},{8,12},{10,14},{12,8},{14,10},{16,20},{18,... | collective-permute-start | bytes 1769480 | tf_op jit(solution)/shard_map/ppermute | solution.py:450
  94.3 15.5 %collective-permute-start.14 = (f32[96,1536]{1,0:T(8,128)S(1)}, f32[96,1536]{1,0:T(8,128)S(1)}, u32[]{:S(2)}, u32[]{:S(2)}) collective-permute-start(f32[96,1536]{1,0:T(8,128)S(1)} %get-tuple-element.178), channel_id=1, source_target_pairs={{0,8},{2,10},{4,12},{6,14},{8,0},{10,2},{12,4},{14,6},{16,24},{18,... | collective-permute-start | bytes 1769480 | tf_op jit(solution)/shard_map/ppermute | solution.py:450
  96.0 19.9 %collective-permute-start.15 = (f32[96,1536]{1,0:T(8,128)S(1)}, f32[96,1536]{1,0:T(8,128)S(1)}, u32[]{:S(2)}, u32[]{:S(2)}) collective-permute-start(f32[96,1536]{1,0:T(8,128)S(1)} %get-tuple-element.180), channel_id=1, source_target_pairs={{0,4},{2,6},{4,0},{6,2},{8,12},{10,14},{12,8},{14,10},{16,20},{18,... | collective-permute-start | bytes 1769480 | tf_op jit(solution)/shard_map/ppermute | solution.py:450
  101.3 16.3 %collective-permute-start.16 = (f32[392,1536]{1,0:T(8,128)S(1)}, f32[392,1536]{1,0:T(8,128)S(1)}, u32[]{:S(2)}, u32[]{:S(2)}) collective-permute-start(f32[392,1536]{1,0:T(8,128)S(1)} %get-tuple-element.183), channel_id=1, source_target_pairs={{0,2},{2,0},{4,6},{6,4},{8,10},{10,8},{12,14},{14,12},{16,18},{18,... | collective-permute-start | bytes 7225352 | tf_op jit(solution)/shard_map/ppermute | solution.py:450
  109.8 15.6 %collective-permute-start.17 = (f32[48,1536]{1,0:T(8,128)S(1)}, f32[48,1536]{1,0:T(8,128)S(1)}, u32[]{:S(2)}, u32[]{:S(2)}) collective-permute-start(f32[48,1536]{1,0:T(8,128)S(1)} %get-tuple-element.186), channel_id=1, source_target_pairs={{0,16},{2,18},{4,20},{6,22},{8,24},{10,26},{12,28},{14,30},{16,0},... | collective-permute-start | bytes 884744 | tf_op jit(solution)/shard_map/ppermute | solution.py:450
  112.5 16.3 %collective-permute-start.18 = (f32[96,1536]{1,0:T(8,128)S(1)}, f32[96,1536]{1,0:T(8,128)S(1)}, u32[]{:S(2)}, u32[]{:S(2)}) collective-permute-start(f32[96,1536]{1,0:T(8,128)S(1)} %get-tuple-element.188), channel_id=1, source_target_pairs={{0,4},{2,6},{4,0},{6,2},{8,12},{10,14},{12,8},{14,10},{16,20},{18,... | collective-permute-start | bytes 1769480 | tf_op jit(solution)/shard_map/ppermute | solution.py:450
  113.0 51.4 %collective-permute-start.25 = (f32[384,768]{1,0:T(8,128)S(1)}, f32[384,768]{1,0:T(8,128)S(1)}, u32[]{:S(2)}, u32[]{:S(2)}) collective-permute-start(f32[384,768]{1,0:T(8,128)S(1)} %get-tuple-element.202.refs_1_), channel_id=1, source_target_pairs={{0,1},{1,0},{2,3},{3,2},{4,5},{5,4},{6,7},{7,6},{8,9},{9,8},{10,11... | collective-permute-start | bytes 3538952 | tf_op jit(solution)/shard_map/ppermute | solution.py:447
  116.0 19.7 %collective-permute-start.19 = (f32[96,1536]{1,0:T(8,128)S(1)}, f32[96,1536]{1,0:T(8,128)S(1)}, u32[]{:S(2)}, u32[]{:S(2)}) collective-permute-start(f32[96,1536]{1,0:T(8,128)S(1)} %get-tuple-element.189), channel_id=1, source_target_pairs={{0,8},{2,10},{4,12},{6,14},{8,0},{10,2},{12,4},{14,6},{16,24},{18,... | collective-permute-start | bytes 1769480 | tf_op jit(solution)/shard_map/ppermute | solution.py:450
  117.6 24.9 %collective-permute-start.20 = (f32[104,1536]{1,0:T(8,128)S(1)}, f32[104,1536]{1,0:T(8,128)S(1)}, u32[]{:S(2)}, u32[]{:S(2)}) collective-permute-start(f32[104,1536]{1,0:T(8,128)S(1)} %get-tuple-element.191), channel_id=1, source_target_pairs={{0,4},{2,6},{4,0},{6,2},{8,12},{10,14},{12,8},{14,10},{16,20},{18,... | collective-permute-start | bytes 1916936 | tf_op jit(solution)/shard_map/ppermute | solution.py:450
  125.5 28.9 %collective-permute-start.22 = (f32[96,1536]{1,0:T(8,128)S(1)}, f32[96,1536]{1,0:T(8,128)S(1)}, u32[]{:S(2)}, u32[]{:S(2)}) collective-permute-start(f32[96,1536]{1,0:T(8,128)S(1)} %get-tuple-element.196), channel_id=1, source_target_pairs={{0,4},{2,6},{4,0},{6,2},{8,12},{10,14},{12,8},{14,10},{16,20},{18,... | collective-permute-start | bytes 1769480 | tf_op jit(solution)/shard_map/ppermute | solution.py:450
  135.8 15.4 %collective-permute-start.21 = (f32[48,1536]{1,0:T(8,128)S(1)}, f32[48,1536]{1,0:T(8,128)S(1)}, u32[]{:S(2)}, u32[]{:S(2)}) collective-permute-start(f32[48,1536]{1,0:T(8,128)S(1)} %get-tuple-element.194), channel_id=1, source_target_pairs={{0,16},{2,18},{4,20},{6,22},{8,24},{10,26},{12,28},{14,30},{16,0},... | collective-permute-start | bytes 884744 | tf_op jit(solution)/shard_map/ppermute | solution.py:450
  142.5 15.4 %collective-permute-start.23 = (f32[56,1536]{1,0:T(8,128)S(1)}, f32[56,1536]{1,0:T(8,128)S(1)}, u32[]{:S(2)}, u32[]{:S(2)}) collective-permute-start(f32[56,1536]{1,0:T(8,128)S(1)} %get-tuple-element.197), channel_id=1, source_target_pairs={{0,8},{2,10},{4,12},{6,14},{8,0},{10,2},{12,4},{14,6},{16,24},{18,... | collective-permute-start | bytes 1032200 | tf_op jit(solution)/shard_map/ppermute | solution.py:450
  144.2 20.1 %collective-permute-start.24 = (f32[48,1536]{1,0:T(8,128)S(1)}, f32[48,1536]{1,0:T(8,128)S(1)}, u32[]{:S(2)}, u32[]{:S(2)}) collective-permute-start(f32[48,1536]{1,0:T(8,128)S(1)} %get-tuple-element.200), channel_id=1, source_target_pairs={{0,8},{2,10},{4,12},{6,14},{8,0},{10,2},{12,4},{14,6},{16,24},{18,... | collective-permute-start | bytes 884744 | tf_op jit(solution)/shard_map/ppermute | solution.py:450
  158.0 7.8 %collective-permute-start.26 = (f32[8,1536]{1,0:T(8,128)S(1)}, f32[8,1536]{1,0:T(8,128)S(1)}, u32[]{:S(2)}, u32[]{:S(2)}) collective-permute-start(f32[8,1536]{1,0:T(8,128)S(1)} %get-tuple-element.207.refs_1_), channel_id=1, source_target_pairs={{0,16},{2,18},{4,20},{6,22},{8,24},{10,26},{12,28},{14,30},{16,0},... | collective-permute-start | bytes 147464 | tf_op jit(solution)/shard_map/ppermute | solution.py:450
  160.2 15.3 %collective-permute-start.27 = (f32[48,1536]{1,0:T(8,128)S(1)}, f32[48,1536]{1,0:T(8,128)S(1)}, u32[]{:S(2)}, u32[]{:S(2)}) collective-permute-start(f32[48,1536]{1,0:T(8,128)S(1)} %get-tuple-element.210), channel_id=1, source_target_pairs={{0,16},{2,18},{4,20},{6,22},{8,24},{10,26},{12,28},{14,30},{16,0},... | collective-permute-start | bytes 884744 | tf_op jit(solution)/shard_map/ppermute | solution.py:450
  (19 other events, 90.9 us)

commit v5 on v4

--- a/solution.py
+++ b/solution.py
@@ -554,103 +554,131 @@
             outs = [jnp.concatenate([out] + riders, 0) for out in outs]
         return outs
 
-    def pick(held, begin, end):
-        return [(array, first) for array, first in held if first <= begin and end <= first + array.shape[0]]
-
-    def add(held, begin, end, flops=None, extra=()):
-        wide = held[0][0].shape[1]
-        if not fused:
-            parts = []
-            for row in range(begin, end, size):
-                parts.append(functools.reduce(jnp.add, [a[row - f : row - f + size] for a, f in pick(held, row, row + size)]))
-            if extra:
-                parts.append(functools.reduce(jnp.add, [a[row : row + 8] for a, row in extra]))
-            return jnp.concatenate(parts, 0)
-        operands, specs, counts = [], [], []
-
-        def take(array, row, height):
-            operands.append(array)
-            specs.append(pl.BlockSpec((height, wide), functools.partial(lambda index, n: (index, 0), row // height)))
-
-        for row in range(begin, end, size):
-            inside = pick(held, row, row + size)
-            counts.append(len(inside))
-            for array, first in inside:
-                take(array, row - first, size)
-        if extra:
-            counts.append(len(extra))
-            for array, row in extra:
-                take(array, row, 8)
-        outs = [shape((end - begin + (8 if extra else 0), wide), F32)]
-        return call(functools.partial(fold_blocks, counts), "fold", operands, specs, outs, full(*outs), flops=flops)[0]
+    class Chunk:
+        def __init__(self, outs, came, wide, column, bits, rides=False):
+            keep = outs[1]
+            self.wide = wide
+            self.parts = {p: [(keep, p, column), (came, p, column)] for p in range(ranks // 2)}
+            self.alive = list(self.parts)
+            self.bits = list(bits)
+            self.extra = [(keep, width // 16), (came, width // 16)] if rides else []
+
+        def add(self, places, flops, rides=False):
+            wide = self.wide
+            if not fused:
+                sums = []
+                for p in places:
+                    found = [
+                        array[row * size : (row + 1) * size, column * wide : (column + 1) * wide]
+                        for array, row, column in self.parts[p]
+                    ]
+                    sums.append(functools.reduce(jnp.add, found))
+                if rides:
+                    sums.append(functools.reduce(jnp.add, [a[8 * row : 8 * row + 8] for a, row in self.extra]))
+                return jnp.concatenate(sums, 0)
+            operands, specs, counts = [], [], []
+            for p in places:
+                counts.append(len(self.parts[p]))
+                for array, row, column in self.parts[p]:
+                    operands.append(array)
+                    specs.append(pl.BlockSpec((size, wide), functools.partial(lambda r, c, n: (r, c), row, column)))
+            if rides:
+                counts.append(len(self.extra))
+                for array, row in self.extra:
+                    operands.append(array)
+                    specs.append(pl.BlockSpec((8, wide), functools.partial(lambda r, n: (r, 0), row)))
+            outs = [shape((len(places) * size + (8 if rides else 0), wide), F32)]
+            return call(
+                functools.partial(fold_blocks, counts), "fold", operands, specs, outs, full(*outs), flops=flops
+            )[0]
+
+        def weight(self, bit):
+            return ranks // (2 * bit)
+
+        def send(self, places, flops, rides):
+            bit = self.bits[0]
+            rides = rides and self.extra and len(self.bits) > 1
+            came = swap_dp(self.add(places, flops, rides), bit)
+            self.arrived = getattr(self, "arrived", [])
+            for i, p in enumerate(places):
+                self.arrived.append((p ^ self.weight(bit), (came, i, 0)))
+            if rides:
+                self.extra = self.extra + [(came, len(places) * size // 8)]
+
+        def close(self):
+            for p, part in self.arrived:
+                self.parts[p].append(part)
+            self.arrived = []
+            weight = self.weight(self.bits.pop(0))
+            self.alive = [p for p in self.alive if not p & weight]
+
+        def leaving(self):
+            weight = self.weight(self.bits[0])
+            return [p for p in self.alive if p & weight]
+
+        def step(self, flops=None):
+            self.send(self.leaving(), flops, True)
+            self.close()
+
+        def high(self, flops=None):
+            if len(self.bits) == 1:
+                self.step(flops)
+            else:
+                after = self.weight(self.bits[1])
+                self.send([p for p in self.leaving() if p & after], flops, True)
+
+        def low(self, flops=None):
+            after = self.weight(self.bits[1])
+            self.send([p for p in self.leaving() if not p & after], flops, False)
+            self.close()
+
+        def rest(self):
+            while self.bits:
+                self.step()
+
+        def all_but_last(self):
+            last = self.parts[0].pop()
+            self.parts[0] = [(self.add([0], None), 0, 0), last]
+
+        def last(self, flops=None):
+            self.rest()
+            return self.add([0], flops)
 
     def add_extra(extra):
         if not fused:
-            return functools.reduce(jnp.add, [a[row : row + 8] for a, row in extra])
+            return functools.reduce(jnp.add, [a[8 * row : 8 * row + 8] for a, row in extra])
         wide = extra[0][0].shape[1]
-        specs = [pl.BlockSpec((8, wide), functools.partial(lambda index, n: (index, 0), row // 8)) for _, row in extra]
+        specs = [pl.BlockSpec((8, wide), functools.partial(lambda index, n: (index, 0), row)) for _, row in extra]
         outs = [shape((8, wide), F32)]
         return call(fold, "fold", [array for array, _ in extra], specs, outs, full(*outs))[0]
 
-    class Chunk:
-        def __init__(self, outs, rides=False):
-            sent, keep = outs
-            came = swap_dp(sent, stages[0])
-            self.held = [(keep, 0), (came, 0)]
-            self.extra = [(keep, width // 2), (came, width // 2)] if rides else []
-            self.stage = 0
-
-        def send(self, begin, end, flops, rides):
-            rides = rides and self.extra and self.stage < len(stages) - 1
-            came = swap_dp(add(self.held, begin, end, flops, self.extra if rides else ()), stages[self.stage])
-            if rides:
-                self.extra = self.extra + [(came, end - begin)]
-            return came
-
-        def step(self, flops=None):
-            self.stage += 1
-            half = width // (4 << (self.stage - 1))
-            self.held = self.held + [(self.send(half, 2 * half, flops, True), 0)]
-
-        def high(self, flops=None):
-            half = self.half = width // (4 << self.stage)
-            if half == size:
-                self.step(flops)
-            else:
-                self.stage += 1
-                self.came = [(self.send(half + half // 2, 2 * half, flops, True), half // 2)]
-
-        def low(self, flops=None):
-            part = self.send(self.half, self.half + self.half // 2, flops, False)
-            self.held = self.held + self.came + [(part, 0)]
-
-        def all_but_last(self):
-            self.held = [(add(self.held[:-1], 0, size), 0), self.held[-1]]
-
-        def last(self, flops=None):
-            self.rest()
-            return add(self.held, 0, size, flops)
-
-        def rest(self):
-            while self.stage < len(stages) - 1:
-                self.step()
-            return [(array, first) for array, first in self.held if first == 0]
-
-    down = Chunk(gradient([o[2] for o in back], [s[3] for s in saved], blocks, [0] * tiles, tile))
+    straight, turned = stages[1:], stages[2:] + stages[1:2]
+    outs = gradient([o[2] for o in back], [s[3] for s in saved], blocks, [0] * tiles, tile)
+    came = swap_dp(outs[0], stages[0])
+    down = Chunk(outs, came, hidden // 3 * 2, 0, straight)
+    early = Chunk(outs, came, hidden // 3, 2, turned)
     wide = 4 * local
 
     def first_norm(i):
         outs = [shape((blocks[i], width), F32), shape((blocks[i], width), LOW), shape((8, wide), F32)]
         operands = [back[i][1], back[i][4], back[i][7], saved[i][0], saved[i][1], back[i][5], back[i][6], vectors]
         operands += [norms[-1][2]] if norms else []
-        norms.append(call(norm_one_back, "norm_one_back", operands, full(*operands), outs, full(*outs), flops=2 * 10**10 if i == 0 else None))
+        flops = 2 * 10**10 if i == 0 else None
+        norms.append(call(norm_one_back, "norm_one_back", operands, full(*operands), outs, full(*outs), flops=flops))
 
     norms = []
     first_norm(0)
     down.high()
     down.low()
+    early.step()
+    outs = gradient([s[2] for s in saved], [o[3] for o in back], blocks, [0] * tiles, tile)
+    up = Chunk(outs, swap_dp(outs[0], stages[0]), hidden, 0, straight)
     first_norm(1)
-    up = Chunk(gradient([s[2] for s in saved], [o[3] for o in back], blocks, [0] * tiles, tile))
+    early.step()
+    down.step(2 * 10**10)
+    up.high()
+    up.low()
+    pace[0] = 10**8
     dr1s, lows = [n[0] for n in norms], [n[1] for n in norms]
     outs = [shape((rows, 4 * local), LOW), shape((8, wide), F32)]
     operands = lows + [w_out, qkv, context, lse, lengths, pad_row, norms[-1][2]]
@@ -659,11 +687,11 @@
         full(*lows) + [far_off] * 3 + full(lse) + [smem] + full(pad_row, norms[-1][2]), outs, full(*outs),
         scratch=[pltpu.VMEM((local, width), LOW), pltpu.VMEM((rows, 3 * local), LOW), dma((3,))],
     )
-    down.step(2 * 10**10)
-    up.high()
-    up.low()
-    mixed = Chunk(rides=True, outs=gradient([tokens] + lows, [e], [rows], [0, 0, 0, 1], local, bias))
-
+    outs = gradient([tokens] + lows, [e], [rows], [0, 0, 0, 1], local, bias)
+    mixed = Chunk(outs, swap_dp(outs[0], stages[0]), wide, 0, straight, rides=True)
+
+    while early.bits:
+        early.step()
     outs = [shape((rows, width), F32)]
     (partial,) = call(
         back_tokens, "back_tokens", [e, w_qkv], full(e) + [far_off], outs, full(*outs),
@@ -671,8 +699,7 @@
     )
     pace[0] = 10**9
     partial_far = swap_tp(partial)
-    pace[0] = 10**9
-    down.step()
+    down.step(2 * 10**10)
     up.step(2 * 10**10)
     mixed.high()
     mixed.low()
@@ -681,30 +708,24 @@
     mixed.high()
     mixed.low()
     up = up.last()
-    while mixed.stage < len(stages) - 1:
-        mixed.high()
-        if mixed.half > size:
-            mixed.low()
+    mixed.rest()
     bias = add_extra(mixed.extra)
     bias_far = swap_dp(bias, stages[-1])
     mixed.all_but_last()
+    early = early.last()
     (d_tokens,) = call(
         join, "join", [partial, partial_far] + dr1s, full(partial, partial_far, *dr1s), outs, full(*outs)
     )
     (bias,) = call(fold, "fold", [bias, bias_far], full(bias, bias_far), [shape(bias.shape, F32)], full(bias))
-    mixed = mixed.rest()
-
-    def finish(held):
-        return functools.reduce(jnp.add, [array[:size] for array, _ in held])
-
     if fused:
         outs = [shape((3, size, local), F32), shape((size, local), F32)]
+        operands = [array for array, _, _ in mixed.parts[0]]
         d_w_qkv, d_w_out = call(
-            functools.partial(spread, local), "spread", [array for array, _ in mixed],
-            [pl.BlockSpec((size, 4 * local), lambda n: (0, 0))] * len(mixed), outs, full(*outs),
+            functools.partial(spread, local), "spread", operands,
+            [pl.BlockSpec((size, wide), lambda n: (0, 0))] * len(operands), outs, full(*outs),
         )
     else:
-        last = finish(mixed)
+        last = mixed.add([0], None)
         d_w_qkv = last[:, : 3 * local].reshape(size, 3, local).transpose(1, 0, 2)
         d_w_out = last[:, 3 * local :]
     return (
@@ -718,7 +739,7 @@
         bias[4, :width],
         up,
         bias[6, :hidden],
-        down.T,
+        jnp.concatenate([down.T, early.T], 0),
         bias[2, :width],
         bias[0, :width],
         bias[1, :width],

time: 177 us -> 166 us (0.938)
  waiting for transfers between devices: 86.6 us -> 74.5 us
    ppermute x20 -> x23, waiting for transfers between devices: 48.9 us -> 42.1 us  [swap_dp(): return lax.ppermute(array, 'dp', [(i, i ^ bits) for i in range(ranks)])]
    ppermute x8, waiting for transfers between devices: 37.6 us -> 32.4 us  [swap_tp(): return lax.ppermute(array, 'tp', pairs)]
    ppermute x20 -> x23, starting transfers between devices: 20.4 us -> 22.1 us  [swap_dp(): return lax.ppermute(array, 'dp', [(i, i ^ bits) for i in range(ranks)])]
    pallas_call x33 -> x37, Pallas kernels: 47.9 us -> 47.3 us  [call(): pl.pallas_call(chained(kernel, len(operands), len(out_shape)), grid=grid,...]
  transfers between devices with their start and end apart: 28 -> 31, of which waited for: 17 -> 16; matrix products, arithmetic and copies ran while one was open for 2% -> 2% of each run, Pallas kernels for 27% -> 28%
where the time goes in v5:
time: 166 us
  waiting for transfers between devices  74.5 us (45%)
  Pallas kernels  47.3 us (28%)
  starting transfers between devices  34.6 us (21%)
  local copies, waits for them, and re-layouts  5.46 us (3%)
  other arithmetic  2.67 us (2%)
    pallas_call x37, Pallas kernels, call(): pl.pallas_call(chained(kernel, len(operands), len(out_shape)), grid=grid,...  47.3 us
    ppermute x23, waiting for transfers between devices, swap_dp(): return lax.ppermute(array, 'dp', [(i, i ^ bits) for i in range(ranks)])  42.1 us
    ppermute x8, waiting for transfers between devices, swap_tp(): return lax.ppermute(array, 'tp', pairs)  32.4 us
    ppermute x23, starting transfers between devices, swap_dp(): return lax.ppermute(array, 'dp', [(i, i ^ bits) for i in range(ranks)])  22.1 us
    ppermute x8, starting transfers between devices, swap_tp(): return lax.ppermute(array, 'tp', pairs)  12.5 us
    unnamed x46, local copies, waits for them, and re-layouts  3.57 us
  transfers between devices with their start and end apart: 31, of which 16 were waited for; matrix products, arithmetic and copies ran while one was open for 2% of the time, Pallas kernels for 28%

profile of v5, /device:TPU:0, one launch (start us, length us, event | category | flops | bytes accessed | tf_op | source)
XLA Modules:
  0.0 165.6 jit_solution(4626979148619435500)
XLA Ops:
  1.7 3.0 %collective-permute-start = (f32[192,768]{1,0:T(8,128)S(1)}, f32[192,768]{1,0:T(8,128)S(1)}, u32[]{:S(2)}, u32[]{:S(2)}) collective-permute-start(f32[192,768]{1,0:T(8,128)S(1)} %dynamic-slice_convert_fusion), channel_id=1, source_target_pairs={{0,1},{1,0},{2,3},{3,2},{4,5},{5,4},{6,7},{7,6},{8,9},{9,8},{10,11... | collective-permute-start | bytes 1769480 | tf_op jit(solution)/shard_map/ppermute | solution.py:447
  4.8 7.7 %attend.1 = (bf16[384,1152]{1,0:T(8,128)(2,1)}, bf16[384,384]{1,0:T(8,128)(2,1)}, f32[8,384]{1,0:T(8,128)}, f32[192,384]{1,0:T(8,128)}, f32[192,384]{1,0:T(8,128)}, /*index=5*/f32[8,128]{1,0:T(8,128)}) custom-call(bf16[384,768]{1,0:T(8,128)(2,1)} %refs_2_.10, bf16[384,768]{1,0:T(8,128)(2,1)} %refs_2_.10, bf16[3,768,384]{2,1,0:T(8,128)(2,1)} %refs_2_.11, ...), custom_call_target="tpu_custom_call" | custom-call | flops 10000000000 | bytes 1000000 | tf_op jit(solution)/shard_map/attend/pallas_call | solution.py:429
  12.6 6.4 %collective-permute-done.refs_1_ = f32[192,768]{1,0:T(8,128)S(1)} collective-permute-done((f32[192,768]{1,0:T(8,128)S(1)}, f32[192,768]{1,0:T(8,128)S(1)}, u32[]{:S(2)}, u32[]{:S(2)}) %collective-permute-start) | collective-permute-done | bytes 589856 | tf_op jit(solution)/shard_map/ppermute | solution.py:447
  21.0 2.1 %collective-permute-start.5 = (f32[192,384]{1,0:T(8,128)S(1)}, f32[192,384]{1,0:T(8,128)S(1)}, u32[]{:S(2)}, u32[]{:S(2)}) collective-permute-start(f32[192,384]{1,0:T(8,128)S(1)} %copy-done.17), channel_id=1, source_target_pairs={{0,1},{1,0},{2,3},{3,2},{4,5},{5,4},{6,7},{7,6},{8,9},{9,8},{10,11... | collective-permute-start | bytes 884744 | tf_op jit(solution)/shard_map/ppermute | solution.py:447
  25.3 5.7 %feed.2 = (f32[192,768]{1,0:T(8,128)S(1)}, f32[192,128]{1,0:T(8,128)S(1)}, bf16[192,768]{1,0:T(8,128)(2,1)S(1)}, bf16[192,1536]{1,0:T(8,128)(2,1)S(1)}, f32[192,...) custom-call(f32[8,128]{1,0:T(8,128)S(1)} %get-tuple-element.124.refs_0_, s32[3]{0:T(128)S(1)} %pad_add_fusion.refs_1_, ...), custom_call_target="tpu_custom_call" | custom-call | flops 10000000000 | bytes 1000000 | tf_op jit(solution)/shard_map/feed/pallas_call | solution.py:429
  31.0 1.8 %collective-permute-start.6 = (f32[192,768]{1,0:T(8,128)S(1)}, f32[192,768]{1,0:T(8,128)S(1)}, u32[]{:S(2)}, u32[]{:S(2)}) collective-permute-start(f32[192,768]{1,0:T(8,128)S(1)} %get-tuple-element.132.refs_1_), channel_id=1, source_target_pairs={{0,1},{1,0},{2,3},{3,2},{4,5},{5,4},{6,7},{7,6},{8,9},{9,8},{10,11... | collective-permute-start | bytes 1769480 | tf_op jit(solution)/shard_map/ppermute | solution.py:447
  33.6 4.7 %feed.3 = (f32[192,768]{1,0:T(8,128)S(1)}, f32[192,128]{1,0:T(8,128)S(1)}, bf16[192,768]{1,0:T(8,128)(2,1)S(1)}, bf16[192,1536]{1,0:T(8,128)(2,1)S(1)}, f32[192,...) custom-call(f32[8,128]{1,0:T(8,128)S(1)} %get-tuple-element.129.refs_0_, s32[3]{0:T(128)S(1)} %pad_add_fusion.refs_1_, ...), custom_call_target="tpu_custom_call" | custom-call | flops 10000000000 | bytes 1000000 | tf_op jit(solution)/shard_map/feed/pallas_call | solution.py:429
  38.6 8.8 %collective-permute-done.6.refs_2_ = f32[192,768]{1,0:T(8,128)S(1)} collective-permute-done((f32[192,768]{1,0:T(8,128)S(1)}, f32[192,768]{1,0:T(8,128)S(1)}, u32[]{:S(2)}, u32[]{:S(2)}) %collective-permute-start.6) | collective-permute-done | bytes 589856 | tf_op jit(solution)/shard_map/ppermute | solution.py:447
  47.4 3.2 %feed_back.2 = (bf16[192,768]{1,0:T(8,128)(2,1)S(1)}, f32[192,768]{1,0:T(8,128)S(1)}, bf16[192,768]{1,0:T(8,128)(2,1)S(1)}, bf16[192,1536]{1,0:T(8,128)(2,1)S(1)...) custom-call(f32[8,128]{1,0:T(8,128)S(1)} %get-tuple-element.131.refs_0_, ...), custom_call_target="tpu_custom_call" | custom-call | flops 10000000000 | bytes 1000000 | tf_op jit(solution)/shard_map/feed_back/pallas_call | solution.py:429
  50.5 1.8 %collective-permute-start.8 = (f32[192,768]{1,0:T(8,128)S(1)}, f32[192,768]{1,0:T(8,128)S(1)}, u32[]{:S(2)}, u32[]{:S(2)}) collective-permute-start(f32[192,768]{1,0:T(8,128)S(1)} %get-tuple-element.148.refs_2_), channel_id=1, source_target_pairs={{0,1},{1,0},{2,3},{3,2},{4,5},{5,4},{6,7},{7,6},{8,9},{9,8},{10,11... | collective-permute-start | bytes 1769480 | tf_op jit(solution)/shard_map/ppermute | solution.py:447
  52.3 7.7 %collective-permute-done.7.refs_2_ = f32[192,768]{1,0:T(8,128)S(1)} collective-permute-done((f32[192,768]{1,0:T(8,128)S(1)}, f32[192,768]{1,0:T(8,128)S(1)}, u32[]{:S(2)}, u32[]{:S(2)}) %collective-permute-start.7) | collective-permute-done | bytes 589856 | tf_op jit(solution)/shard_map/ppermute | solution.py:447
  60.0 3.2 %feed_back.3 = (bf16[192,768]{1,0:T(8,128)(2,1)S(1)}, f32[192,768]{1,0:T(8,128)S(1)}, bf16[192,768]{1,0:T(8,128)(2,1)S(1)}, bf16[192,1536]{1,0:T(8,128)(2,1)S(1)...) custom-call(f32[8,128]{1,0:T(8,128)S(1)} %get-tuple-element.136.refs_0_, ...), custom_call_target="tpu_custom_call" | custom-call | flops 10000000000 | bytes 1000000 | tf_op jit(solution)/shard_map/feed_back/pallas_call | solution.py:429
  63.2 3.1 %outer.3 = (f32[384,1536]{1,0:T(8,128)S(1)}, f32[384,1536]{1,0:T(8,128)S(1)}, f32[8,128]{1,0:T(8,128)S(1)}) custom-call(f32[8,128]{1,0:T(8,128)S(1)} %get-tuple-element.141.refs_0_, s32[3]{0:T(128)S(1)} %pad_add_fusion.refs_1_, bf16[192,768]{1,0:T(8,128)(2,1)S(1)} %get-tuple-element.142.refs_2_, bf16[192,768]{1,0:T(8,128)(2,1)S(1)} %get-tuple-element.143.refs_3_, ...), custom_call_target="tpu_custom_call" | custom-call | flops 10000000000 | bytes 1000000 | tf_op jit(solution)/shard_map/outer/pallas_call | solution.py:429
  66.4 1.8 %collective-permute-start.10 = (f32[192,768]{1,0:T(8,128)S(1)}, f32[192,768]{1,0:T(8,128)S(1)}, u32[]{:S(2)}, u32[]{:S(2)}) collective-permute-start(f32[192,768]{1,0:T(8,128)S(1)} %get-tuple-element.164.refs_2_), channel_id=1, source_target_pairs={{0,1},{1,0},{2,3},{3,2},{4,5},{5,4},{6,7},{7,6},{8,9},{9,8},{10,11... | collective-permute-start | bytes 1769480 | tf_op jit(solution)/shard_map/ppermute | solution.py:447
  68.2 4.0 %collective-permute-done.8.refs_3_ = f32[192,768]{1,0:T(8,128)S(1)} collective-permute-done((f32[192,768]{1,0:T(8,128)S(1)}, f32[192,768]{1,0:T(8,128)S(1)}, u32[]{:S(2)}, u32[]{:S(2)}) %collective-permute-start.8) | collective-permute-done | bytes 589856 | tf_op jit(solution)/shard_map/ppermute | solution.py:447
  75.6 2.9 %outer.4 = (f32[384,1536]{1,0:T(8,128)S(1)}, f32[384,1536]{1,0:T(8,128)S(1)}, f32[8,128]{1,0:T(8,128)S(1)}) custom-call(f32[8,128]{1,0:T(8,128)S(1)} %get-tuple-element.157.refs_0_, s32[3]{0:T(128)S(1)} %pad_add_fusion.refs_1_, bf16[192,768]{1,0:T(8,128)(2,1)S(1)} %get-tuple-element.158.refs_2_, bf16[192,768]{1,0:T(8,128)(2,1)S(1)} %get-tuple-element.159.refs_3_, ...), custom_call_target="tpu_custom_call" | custom-call | flops 10000000000 | bytes 1000000 | tf_op jit(solution)/shard_map/outer/pallas_call | solution.py:429
  79.2 4.4 %collective-permute-done.10.refs_3_ = f32[192,768]{1,0:T(8,128)S(1)} collective-permute-done((f32[192,768]{1,0:T(8,128)S(1)}, f32[192,768]{1,0:T(8,128)S(1)}, u32[]{:S(2)}, u32[]{:S(2)}) %collective-permute-start.10) | collective-permute-done | bytes 589856 | tf_op jit(solution)/shard_map/ppermute | solution.py:447
  84.1 2.6 %collective-permute-start.14 = (f32[96,512]{1,0:T(8,128)S(1)}, f32[96,512]{1,0:T(8,128)S(1)}, u32[]{:S(2)}, u32[]{:S(2)}) collective-permute-start(f32[96,512]{1,0:T(8,128)S(1)} %get-tuple-element.187), channel_id=1, source_target_pairs={{0,16},{2,18},{4,20},{6,22},{8,24},{10,26},{12,28},{14,30},{16,0},... | collective-permute-start | bytes 589832 | tf_op jit(solution)/shard_map/ppermute | solution.py:450
  90.7 5.7 %attend_back.1 = (bf16[384,1536]{1,0:T(8,128)(2,1)S(1)}, f32[8,1536]{1,0:T(8,128)S(1)}, f32[8,128]{1,0:T(8,128)S(1)}) custom-call(f32[8,128]{1,0:T(8,128)S(1)} %get-tuple-element.177.refs_0_, bf16[192,768]{1,0:T(8,128)(2,1)S(1)} %get-tuple-element.178.refs_1_.refs_3_, bf16[192,768]{1,0:T(8,128)(2,1)S(1)} %get-tuple-element.179.refs_2_.refs_4_, ...), custom_call_target="tpu_custom_call" | custom-call | flops 100000000 | bytes 1000000 | tf_op jit(solution)/shard_map/attend_back/pallas_call | solution.py:429
  96.4 3.6 %outer.5 = (f32[392,1536]{1,0:T(8,128)S(1)}, f32[392,1536]{1,0:T(8,128)S(1)}, f32[8,128]{1,0:T(8,128)S(1)}) custom-call(f32[8,128]{1,0:T(8,128)S(1)} %get-tuple-element.183.refs_0_, s32[3]{0:T(128)S(1)} %pad_add_fusion.refs_1_, bf16[384,768]{1,0:T(8,128)(2,1)S(1)} %copy-done.1, bf16[192,768]{1,0:T(8,128)(2,1)S(1)} %get-tuple-element.178.refs_1_.refs_3_, ...), custom_call_target="tpu_custom_call" | custom-call | flops 100000000 | bytes 1000000 | tf_op jit(solution)/shard_map/outer/pallas_call | solution.py:429
  100.1 2.7 %back_tokens.1 = (f32[384,768]{1,0:T(8,128)S(1)}, f32[8,128]{1,0:T(8,128)S(1)}) custom-call(f32[8,128]{1,0:T(8,128)S(1)} %get-tuple-element.188.refs_0_, bf16[384,1536]{1,0:T(8,128)(2,1)S(1)} %get-tuple-element.184.refs_5_.refs_1_, bf16[3,768,384]{2,1,0:T(8,128)(2,1)} %refs_2_.11), custom_call_target="tpu_custom_call" | custom-call | flops 100000000 | bytes 1000000 | tf_op jit(solution)/shard_map/back_tokens/pallas_call | solution.py:429
  105.7 1.7 collective-permute-start.21
  107.4 1.9 %collective-permute-start.22 = (f32[104,1536]{1,0:T(8,128)S(1)}, f32[104,1536]{1,0:T(8,128)S(1)}, u32[]{:S(2)}, u32[]{:S(2)}) collective-permute-start(f32[104,1536]{1,0:T(8,128)S(1)} %get-tuple-element.204), channel_id=1, source_target_pairs={{0,4},{2,6},{4,0},{6,2},{8,12},{10,14},{12,8},{14,10},{16,20},{18,... | collective-permute-start | bytes 1916936 | tf_op jit(solution)/shard_map/ppermute | solution.py:450
  109.4 5.9 %collective-permute-done.19.refs_5_ = f32[48,1024]{1,0:T(8,128)S(1)} collective-permute-done((f32[48,1024]{1,0:T(8,128)S(1)}, f32[48,1024]{1,0:T(8,128)S(1)}, u32[]{:S(2)}, u32[]{:S(2)}) %collective-permute-start.19) | collective-permute-done | bytes 196640 | tf_op jit(solution)/shard_map/ppermute | solution.py:450
  115.9 4.2 %collective-permute-done.20.refs_3_ = f32[96,1536]{1,0:T(8,128)S(1)} collective-permute-done((f32[96,1536]{1,0:T(8,128)S(1)}, f32[96,1536]{1,0:T(8,128)S(1)}, u32[]{:S(2)}, u32[]{:S(2)}) %collective-permute-start.20) | collective-permute-done | bytes 589856 | tf_op jit(solution)/shard_map/ppermute | solution.py:450
  120.1 4.8 %collective-permute-done.21.refs_4_ = f32[96,1536]{1,0:T(8,128)S(1)} collective-permute-done((f32[96,1536]{1,0:T(8,128)S(1)}, f32[96,1536]{1,0:T(8,128)S(1)}, u32[]{:S(2)}, u32[]{:S(2)}) %collective-permute-start.21) | collective-permute-done | bytes 589856 | tf_op jit(solution)/shard_map/ppermute | solution.py:450
  125.2 8.6 %collective-permute-done.22.refs_3_.refs_6_ = f32[104,1536]{1,0:T(8,128)S(1)} collective-permute-done((f32[104,1536]{1,0:T(8,128)S(1)}, f32[104,1536]{1,0:T(8,128)S(1)}, u32[]{:S(2)}, u32[]{:S(2)}) %collective-permute-start.22) | collective-permute-done | bytes 639008 | tf_op jit(solution)/shard_map/ppermute | solution.py:450
  136.9 2.6 %collective-permute-done.23.refs_5_ = f32[48,1536]{1,0:T(8,128)S(1)} collective-permute-done((f32[48,1536]{1,0:T(8,128)S(1)}, f32[48,1536]{1,0:T(8,128)S(1)}, u32[]{:S(2)}, u32[]{:S(2)}) %collective-permute-start.23) | collective-permute-done | bytes 294944 | tf_op jit(solution)/shard_map/ppermute | solution.py:450
  141.8 4.6 %collective-permute-done.24.refs_3_ = f32[96,1536]{1,0:T(8,128)S(1)} collective-permute-done((f32[96,1536]{1,0:T(8,128)S(1)}, f32[96,1536]{1,0:T(8,128)S(1)}, u32[]{:S(2)}, u32[]{:S(2)}) %collective-permute-start.24) | collective-permute-done | bytes 589856 | tf_op jit(solution)/shard_map/ppermute | solution.py:450
  149.9 4.6 %collective-permute-done.26.refs_4_ = f32[48,1536]{1,0:T(8,128)S(1)} collective-permute-done((f32[48,1536]{1,0:T(8,128)S(1)}, f32[48,1536]{1,0:T(8,128)S(1)}, u32[]{:S(2)}, u32[]{:S(2)}) %collective-permute-start.26) | collective-permute-done | bytes 294944 | tf_op jit(solution)/shard_map/ppermute | solution.py:450
  156.6 2.8 %collective-permute-done.29.refs_2_ = f32[8,1536]{1,0:T(8,128)S(1)} collective-permute-done((f32[8,1536]{1,0:T(8,128)S(1)}, f32[8,1536]{1,0:T(8,128)S(1)}, u32[]{:S(2)}, u32[]{:S(2)}) %collective-permute-start.29) | collective-permute-done | bytes 49184 | tf_op jit(solution)/shard_map/ppermute | solution.py:450
  161.2 3.6 %collective-permute-done.30.refs_2_ = f32[48,1536]{1,0:T(8,128)S(1)} collective-permute-done((f32[48,1536]{1,0:T(8,128)S(1)}, f32[48,1536]{1,0:T(8,128)S(1)}, u32[]{:S(2)}, u32[]{:S(2)}) %collective-permute-start.30) | collective-permute-done | bytes 294944 | tf_op jit(solution)/shard_map/ppermute | solution.py:450
  (121 shorter events, 32.8 us)
Async XLA Ops:
  1.7 17.3 %copy-start.8 = (bf16[768]{0:T(1024)(128)(2,1)S(1)}, bf16[768]{0:T(1024)(128)(2,1)}, u32[]{:S(2)}) copy-start(bf16[768]{0:T(1024)(128)(2,1)} %refs_2_.7) | copy-start | bytes 4612
  1.7 17.2 %collective-permute-start = (f32[192,768]{1,0:T(8,128)S(1)}, f32[192,768]{1,0:T(8,128)S(1)}, u32[]{:S(2)}, u32[]{:S(2)}) collective-permute-start(f32[192,768]{1,0:T(8,128)S(1)} %dynamic-slice_convert_fusion), channel_id=1, source_target_pairs={{0,1},{1,0},{2,3},{3,2},{4,5},{5,4},{6,7},{7,6},{8,9},{9,8},{10,11... | collective-permute-start | bytes 1769480 | tf_op jit(solution)/shard_map/ppermute | solution.py:447
  12.5 11.9 %collective-permute-start.1 = (f32[192,384]{1,0:T(8,128)}, f32[192,384]{1,0:T(8,128)S(1)}, u32[]{:S(2)}, u32[]{:S(2)}) collective-permute-start(f32[192,384]{1,0:T(8,128)} %get-tuple-element.126), channel_id=1, source_target_pairs={{0,1},{1,0},{2,3},{3,2},{4,5},{5,4},{6,7},{7,6},{8,9},{9,8},{10,11... | collective-permute-start | bytes 884744 | tf_op jit(solution)/shard_map/ppermute | solution.py:447
  20.4 4.0 %collective-permute-start.2 = (f32[64,768]{1,0:T(8,128)S(1)}, f32[64,768]{1,0:T(8,128)S(1)}, u32[]{:S(2)}, u32[]{:S(2)}) collective-permute-start(f32[64,768]{1,0:T(8,128)S(1)} %get-tuple-element.241), channel_id=1, source_target_pairs={{0,2},{2,0},{4,6},{6,4},{8,10},{10,8},{12,14},{14,12},{16,18},{18,... | collective-permute-start | bytes 589832 | tf_op jit(solution)/shard_map/ppermute | solution.py:450
  20.5 4.0 %collective-permute-start.3 = (f32[64,768]{1,0:T(8,128)S(1)}, f32[64,768]{1,0:T(8,128)S(1)}, u32[]{:S(2)}, u32[]{:S(2)}) collective-permute-start(f32[64,768]{1,0:T(8,128)S(1)} %get-tuple-element.240), channel_id=1, source_target_pairs={{0,2},{2,0},{4,6},{6,4},{8,10},{10,8},{12,14},{14,12},{16,18},{18,... | collective-permute-start | bytes 589832 | tf_op jit(solution)/shard_map/ppermute | solution.py:450
  21.0 3.5 %collective-permute-start.4 = (f32[64,768]{1,0:T(8,128)S(1)}, f32[64,768]{1,0:T(8,128)S(1)}, u32[]{:S(2)}, u32[]{:S(2)}) collective-permute-start(f32[64,768]{1,0:T(8,128)S(1)} %get-tuple-element.239), channel_id=1, source_target_pairs={{0,2},{2,0},{4,6},{6,4},{8,10},{10,8},{12,14},{14,12},{16,18},{18,... | collective-permute-start | bytes 589832 | tf_op jit(solution)/shard_map/ppermute | solution.py:450
  21.0 11.8 %collective-permute-start.5 = (f32[192,384]{1,0:T(8,128)S(1)}, f32[192,384]{1,0:T(8,128)S(1)}, u32[]{:S(2)}, u32[]{:S(2)}) collective-permute-start(f32[192,384]{1,0:T(8,128)S(1)} %copy-done.17), channel_id=1, source_target_pairs={{0,1},{1,0},{2,3},{3,2},{4,5},{5,4},{6,7},{7,6},{8,9},{9,8},{10,11... | collective-permute-start | bytes 884744 | tf_op jit(solution)/shard_map/ppermute | solution.py:447
  31.0 16.3 %collective-permute-start.6 = (f32[192,768]{1,0:T(8,128)S(1)}, f32[192,768]{1,0:T(8,128)S(1)}, u32[]{:S(2)}, u32[]{:S(2)}) collective-permute-start(f32[192,768]{1,0:T(8,128)S(1)} %get-tuple-element.132.refs_1_), channel_id=1, source_target_pairs={{0,1},{1,0},{2,3},{3,2},{4,5},{5,4},{6,7},{7,6},{8,9},{9,8},{10,11... | collective-permute-start | bytes 1769480 | tf_op jit(solution)/shard_map/ppermute | solution.py:447
  38.2 21.8 %collective-permute-start.7 = (f32[192,768]{1,0:T(8,128)S(1)}, f32[192,768]{1,0:T(8,128)S(1)}, u32[]{:S(2)}, u32[]{:S(2)}) collective-permute-start(f32[192,768]{1,0:T(8,128)S(1)} %get-tuple-element.137.refs_1_), channel_id=1, source_target_pairs={{0,1},{1,0},{2,3},{3,2},{4,5},{5,4},{6,7},{7,6},{8,9},{9,8},{10,11... | collective-permute-start | bytes 1769480 | tf_op jit(solution)/shard_map/ppermute | solution.py:447
  50.5 21.7 %collective-permute-start.8 = (f32[192,768]{1,0:T(8,128)S(1)}, f32[192,768]{1,0:T(8,128)S(1)}, u32[]{:S(2)}, u32[]{:S(2)}) collective-permute-start(f32[192,768]{1,0:T(8,128)S(1)} %get-tuple-element.148.refs_2_), channel_id=1, source_target_pairs={{0,1},{1,0},{2,3},{3,2},{4,5},{5,4},{6,7},{7,6},{8,9},{9,8},{10,11... | collective-permute-start | bytes 1769480 | tf_op jit(solution)/shard_map/ppermute | solution.py:447
  66.3 6.4 %collective-permute-start.9 = (f32[384,1536]{1,0:T(8,128)S(1)}, f32[384,1536]{1,0:T(8,128)S(1)}, u32[]{:S(2)}, u32[]{:S(2)}) collective-permute-start(f32[384,1536]{1,0:T(8,128)S(1)} %get-tuple-element.154), channel_id=1, source_target_pairs={{0,2},{2,0},{4,6},{6,4},{8,10},{10,8},{12,14},{14,12},{16,18},{18,... | collective-permute-start | bytes 7077896 | tf_op jit(solution)/shard_map/ppermute | solution.py:450
  66.4 17.1 %collective-permute-start.10 = (f32[192,768]{1,0:T(8,128)S(1)}, f32[192,768]{1,0:T(8,128)S(1)}, u32[]{:S(2)}, u32[]{:S(2)}) collective-permute-start(f32[192,768]{1,0:T(8,128)S(1)} %get-tuple-element.164.refs_2_), channel_id=1, source_target_pairs={{0,1},{1,0},{2,3},{3,2},{4,5},{5,4},{6,7},{7,6},{8,9},{9,8},{10,11... | collective-permute-start | bytes 1769480 | tf_op jit(solution)/shard_map/ppermute | solution.py:447
  72.9 11.1 %collective-permute-start.11 = (f32[192,512]{1,0:T(8,128)S(1)}, f32[192,512]{1,0:T(8,128)S(1)}, u32[]{:S(2)}, u32[]{:S(2)}) collective-permute-start(f32[192,512]{1,0:T(8,128)S(1)} %get-tuple-element.170), channel_id=1, source_target_pairs={{0,8},{2,10},{4,12},{6,14},{8,0},{10,2},{12,4},{14,6},{16,24},{18,... | collective-permute-start | bytes 1179656 | tf_op jit(solution)/shard_map/ppermute | solution.py:450
  74.1 12.5 %collective-permute-start.12 = (f32[96,1024]{1,0:T(8,128)S(1)}, f32[96,1024]{1,0:T(8,128)S(1)}, u32[]{:S(2)}, u32[]{:S(2)}) collective-permute-start(f32[96,1024]{1,0:T(8,128)S(1)} %get-tuple-element.172), channel_id=1, source_target_pairs={{0,4},{2,6},{4,0},{6,2},{8,12},{10,14},{12,8},{14,10},{16,20},{18,... | collective-permute-start | bytes 1179656 | tf_op jit(solution)/shard_map/ppermute | solution.py:450
  78.5 9.8 %collective-permute-start.13 = (f32[384,1536]{1,0:T(8,128)S(1)}, f32[384,1536]{1,0:T(8,128)S(1)}, u32[]{:S(2)}, u32[]{:S(2)}) collective-permute-start(f32[384,1536]{1,0:T(8,128)S(1)} %get-tuple-element.175), channel_id=1, source_target_pairs={{0,2},{2,0},{4,6},{6,4},{8,10},{10,8},{12,14},{14,12},{16,18},{18,... | collective-permute-start | bytes 7077896 | tf_op jit(solution)/shard_map/ppermute | solution.py:450
  78.6 24.2 %collective-permute-start.15 = (f32[96,1024]{1,0:T(8,128)S(1)}, f32[96,1024]{1,0:T(8,128)S(1)}, u32[]{:S(2)}, u32[]{:S(2)}) collective-permute-start(f32[96,1024]{1,0:T(8,128)S(1)} %get-tuple-element.190), channel_id=1, source_target_pairs={{0,4},{2,6},{4,0},{6,2},{8,12},{10,14},{12,8},{14,10},{16,20},{18,... | collective-permute-start | bytes 1179656 | tf_op jit(solution)/shard_map/ppermute | solution.py:450
  84.1 16.0 %collective-permute-start.14 = (f32[96,512]{1,0:T(8,128)S(1)}, f32[96,512]{1,0:T(8,128)S(1)}, u32[]{:S(2)}, u32[]{:S(2)}) collective-permute-start(f32[96,512]{1,0:T(8,128)S(1)} %get-tuple-element.187), channel_id=1, source_target_pairs={{0,16},{2,18},{4,20},{6,22},{8,24},{10,26},{12,28},{14,30},{16,0},... | collective-permute-start | bytes 589832 | tf_op jit(solution)/shard_map/ppermute | solution.py:450
  86.7 16.1 %collective-permute-start.16 = (f32[96,1024]{1,0:T(8,128)S(1)}, f32[96,1024]{1,0:T(8,128)S(1)}, u32[]{:S(2)}, u32[]{:S(2)}) collective-permute-start(f32[96,1024]{1,0:T(8,128)S(1)} %get-tuple-element.191), channel_id=1, source_target_pairs={{0,8},{2,10},{4,12},{6,14},{8,0},{10,2},{12,4},{14,6},{16,24},{18,... | collective-permute-start | bytes 1179656 | tf_op jit(solution)/shard_map/ppermute | solution.py:450
  88.4 17.2 %collective-permute-start.17 = (f32[96,1536]{1,0:T(8,128)S(1)}, f32[96,1536]{1,0:T(8,128)S(1)}, u32[]{:S(2)}, u32[]{:S(2)}) collective-permute-start(f32[96,1536]{1,0:T(8,128)S(1)} %get-tuple-element.193), channel_id=1, source_target_pairs={{0,4},{2,6},{4,0},{6,2},{8,12},{10,14},{12,8},{14,10},{16,20},{18,... | collective-permute-start | bytes 1769480 | tf_op jit(solution)/shard_map/ppermute | solution.py:450
  100.0 7.4 %collective-permute-start.18 = (f32[392,1536]{1,0:T(8,128)S(1)}, f32[392,1536]{1,0:T(8,128)S(1)}, u32[]{:S(2)}, u32[]{:S(2)}) collective-permute-start(f32[392,1536]{1,0:T(8,128)S(1)} %get-tuple-element.196), channel_id=1, source_target_pairs={{0,2},{2,0},{4,6},{6,4},{8,10},{10,8},{12,14},{14,12},{16,18},{18,... | collective-permute-start | bytes 7225352 | tf_op jit(solution)/shard_map/ppermute | solution.py:450
  102.8 12.5 %collective-permute-start.19 = (f32[48,1024]{1,0:T(8,128)S(1)}, f32[48,1024]{1,0:T(8,128)S(1)}, u32[]{:S(2)}, u32[]{:S(2)}) collective-permute-start(f32[48,1024]{1,0:T(8,128)S(1)} %get-tuple-element.199), channel_id=1, source_target_pairs={{0,16},{2,18},{4,20},{6,22},{8,24},{10,26},{12,28},{14,30},{16,0},... | collective-permute-start | bytes 589832 | tf_op jit(solution)/shard_map/ppermute | solution.py:450
  103.9 16.2 %collective-permute-start.20 = (f32[96,1536]{1,0:T(8,128)S(1)}, f32[96,1536]{1,0:T(8,128)S(1)}, u32[]{:S(2)}, u32[]{:S(2)}) collective-permute-start(f32[96,1536]{1,0:T(8,128)S(1)} %get-tuple-element.201), channel_id=1, source_target_pairs={{0,4},{2,6},{4,0},{6,2},{8,12},{10,14},{12,8},{14,10},{16,20},{18,... | collective-permute-start | bytes 1769480 | tf_op jit(solution)/shard_map/ppermute | solution.py:450
  104.1 51.3 %collective-permute-start.28 = (f32[384,768]{1,0:T(8,128)S(1)}, f32[384,768]{1,0:T(8,128)S(1)}, u32[]{:S(2)}, u32[]{:S(2)}) collective-permute-start(f32[384,768]{1,0:T(8,128)S(1)} %get-tuple-element.217.refs_1_), channel_id=1, source_target_pairs={{0,1},{1,0},{2,3},{3,2},{4,5},{5,4},{6,7},{7,6},{8,9},{9,8},{10,11... | collective-permute-start | bytes 3538952 | tf_op jit(solution)/shard_map/ppermute | solution.py:447
  105.7 19.2 %collective-permute-start.21 = (f32[96,1536]{1,0:T(8,128)S(1)}, f32[96,1536]{1,0:T(8,128)S(1)}, u32[]{:S(2)}, u32[]{:S(2)}) collective-permute-start(f32[96,1536]{1,0:T(8,128)S(1)} %get-tuple-element.202), channel_id=1, source_target_pairs={{0,8},{2,10},{4,12},{6,14},{8,0},{10,2},{12,4},{14,6},{16,24},{18,... | collective-permute-start | bytes 1769480 | tf_op jit(solution)/shard_map/ppermute | solution.py:450
  107.4 26.3 %collective-permute-start.22 = (f32[104,1536]{1,0:T(8,128)S(1)}, f32[104,1536]{1,0:T(8,128)S(1)}, u32[]{:S(2)}, u32[]{:S(2)}) collective-permute-start(f32[104,1536]{1,0:T(8,128)S(1)} %get-tuple-element.204), channel_id=1, source_target_pairs={{0,4},{2,6},{4,0},{6,2},{8,12},{10,14},{12,8},{14,10},{16,20},{18,... | collective-permute-start | bytes 1916936 | tf_op jit(solution)/shard_map/ppermute | solution.py:450
  115.3 31.1 %collective-permute-start.24 = (f32[96,1536]{1,0:T(8,128)S(1)}, f32[96,1536]{1,0:T(8,128)S(1)}, u32[]{:S(2)}, u32[]{:S(2)}) collective-permute-start(f32[96,1536]{1,0:T(8,128)S(1)} %get-tuple-element.209), channel_id=1, source_target_pairs={{0,4},{2,6},{4,0},{6,2},{8,12},{10,14},{12,8},{14,10},{16,20},{18,... | collective-permute-start | bytes 1769480 | tf_op jit(solution)/shard_map/ppermute | solution.py:450
  125.0 14.5 %collective-permute-start.23 = (f32[48,1536]{1,0:T(8,128)S(1)}, f32[48,1536]{1,0:T(8,128)S(1)}, u32[]{:S(2)}, u32[]{:S(2)}) collective-permute-start(f32[48,1536]{1,0:T(8,128)S(1)} %get-tuple-element.207), channel_id=1, source_target_pairs={{0,16},{2,18},{4,20},{6,22},{8,24},{10,26},{12,28},{14,30},{16,0},... | collective-permute-start | bytes 884744 | tf_op jit(solution)/shard_map/ppermute | solution.py:450
  133.8 13.0 %collective-permute-start.25 = (f32[56,1536]{1,0:T(8,128)S(1)}, f32[56,1536]{1,0:T(8,128)S(1)}, u32[]{:S(2)}, u32[]{:S(2)}) collective-permute-start(f32[56,1536]{1,0:T(8,128)S(1)} %get-tuple-element.210), channel_id=1, source_target_pairs={{0,8},{2,10},{4,12},{6,14},{8,0},{10,2},{12,4},{14,6},{16,24},{18,... | collective-permute-start | bytes 1032200 | tf_op jit(solution)/shard_map/ppermute | solution.py:450
  135.5 19.0 %collective-permute-start.26 = (f32[48,1536]{1,0:T(8,128)S(1)}, f32[48,1536]{1,0:T(8,128)S(1)}, u32[]{:S(2)}, u32[]{:S(2)}) collective-permute-start(f32[48,1536]{1,0:T(8,128)S(1)} %get-tuple-element.213), channel_id=1, source_target_pairs={{0,8},{2,10},{4,12},{6,14},{8,0},{10,2},{12,4},{14,6},{16,24},{18,... | collective-permute-start | bytes 884744 | tf_op jit(solution)/shard_map/ppermute | solution.py:450
  139.4 15.2 %collective-permute-start.27 = (f32[48,512]{1,0:T(8,128)S(1)}, f32[48,512]{1,0:T(8,128)S(1)}, u32[]{:S(2)}, u32[]{:S(2)}) collective-permute-start(f32[48,512]{1,0:T(8,128)S(1)} %get-tuple-element.215), channel_id=1, source_target_pairs={{0,4},{2,6},{4,0},{6,2},{8,12},{10,14},{12,8},{14,10},{16,20},{18,... | collective-permute-start | bytes 294920 | tf_op jit(solution)/shard_map/ppermute | solution.py:450
  147.0 12.4 %collective-permute-start.29 = (f32[8,1536]{1,0:T(8,128)S(1)}, f32[8,1536]{1,0:T(8,128)S(1)}, u32[]{:S(2)}, u32[]{:S(2)}) collective-permute-start(f32[8,1536]{1,0:T(8,128)S(1)} %get-tuple-element.222.refs_1_), channel_id=1, source_target_pairs={{0,16},{2,18},{4,20},{6,22},{8,24},{10,26},{12,28},{14,30},{16,0},... | collective-permute-start | bytes 147464 | tf_op jit(solution)/shard_map/ppermute | solution.py:450
  148.5 16.3 %collective-permute-start.30 = (f32[48,1536]{1,0:T(8,128)S(1)}, f32[48,1536]{1,0:T(8,128)S(1)}, u32[]{:S(2)}, u32[]{:S(2)}) collective-permute-start(f32[48,1536]{1,0:T(8,128)S(1)} %get-tuple-element.225), channel_id=1, source_target_pairs={{0,16},{2,18},{4,20},{6,22},{8,24},{10,26},{12,28},{14,30},{16,0},... | collective-permute-start | bytes 884744 | tf_op jit(solution)/shard_map/ppermute | solution.py:450
  (22 other events, 136.5 us)

commit v6 on v5

--- a/solution.py
+++ b/solution.py
@@ -148,7 +148,7 @@
 
 def feed(taken, tile, far_parts, streamed, place_ref, x_hbm, own_hbm, far_hbm, w_own_hbm, w_near_hbm, *refs):
     w_fars, refs = refs[:far_parts], refs[far_parts:]
-    vec_hbm, b_up_ref, w_up, w_down, normed_ref, inverse_ref, low_ref, act_ref, slope_ref, part_ref = refs[:10]
+    vec_hbm, b_up_ref, w_up, w_down, normed_ref, inverse_ref, low_ref, act_ref, pre_ref, part_ref = refs[:10]
     x_ref, far_ref, vec_ref, w_far, w_full, ctx_full, sems = refs[10:17]
     local = own_hbm.shape[1]
     half = w_near_hbm.shape[0]
@@ -189,7 +189,7 @@
         share = 0.5 * (1.0 + lax.erf(pre * 0.7071067811865476))
         act = (pre * share).astype(LOW)
         act_ref[:, span] = act
-        slope_ref[:, span] = share + pre * jnp.exp(-0.5 * pre * pre) * 0.3989422804014327
+        pre_ref[:, span] = pre
         if streamed:
             came[needed + 2 * i + 1].wait()
         added = dot(act, w_down[span, :])
@@ -197,6 +197,12 @@
             part_ref[...] = added
         else:
             part_ref[...] += added
+
+
+def slopes(pre_ref, out_ref):
+    pre = pre_ref[...]
+    share = 0.5 * (1.0 + lax.erf(pre * 0.7071067811865476))
+    out_ref[...] = share + pre * jnp.exp(-0.5 * pre * pre) * 0.3989422804014327
 
 
 def feed_back(
@@ -515,8 +521,11 @@
         )
         saved.append(outs + [swap_tp(outs[5])])
 
+    slope_of = [
+        call(slopes, "slopes", [s[4]], full(s[4]), [shape(s[4].shape, F32)], full(s[4]))[0] for s in saved
+    ]
     back = []
-    for begin, block, (normed, inverse, low, act, slope, own, far) in zip(starts, blocks, saved):
+    for begin, block, slope, (normed, inverse, low, act, _, own, far) in zip(starts, blocks, slope_of, saved):
         outs = [
             shape((block, width), LOW), shape((block, width), F32), shape((block, width), LOW),
             shape((block, hidden), LOW), shape((block, width), F32), shape((8, width), F32), shape((8, hidden), F32),
@@ -669,15 +678,15 @@
     norms = []
     first_norm(0)
     down.high()
-    down.low()
     early.step()
     outs = gradient([s[2] for s in saved], [o[3] for o in back], blocks, [0] * tiles, tile)
     up = Chunk(outs, swap_dp(outs[0], stages[0]), hidden, 0, straight)
-    first_norm(1)
+    down.low()
+    pace[0] = 10**10
     early.step()
     down.step(2 * 10**10)
     up.high()
-    up.low()
+    first_norm(1)
     pace[0] = 10**8
     dr1s, lows = [n[0] for n in norms], [n[1] for n in norms]
     outs = [shape((rows, 4 * local), LOW), shape((8, wide), F32)]
@@ -687,11 +696,16 @@
         full(*lows) + [far_off] * 3 + full(lse) + [smem] + full(pad_row, norms[-1][2]), outs, full(*outs),
         scratch=[pltpu.VMEM((local, width), LOW), pltpu.VMEM((rows, 3 * local), LOW), dma((3,))],
     )
+    up.low()
     outs = gradient([tokens] + lows, [e], [rows], [0, 0, 0, 1], local, bias)
     mixed = Chunk(outs, swap_dp(outs[0], stages[0]), wide, 0, straight, rides=True)
 
     while early.bits:
         early.step()
+    down.step(5 * 10**9)
+    up.step(4 * 10**10)
+    mixed.high()
+    mixed.low()
     outs = [shape((rows, width), F32)]
     (partial,) = call(
         back_tokens, "back_tokens", [e, w_qkv], full(e) + [far_off], outs, full(*outs),
@@ -699,10 +713,6 @@
     )
     pace[0] = 10**9
     partial_far = swap_tp(partial)
-    down.step(2 * 10**10)
-    up.step(2 * 10**10)
-    mixed.high()
-    mixed.low()
     down = down.last(5 * 10**9)
     up.step()
     mixed.high()

time: 166 us -> 162 us (0.976)
  waiting for transfers between devices: 74.5 us -> 68.7 us
    ppermute x8, waiting for transfers between devices: 32.4 us -> 27.3 us  [swap_tp(): return lax.ppermute(array, 'tp', pairs)]
    ppermute x23, starting transfers between devices: 22.1 us -> 24.1 us  [swap_dp(): return lax.ppermute(array, 'dp', [(i, i ^ bits) for i in range(ranks)])]
    pallas_call x37 -> x39, Pallas kernels: 47.3 us -> 47.8 us  [call(): pl.pallas_call(chained(kernel, len(operands), len(out_shape)), grid=grid,...]
  transfers between devices with their start and end apart: 31 -> 31, of which waited for: 16 -> 14; matrix products, arithmetic and copies ran while one was open for 2% -> 2% of each run, Pallas kernels for 28% -> 29%
where the time goes in v6:
time: 162 us
  waiting for transfers between devices  68.7 us (42%)
  Pallas kernels  47.8 us (30%)
  starting transfers between devices  36.2 us (22%)
  local copies, waits for them, and re-layouts  5.17 us (3%)
  other arithmetic  2.67 us (2%)
    pallas_call x39, Pallas kernels, call(): pl.pallas_call(chained(kernel, len(operands), len(out_shape)), grid=grid,...  47.8 us
    ppermute x23, waiting for transfers between devices, swap_dp(): return lax.ppermute(array, 'dp', [(i, i ^ bits) for i in range(ranks)])  41.4 us
    ppermute x8, waiting for transfers between devices, swap_tp(): return lax.ppermute(array, 'tp', pairs)  27.3 us
    ppermute x23, starting transfers between devices, swap_dp(): return lax.ppermute(array, 'dp', [(i, i ^ bits) for i in range(ranks)])  24.1 us
    ppermute x8, starting transfers between devices, swap_tp(): return lax.ppermute(array, 'tp', pairs)  12.1 us
    unnamed x46, local copies, waits for them, and re-layouts  3.28 us
  transfers between devices with their start and end apart: 31, of which 14 were waited for; matrix products, arithmetic and copies ran while one was open for 2% of the time, Pallas kernels for 29%

profile of v6, /device:TPU:0, one launch (start us, length us, event | category | flops | bytes accessed | tf_op | source)
XLA Modules:
  0.0 161.7 jit_solution(4329594448964111224)
XLA Ops:
  1.7 3.0 %collective-permute-start = (f32[192,768]{1,0:T(8,128)S(1)}, f32[192,768]{1,0:T(8,128)S(1)}, u32[]{:S(2)}, u32[]{:S(2)}) collective-permute-start(f32[192,768]{1,0:T(8,128)S(1)} %dynamic-slice_convert_fusion), channel_id=1, source_target_pairs={{0,1},{1,0},{2,3},{3,2},{4,5},{5,4},{6,7},{7,6},{8,9},{9,8},{10,11... | collective-permute-start | bytes 1769480 | tf_op jit(solution)/shard_map/ppermute | solution.py:453
  4.8 7.7 %attend.1 = (bf16[384,1152]{1,0:T(8,128)(2,1)}, bf16[384,384]{1,0:T(8,128)(2,1)}, f32[8,384]{1,0:T(8,128)}, f32[192,384]{1,0:T(8,128)}, f32[192,384]{1,0:T(8,128)}, /*index=5*/f32[8,128]{1,0:T(8,128)}) custom-call(bf16[384,768]{1,0:T(8,128)(2,1)} %refs_2_.10, bf16[384,768]{1,0:T(8,128)(2,1)} %refs_2_.10, bf16[3,768,384]{2,1,0:T(8,128)(2,1)} %refs_2_.11, ...), custom_call_target="tpu_custom_call" | custom-call | flops 10000000000 | bytes 1000000 | tf_op jit(solution)/shard_map/attend/pallas_call | solution.py:435
  12.6 6.3 %collective-permute-done.refs_1_ = f32[192,768]{1,0:T(8,128)S(1)} collective-permute-done((f32[192,768]{1,0:T(8,128)S(1)}, f32[192,768]{1,0:T(8,128)S(1)}, u32[]{:S(2)}, u32[]{:S(2)}) %collective-permute-start) | collective-permute-done | bytes 589856 | tf_op jit(solution)/shard_map/ppermute | solution.py:453
  21.0 2.1 %collective-permute-start.5 = (f32[192,384]{1,0:T(8,128)S(1)}, f32[192,384]{1,0:T(8,128)S(1)}, u32[]{:S(2)}, u32[]{:S(2)}) collective-permute-start(f32[192,384]{1,0:T(8,128)S(1)} %copy-done.17), channel_id=1, source_target_pairs={{0,1},{1,0},{2,3},{3,2},{4,5},{5,4},{6,7},{7,6},{8,9},{9,8},{10,11... | collective-permute-start | bytes 884744 | tf_op jit(solution)/shard_map/ppermute | solution.py:453
  25.3 5.4 %feed.2 = (f32[192,768]{1,0:T(8,128)S(1)}, f32[192,128]{1,0:T(8,128)S(1)}, bf16[192,768]{1,0:T(8,128)(2,1)S(1)}, bf16[192,1536]{1,0:T(8,128)(2,1)S(1)}, f32[192,...) custom-call(f32[8,128]{1,0:T(8,128)S(1)} %get-tuple-element.128.refs_0_, s32[3]{0:T(128)S(1)} %pad_add_fusion.refs_1_, ...), custom_call_target="tpu_custom_call" | custom-call | flops 10000000000 | bytes 1000000 | tf_op jit(solution)/shard_map/feed/pallas_call | solution.py:435
  30.8 1.8 %collective-permute-start.6 = (f32[192,768]{1,0:T(8,128)S(1)}, f32[192,768]{1,0:T(8,128)S(1)}, u32[]{:S(2)}, u32[]{:S(2)}) collective-permute-start(f32[192,768]{1,0:T(8,128)S(1)} %get-tuple-element.140.refs_1_), channel_id=1, source_target_pairs={{0,1},{1,0},{2,3},{3,2},{4,5},{5,4},{6,7},{7,6},{8,9},{9,8},{10,11... | collective-permute-start | bytes 1769480 | tf_op jit(solution)/shard_map/ppermute | solution.py:453
  33.3 4.6 %feed.3 = (f32[192,768]{1,0:T(8,128)S(1)}, f32[192,128]{1,0:T(8,128)S(1)}, bf16[192,768]{1,0:T(8,128)(2,1)S(1)}, bf16[192,1536]{1,0:T(8,128)(2,1)S(1)}, f32[192,...) custom-call(f32[8,128]{1,0:T(8,128)S(1)} %get-tuple-element.133.refs_0_, s32[3]{0:T(128)S(1)} %pad_add_fusion.refs_1_, ...), custom_call_target="tpu_custom_call" | custom-call | flops 10000000000 | bytes 1000000 | tf_op jit(solution)/shard_map/feed/pallas_call | solution.py:435
  39.1 8.0 %collective-permute-done.6.refs_2_ = f32[192,768]{1,0:T(8,128)S(1)} collective-permute-done((f32[192,768]{1,0:T(8,128)S(1)}, f32[192,768]{1,0:T(8,128)S(1)}, u32[]{:S(2)}, u32[]{:S(2)}) %collective-permute-start.6) | collective-permute-done | bytes 589856 | tf_op jit(solution)/shard_map/ppermute | solution.py:453
  47.1 3.2 %feed_back.2 = (bf16[192,768]{1,0:T(8,128)(2,1)S(1)}, f32[192,768]{1,0:T(8,128)S(1)}, bf16[192,768]{1,0:T(8,128)(2,1)S(1)}, bf16[192,1536]{1,0:T(8,128)(2,1)S(1)...) custom-call(f32[8,128]{1,0:T(8,128)S(1)} %get-tuple-element.139.refs_0_, ...), custom_call_target="tpu_custom_call" | custom-call | flops 10000000000 | bytes 1000000 | tf_op jit(solution)/shard_map/feed_back/pallas_call | solution.py:435
  50.2 1.8 %collective-permute-start.8 = (f32[192,768]{1,0:T(8,128)S(1)}, f32[192,768]{1,0:T(8,128)S(1)}, u32[]{:S(2)}, u32[]{:S(2)}) collective-permute-start(f32[192,768]{1,0:T(8,128)S(1)} %get-tuple-element.156.refs_2_), channel_id=1, source_target_pairs={{0,1},{1,0},{2,3},{3,2},{4,5},{5,4},{6,7},{7,6},{8,9},{9,8},{10,11... | collective-permute-start | bytes 1769480 | tf_op jit(solution)/shard_map/ppermute | solution.py:453
  52.0 7.7 %collective-permute-done.7.refs_2_ = f32[192,768]{1,0:T(8,128)S(1)} collective-permute-done((f32[192,768]{1,0:T(8,128)S(1)}, f32[192,768]{1,0:T(8,128)S(1)}, u32[]{:S(2)}, u32[]{:S(2)}) %collective-permute-start.7) | collective-permute-done | bytes 589856 | tf_op jit(solution)/shard_map/ppermute | solution.py:453
  59.7 3.3 %feed_back.3 = (bf16[192,768]{1,0:T(8,128)(2,1)S(1)}, f32[192,768]{1,0:T(8,128)S(1)}, bf16[192,768]{1,0:T(8,128)(2,1)S(1)}, bf16[192,1536]{1,0:T(8,128)(2,1)S(1)...) custom-call(f32[8,128]{1,0:T(8,128)S(1)} %get-tuple-element.144.refs_0_, ...), custom_call_target="tpu_custom_call" | custom-call | flops 10000000000 | bytes 1000000 | tf_op jit(solution)/shard_map/feed_back/pallas_call | solution.py:435
  63.1 2.9 %outer.3 = (f32[384,1536]{1,0:T(8,128)S(1)}, f32[384,1536]{1,0:T(8,128)S(1)}, f32[8,128]{1,0:T(8,128)S(1)}) custom-call(f32[8,128]{1,0:T(8,128)S(1)} %get-tuple-element.149.refs_0_, s32[3]{0:T(128)S(1)} %pad_add_fusion.refs_1_, bf16[192,768]{1,0:T(8,128)(2,1)S(1)} %get-tuple-element.150.refs_2_, bf16[192,768]{1,0:T(8,128)(2,1)S(1)} %get-tuple-element.151.refs_3_, ...), custom_call_target="tpu_custom_call" | custom-call | flops 10000000000 | bytes 1000000 | tf_op jit(solution)/shard_map/outer/pallas_call | solution.py:435
  66.1 1.8 %collective-permute-start.13 = (f32[192,768]{1,0:T(8,128)S(1)}, f32[192,768]{1,0:T(8,128)S(1)}, u32[]{:S(2)}, u32[]{:S(2)}) collective-permute-start(f32[192,768]{1,0:T(8,128)S(1)} %get-tuple-element.179.refs_2_), channel_id=1, source_target_pairs={{0,1},{1,0},{2,3},{3,2},{4,5},{5,4},{6,7},{7,6},{8,9},{9,8},{10,11... | collective-permute-start | bytes 1769480 | tf_op jit(solution)/shard_map/ppermute | solution.py:453
  67.9 4.0 %collective-permute-done.8.refs_3_ = f32[192,768]{1,0:T(8,128)S(1)} collective-permute-done((f32[192,768]{1,0:T(8,128)S(1)}, f32[192,768]{1,0:T(8,128)S(1)}, u32[]{:S(2)}, u32[]{:S(2)}) %collective-permute-start.8) | collective-permute-done | bytes 589856 | tf_op jit(solution)/shard_map/ppermute | solution.py:453
  73.8 1.5 collective-permute-start.11
  75.3 2.9 %outer.4 = (f32[384,1536]{1,0:T(8,128)S(1)}, f32[384,1536]{1,0:T(8,128)S(1)}, f32[8,128]{1,0:T(8,128)S(1)}) custom-call(f32[8,128]{1,0:T(8,128)S(1)} %get-tuple-element.164.refs_0_, s32[3]{0:T(128)S(1)} %pad_add_fusion.refs_1_, bf16[192,768]{1,0:T(8,128)(2,1)S(1)} %get-tuple-element.165.refs_2_, bf16[192,768]{1,0:T(8,128)(2,1)S(1)} %get-tuple-element.166.refs_3_, ...), custom_call_target="tpu_custom_call" | custom-call | flops 10000000000 | bytes 1000000 | tf_op jit(solution)/shard_map/outer/pallas_call | solution.py:435
  78.8 3.2 %collective-permute-done.10.refs_3_.refs_6_ = f32[192,512]{1,0:T(8,128)S(1)} collective-permute-done((f32[192,512]{1,0:T(8,128)S(1)}, f32[192,512]{1,0:T(8,128)S(1)}, u32[]{:S(2)}, u32[]{:S(2)}) %collective-permute-start.10) | collective-permute-done | bytes 393248 | tf_op jit(solution)/shard_map/ppermute | solution.py:456
  82.0 2.8 %collective-permute-start.14 = (f32[96,512]{1,0:T(8,128)S(1)}, f32[96,512]{1,0:T(8,128)S(1)}, u32[]{:S(2)}, u32[]{:S(2)}) collective-permute-start(f32[96,512]{1,0:T(8,128)S(1)} %get-tuple-element.195), channel_id=1, source_target_pairs={{0,16},{2,18},{4,20},{6,22},{8,24},{10,26},{12,28},{14,30},{16,0},... | collective-permute-start | bytes 589832 | tf_op jit(solution)/shard_map/ppermute | solution.py:456
  88.9 5.7 %attend_back.1 = (bf16[384,1536]{1,0:T(8,128)(2,1)S(1)}, f32[8,1536]{1,0:T(8,128)S(1)}, f32[8,128]{1,0:T(8,128)S(1)}) custom-call(f32[8,128]{1,0:T(8,128)S(1)} %get-tuple-element.184.refs_0_, bf16[192,768]{1,0:T(8,128)(2,1)S(1)} %get-tuple-element.185.refs_1_.refs_3_, bf16[192,768]{1,0:T(8,128)(2,1)S(1)} %get-tuple-element.186.refs_2_.refs_4_, ...), custom_call_target="tpu_custom_call" | custom-call | flops 100000000 | bytes 1000000 | tf_op jit(solution)/shard_map/attend_back/pallas_call | solution.py:435
  95.7 3.5 %outer.5 = (f32[392,1536]{1,0:T(8,128)S(1)}, f32[392,1536]{1,0:T(8,128)S(1)}, f32[8,128]{1,0:T(8,128)S(1)}) custom-call(f32[8,128]{1,0:T(8,128)S(1)} %get-tuple-element.191.refs_0_, s32[3]{0:T(128)S(1)} %pad_add_fusion.refs_1_, bf16[384,768]{1,0:T(8,128)(2,1)S(1)} %copy-done.1, bf16[192,768]{1,0:T(8,128)(2,1)S(1)} %get-tuple-element.185.refs_1_.refs_3_, ...), custom_call_target="tpu_custom_call" | custom-call | flops 100000000 | bytes 1000000 | tf_op jit(solution)/shard_map/outer/pallas_call | solution.py:435
  99.3 2.5 %collective-permute-start.19 = (f32[48,1024]{1,0:T(8,128)S(1)}, f32[48,1024]{1,0:T(8,128)S(1)}, u32[]{:S(2)}, u32[]{:S(2)}) collective-permute-start(f32[48,1024]{1,0:T(8,128)S(1)} %get-tuple-element.207), channel_id=1, source_target_pairs={{0,16},{2,18},{4,20},{6,22},{8,24},{10,26},{12,28},{14,30},{16,0},... | collective-permute-start | bytes 589832 | tf_op jit(solution)/shard_map/ppermute | solution.py:456
  101.8 5.1 %collective-permute-done.17.refs_3_.refs_6_ = f32[96,1536]{1,0:T(8,128)S(1)} collective-permute-done((f32[96,1536]{1,0:T(8,128)S(1)}, f32[96,1536]{1,0:T(8,128)S(1)}, u32[]{:S(2)}, u32[]{:S(2)}) %collective-permute-start.17) | collective-permute-done | bytes 589856 | tf_op jit(solution)/shard_map/ppermute | solution.py:456
  110.2 2.7 %back_tokens.1 = (f32[384,768]{1,0:T(8,128)S(1)}, f32[8,128]{1,0:T(8,128)S(1)}) custom-call(f32[8,128]{1,0:T(8,128)S(1)} %get-tuple-element.205.refs_0_, bf16[384,1536]{1,0:T(8,128)(2,1)S(1)} %get-tuple-element.192.refs_5_.refs_1_, bf16[3,768,384]{2,1,0:T(8,128)(2,1)} %refs_2_.11), custom_call_target="tpu_custom_call" | custom-call | flops 100000000 | bytes 1000000 | tf_op jit(solution)/shard_map/back_tokens/pallas_call | solution.py:435
  114.1 5.4 %collective-permute-done.20.refs_3_ = f32[96,1536]{1,0:T(8,128)S(1)} collective-permute-done((f32[96,1536]{1,0:T(8,128)S(1)}, f32[96,1536]{1,0:T(8,128)S(1)}, u32[]{:S(2)}, u32[]{:S(2)}) %collective-permute-start.20) | collective-permute-done | bytes 589856 | tf_op jit(solution)/shard_map/ppermute | solution.py:456
  120.3 2.0 %collective-permute-start.23 = (f32[48,1536]{1,0:T(8,128)S(1)}, f32[48,1536]{1,0:T(8,128)S(1)}, u32[]{:S(2)}, u32[]{:S(2)}) collective-permute-start(f32[48,1536]{1,0:T(8,128)S(1)} %get-tuple-element.215), channel_id=1, source_target_pairs={{0,16},{2,18},{4,20},{6,22},{8,24},{10,26},{12,28},{14,30},{16,0},... | collective-permute-start | bytes 884744 | tf_op jit(solution)/shard_map/ppermute | solution.py:456
  122.3 10.9 %collective-permute-done.22.refs_3_.refs_6_ = f32[104,1536]{1,0:T(8,128)S(1)} collective-permute-done((f32[104,1536]{1,0:T(8,128)S(1)}, f32[104,1536]{1,0:T(8,128)S(1)}, u32[]{:S(2)}, u32[]{:S(2)}) %collective-permute-start.22) | collective-permute-done | bytes 639008 | tf_op jit(solution)/shard_map/ppermute | solution.py:456
  136.3 1.5 collective-permute-start.27
  138.7 5.9 %collective-permute-done.24.refs_3_ = f32[96,1536]{1,0:T(8,128)S(1)} collective-permute-done((f32[96,1536]{1,0:T(8,128)S(1)}, f32[96,1536]{1,0:T(8,128)S(1)}, u32[]{:S(2)}, u32[]{:S(2)}) %collective-permute-start.24) | collective-permute-done | bytes 589856 | tf_op jit(solution)/shard_map/ppermute | solution.py:456
  144.7 2.6 %collective-permute-start.29 = (f32[8,1536]{1,0:T(8,128)S(1)}, f32[8,1536]{1,0:T(8,128)S(1)}, u32[]{:S(2)}, u32[]{:S(2)}) collective-permute-start(f32[8,1536]{1,0:T(8,128)S(1)} %get-tuple-element.230.refs_1_), channel_id=1, source_target_pairs={{0,16},{2,18},{4,20},{6,22},{8,24},{10,26},{12,28},{14,30},{16,0},... | collective-permute-start | bytes 147464 | tf_op jit(solution)/shard_map/ppermute | solution.py:456
  149.9 5.8 %collective-permute-done.29.refs_2_ = f32[8,1536]{1,0:T(8,128)S(1)} collective-permute-done((f32[8,1536]{1,0:T(8,128)S(1)}, f32[8,1536]{1,0:T(8,128)S(1)}, u32[]{:S(2)}, u32[]{:S(2)}) %collective-permute-start.29) | collective-permute-done | bytes 49184 | tf_op jit(solution)/shard_map/ppermute | solution.py:456
  157.5 3.4 %collective-permute-done.30.refs_2_ = f32[48,1536]{1,0:T(8,128)S(1)} collective-permute-done((f32[48,1536]{1,0:T(8,128)S(1)}, f32[48,1536]{1,0:T(8,128)S(1)}, u32[]{:S(2)}, u32[]{:S(2)}) %collective-permute-start.30) | collective-permute-done | bytes 294944 | tf_op jit(solution)/shard_map/ppermute | solution.py:456
  (123 shorter events, 29.5 us)
Async XLA Ops:
  1.7 17.3 %copy-start.8 = (bf16[768]{0:T(1024)(128)(2,1)S(1)}, bf16[768]{0:T(1024)(128)(2,1)}, u32[]{:S(2)}) copy-start(bf16[768]{0:T(1024)(128)(2,1)} %refs_2_.7) | copy-start | bytes 4612
  1.7 17.2 %collective-permute-start = (f32[192,768]{1,0:T(8,128)S(1)}, f32[192,768]{1,0:T(8,128)S(1)}, u32[]{:S(2)}, u32[]{:S(2)}) collective-permute-start(f32[192,768]{1,0:T(8,128)S(1)} %dynamic-slice_convert_fusion), channel_id=1, source_target_pairs={{0,1},{1,0},{2,3},{3,2},{4,5},{5,4},{6,7},{7,6},{8,9},{9,8},{10,11... | collective-permute-start | bytes 1769480 | tf_op jit(solution)/shard_map/ppermute | solution.py:453
  12.5 11.9 %collective-permute-start.1 = (f32[192,384]{1,0:T(8,128)}, f32[192,384]{1,0:T(8,128)S(1)}, u32[]{:S(2)}, u32[]{:S(2)}) collective-permute-start(f32[192,384]{1,0:T(8,128)} %get-tuple-element.130), channel_id=1, source_target_pairs={{0,1},{1,0},{2,3},{3,2},{4,5},{5,4},{6,7},{7,6},{8,9},{9,8},{10,11... | collective-permute-start | bytes 884744 | tf_op jit(solution)/shard_map/ppermute | solution.py:453
  20.4 4.0 %collective-permute-start.4 = (f32[64,768]{1,0:T(8,128)S(1)}, f32[64,768]{1,0:T(8,128)S(1)}, u32[]{:S(2)}, u32[]{:S(2)}) collective-permute-start(f32[64,768]{1,0:T(8,128)S(1)} %get-tuple-element.247), channel_id=1, source_target_pairs={{0,2},{2,0},{4,6},{6,4},{8,10},{10,8},{12,14},{14,12},{16,18},{18,... | collective-permute-start | bytes 589832 | tf_op jit(solution)/shard_map/ppermute | solution.py:456
  20.5 4.0 %collective-permute-start.3 = (f32[64,768]{1,0:T(8,128)S(1)}, f32[64,768]{1,0:T(8,128)S(1)}, u32[]{:S(2)}, u32[]{:S(2)}) collective-permute-start(f32[64,768]{1,0:T(8,128)S(1)} %get-tuple-element.248), channel_id=1, source_target_pairs={{0,2},{2,0},{4,6},{6,4},{8,10},{10,8},{12,14},{14,12},{16,18},{18,... | collective-permute-start | bytes 589832 | tf_op jit(solution)/shard_map/ppermute | solution.py:456
  21.0 3.5 %collective-permute-start.2 = (f32[64,768]{1,0:T(8,128)S(1)}, f32[64,768]{1,0:T(8,128)S(1)}, u32[]{:S(2)}, u32[]{:S(2)}) collective-permute-start(f32[64,768]{1,0:T(8,128)S(1)} %get-tuple-element.249), channel_id=1, source_target_pairs={{0,2},{2,0},{4,6},{6,4},{8,10},{10,8},{12,14},{14,12},{16,18},{18,... | collective-permute-start | bytes 589832 | tf_op jit(solution)/shard_map/ppermute | solution.py:456
  21.0 11.5 %collective-permute-start.5 = (f32[192,384]{1,0:T(8,128)S(1)}, f32[192,384]{1,0:T(8,128)S(1)}, u32[]{:S(2)}, u32[]{:S(2)}) collective-permute-start(f32[192,384]{1,0:T(8,128)S(1)} %copy-done.17), channel_id=1, source_target_pairs={{0,1},{1,0},{2,3},{3,2},{4,5},{5,4},{6,7},{7,6},{8,9},{9,8},{10,11... | collective-permute-start | bytes 884744 | tf_op jit(solution)/shard_map/ppermute | solution.py:453
  30.8 16.3 %collective-permute-start.6 = (f32[192,768]{1,0:T(8,128)S(1)}, f32[192,768]{1,0:T(8,128)S(1)}, u32[]{:S(2)}, u32[]{:S(2)}) collective-permute-start(f32[192,768]{1,0:T(8,128)S(1)} %get-tuple-element.140.refs_1_), channel_id=1, source_target_pairs={{0,1},{1,0},{2,3},{3,2},{4,5},{5,4},{6,7},{7,6},{8,9},{9,8},{10,11... | collective-permute-start | bytes 1769480 | tf_op jit(solution)/shard_map/ppermute | solution.py:453
  37.9 21.8 %collective-permute-start.7 = (f32[192,768]{1,0:T(8,128)S(1)}, f32[192,768]{1,0:T(8,128)S(1)}, u32[]{:S(2)}, u32[]{:S(2)}) collective-permute-start(f32[192,768]{1,0:T(8,128)S(1)} %get-tuple-element.145.refs_1_), channel_id=1, source_target_pairs={{0,1},{1,0},{2,3},{3,2},{4,5},{5,4},{6,7},{7,6},{8,9},{9,8},{10,11... | collective-permute-start | bytes 1769480 | tf_op jit(solution)/shard_map/ppermute | solution.py:453
  50.2 21.7 %collective-permute-start.8 = (f32[192,768]{1,0:T(8,128)S(1)}, f32[192,768]{1,0:T(8,128)S(1)}, u32[]{:S(2)}, u32[]{:S(2)}) collective-permute-start(f32[192,768]{1,0:T(8,128)S(1)} %get-tuple-element.156.refs_2_), channel_id=1, source_target_pairs={{0,1},{1,0},{2,3},{3,2},{4,5},{5,4},{6,7},{7,6},{8,9},{9,8},{10,11... | collective-permute-start | bytes 1769480 | tf_op jit(solution)/shard_map/ppermute | solution.py:453
  66.0 6.4 %collective-permute-start.9 = (f32[384,1536]{1,0:T(8,128)S(1)}, f32[384,1536]{1,0:T(8,128)S(1)}, u32[]{:S(2)}, u32[]{:S(2)}) collective-permute-start(f32[384,1536]{1,0:T(8,128)S(1)} %get-tuple-element.162), channel_id=1, source_target_pairs={{0,2},{2,0},{4,6},{6,4},{8,10},{10,8},{12,14},{14,12},{16,18},{18,... | collective-permute-start | bytes 7077896 | tf_op jit(solution)/shard_map/ppermute | solution.py:456
  66.1 22.1 %collective-permute-start.13 = (f32[192,768]{1,0:T(8,128)S(1)}, f32[192,768]{1,0:T(8,128)S(1)}, u32[]{:S(2)}, u32[]{:S(2)}) collective-permute-start(f32[192,768]{1,0:T(8,128)S(1)} %get-tuple-element.179.refs_2_), channel_id=1, source_target_pairs={{0,1},{1,0},{2,3},{3,2},{4,5},{5,4},{6,7},{7,6},{8,9},{9,8},{10,11... | collective-permute-start | bytes 1769480 | tf_op jit(solution)/shard_map/ppermute | solution.py:453
  72.5 9.5 %collective-permute-start.10 = (f32[192,512]{1,0:T(8,128)S(1)}, f32[192,512]{1,0:T(8,128)S(1)}, u32[]{:S(2)}, u32[]{:S(2)}) collective-permute-start(f32[192,512]{1,0:T(8,128)S(1)} %get-tuple-element.171), channel_id=1, source_target_pairs={{0,8},{2,10},{4,12},{6,14},{8,0},{10,2},{12,4},{14,6},{16,24},{18,... | collective-permute-start | bytes 1179656 | tf_op jit(solution)/shard_map/ppermute | solution.py:456
  73.8 12.1 %collective-permute-start.11 = (f32[96,1024]{1,0:T(8,128)S(1)}, f32[96,1024]{1,0:T(8,128)S(1)}, u32[]{:S(2)}, u32[]{:S(2)}) collective-permute-start(f32[96,1024]{1,0:T(8,128)S(1)} %get-tuple-element.173), channel_id=1, source_target_pairs={{0,4},{2,6},{4,0},{6,2},{8,12},{10,14},{12,8},{14,10},{16,20},{18,... | collective-permute-start | bytes 1179656 | tf_op jit(solution)/shard_map/ppermute | solution.py:456
  78.2 21.0 %collective-permute-start.15 = (f32[96,1024]{1,0:T(8,128)S(1)}, f32[96,1024]{1,0:T(8,128)S(1)}, u32[]{:S(2)}, u32[]{:S(2)}) collective-permute-start(f32[96,1024]{1,0:T(8,128)S(1)} %get-tuple-element.197), channel_id=1, source_target_pairs={{0,4},{2,6},{4,0},{6,2},{8,12},{10,14},{12,8},{14,10},{16,20},{18,... | collective-permute-start | bytes 1179656 | tf_op jit(solution)/shard_map/ppermute | solution.py:456
  78.8 8.0 %collective-permute-start.12 = (f32[384,1536]{1,0:T(8,128)S(1)}, f32[384,1536]{1,0:T(8,128)S(1)}, u32[]{:S(2)}, u32[]{:S(2)}) collective-permute-start(f32[384,1536]{1,0:T(8,128)S(1)} %get-tuple-element.176), channel_id=1, source_target_pairs={{0,2},{2,0},{4,6},{6,4},{8,10},{10,8},{12,14},{14,12},{16,18},{18,... | collective-permute-start | bytes 7077896 | tf_op jit(solution)/shard_map/ppermute | solution.py:456
  82.0 17.2 %collective-permute-start.14 = (f32[96,512]{1,0:T(8,128)S(1)}, f32[96,512]{1,0:T(8,128)S(1)}, u32[]{:S(2)}, u32[]{:S(2)}) collective-permute-start(f32[96,512]{1,0:T(8,128)S(1)} %get-tuple-element.195), channel_id=1, source_target_pairs={{0,16},{2,18},{4,20},{6,22},{8,24},{10,26},{12,28},{14,30},{16,0},... | collective-permute-start | bytes 589832 | tf_op jit(solution)/shard_map/ppermute | solution.py:456
  85.9 13.4 %collective-permute-start.16 = (f32[96,1024]{1,0:T(8,128)S(1)}, f32[96,1024]{1,0:T(8,128)S(1)}, u32[]{:S(2)}, u32[]{:S(2)}) collective-permute-start(f32[96,1024]{1,0:T(8,128)S(1)} %get-tuple-element.198), channel_id=1, source_target_pairs={{0,8},{2,10},{4,12},{6,14},{8,0},{10,2},{12,4},{14,6},{16,24},{18,... | collective-permute-start | bytes 1179656 | tf_op jit(solution)/shard_map/ppermute | solution.py:456
  86.9 20.0 %collective-permute-start.17 = (f32[96,1536]{1,0:T(8,128)S(1)}, f32[96,1536]{1,0:T(8,128)S(1)}, u32[]{:S(2)}, u32[]{:S(2)}) collective-permute-start(f32[96,1536]{1,0:T(8,128)S(1)} %get-tuple-element.200), channel_id=1, source_target_pairs={{0,4},{2,6},{4,0},{6,2},{8,12},{10,14},{12,8},{14,10},{16,20},{18,... | collective-permute-start | bytes 1769480 | tf_op jit(solution)/shard_map/ppermute | solution.py:456
  94.7 24.8 %collective-permute-start.20 = (f32[96,1536]{1,0:T(8,128)S(1)}, f32[96,1536]{1,0:T(8,128)S(1)}, u32[]{:S(2)}, u32[]{:S(2)}) collective-permute-start(f32[96,1536]{1,0:T(8,128)S(1)} %get-tuple-element.209), channel_id=1, source_target_pairs={{0,4},{2,6},{4,0},{6,2},{8,12},{10,14},{12,8},{14,10},{16,20},{18,... | collective-permute-start | bytes 1769480 | tf_op jit(solution)/shard_map/ppermute | solution.py:456
  99.3 13.6 %collective-permute-start.19 = (f32[48,1024]{1,0:T(8,128)S(1)}, f32[48,1024]{1,0:T(8,128)S(1)}, u32[]{:S(2)}, u32[]{:S(2)}) collective-permute-start(f32[48,1024]{1,0:T(8,128)S(1)} %get-tuple-element.207), channel_id=1, source_target_pairs={{0,16},{2,18},{4,20},{6,22},{8,24},{10,26},{12,28},{14,30},{16,0},... | collective-permute-start | bytes 589832 | tf_op jit(solution)/shard_map/ppermute | solution.py:456
  101.8 6.1 %collective-permute-start.18 = (f32[392,1536]{1,0:T(8,128)S(1)}, f32[392,1536]{1,0:T(8,128)S(1)}, u32[]{:S(2)}, u32[]{:S(2)}) collective-permute-start(f32[392,1536]{1,0:T(8,128)S(1)} %get-tuple-element.203), channel_id=1, source_target_pairs={{0,2},{2,0},{4,6},{6,4},{8,10},{10,8},{12,14},{14,12},{16,18},{18,... | collective-permute-start | bytes 7225352 | tf_op jit(solution)/shard_map/ppermute | solution.py:456
  107.0 13.2 %collective-permute-start.21 = (f32[96,1536]{1,0:T(8,128)S(1)}, f32[96,1536]{1,0:T(8,128)S(1)}, u32[]{:S(2)}, u32[]{:S(2)}) collective-permute-start(f32[96,1536]{1,0:T(8,128)S(1)} %get-tuple-element.210), channel_id=1, source_target_pairs={{0,8},{2,10},{4,12},{6,14},{8,0},{10,2},{12,4},{14,6},{16,24},{18,... | collective-permute-start | bytes 1769480 | tf_op jit(solution)/shard_map/ppermute | solution.py:456
  108.0 25.2 %collective-permute-start.22 = (f32[104,1536]{1,0:T(8,128)S(1)}, f32[104,1536]{1,0:T(8,128)S(1)}, u32[]{:S(2)}, u32[]{:S(2)}) collective-permute-start(f32[104,1536]{1,0:T(8,128)S(1)} %get-tuple-element.212), channel_id=1, source_target_pairs={{0,4},{2,6},{4,0},{6,2},{8,12},{10,14},{12,8},{14,10},{16,20},{18,... | collective-permute-start | bytes 1916936 | tf_op jit(solution)/shard_map/ppermute | solution.py:456
  109.2 35.4 %collective-permute-start.24 = (f32[96,1536]{1,0:T(8,128)S(1)}, f32[96,1536]{1,0:T(8,128)S(1)}, u32[]{:S(2)}, u32[]{:S(2)}) collective-permute-start(f32[96,1536]{1,0:T(8,128)S(1)} %get-tuple-element.217), channel_id=1, source_target_pairs={{0,4},{2,6},{4,0},{6,2},{8,12},{10,14},{12,8},{14,10},{16,20},{18,... | collective-permute-start | bytes 1769480 | tf_op jit(solution)/shard_map/ppermute | solution.py:456
  112.9 35.7 %collective-permute-start.28 = (f32[384,768]{1,0:T(8,128)S(1)}, f32[384,768]{1,0:T(8,128)S(1)}, u32[]{:S(2)}, u32[]{:S(2)}) collective-permute-start(f32[384,768]{1,0:T(8,128)S(1)} %get-tuple-element.225.refs_1_), channel_id=1, source_target_pairs={{0,1},{1,0},{2,3},{3,2},{4,5},{5,4},{6,7},{7,6},{8,9},{9,8},{10,11... | collective-permute-start | bytes 3538952 | tf_op jit(solution)/shard_map/ppermute | solution.py:453
  120.3 16.0 %collective-permute-start.23 = (f32[48,1536]{1,0:T(8,128)S(1)}, f32[48,1536]{1,0:T(8,128)S(1)}, u32[]{:S(2)}, u32[]{:S(2)}) collective-permute-start(f32[48,1536]{1,0:T(8,128)S(1)} %get-tuple-element.215), channel_id=1, source_target_pairs={{0,16},{2,18},{4,20},{6,22},{8,24},{10,26},{12,28},{14,30},{16,0},... | collective-permute-start | bytes 884744 | tf_op jit(solution)/shard_map/ppermute | solution.py:456
  133.3 11.3 %collective-permute-start.25 = (f32[56,1536]{1,0:T(8,128)S(1)}, f32[56,1536]{1,0:T(8,128)S(1)}, u32[]{:S(2)}, u32[]{:S(2)}) collective-permute-start(f32[56,1536]{1,0:T(8,128)S(1)} %get-tuple-element.218), channel_id=1, source_target_pairs={{0,8},{2,10},{4,12},{6,14},{8,0},{10,2},{12,4},{14,6},{16,24},{18,... | collective-permute-start | bytes 1032200 | tf_op jit(solution)/shard_map/ppermute | solution.py:456
  134.3 13.4 %collective-permute-start.26 = (f32[48,1536]{1,0:T(8,128)S(1)}, f32[48,1536]{1,0:T(8,128)S(1)}, u32[]{:S(2)}, u32[]{:S(2)}) collective-permute-start(f32[48,1536]{1,0:T(8,128)S(1)} %get-tuple-element.221), channel_id=1, source_target_pairs={{0,8},{2,10},{4,12},{6,14},{8,0},{10,2},{12,4},{14,6},{16,24},{18,... | collective-permute-start | bytes 884744 | tf_op jit(solution)/shard_map/ppermute | solution.py:456
  136.3 11.5 %collective-permute-start.27 = (f32[48,512]{1,0:T(8,128)S(1)}, f32[48,512]{1,0:T(8,128)S(1)}, u32[]{:S(2)}, u32[]{:S(2)}) collective-permute-start(f32[48,512]{1,0:T(8,128)S(1)} %get-tuple-element.223), channel_id=1, source_target_pairs={{0,4},{2,6},{4,0},{6,2},{8,12},{10,14},{12,8},{14,10},{16,20},{18,... | collective-permute-start | bytes 294920 | tf_op jit(solution)/shard_map/ppermute | solution.py:456
  144.7 10.9 %collective-permute-start.29 = (f32[8,1536]{1,0:T(8,128)S(1)}, f32[8,1536]{1,0:T(8,128)S(1)}, u32[]{:S(2)}, u32[]{:S(2)}) collective-permute-start(f32[8,1536]{1,0:T(8,128)S(1)} %get-tuple-element.230.refs_1_), channel_id=1, source_target_pairs={{0,16},{2,18},{4,20},{6,22},{8,24},{10,26},{12,28},{14,30},{16,0},... | collective-permute-start | bytes 147464 | tf_op jit(solution)/shard_map/ppermute | solution.py:456
  147.4 13.6 %collective-permute-start.30 = (f32[48,1536]{1,0:T(8,128)S(1)}, f32[48,1536]{1,0:T(8,128)S(1)}, u32[]{:S(2)}, u32[]{:S(2)}) collective-permute-start(f32[48,1536]{1,0:T(8,128)S(1)} %get-tuple-element.233), channel_id=1, source_target_pairs={{0,16},{2,18},{4,20},{6,22},{8,24},{10,26},{12,28},{14,30},{16,0},... | collective-permute-start | bytes 884744 | tf_op jit(solution)/shard_map/ppermute | solution.py:456
  (22 other events, 130.5 us)

commit v7 on v6

--- a/solution.py
+++ b/solution.py
@@ -146,40 +146,53 @@
     return ref[...].astype(F32)
 
 
-def feed(taken, tile, far_parts, streamed, place_ref, x_hbm, own_hbm, far_hbm, w_own_hbm, w_near_hbm, *refs):
-    w_fars, refs = refs[:far_parts], refs[far_parts:]
-    vec_hbm, b_up_ref, w_up, w_down, normed_ref, inverse_ref, low_ref, act_ref, pre_ref, part_ref = refs[:10]
-    x_ref, far_ref, vec_ref, w_far, w_full, ctx_full, sems = refs[10:17]
-    local = own_hbm.shape[1]
-    half = w_near_hbm.shape[0]
-    piece = half // far_parts
-    hidden = w_up.shape[1]
+def gather(far_parts, place_ref, w_own_hbm, w_near_ref, *refs):
+    w_fars, (out_ref, sems) = refs[:far_parts], refs[far_parts:]
+    local = w_own_hbm.shape[0]
+    half = w_near_ref.shape[0]
     core, side = place_ref[0], place_ref[1]
     here = pl.multiple_of(side * local, LANES)
     there = pl.multiple_of((1 - side) * local, LANES)
+    (came,) = fetch([w_own_hbm], [out_ref.at[pl.ds(here, local)]], sems)
+    out_ref[pl.ds(pl.multiple_of(there + core * half, 16), half), :] = w_near_ref[...].astype(LOW)
+    at = there + (1 - core) * half
+    for ref in w_fars:
+        size = ref.shape[0]
+        out_ref[pl.ds(pl.multiple_of(at, 16), size), :] = ref[...].astype(LOW)
+        at = at + size
+    came.wait()
+
+
+def feed(taken, tile, streamed, place_ref, far_ref, w_full, x_hbm, own_hbm, *refs):
+    vec_hbm, b_up_ref, w_up, w_down = refs[:4]
+    normed_ref, inverse_ref, low_ref, act_ref, pre_ref, part_ref, base_ref = refs[4:11]
+    x_ref, vec_ref, ctx_full, sems = refs[11:15]
+    local = own_hbm.shape[1]
+    hidden = w_up.shape[1]
+    side = place_ref[1]
+    here = pl.multiple_of(side * local, LANES)
+    there = pl.multiple_of((1 - side) * local, LANES)
     spans = [slice(at, at + tile) for at in range(0, hidden, tile)]
-    sources = [w_near_hbm] + list(w_fars) + [w_own_hbm, own_hbm.at[taken], far_hbm, x_hbm.at[taken], vec_hbm]
-    targets = [w_far.at[0]] + [w_far.at[1, i * piece : (i + 1) * piece] for i in range(far_parts)]
-    targets += [w_full.at[pl.ds(here, local)], ctx_full.at[:, pl.ds(here, local)], far_ref, x_ref, vec_ref]
+    sources = [own_hbm.at[taken], x_hbm.at[taken], vec_hbm]
+    targets = [ctx_full.at[:, pl.ds(here, local)], x_ref, vec_ref]
     needed = len(sources)
     if streamed:
-        w_up_vmem, w_down_vmem = refs[17:]
+        w_up_vmem, w_down_vmem = refs[15:]
         for span in spans:
             sources += [w_up.at[:, span], w_down.at[span]]
             targets += [w_up_vmem.at[:, span], w_down_vmem.at[span]]
         w_up, w_down = w_up_vmem, w_down_vmem
     came = fetch(sources, targets, sems)
+    ctx_full[:, pl.ds(there, local)] = far_ref[...].astype(LOW)
     for copy in came[:needed]:
         copy.wait()
-    for i in range(2):
-        at = pl.multiple_of(there + (core ^ i) * half, 16)
-        w_full[pl.ds(at, half), :] = w_far[i].astype(LOW)
-    ctx_full[:, pl.ds(there, local)] = far_ref[...].astype(LOW)
     attn = dot(ctx_full[...], w_full[...])
     normed, inverse = norm_rows(x_ref[...].astype(F32) + attn + vec_ref[0:1, :])
     normed_ref[...] = normed
     inverse_ref[...] = jnp.broadcast_to(inverse, inverse_ref.shape)
-    low = (normed * vec_ref[1:2, :] + vec_ref[2:3, :]).astype(LOW)
+    hidden_rows = normed * vec_ref[1:2, :] + vec_ref[2:3, :]
+    base_ref[...] = hidden_rows + vec_ref[3:4, :]
+    low = hidden_rows.astype(LOW)
     low_ref[...] = low
     b_up = b_up_ref[...].astype(F32).reshape(1, -1)
     for i, span in enumerate(spans):
@@ -206,16 +219,15 @@
 
 
 def feed_back(
-    taken, tile, own_ref, far_ref, normed_ref, slope_ref, vec_hbm, up_hbm, w_up, w_down,
+    taken, tile, own_ref, far_ref, base_ref, slope_ref, vec_hbm, up_hbm, w_up, w_down,
     out_ref, grad_ref, low_ref, pre_ref, part_ref, sums_ref, b_up_ref,
     vec_ref, up_ref, sems,
 ):
     hidden = w_up.shape[1]
     spans = [slice(at, at + tile) for at in range(0, hidden, tile)]
     came = fetch([up_hbm.at[taken], vec_hbm], [up_ref, vec_ref], sems)
+    normed, inverse = norm_rows(base_ref[...] + (own_ref[...] + far_ref[...]))
     came[1].wait()
-    hidden_rows = normed_ref[...] * vec_ref[1:2, :] + vec_ref[2:3, :]
-    normed, inverse = norm_rows(hidden_rows + (own_ref[...] + far_ref[...]) + vec_ref[3:4, :])
     gain = vec_ref[4:5, :]
     out_ref[...] = (normed * gain + vec_ref[5:6, :]).astype(LOW)
     came[0].wait()
@@ -490,6 +502,11 @@
     far_parts = 3 if half % 48 == 0 else 1
     piece = half // far_parts
     w_fars = [swap_dp(w_near[i * piece : (i + 1) * piece], 1) for i in range(far_parts)]
+    outs = [shape((2 * local, width), LOW)]
+    (w_whole,) = call(
+        functools.partial(gather, far_parts), "gather", [place_arr, w_out, w_near, *w_fars],
+        [smem, far_off] + full(w_near, *w_fars), outs, full(*outs), scratch=[dma((1,))], flops=10**8,
+    )
 
     tile = min(hidden, 512)
     tiles = hidden // tile
@@ -502,20 +519,18 @@
         outs = [
             shape((block, width), F32), shape((block, LANES), F32), shape((block, width), LOW),
             shape((block, hidden), LOW), shape((block, hidden), F32), shape((block, width), F32),
+            shape((block, width), F32),
         ]
         outs = call(
-            functools.partial(feed, slice(begin, begin + block), tile, far_parts, begin == 0), "feed",
-            [place_arr, tokens, context, far, w_out, w_near, *w_fars, vectors, b_up, w_up, w_down],
-            [smem] + [far_off] * (6 + far_parts) + full(b_up) + [far_off if begin == 0 else near] * 2,
+            functools.partial(feed, slice(begin, begin + block), tile, begin == 0), "feed",
+            [place_arr, far, w_whole, tokens, context, vectors, b_up, w_up, w_down],
+            [smem] + full(far, w_whole) + [far_off] * 3 + full(b_up) + [far_off if begin == 0 else near] * 2,
             outs, full(*outs),
             scratch=[
                 pltpu.VMEM((block, width), LOW),
-                pltpu.VMEM((block, local), F32),
                 pltpu.VMEM((8, width), F32),
-                pltpu.VMEM((2, half, width), F32),
-                pltpu.VMEM((2 * local, width), LOW),
                 pltpu.VMEM((block, 2 * local), LOW),
-                dma((6 + far_parts + 2 * tiles,)),
+                dma((3 + 2 * tiles,)),
             ]
             + ([pltpu.VMEM((width, hidden), LOW), pltpu.VMEM((hidden, width), LOW)] if begin == 0 else []),
         )
@@ -525,15 +540,15 @@
         call(slopes, "slopes", [s[4]], full(s[4]), [shape(s[4].shape, F32)], full(s[4]))[0] for s in saved
     ]
     back = []
-    for begin, block, slope, (normed, inverse, low, act, _, own, far) in zip(starts, blocks, slope_of, saved):
+    for begin, block, slope, (_, _, _, _, _, own, base, far) in zip(starts, blocks, slope_of, saved):
         outs = [
             shape((block, width), LOW), shape((block, width), F32), shape((block, width), LOW),
             shape((block, hidden), LOW), shape((block, width), F32), shape((8, width), F32), shape((8, hidden), F32),
         ]
         outs = call(
             functools.partial(feed_back, slice(begin, begin + block), tile), "feed_back",
-            [own, far, normed, slope, vectors, cotangent, w_up, w_down],
-            full(own, far, normed, slope) + [far_off] * 2 + [near] * 2,
+            [own, far, base, slope, vectors, cotangent, w_up, w_down],
+            full(own, far, base, slope) + [far_off] * 2 + [near] * 2,
             outs, full(*outs),
             scratch=[pltpu.VMEM((8, width), F32), pltpu.VMEM((block, width), LOW), dma((2,))],
         )
@@ -677,8 +692,8 @@
 
     norms = []
     first_norm(0)
+    early.step()
     down.high()
-    early.step()
     outs = gradient([s[2] for s in saved], [o[3] for o in back], blocks, [0] * tiles, tile)
     up = Chunk(outs, swap_dp(outs[0], stages[0]), hidden, 0, straight)
     down.low()

time: 162 us -> 159 us (0.981)
  waiting for transfers between devices: 68.7 us -> 64.7 us
  starting transfers between devices: 36.2 us -> 39.4 us
  local copies, waits for them, and re-layouts: 5.17 us -> 3.05 us
    ppermute x23, waiting for transfers between devices: 41.4 us -> 36.7 us  [swap_dp(): return lax.ppermute(array, 'dp', [(i, i ^ bits) for i in range(ranks)])]
    ppermute x23, starting transfers between devices: 24.1 us -> 26.4 us  [swap_dp(): return lax.ppermute(array, 'dp', [(i, i ^ bits) for i in range(ranks)])]
    unnamed x46 -> x34, local copies, waits for them, and re-layouts: 3.28 us -> 1.16 us
    pallas_call x39 -> x40, Pallas kernels: 47.8 us -> 47.8 us  [call(): pl.pallas_call(chained(kernel, len(operands), len(out_shape)), grid=grid,...]
  transfers between devices with their start and end apart: 31 -> 31, of which waited for: 14 -> 15; matrix products, arithmetic and copies ran while one was open for 2% -> 2% of each run, Pallas kernels for 29% -> 30%
where the time goes in v7:
time: 159 us
  waiting for transfers between devices  64.7 us (41%)
  Pallas kernels  47.8 us (30%)
  starting transfers between devices  39.4 us (25%)
  local copies, waits for them, and re-layouts  3.05 us (2%)
  other arithmetic  2.67 us (2%)
    pallas_call x40, Pallas kernels, call(): pl.pallas_call(chained(kernel, len(operands), len(out_shape)), grid=grid,...  47.8 us
    ppermute x23, waiting for transfers between devices, swap_dp(): return lax.ppermute(array, 'dp', [(i, i ^ bits) for i in range(ranks)])  36.7 us
    ppermute x8, waiting for transfers between devices, swap_tp(): return lax.ppermute(array, 'tp', pairs)  28 us
    ppermute x23, starting transfers between devices, swap_dp(): return lax.ppermute(array, 'dp', [(i, i ^ bits) for i in range(ranks)])  26.4 us
    ppermute x8, starting transfers between devices, swap_tp(): return lax.ppermute(array, 'tp', pairs)  13 us
  transfers between devices with their start and end apart: 31, of which 15 were waited for; matrix products, arithmetic and copies ran while one was open for 2% of the time, Pallas kernels for 30%

profile of v7, /device:TPU:0, one launch (start us, length us, event | category | flops | bytes accessed | tf_op | source)
XLA Modules:
  0.0 158.7 jit_solution(3785812873838144652)
XLA Ops:
  1.7 3.0 %collective-permute-start = (f32[192,768]{1,0:T(8,128)S(1)}, f32[192,768]{1,0:T(8,128)S(1)}, u32[]{:S(2)}, u32[]{:S(2)}) collective-permute-start(f32[192,768]{1,0:T(8,128)S(1)} %dynamic-slice_convert_fusion), channel_id=1, source_target_pairs={{0,1},{1,0},{2,3},{3,2},{4,5},{5,4},{6,7},{7,6},{8,9},{9,8},{10,11... | collective-permute-start | bytes 1769480 | tf_op jit(solution)/shard_map/ppermute | solution.py:465
  4.8 7.7 %attend.1 = (bf16[384,1152]{1,0:T(8,128)(2,1)}, bf16[384,384]{1,0:T(8,128)(2,1)}, f32[8,384]{1,0:T(8,128)}, f32[192,384]{1,0:T(8,128)}, f32[192,384]{1,0:T(8,128)}, /*index=5*/f32[8,128]{1,0:T(8,128)}) custom-call(bf16[384,768]{1,0:T(8,128)(2,1)} %refs_2_.8, bf16[384,768]{1,0:T(8,128)(2,1)} %refs_2_.8, bf16[3,768,384]{2,1,0:T(8,128)(2,1)} %refs_2_.9, ...), custom_call_target="tpu_custom_call" | custom-call | flops 10000000000 | bytes 1000000 | tf_op jit(solution)/shard_map/attend/pallas_call | solution.py:447
  12.6 6.4 %collective-permute-done.refs_1_ = f32[192,768]{1,0:T(8,128)S(1)} collective-permute-done((f32[192,768]{1,0:T(8,128)S(1)}, f32[192,768]{1,0:T(8,128)S(1)}, u32[]{:S(2)}, u32[]{:S(2)}) %collective-permute-start) | collective-permute-done | bytes 589856 | tf_op jit(solution)/shard_map/ppermute | solution.py:465
  20.6 2.1 %collective-permute-start.5 = (f32[192,384]{1,0:T(8,128)S(1)}, f32[192,384]{1,0:T(8,128)S(1)}, u32[]{:S(2)}, u32[]{:S(2)}) collective-permute-start(f32[192,384]{1,0:T(8,128)S(1)} %copy-done.16), channel_id=1, source_target_pairs={{0,1},{1,0},{2,3},{3,2},{4,5},{5,4},{6,7},{7,6},{8,9},{9,8},{10,11... | collective-permute-start | bytes 884744 | tf_op jit(solution)/shard_map/ppermute | solution.py:465
  25.0 4.7 %feed.2 = (f32[192,768]{1,0:T(8,128)S(1)}, f32[192,128]{1,0:T(8,128)S(1)}, bf16[192,768]{1,0:T(8,128)(2,1)S(1)}, bf16[192,1536]{1,0:T(8,128)(2,1)S(1)}, f32[192,...) custom-call(f32[8,128]{1,0:T(8,128)S(1)} %get-tuple-element.134.refs_0_, ...), custom_call_target="tpu_custom_call" | custom-call | flops 10000000000 | bytes 1000000 | tf_op jit(solution)/shard_map/feed/pallas_call | solution.py:447
  29.7 1.8 %collective-permute-start.6 = (f32[192,768]{1,0:T(8,128)S(1)}, f32[192,768]{1,0:T(8,128)S(1)}, u32[]{:S(2)}, u32[]{:S(2)}) collective-permute-start(f32[192,768]{1,0:T(8,128)S(1)} %get-tuple-element.146.refs_1_), channel_id=1, source_target_pairs={{0,1},{1,0},{2,3},{3,2},{4,5},{5,4},{6,7},{7,6},{8,9},{9,8},{10,11... | collective-permute-start | bytes 1769480 | tf_op jit(solution)/shard_map/ppermute | solution.py:465
  31.5 3.9 %feed.3 = (f32[192,768]{1,0:T(8,128)S(1)}, f32[192,128]{1,0:T(8,128)S(1)}, bf16[192,768]{1,0:T(8,128)(2,1)S(1)}, bf16[192,1536]{1,0:T(8,128)(2,1)S(1)}, f32[192,...) custom-call(f32[8,128]{1,0:T(8,128)S(1)} %get-tuple-element.139.refs_0_, ...), custom_call_target="tpu_custom_call" | custom-call | flops 10000000000 | bytes 1000000 | tf_op jit(solution)/shard_map/feed/pallas_call | solution.py:447
  37.3 8.7 %collective-permute-done.6.refs_2_ = f32[192,768]{1,0:T(8,128)S(1)} collective-permute-done((f32[192,768]{1,0:T(8,128)S(1)}, f32[192,768]{1,0:T(8,128)S(1)}, u32[]{:S(2)}, u32[]{:S(2)}) %collective-permute-start.6) | collective-permute-done | bytes 589856 | tf_op jit(solution)/shard_map/ppermute | solution.py:465
  46.0 3.1 %feed_back.2 = (bf16[192,768]{1,0:T(8,128)(2,1)S(1)}, f32[192,768]{1,0:T(8,128)S(1)}, bf16[192,768]{1,0:T(8,128)(2,1)S(1)}, bf16[192,1536]{1,0:T(8,128)(2,1)S(1)...) custom-call(f32[8,128]{1,0:T(8,128)S(1)} %get-tuple-element.145.refs_0_, ...), custom_call_target="tpu_custom_call" | custom-call | flops 10000000000 | bytes 1000000 | tf_op jit(solution)/shard_map/feed_back/pallas_call | solution.py:447
  50.9 7.7 %collective-permute-done.7.refs_2_ = f32[192,768]{1,0:T(8,128)S(1)} collective-permute-done((f32[192,768]{1,0:T(8,128)S(1)}, f32[192,768]{1,0:T(8,128)S(1)}, u32[]{:S(2)}, u32[]{:S(2)}) %collective-permute-start.7) | collective-permute-done | bytes 589856 | tf_op jit(solution)/shard_map/ppermute | solution.py:465
  58.7 3.1 %feed_back.3 = (bf16[192,768]{1,0:T(8,128)(2,1)S(1)}, f32[192,768]{1,0:T(8,128)S(1)}, bf16[192,768]{1,0:T(8,128)(2,1)S(1)}, bf16[192,1536]{1,0:T(8,128)(2,1)S(1)...) custom-call(f32[8,128]{1,0:T(8,128)S(1)} %get-tuple-element.150.refs_0_, ...), custom_call_target="tpu_custom_call" | custom-call | flops 10000000000 | bytes 1000000 | tf_op jit(solution)/shard_map/feed_back/pallas_call | solution.py:447
  61.8 2.9 %outer.3 = (f32[384,1536]{1,0:T(8,128)S(1)}, f32[384,1536]{1,0:T(8,128)S(1)}, f32[8,128]{1,0:T(8,128)S(1)}) custom-call(f32[8,128]{1,0:T(8,128)S(1)} %get-tuple-element.155.refs_0_, s32[3]{0:T(128)S(1)} %pad_add_fusion.refs_1_, bf16[192,768]{1,0:T(8,128)(2,1)S(1)} %get-tuple-element.156.refs_2_, bf16[192,768]{1,0:T(8,128)(2,1)S(1)} %get-tuple-element.157.refs_3_, ...), custom_call_target="tpu_custom_call" | custom-call | flops 10000000000 | bytes 1000000 | tf_op jit(solution)/shard_map/outer/pallas_call | solution.py:447
  64.9 1.8 %collective-permute-start.13 = (f32[192,768]{1,0:T(8,128)S(1)}, f32[192,768]{1,0:T(8,128)S(1)}, u32[]{:S(2)}, u32[]{:S(2)}) collective-permute-start(f32[192,768]{1,0:T(8,128)S(1)} %get-tuple-element.186.refs_2_), channel_id=1, source_target_pairs={{0,1},{1,0},{2,3},{3,2},{4,5},{5,4},{6,7},{7,6},{8,9},{9,8},{10,11... | collective-permute-start | bytes 1769480 | tf_op jit(solution)/shard_map/ppermute | solution.py:465
  66.7 4.7 %collective-permute-done.8.refs_3_ = f32[192,768]{1,0:T(8,128)S(1)} collective-permute-done((f32[192,768]{1,0:T(8,128)S(1)}, f32[192,768]{1,0:T(8,128)S(1)}, u32[]{:S(2)}, u32[]{:S(2)}) %collective-permute-start.8) | collective-permute-done | bytes 589856 | tf_op jit(solution)/shard_map/ppermute | solution.py:465
  75.0 2.9 %outer.4 = (f32[384,1536]{1,0:T(8,128)S(1)}, f32[384,1536]{1,0:T(8,128)S(1)}, f32[8,128]{1,0:T(8,128)S(1)}) custom-call(f32[8,128]{1,0:T(8,128)S(1)} %get-tuple-element.171.refs_0_, s32[3]{0:T(128)S(1)} %pad_add_fusion.refs_1_, bf16[192,768]{1,0:T(8,128)(2,1)S(1)} %get-tuple-element.172.refs_2_, bf16[192,768]{1,0:T(8,128)(2,1)S(1)} %get-tuple-element.173.refs_3_, ...), custom_call_target="tpu_custom_call" | custom-call | flops 10000000000 | bytes 1000000 | tf_op jit(solution)/shard_map/outer/pallas_call | solution.py:447
  78.6 3.6 %collective-permute-done.10.refs_3_.refs_6_ = f32[192,512]{1,0:T(8,128)S(1)} collective-permute-done((f32[192,512]{1,0:T(8,128)S(1)}, f32[192,512]{1,0:T(8,128)S(1)}, u32[]{:S(2)}, u32[]{:S(2)}) %collective-permute-start.10) | collective-permute-done | bytes 393248 | tf_op jit(solution)/shard_map/ppermute | solution.py:468
  82.2 3.2 %collective-permute-start.14 = (f32[96,512]{1,0:T(8,128)S(1)}, f32[96,512]{1,0:T(8,128)S(1)}, u32[]{:S(2)}, u32[]{:S(2)}) collective-permute-start(f32[96,512]{1,0:T(8,128)S(1)} %get-tuple-element.203), channel_id=1, source_target_pairs={{0,16},{2,18},{4,20},{6,22},{8,24},{10,26},{12,28},{14,30},{16,0},... | collective-permute-start | bytes 589832 | tf_op jit(solution)/shard_map/ppermute | solution.py:468
  88.2 5.7 %attend_back.1 = (bf16[384,1536]{1,0:T(8,128)(2,1)S(1)}, f32[8,1536]{1,0:T(8,128)S(1)}, f32[8,128]{1,0:T(8,128)S(1)}) custom-call(f32[8,128]{1,0:T(8,128)S(1)} %get-tuple-element.192.refs_0_, bf16[192,768]{1,0:T(8,128)(2,1)S(1)} %get-tuple-element.193.refs_1_.refs_3_, bf16[192,768]{1,0:T(8,128)(2,1)S(1)} %get-tuple-element.194.refs_2_.refs_4_, ...), custom_call_target="tpu_custom_call" | custom-call | flops 100000000 | bytes 1000000 | tf_op jit(solution)/shard_map/attend_back/pallas_call | solution.py:447
  95.5 3.5 %outer.5 = (f32[392,1536]{1,0:T(8,128)S(1)}, f32[392,1536]{1,0:T(8,128)S(1)}, f32[8,128]{1,0:T(8,128)S(1)}) custom-call(f32[8,128]{1,0:T(8,128)S(1)} %get-tuple-element.199.refs_0_, s32[3]{0:T(128)S(1)} %pad_add_fusion.refs_1_, bf16[384,768]{1,0:T(8,128)(2,1)S(1)} %copy-done, bf16[192,768]{1,0:T(8,128)(2,1)S(1)} %get-tuple-element.193.refs_1_.refs_3_, ...), custom_call_target="tpu_custom_call" | custom-call | flops 100000000 | bytes 1000000 | tf_op jit(solution)/shard_map/outer/pallas_call | solution.py:447
  99.2 1.9 %collective-permute-start.19 = (f32[48,1024]{1,0:T(8,128)S(1)}, f32[48,1024]{1,0:T(8,128)S(1)}, u32[]{:S(2)}, u32[]{:S(2)}) collective-permute-start(f32[48,1024]{1,0:T(8,128)S(1)} %get-tuple-element.215), channel_id=1, source_target_pairs={{0,16},{2,18},{4,20},{6,22},{8,24},{10,26},{12,28},{14,30},{16,0},... | collective-permute-start | bytes 589832 | tf_op jit(solution)/shard_map/ppermute | solution.py:468
  101.1 3.3 %collective-permute-done.17.refs_3_.refs_6_ = f32[96,1536]{1,0:T(8,128)S(1)} collective-permute-done((f32[96,1536]{1,0:T(8,128)S(1)}, f32[96,1536]{1,0:T(8,128)S(1)}, u32[]{:S(2)}, u32[]{:S(2)}) %collective-permute-start.17) | collective-permute-done | bytes 589856 | tf_op jit(solution)/shard_map/ppermute | solution.py:468
  104.5 2.3 %collective-permute-start.21 = (f32[96,1536]{1,0:T(8,128)S(1)}, f32[96,1536]{1,0:T(8,128)S(1)}, u32[]{:S(2)}, u32[]{:S(2)}) collective-permute-start(f32[96,1536]{1,0:T(8,128)S(1)} %get-tuple-element.218), channel_id=1, source_target_pairs={{0,8},{2,10},{4,12},{6,14},{8,0},{10,2},{12,4},{14,6},{16,24},{18,... | collective-permute-start | bytes 1769480 | tf_op jit(solution)/shard_map/ppermute | solution.py:468
  109.1 2.7 %back_tokens.1 = (f32[384,768]{1,0:T(8,128)S(1)}, f32[8,128]{1,0:T(8,128)S(1)}) custom-call(f32[8,128]{1,0:T(8,128)S(1)} %get-tuple-element.213.refs_0_, bf16[384,1536]{1,0:T(8,128)(2,1)S(1)} %get-tuple-element.200.refs_5_.refs_1_, bf16[3,768,384]{2,1,0:T(8,128)(2,1)} %refs_2_.9), custom_call_target="tpu_custom_call" | custom-call | flops 100000000 | bytes 1000000 | tf_op jit(solution)/shard_map/back_tokens/pallas_call | solution.py:447
  113.2 3.8 %collective-permute-done.20.refs_3_ = f32[96,1536]{1,0:T(8,128)S(1)} collective-permute-done((f32[96,1536]{1,0:T(8,128)S(1)}, f32[96,1536]{1,0:T(8,128)S(1)}, u32[]{:S(2)}, u32[]{:S(2)}) %collective-permute-start.20) | collective-permute-done | bytes 589856 | tf_op jit(solution)/shard_map/ppermute | solution.py:468
  117.0 1.8 %collective-permute-done.21.refs_4_ = f32[96,1536]{1,0:T(8,128)S(1)} collective-permute-done((f32[96,1536]{1,0:T(8,128)S(1)}, f32[96,1536]{1,0:T(8,128)S(1)}, u32[]{:S(2)}, u32[]{:S(2)}) %collective-permute-start.21) | collective-permute-done | bytes 589856 | tf_op jit(solution)/shard_map/ppermute | solution.py:468
  120.5 10.2 %collective-permute-done.22.refs_3_.refs_6_ = f32[104,1536]{1,0:T(8,128)S(1)} collective-permute-done((f32[104,1536]{1,0:T(8,128)S(1)}, f32[104,1536]{1,0:T(8,128)S(1)}, u32[]{:S(2)}, u32[]{:S(2)}) %collective-permute-start.22) | collective-permute-done | bytes 639008 | tf_op jit(solution)/shard_map/ppermute | solution.py:468
  130.8 2.3 %collective-permute-start.25 = (f32[56,1536]{1,0:T(8,128)S(1)}, f32[56,1536]{1,0:T(8,128)S(1)}, u32[]{:S(2)}, u32[]{:S(2)}) collective-permute-start(f32[56,1536]{1,0:T(8,128)S(1)} %get-tuple-element.226), channel_id=1, source_target_pairs={{0,8},{2,10},{4,12},{6,14},{8,0},{10,2},{12,4},{14,6},{16,24},{18,... | collective-permute-start | bytes 1032200 | tf_op jit(solution)/shard_map/ppermute | solution.py:468
  134.1 1.9 %collective-permute-start.27 = (f32[48,512]{1,0:T(8,128)S(1)}, f32[48,512]{1,0:T(8,128)S(1)}, u32[]{:S(2)}, u32[]{:S(2)}) collective-permute-start(f32[48,512]{1,0:T(8,128)S(1)} %get-tuple-element.231), channel_id=1, source_target_pairs={{0,4},{2,6},{4,0},{6,2},{8,12},{10,14},{12,8},{14,10},{16,20},{18,... | collective-permute-start | bytes 294920 | tf_op jit(solution)/shard_map/ppermute | solution.py:468
  136.8 5.0 %collective-permute-done.24.refs_3_ = f32[96,1536]{1,0:T(8,128)S(1)} collective-permute-done((f32[96,1536]{1,0:T(8,128)S(1)}, f32[96,1536]{1,0:T(8,128)S(1)}, u32[]{:S(2)}, u32[]{:S(2)}) %collective-permute-start.24) | collective-permute-done | bytes 589856 | tf_op jit(solution)/shard_map/ppermute | solution.py:468
  142.2 2.6 %collective-permute-start.29 = (f32[8,1536]{1,0:T(8,128)S(1)}, f32[8,1536]{1,0:T(8,128)S(1)}, u32[]{:S(2)}, u32[]{:S(2)}) collective-permute-start(f32[8,1536]{1,0:T(8,128)S(1)} %get-tuple-element.238.refs_1_), channel_id=1, source_target_pairs={{0,16},{2,18},{4,20},{6,22},{8,24},{10,26},{12,28},{14,30},{16,0},... | collective-permute-start | bytes 147464 | tf_op jit(solution)/shard_map/ppermute | solution.py:468
  145.2 1.9 %collective-permute-done.26.refs_4_ = f32[48,1536]{1,0:T(8,128)S(1)} collective-permute-done((f32[48,1536]{1,0:T(8,128)S(1)}, f32[48,1536]{1,0:T(8,128)S(1)}, u32[]{:S(2)}, u32[]{:S(2)}) %collective-permute-start.26) | collective-permute-done | bytes 294944 | tf_op jit(solution)/shard_map/ppermute | solution.py:468
  151.8 6.2 %collective-permute-done.30.refs_2_ = f32[48,1536]{1,0:T(8,128)S(1)} collective-permute-done((f32[48,1536]{1,0:T(8,128)S(1)}, f32[48,1536]{1,0:T(8,128)S(1)}, u32[]{:S(2)}, u32[]{:S(2)}) %collective-permute-start.30) | collective-permute-done | bytes 294944 | tf_op jit(solution)/shard_map/ppermute | solution.py:468
  (112 shorter events, 31.2 us)
Async XLA Ops:
  1.7 17.3 %copy-start.7 = (bf16[768]{0:T(1024)(128)(2,1)S(1)}, bf16[768]{0:T(1024)(128)(2,1)}, u32[]{:S(2)}) copy-start(bf16[768]{0:T(1024)(128)(2,1)} %refs_2_.6) | copy-start | bytes 4612
  1.7 17.2 %collective-permute-start = (f32[192,768]{1,0:T(8,128)S(1)}, f32[192,768]{1,0:T(8,128)S(1)}, u32[]{:S(2)}, u32[]{:S(2)}) collective-permute-start(f32[192,768]{1,0:T(8,128)S(1)} %dynamic-slice_convert_fusion), channel_id=1, source_target_pairs={{0,1},{1,0},{2,3},{3,2},{4,5},{5,4},{6,7},{7,6},{8,9},{9,8},{10,11... | collective-permute-start | bytes 1769480 | tf_op jit(solution)/shard_map/ppermute | solution.py:465
  12.5 12.5 %collective-permute-start.4 = (f32[192,384]{1,0:T(8,128)}, f32[192,384]{1,0:T(8,128)S(1)}, u32[]{:S(2)}, u32[]{:S(2)}) collective-permute-start(f32[192,384]{1,0:T(8,128)} %get-tuple-element.135), channel_id=1, source_target_pairs={{0,1},{1,0},{2,3},{3,2},{4,5},{5,4},{6,7},{7,6},{8,9},{9,8},{10,11... | collective-permute-start | bytes 884744 | tf_op jit(solution)/shard_map/ppermute | solution.py:465
  19.8 3.0 %collective-permute-start.3 = (f32[64,768]{1,0:T(8,128)S(1)}, f32[64,768]{1,0:T(8,128)S(1)}, u32[]{:S(2)}, u32[]{:S(2)}) collective-permute-start(f32[64,768]{1,0:T(8,128)S(1)} %get-tuple-element.255), channel_id=1, source_target_pairs={{0,2},{2,0},{4,6},{6,4},{8,10},{10,8},{12,14},{14,12},{16,18},{18,... | collective-permute-start | bytes 589832 | tf_op jit(solution)/shard_map/ppermute | solution.py:468
  19.9 2.9 %collective-permute-start.2 = (f32[64,768]{1,0:T(8,128)S(1)}, f32[64,768]{1,0:T(8,128)S(1)}, u32[]{:S(2)}, u32[]{:S(2)}) collective-permute-start(f32[64,768]{1,0:T(8,128)S(1)} %get-tuple-element.256), channel_id=1, source_target_pairs={{0,2},{2,0},{4,6},{6,4},{8,10},{10,8},{12,14},{14,12},{16,18},{18,... | collective-permute-start | bytes 589832 | tf_op jit(solution)/shard_map/ppermute | solution.py:468
  20.4 2.4 %collective-permute-start.1 = (f32[64,768]{1,0:T(8,128)S(1)}, f32[64,768]{1,0:T(8,128)S(1)}, u32[]{:S(2)}, u32[]{:S(2)}) collective-permute-start(f32[64,768]{1,0:T(8,128)S(1)} %get-tuple-element.257), channel_id=1, source_target_pairs={{0,2},{2,0},{4,6},{6,4},{8,10},{10,8},{12,14},{14,12},{16,18},{18,... | collective-permute-start | bytes 589832 | tf_op jit(solution)/shard_map/ppermute | solution.py:468
  20.6 10.9 %collective-permute-start.5 = (f32[192,384]{1,0:T(8,128)S(1)}, f32[192,384]{1,0:T(8,128)S(1)}, u32[]{:S(2)}, u32[]{:S(2)}) collective-permute-start(f32[192,384]{1,0:T(8,128)S(1)} %copy-done.16), channel_id=1, source_target_pairs={{0,1},{1,0},{2,3},{3,2},{4,5},{5,4},{6,7},{7,6},{8,9},{9,8},{10,11... | collective-permute-start | bytes 884744 | tf_op jit(solution)/shard_map/ppermute | solution.py:465
  29.7 16.3 %collective-permute-start.6 = (f32[192,768]{1,0:T(8,128)S(1)}, f32[192,768]{1,0:T(8,128)S(1)}, u32[]{:S(2)}, u32[]{:S(2)}) collective-permute-start(f32[192,768]{1,0:T(8,128)S(1)} %get-tuple-element.146.refs_1_), channel_id=1, source_target_pairs={{0,1},{1,0},{2,3},{3,2},{4,5},{5,4},{6,7},{7,6},{8,9},{9,8},{10,11... | collective-permute-start | bytes 1769480 | tf_op jit(solution)/shard_map/ppermute | solution.py:465
  35.4 23.2 %collective-permute-start.7 = (f32[192,768]{1,0:T(8,128)S(1)}, f32[192,768]{1,0:T(8,128)S(1)}, u32[]{:S(2)}, u32[]{:S(2)}) collective-permute-start(f32[192,768]{1,0:T(8,128)S(1)} %get-tuple-element.151.refs_1_), channel_id=1, source_target_pairs={{0,1},{1,0},{2,3},{3,2},{4,5},{5,4},{6,7},{7,6},{8,9},{9,8},{10,11... | collective-permute-start | bytes 1769480 | tf_op jit(solution)/shard_map/ppermute | solution.py:465
  49.1 22.2 %collective-permute-start.8 = (f32[192,768]{1,0:T(8,128)S(1)}, f32[192,768]{1,0:T(8,128)S(1)}, u32[]{:S(2)}, u32[]{:S(2)}) collective-permute-start(f32[192,768]{1,0:T(8,128)S(1)} %get-tuple-element.162.refs_2_), channel_id=1, source_target_pairs={{0,1},{1,0},{2,3},{3,2},{4,5},{5,4},{6,7},{7,6},{8,9},{9,8},{10,11... | collective-permute-start | bytes 1769480 | tf_op jit(solution)/shard_map/ppermute | solution.py:465
  64.8 7.0 %collective-permute-start.9 = (f32[384,1536]{1,0:T(8,128)S(1)}, f32[384,1536]{1,0:T(8,128)S(1)}, u32[]{:S(2)}, u32[]{:S(2)}) collective-permute-start(f32[384,1536]{1,0:T(8,128)S(1)} %get-tuple-element.169), channel_id=1, source_target_pairs={{0,2},{2,0},{4,6},{6,4},{8,10},{10,8},{12,14},{14,12},{16,18},{18,... | collective-permute-start | bytes 7077896 | tf_op jit(solution)/shard_map/ppermute | solution.py:468
  64.9 22.6 %collective-permute-start.13 = (f32[192,768]{1,0:T(8,128)S(1)}, f32[192,768]{1,0:T(8,128)S(1)}, u32[]{:S(2)}, u32[]{:S(2)}) collective-permute-start(f32[192,768]{1,0:T(8,128)S(1)} %get-tuple-element.186.refs_2_), channel_id=1, source_target_pairs={{0,1},{1,0},{2,3},{3,2},{4,5},{5,4},{6,7},{7,6},{8,9},{9,8},{10,11... | collective-permute-start | bytes 1769480 | tf_op jit(solution)/shard_map/ppermute | solution.py:465
  71.9 13.5 %collective-permute-start.11 = (f32[96,1024]{1,0:T(8,128)S(1)}, f32[96,1024]{1,0:T(8,128)S(1)}, u32[]{:S(2)}, u32[]{:S(2)}) collective-permute-start(f32[96,1024]{1,0:T(8,128)S(1)} %get-tuple-element.180), channel_id=1, source_target_pairs={{0,4},{2,6},{4,0},{6,2},{8,12},{10,14},{12,8},{14,10},{16,20},{18,... | collective-permute-start | bytes 1179656 | tf_op jit(solution)/shard_map/ppermute | solution.py:468
  73.4 8.7 %collective-permute-start.10 = (f32[192,512]{1,0:T(8,128)S(1)}, f32[192,512]{1,0:T(8,128)S(1)}, u32[]{:S(2)}, u32[]{:S(2)}) collective-permute-start(f32[192,512]{1,0:T(8,128)S(1)} %get-tuple-element.178), channel_id=1, source_target_pairs={{0,8},{2,10},{4,12},{6,14},{8,0},{10,2},{12,4},{14,6},{16,24},{18,... | collective-permute-start | bytes 1179656 | tf_op jit(solution)/shard_map/ppermute | solution.py:468
  78.0 21.2 %collective-permute-start.15 = (f32[96,1024]{1,0:T(8,128)S(1)}, f32[96,1024]{1,0:T(8,128)S(1)}, u32[]{:S(2)}, u32[]{:S(2)}) collective-permute-start(f32[96,1024]{1,0:T(8,128)S(1)} %get-tuple-element.205), channel_id=1, source_target_pairs={{0,4},{2,6},{4,0},{6,2},{8,12},{10,14},{12,8},{14,10},{16,20},{18,... | collective-permute-start | bytes 1179656 | tf_op jit(solution)/shard_map/ppermute | solution.py:468
  78.6 8.3 %collective-permute-start.12 = (f32[384,1536]{1,0:T(8,128)S(1)}, f32[384,1536]{1,0:T(8,128)S(1)}, u32[]{:S(2)}, u32[]{:S(2)}) collective-permute-start(f32[384,1536]{1,0:T(8,128)S(1)} %get-tuple-element.183), channel_id=1, source_target_pairs={{0,2},{2,0},{4,6},{6,4},{8,10},{10,8},{12,14},{14,12},{16,18},{18,... | collective-permute-start | bytes 7077896 | tf_op jit(solution)/shard_map/ppermute | solution.py:468
  82.2 16.9 %collective-permute-start.14 = (f32[96,512]{1,0:T(8,128)S(1)}, f32[96,512]{1,0:T(8,128)S(1)}, u32[]{:S(2)}, u32[]{:S(2)}) collective-permute-start(f32[96,512]{1,0:T(8,128)S(1)} %get-tuple-element.203), channel_id=1, source_target_pairs={{0,16},{2,18},{4,20},{6,22},{8,24},{10,26},{12,28},{14,30},{16,0},... | collective-permute-start | bytes 589832 | tf_op jit(solution)/shard_map/ppermute | solution.py:468
  85.5 13.7 %collective-permute-start.16 = (f32[96,1024]{1,0:T(8,128)S(1)}, f32[96,1024]{1,0:T(8,128)S(1)}, u32[]{:S(2)}, u32[]{:S(2)}) collective-permute-start(f32[96,1024]{1,0:T(8,128)S(1)} %get-tuple-element.206), channel_id=1, source_target_pairs={{0,8},{2,10},{4,12},{6,14},{8,0},{10,2},{12,4},{14,6},{16,24},{18,... | collective-permute-start | bytes 1179656 | tf_op jit(solution)/shard_map/ppermute | solution.py:468
  86.9 17.5 %collective-permute-start.17 = (f32[96,1536]{1,0:T(8,128)S(1)}, f32[96,1536]{1,0:T(8,128)S(1)}, u32[]{:S(2)}, u32[]{:S(2)}) collective-permute-start(f32[96,1536]{1,0:T(8,128)S(1)} %get-tuple-element.208), channel_id=1, source_target_pairs={{0,4},{2,6},{4,0},{6,2},{8,12},{10,14},{12,8},{14,10},{16,20},{18,... | collective-permute-start | bytes 1769480 | tf_op jit(solution)/shard_map/ppermute | solution.py:468
  94.0 23.0 %collective-permute-start.20 = (f32[96,1536]{1,0:T(8,128)S(1)}, f32[96,1536]{1,0:T(8,128)S(1)}, u32[]{:S(2)}, u32[]{:S(2)}) collective-permute-start(f32[96,1536]{1,0:T(8,128)S(1)} %get-tuple-element.217), channel_id=1, source_target_pairs={{0,4},{2,6},{4,0},{6,2},{8,12},{10,14},{12,8},{14,10},{16,20},{18,... | collective-permute-start | bytes 1769480 | tf_op jit(solution)/shard_map/ppermute | solution.py:468
  99.2 12.6 %collective-permute-start.19 = (f32[48,1024]{1,0:T(8,128)S(1)}, f32[48,1024]{1,0:T(8,128)S(1)}, u32[]{:S(2)}, u32[]{:S(2)}) collective-permute-start(f32[48,1024]{1,0:T(8,128)S(1)} %get-tuple-element.215), channel_id=1, source_target_pairs={{0,16},{2,18},{4,20},{6,22},{8,24},{10,26},{12,28},{14,30},{16,0},... | collective-permute-start | bytes 589832 | tf_op jit(solution)/shard_map/ppermute | solution.py:468
  101.1 5.7 %collective-permute-start.18 = (f32[392,1536]{1,0:T(8,128)S(1)}, f32[392,1536]{1,0:T(8,128)S(1)}, u32[]{:S(2)}, u32[]{:S(2)}) collective-permute-start(f32[392,1536]{1,0:T(8,128)S(1)} %get-tuple-element.211), channel_id=1, source_target_pairs={{0,2},{2,0},{4,6},{6,4},{8,10},{10,8},{12,14},{14,12},{16,18},{18,... | collective-permute-start | bytes 7225352 | tf_op jit(solution)/shard_map/ppermute | solution.py:468
  104.5 14.4 %collective-permute-start.21 = (f32[96,1536]{1,0:T(8,128)S(1)}, f32[96,1536]{1,0:T(8,128)S(1)}, u32[]{:S(2)}, u32[]{:S(2)}) collective-permute-start(f32[96,1536]{1,0:T(8,128)S(1)} %get-tuple-element.218), channel_id=1, source_target_pairs={{0,8},{2,10},{4,12},{6,14},{8,0},{10,2},{12,4},{14,6},{16,24},{18,... | collective-permute-start | bytes 1769480 | tf_op jit(solution)/shard_map/ppermute | solution.py:468
  106.9 23.8 %collective-permute-start.22 = (f32[104,1536]{1,0:T(8,128)S(1)}, f32[104,1536]{1,0:T(8,128)S(1)}, u32[]{:S(2)}, u32[]{:S(2)}) collective-permute-start(f32[104,1536]{1,0:T(8,128)S(1)} %get-tuple-element.220), channel_id=1, source_target_pairs={{0,4},{2,6},{4,0},{6,2},{8,12},{10,14},{12,8},{14,10},{16,20},{18,... | collective-permute-start | bytes 1916936 | tf_op jit(solution)/shard_map/ppermute | solution.py:468
  108.5 33.3 %collective-permute-start.24 = (f32[96,1536]{1,0:T(8,128)S(1)}, f32[96,1536]{1,0:T(8,128)S(1)}, u32[]{:S(2)}, u32[]{:S(2)}) collective-permute-start(f32[96,1536]{1,0:T(8,128)S(1)} %get-tuple-element.225), channel_id=1, source_target_pairs={{0,4},{2,6},{4,0},{6,2},{8,12},{10,14},{12,8},{14,10},{16,20},{18,... | collective-permute-start | bytes 1769480 | tf_op jit(solution)/shard_map/ppermute | solution.py:468
  111.8 36.2 %collective-permute-start.28 = (f32[384,768]{1,0:T(8,128)S(1)}, f32[384,768]{1,0:T(8,128)S(1)}, u32[]{:S(2)}, u32[]{:S(2)}) collective-permute-start(f32[384,768]{1,0:T(8,128)S(1)} %get-tuple-element.233.refs_1_), channel_id=1, source_target_pairs={{0,1},{1,0},{2,3},{3,2},{4,5},{5,4},{6,7},{7,6},{8,9},{9,8},{10,11... | collective-permute-start | bytes 3538952 | tf_op jit(solution)/shard_map/ppermute | solution.py:465
  118.9 15.2 %collective-permute-start.23 = (f32[48,1536]{1,0:T(8,128)S(1)}, f32[48,1536]{1,0:T(8,128)S(1)}, u32[]{:S(2)}, u32[]{:S(2)}) collective-permute-start(f32[48,1536]{1,0:T(8,128)S(1)} %get-tuple-element.223), channel_id=1, source_target_pairs={{0,16},{2,18},{4,20},{6,22},{8,24},{10,26},{12,28},{14,30},{16,0},... | collective-permute-start | bytes 884744 | tf_op jit(solution)/shard_map/ppermute | solution.py:468
  130.8 11.3 %collective-permute-start.25 = (f32[56,1536]{1,0:T(8,128)S(1)}, f32[56,1536]{1,0:T(8,128)S(1)}, u32[]{:S(2)}, u32[]{:S(2)}) collective-permute-start(f32[56,1536]{1,0:T(8,128)S(1)} %get-tuple-element.226), channel_id=1, source_target_pairs={{0,8},{2,10},{4,12},{6,14},{8,0},{10,2},{12,4},{14,6},{16,24},{18,... | collective-permute-start | bytes 1032200 | tf_op jit(solution)/shard_map/ppermute | solution.py:468
  133.1 13.9 %collective-permute-start.26 = (f32[48,1536]{1,0:T(8,128)S(1)}, f32[48,1536]{1,0:T(8,128)S(1)}, u32[]{:S(2)}, u32[]{:S(2)}) collective-permute-start(f32[48,1536]{1,0:T(8,128)S(1)} %get-tuple-element.229), channel_id=1, source_target_pairs={{0,8},{2,10},{4,12},{6,14},{8,0},{10,2},{12,4},{14,6},{16,24},{18,... | collective-permute-start | bytes 884744 | tf_op jit(solution)/shard_map/ppermute | solution.py:468
  134.1 13.1 %collective-permute-start.27 = (f32[48,512]{1,0:T(8,128)S(1)}, f32[48,512]{1,0:T(8,128)S(1)}, u32[]{:S(2)}, u32[]{:S(2)}) collective-permute-start(f32[48,512]{1,0:T(8,128)S(1)} %get-tuple-element.231), channel_id=1, source_target_pairs={{0,4},{2,6},{4,0},{6,2},{8,12},{10,14},{12,8},{14,10},{16,20},{18,... | collective-permute-start | bytes 294920 | tf_op jit(solution)/shard_map/ppermute | solution.py:468
  142.2 7.7 %collective-permute-start.29 = (f32[8,1536]{1,0:T(8,128)S(1)}, f32[8,1536]{1,0:T(8,128)S(1)}, u32[]{:S(2)}, u32[]{:S(2)}) collective-permute-start(f32[8,1536]{1,0:T(8,128)S(1)} %get-tuple-element.238.refs_1_), channel_id=1, source_target_pairs={{0,16},{2,18},{4,20},{6,22},{8,24},{10,26},{12,28},{14,30},{16,0},... | collective-permute-start | bytes 147464 | tf_op jit(solution)/shard_map/ppermute | solution.py:468
  144.8 13.2 %collective-permute-start.30 = (f32[48,1536]{1,0:T(8,128)S(1)}, f32[48,1536]{1,0:T(8,128)S(1)}, u32[]{:S(2)}, u32[]{:S(2)}) collective-permute-start(f32[48,1536]{1,0:T(8,128)S(1)} %get-tuple-element.241), channel_id=1, source_target_pairs={{0,16},{2,18},{4,20},{6,22},{8,24},{10,26},{12,28},{14,30},{16,0},... | collective-permute-start | bytes 884744 | tf_op jit(solution)/shard_map/ppermute | solution.py:468
  (16 other events, 120.2 us)

commit v8 on v7

--- a/solution.py
+++ b/solution.py
@@ -407,6 +407,18 @@
     out_ref[...] = value[:, 3 * local :]
 
 
+def pack(width, *refs):
+    out_ref = refs[-1]
+    value = refs[0][...]
+    for ref in refs[1:-1]:
+        value = value + ref[...]
+    out_ref[:, 0:width] = value[:, 0:width]
+    out_ref[:, width:] = jnp.zeros((8, LANES), F32)
+    for i in range(width // LANES):
+        at = width + i * LANES
+        out_ref[i : i + 1, width:] = value[6:7, at : at + LANES]
+
+
 def chained(kernel, inputs, outputs):
     def body(*refs):
         refs[1 + inputs + outputs][...] = jnp.zeros((8, LANES), F32)
@@ -475,6 +487,7 @@
         order = order + [bit + rest for rest in order]
     order = order[ranks // 2 :] + order[: ranks // 2]
     fused = size % 16 == 0
+    packed = fused and hidden == 2 * width and width <= 8 * LANES
     pad_row = pad_mask
     half = w_out.shape[0] // 2
     w_near = swap_tp(lax.dynamic_slice_in_dim(w_out, (me % 2) * half, half, 0).astype(F32))
@@ -673,8 +686,9 @@
             return functools.reduce(jnp.add, [a[8 * row : 8 * row + 8] for a, row in extra])
         wide = extra[0][0].shape[1]
         specs = [pl.BlockSpec((8, wide), functools.partial(lambda index, n: (index, 0), row)) for _, row in extra]
-        outs = [shape((8, wide), F32)]
-        return call(fold, "fold", [array for array, _ in extra], specs, outs, full(*outs))[0]
+        outs = [shape((8, width + LANES if packed else wide), F32)]
+        kernel = functools.partial(pack, width) if packed else fold
+        return call(kernel, "fold", [array for array, _ in extra], specs, outs, full(*outs))[0]
 
     straight, turned = stages[1:], stages[2:] + stages[1:2]
     outs = gradient([o[2] for o in back], [s[3] for s in saved], blocks, [0] * tiles, tile)
@@ -753,6 +767,9 @@
         last = mixed.add([0], None)
         d_w_qkv = last[:, : 3 * local].reshape(size, 3, local).transpose(1, 0, 2)
         d_w_out = last[:, 3 * local :]
+    d_b_up = bias[6, :hidden]
+    if packed:
+        d_b_up = jnp.concatenate([bias[6, :width], bias[: width // LANES, width:].reshape(hidden - width)])
     return (
         layer_out,
         d_tokens,
@@ -763,7 +780,7 @@
         bias[3, :width],
         bias[4, :width],
         up,
-        bias[6, :hidden],
+        d_b_up,
         jnp.concatenate([down.T, early.T], 0),
         bias[2, :width],
         bias[0, :width],

time: 159 us -> 159 us (level)
  no operation moved by 1% of the time
where the time goes in v8:
time: 159 us; the launch traced here: 158 us
  waiting for transfers between devices  64.3 us (40%)
  Pallas kernels  47.8 us (30%)
  starting transfers between devices  39.4 us (25%)
  other arithmetic  3.27 us (2%)
  local copies, waits for them, and re-layouts  2.44 us (2%)
    pallas_call x40, Pallas kernels, call(): pl.pallas_call(chained(kernel, len(operands), len(out_shape)), grid=grid,...  47.8 us
    ppermute x23, waiting for transfers between devices, swap_dp(): return lax.ppermute(array, 'dp', [(i, i ^ bits) for i in range(ranks)])  36.3 us
    ppermute x8, waiting for transfers between devices, swap_tp(): return lax.ppermute(array, 'tp', pairs)  28 us
    ppermute x23, starting transfers between devices, swap_dp(): return lax.ppermute(array, 'dp', [(i, i ^ bits) for i in range(ranks)])  26.4 us
    ppermute x8, starting transfers between devices, swap_tp(): return lax.ppermute(array, 'tp', pairs)  13 us
  transfers between devices with their start and end apart: 31, of which 15 were waited for; matrix products, arithmetic and copies ran while one was open for 2% of the time, Pallas kernels for 30%

profile of v8, /device:TPU:0, one launch (start us, length us, event | category | flops | bytes accessed | tf_op | source)
XLA Modules:
  0.0 158.3 jit_solution(197654948862064851)
XLA Ops:
  1.7 3.0 %collective-permute-start = (f32[192,768]{1,0:T(8,128)S(1)}, f32[192,768]{1,0:T(8,128)S(1)}, u32[]{:S(2)}, u32[]{:S(2)}) collective-permute-start(f32[192,768]{1,0:T(8,128)S(1)} %dynamic-slice_convert_fusion), channel_id=1, source_target_pairs={{0,1},{1,0},{2,3},{3,2},{4,5},{5,4},{6,7},{7,6},{8,9},{9,8},{10,11... | collective-permute-start | bytes 1769480 | tf_op jit(solution)/shard_map/ppermute | solution.py:477
  4.8 7.7 %attend.1 = (bf16[384,1152]{1,0:T(8,128)(2,1)}, bf16[384,384]{1,0:T(8,128)(2,1)}, f32[8,384]{1,0:T(8,128)}, f32[192,384]{1,0:T(8,128)}, f32[192,384]{1,0:T(8,128)}, /*index=5*/f32[8,128]{1,0:T(8,128)}) custom-call(bf16[384,768]{1,0:T(8,128)(2,1)} %refs_2_.8, bf16[384,768]{1,0:T(8,128)(2,1)} %refs_2_.8, bf16[3,768,384]{2,1,0:T(8,128)(2,1)} %refs_2_.9, ...), custom_call_target="tpu_custom_call" | custom-call | flops 10000000000 | bytes 1000000 | tf_op jit(solution)/shard_map/attend/pallas_call | solution.py:459
  12.6 6.4 %collective-permute-done.refs_1_ = f32[192,768]{1,0:T(8,128)S(1)} collective-permute-done((f32[192,768]{1,0:T(8,128)S(1)}, f32[192,768]{1,0:T(8,128)S(1)}, u32[]{:S(2)}, u32[]{:S(2)}) %collective-permute-start) | collective-permute-done | bytes 589856 | tf_op jit(solution)/shard_map/ppermute | solution.py:477
  20.6 2.1 %collective-permute-start.5 = (f32[192,384]{1,0:T(8,128)S(1)}, f32[192,384]{1,0:T(8,128)S(1)}, u32[]{:S(2)}, u32[]{:S(2)}) collective-permute-start(f32[192,384]{1,0:T(8,128)S(1)} %copy-done.16), channel_id=1, source_target_pairs={{0,1},{1,0},{2,3},{3,2},{4,5},{5,4},{6,7},{7,6},{8,9},{9,8},{10,11... | collective-permute-start | bytes 884744 | tf_op jit(solution)/shard_map/ppermute | solution.py:477
  25.0 4.7 %feed.2 = (f32[192,768]{1,0:T(8,128)S(1)}, f32[192,128]{1,0:T(8,128)S(1)}, bf16[192,768]{1,0:T(8,128)(2,1)S(1)}, bf16[192,1536]{1,0:T(8,128)(2,1)S(1)}, f32[192,...) custom-call(f32[8,128]{1,0:T(8,128)S(1)} %get-tuple-element.134.refs_0_, ...), custom_call_target="tpu_custom_call" | custom-call | flops 10000000000 | bytes 1000000 | tf_op jit(solution)/shard_map/feed/pallas_call | solution.py:459
  29.7 1.8 %collective-permute-start.6 = (f32[192,768]{1,0:T(8,128)S(1)}, f32[192,768]{1,0:T(8,128)S(1)}, u32[]{:S(2)}, u32[]{:S(2)}) collective-permute-start(f32[192,768]{1,0:T(8,128)S(1)} %get-tuple-element.146.refs_1_), channel_id=1, source_target_pairs={{0,1},{1,0},{2,3},{3,2},{4,5},{5,4},{6,7},{7,6},{8,9},{9,8},{10,11... | collective-permute-start | bytes 1769480 | tf_op jit(solution)/shard_map/ppermute | solution.py:477
  31.5 3.9 %feed.3 = (f32[192,768]{1,0:T(8,128)S(1)}, f32[192,128]{1,0:T(8,128)S(1)}, bf16[192,768]{1,0:T(8,128)(2,1)S(1)}, bf16[192,1536]{1,0:T(8,128)(2,1)S(1)}, f32[192,...) custom-call(f32[8,128]{1,0:T(8,128)S(1)} %get-tuple-element.139.refs_0_, ...), custom_call_target="tpu_custom_call" | custom-call | flops 10000000000 | bytes 1000000 | tf_op jit(solution)/shard_map/feed/pallas_call | solution.py:459
  37.3 8.7 %collective-permute-done.6.refs_2_ = f32[192,768]{1,0:T(8,128)S(1)} collective-permute-done((f32[192,768]{1,0:T(8,128)S(1)}, f32[192,768]{1,0:T(8,128)S(1)}, u32[]{:S(2)}, u32[]{:S(2)}) %collective-permute-start.6) | collective-permute-done | bytes 589856 | tf_op jit(solution)/shard_map/ppermute | solution.py:477
  46.0 3.1 %feed_back.2 = (bf16[192,768]{1,0:T(8,128)(2,1)S(1)}, f32[192,768]{1,0:T(8,128)S(1)}, bf16[192,768]{1,0:T(8,128)(2,1)S(1)}, bf16[192,1536]{1,0:T(8,128)(2,1)S(1)...) custom-call(f32[8,128]{1,0:T(8,128)S(1)} %get-tuple-element.145.refs_0_, ...), custom_call_target="tpu_custom_call" | custom-call | flops 10000000000 | bytes 1000000 | tf_op jit(solution)/shard_map/feed_back/pallas_call | solution.py:459
  49.1 1.8 %collective-permute-start.8 = (f32[192,768]{1,0:T(8,128)S(1)}, f32[192,768]{1,0:T(8,128)S(1)}, u32[]{:S(2)}, u32[]{:S(2)}) collective-permute-start(f32[192,768]{1,0:T(8,128)S(1)} %get-tuple-element.162.refs_2_), channel_id=1, source_target_pairs={{0,1},{1,0},{2,3},{3,2},{4,5},{5,4},{6,7},{7,6},{8,9},{9,8},{10,11... | collective-permute-start | bytes 1769480 | tf_op jit(solution)/shard_map/ppermute | solution.py:477
  50.9 7.7 %collective-permute-done.7.refs_2_ = f32[192,768]{1,0:T(8,128)S(1)} collective-permute-done((f32[192,768]{1,0:T(8,128)S(1)}, f32[192,768]{1,0:T(8,128)S(1)}, u32[]{:S(2)}, u32[]{:S(2)}) %collective-permute-start.7) | collective-permute-done | bytes 589856 | tf_op jit(solution)/shard_map/ppermute | solution.py:477
  58.7 3.1 %feed_back.3 = (bf16[192,768]{1,0:T(8,128)(2,1)S(1)}, f32[192,768]{1,0:T(8,128)S(1)}, bf16[192,768]{1,0:T(8,128)(2,1)S(1)}, bf16[192,1536]{1,0:T(8,128)(2,1)S(1)...) custom-call(f32[8,128]{1,0:T(8,128)S(1)} %get-tuple-element.150.refs_0_, ...), custom_call_target="tpu_custom_call" | custom-call | flops 10000000000 | bytes 1000000 | tf_op jit(solution)/shard_map/feed_back/pallas_call | solution.py:459
  61.8 2.9 %outer.3 = (f32[384,1536]{1,0:T(8,128)S(1)}, f32[384,1536]{1,0:T(8,128)S(1)}, f32[8,128]{1,0:T(8,128)S(1)}) custom-call(f32[8,128]{1,0:T(8,128)S(1)} %get-tuple-element.155.refs_0_, s32[3]{0:T(128)S(1)} %pad_add_fusion.refs_1_, bf16[192,768]{1,0:T(8,128)(2,1)S(1)} %get-tuple-element.156.refs_2_, bf16[192,768]{1,0:T(8,128)(2,1)S(1)} %get-tuple-element.157.refs_3_, ...), custom_call_target="tpu_custom_call" | custom-call | flops 10000000000 | bytes 1000000 | tf_op jit(solution)/shard_map/outer/pallas_call | solution.py:459
  64.9 1.8 %collective-permute-start.13 = (f32[192,768]{1,0:T(8,128)S(1)}, f32[192,768]{1,0:T(8,128)S(1)}, u32[]{:S(2)}, u32[]{:S(2)}) collective-permute-start(f32[192,768]{1,0:T(8,128)S(1)} %get-tuple-element.186.refs_2_), channel_id=1, source_target_pairs={{0,1},{1,0},{2,3},{3,2},{4,5},{5,4},{6,7},{7,6},{8,9},{9,8},{10,11... | collective-permute-start | bytes 1769480 | tf_op jit(solution)/shard_map/ppermute | solution.py:477
  66.7 4.7 %collective-permute-done.8.refs_3_ = f32[192,768]{1,0:T(8,128)S(1)} collective-permute-done((f32[192,768]{1,0:T(8,128)S(1)}, f32[192,768]{1,0:T(8,128)S(1)}, u32[]{:S(2)}, u32[]{:S(2)}) %collective-permute-start.8) | collective-permute-done | bytes 589856 | tf_op jit(solution)/shard_map/ppermute | solution.py:477
  75.0 2.9 %outer.4 = (f32[384,1536]{1,0:T(8,128)S(1)}, f32[384,1536]{1,0:T(8,128)S(1)}, f32[8,128]{1,0:T(8,128)S(1)}) custom-call(f32[8,128]{1,0:T(8,128)S(1)} %get-tuple-element.171.refs_0_, s32[3]{0:T(128)S(1)} %pad_add_fusion.refs_1_, bf16[192,768]{1,0:T(8,128)(2,1)S(1)} %get-tuple-element.172.refs_2_, bf16[192,768]{1,0:T(8,128)(2,1)S(1)} %get-tuple-element.173.refs_3_, ...), custom_call_target="tpu_custom_call" | custom-call | flops 10000000000 | bytes 1000000 | tf_op jit(solution)/shard_map/outer/pallas_call | solution.py:459
  78.6 3.6 %collective-permute-done.10.refs_3_.refs_6_ = f32[192,512]{1,0:T(8,128)S(1)} collective-permute-done((f32[192,512]{1,0:T(8,128)S(1)}, f32[192,512]{1,0:T(8,128)S(1)}, u32[]{:S(2)}, u32[]{:S(2)}) %collective-permute-start.10) | collective-permute-done | bytes 393248 | tf_op jit(solution)/shard_map/ppermute | solution.py:480
  82.2 3.2 %collective-permute-start.14 = (f32[96,512]{1,0:T(8,128)S(1)}, f32[96,512]{1,0:T(8,128)S(1)}, u32[]{:S(2)}, u32[]{:S(2)}) collective-permute-start(f32[96,512]{1,0:T(8,128)S(1)} %get-tuple-element.203), channel_id=1, source_target_pairs={{0,16},{2,18},{4,20},{6,22},{8,24},{10,26},{12,28},{14,30},{16,0},... | collective-permute-start | bytes 589832 | tf_op jit(solution)/shard_map/ppermute | solution.py:480
  88.2 5.7 %attend_back.1 = (bf16[384,1536]{1,0:T(8,128)(2,1)S(1)}, f32[8,1536]{1,0:T(8,128)S(1)}, f32[8,128]{1,0:T(8,128)S(1)}) custom-call(f32[8,128]{1,0:T(8,128)S(1)} %get-tuple-element.192.refs_0_, bf16[192,768]{1,0:T(8,128)(2,1)S(1)} %get-tuple-element.193.refs_1_.refs_3_, bf16[192,768]{1,0:T(8,128)(2,1)S(1)} %get-tuple-element.194.refs_2_.refs_4_, ...), custom_call_target="tpu_custom_call" | custom-call | flops 100000000 | bytes 1000000 | tf_op jit(solution)/shard_map/attend_back/pallas_call | solution.py:459
  95.5 3.5 %outer.5 = (f32[392,1536]{1,0:T(8,128)S(1)}, f32[392,1536]{1,0:T(8,128)S(1)}, f32[8,128]{1,0:T(8,128)S(1)}) custom-call(f32[8,128]{1,0:T(8,128)S(1)} %get-tuple-element.199.refs_0_, s32[3]{0:T(128)S(1)} %pad_add_fusion.refs_1_, bf16[384,768]{1,0:T(8,128)(2,1)S(1)} %copy-done, bf16[192,768]{1,0:T(8,128)(2,1)S(1)} %get-tuple-element.193.refs_1_.refs_3_, ...), custom_call_target="tpu_custom_call" | custom-call | flops 100000000 | bytes 1000000 | tf_op jit(solution)/shard_map/outer/pallas_call | solution.py:459
  99.2 1.9 %collective-permute-start.19 = (f32[48,1024]{1,0:T(8,128)S(1)}, f32[48,1024]{1,0:T(8,128)S(1)}, u32[]{:S(2)}, u32[]{:S(2)}) collective-permute-start(f32[48,1024]{1,0:T(8,128)S(1)} %get-tuple-element.215), channel_id=1, source_target_pairs={{0,16},{2,18},{4,20},{6,22},{8,24},{10,26},{12,28},{14,30},{16,0},... | collective-permute-start | bytes 589832 | tf_op jit(solution)/shard_map/ppermute | solution.py:480
  101.1 3.3 %collective-permute-done.17.refs_3_.refs_6_ = f32[96,1536]{1,0:T(8,128)S(1)} collective-permute-done((f32[96,1536]{1,0:T(8,128)S(1)}, f32[96,1536]{1,0:T(8,128)S(1)}, u32[]{:S(2)}, u32[]{:S(2)}) %collective-permute-start.17) | collective-permute-done | bytes 589856 | tf_op jit(solution)/shard_map/ppermute | solution.py:480
  104.5 2.3 %collective-permute-start.21 = (f32[96,1536]{1,0:T(8,128)S(1)}, f32[96,1536]{1,0:T(8,128)S(1)}, u32[]{:S(2)}, u32[]{:S(2)}) collective-permute-start(f32[96,1536]{1,0:T(8,128)S(1)} %get-tuple-element.218), channel_id=1, source_target_pairs={{0,8},{2,10},{4,12},{6,14},{8,0},{10,2},{12,4},{14,6},{16,24},{18,... | collective-permute-start | bytes 1769480 | tf_op jit(solution)/shard_map/ppermute | solution.py:480
  109.1 2.7 %back_tokens.1 = (f32[384,768]{1,0:T(8,128)S(1)}, f32[8,128]{1,0:T(8,128)S(1)}) custom-call(f32[8,128]{1,0:T(8,128)S(1)} %get-tuple-element.213.refs_0_, bf16[384,1536]{1,0:T(8,128)(2,1)S(1)} %get-tuple-element.200.refs_5_.refs_1_, bf16[3,768,384]{2,1,0:T(8,128)(2,1)} %refs_2_.9), custom_call_target="tpu_custom_call" | custom-call | flops 100000000 | bytes 1000000 | tf_op jit(solution)/shard_map/back_tokens/pallas_call | solution.py:459
  113.2 3.8 %collective-permute-done.20.refs_3_ = f32[96,1536]{1,0:T(8,128)S(1)} collective-permute-done((f32[96,1536]{1,0:T(8,128)S(1)}, f32[96,1536]{1,0:T(8,128)S(1)}, u32[]{:S(2)}, u32[]{:S(2)}) %collective-permute-start.20) | collective-permute-done | bytes 589856 | tf_op jit(solution)/shard_map/ppermute | solution.py:480
  117.0 1.8 %collective-permute-done.21.refs_4_ = f32[96,1536]{1,0:T(8,128)S(1)} collective-permute-done((f32[96,1536]{1,0:T(8,128)S(1)}, f32[96,1536]{1,0:T(8,128)S(1)}, u32[]{:S(2)}, u32[]{:S(2)}) %collective-permute-start.21) | collective-permute-done | bytes 589856 | tf_op jit(solution)/shard_map/ppermute | solution.py:480
  120.5 10.2 %collective-permute-done.22.refs_3_.refs_6_ = f32[104,1536]{1,0:T(8,128)S(1)} collective-permute-done((f32[104,1536]{1,0:T(8,128)S(1)}, f32[104,1536]{1,0:T(8,128)S(1)}, u32[]{:S(2)}, u32[]{:S(2)}) %collective-permute-start.22) | collective-permute-done | bytes 639008 | tf_op jit(solution)/shard_map/ppermute | solution.py:480
  130.8 2.3 %collective-permute-start.25 = (f32[56,1536]{1,0:T(8,128)S(1)}, f32[56,1536]{1,0:T(8,128)S(1)}, u32[]{:S(2)}, u32[]{:S(2)}) collective-permute-start(f32[56,1536]{1,0:T(8,128)S(1)} %get-tuple-element.226), channel_id=1, source_target_pairs={{0,8},{2,10},{4,12},{6,14},{8,0},{10,2},{12,4},{14,6},{16,24},{18,... | collective-permute-start | bytes 1032200 | tf_op jit(solution)/shard_map/ppermute | solution.py:480
  134.1 1.9 %collective-permute-start.27 = (f32[48,512]{1,0:T(8,128)S(1)}, f32[48,512]{1,0:T(8,128)S(1)}, u32[]{:S(2)}, u32[]{:S(2)}) collective-permute-start(f32[48,512]{1,0:T(8,128)S(1)} %get-tuple-element.231), channel_id=1, source_target_pairs={{0,4},{2,6},{4,0},{6,2},{8,12},{10,14},{12,8},{14,10},{16,20},{18,... | collective-permute-start | bytes 294920 | tf_op jit(solution)/shard_map/ppermute | solution.py:480
  136.8 5.0 %collective-permute-done.24.refs_3_ = f32[96,1536]{1,0:T(8,128)S(1)} collective-permute-done((f32[96,1536]{1,0:T(8,128)S(1)}, f32[96,1536]{1,0:T(8,128)S(1)}, u32[]{:S(2)}, u32[]{:S(2)}) %collective-permute-start.24) | collective-permute-done | bytes 589856 | tf_op jit(solution)/shard_map/ppermute | solution.py:480
  142.2 2.6 %collective-permute-start.29 = (f32[8,896]{1,0:T(8,128)S(1)}, f32[8,896]{1,0:T(8,128)S(1)}, u32[]{:S(2)}, u32[]{:S(2)}) collective-permute-start(f32[8,896]{1,0:T(8,128)S(1)} %get-tuple-element.238.refs_1_), channel_id=1, source_target_pairs={{0,16},{2,18},{4,20},{6,22},{8,24},{10,26},{12,28},{14,30},{16,0},... | collective-permute-start | bytes 86024 | tf_op jit(solution)/shard_map/ppermute | solution.py:480
  151.1 6.4 %collective-permute-done.30.refs_2_ = f32[48,1536]{1,0:T(8,128)S(1)} collective-permute-done((f32[48,1536]{1,0:T(8,128)S(1)}, f32[48,1536]{1,0:T(8,128)S(1)}, u32[]{:S(2)}, u32[]{:S(2)}) %collective-permute-start.30) | collective-permute-done | bytes 294944 | tf_op jit(solution)/shard_map/ppermute | solution.py:480
  (113 shorter events, 30.6 us)
Async XLA Ops:
  1.7 17.3 %copy-start.7 = (bf16[768]{0:T(1024)(128)(2,1)S(1)}, bf16[768]{0:T(1024)(128)(2,1)}, u32[]{:S(2)}) copy-start(bf16[768]{0:T(1024)(128)(2,1)} %refs_2_.6) | copy-start | bytes 4612
  1.7 17.2 %collective-permute-start = (f32[192,768]{1,0:T(8,128)S(1)}, f32[192,768]{1,0:T(8,128)S(1)}, u32[]{:S(2)}, u32[]{:S(2)}) collective-permute-start(f32[192,768]{1,0:T(8,128)S(1)} %dynamic-slice_convert_fusion), channel_id=1, source_target_pairs={{0,1},{1,0},{2,3},{3,2},{4,5},{5,4},{6,7},{7,6},{8,9},{9,8},{10,11... | collective-permute-start | bytes 1769480 | tf_op jit(solution)/shard_map/ppermute | solution.py:477
  12.5 12.5 %collective-permute-start.4 = (f32[192,384]{1,0:T(8,128)}, f32[192,384]{1,0:T(8,128)S(1)}, u32[]{:S(2)}, u32[]{:S(2)}) collective-permute-start(f32[192,384]{1,0:T(8,128)} %get-tuple-element.135), channel_id=1, source_target_pairs={{0,1},{1,0},{2,3},{3,2},{4,5},{5,4},{6,7},{7,6},{8,9},{9,8},{10,11... | collective-permute-start | bytes 884744 | tf_op jit(solution)/shard_map/ppermute | solution.py:477
  19.8 3.0 %collective-permute-start.3 = (f32[64,768]{1,0:T(8,128)S(1)}, f32[64,768]{1,0:T(8,128)S(1)}, u32[]{:S(2)}, u32[]{:S(2)}) collective-permute-start(f32[64,768]{1,0:T(8,128)S(1)} %get-tuple-element.256), channel_id=1, source_target_pairs={{0,2},{2,0},{4,6},{6,4},{8,10},{10,8},{12,14},{14,12},{16,18},{18,... | collective-permute-start | bytes 589832 | tf_op jit(solution)/shard_map/ppermute | solution.py:480
  19.9 2.9 %collective-permute-start.2 = (f32[64,768]{1,0:T(8,128)S(1)}, f32[64,768]{1,0:T(8,128)S(1)}, u32[]{:S(2)}, u32[]{:S(2)}) collective-permute-start(f32[64,768]{1,0:T(8,128)S(1)} %get-tuple-element.257), channel_id=1, source_target_pairs={{0,2},{2,0},{4,6},{6,4},{8,10},{10,8},{12,14},{14,12},{16,18},{18,... | collective-permute-start | bytes 589832 | tf_op jit(solution)/shard_map/ppermute | solution.py:480
  20.4 2.4 %collective-permute-start.1 = (f32[64,768]{1,0:T(8,128)S(1)}, f32[64,768]{1,0:T(8,128)S(1)}, u32[]{:S(2)}, u32[]{:S(2)}) collective-permute-start(f32[64,768]{1,0:T(8,128)S(1)} %get-tuple-element.258), channel_id=1, source_target_pairs={{0,2},{2,0},{4,6},{6,4},{8,10},{10,8},{12,14},{14,12},{16,18},{18,... | collective-permute-start | bytes 589832 | tf_op jit(solution)/shard_map/ppermute | solution.py:480
  20.6 10.9 %collective-permute-start.5 = (f32[192,384]{1,0:T(8,128)S(1)}, f32[192,384]{1,0:T(8,128)S(1)}, u32[]{:S(2)}, u32[]{:S(2)}) collective-permute-start(f32[192,384]{1,0:T(8,128)S(1)} %copy-done.16), channel_id=1, source_target_pairs={{0,1},{1,0},{2,3},{3,2},{4,5},{5,4},{6,7},{7,6},{8,9},{9,8},{10,11... | collective-permute-start | bytes 884744 | tf_op jit(solution)/shard_map/ppermute | solution.py:477
  29.7 16.3 %collective-permute-start.6 = (f32[192,768]{1,0:T(8,128)S(1)}, f32[192,768]{1,0:T(8,128)S(1)}, u32[]{:S(2)}, u32[]{:S(2)}) collective-permute-start(f32[192,768]{1,0:T(8,128)S(1)} %get-tuple-element.146.refs_1_), channel_id=1, source_target_pairs={{0,1},{1,0},{2,3},{3,2},{4,5},{5,4},{6,7},{7,6},{8,9},{9,8},{10,11... | collective-permute-start | bytes 1769480 | tf_op jit(solution)/shard_map/ppermute | solution.py:477
  35.4 23.2 %collective-permute-start.7 = (f32[192,768]{1,0:T(8,128)S(1)}, f32[192,768]{1,0:T(8,128)S(1)}, u32[]{:S(2)}, u32[]{:S(2)}) collective-permute-start(f32[192,768]{1,0:T(8,128)S(1)} %get-tuple-element.151.refs_1_), channel_id=1, source_target_pairs={{0,1},{1,0},{2,3},{3,2},{4,5},{5,4},{6,7},{7,6},{8,9},{9,8},{10,11... | collective-permute-start | bytes 1769480 | tf_op jit(solution)/shard_map/ppermute | solution.py:477
  49.1 22.2 %collective-permute-start.8 = (f32[192,768]{1,0:T(8,128)S(1)}, f32[192,768]{1,0:T(8,128)S(1)}, u32[]{:S(2)}, u32[]{:S(2)}) collective-permute-start(f32[192,768]{1,0:T(8,128)S(1)} %get-tuple-element.162.refs_2_), channel_id=1, source_target_pairs={{0,1},{1,0},{2,3},{3,2},{4,5},{5,4},{6,7},{7,6},{8,9},{9,8},{10,11... | collective-permute-start | bytes 1769480 | tf_op jit(solution)/shard_map/ppermute | solution.py:477
  64.8 7.0 %collective-permute-start.9 = (f32[384,1536]{1,0:T(8,128)S(1)}, f32[384,1536]{1,0:T(8,128)S(1)}, u32[]{:S(2)}, u32[]{:S(2)}) collective-permute-start(f32[384,1536]{1,0:T(8,128)S(1)} %get-tuple-element.169), channel_id=1, source_target_pairs={{0,2},{2,0},{4,6},{6,4},{8,10},{10,8},{12,14},{14,12},{16,18},{18,... | collective-permute-start | bytes 7077896 | tf_op jit(solution)/shard_map/ppermute | solution.py:480
  64.9 22.6 %collective-permute-start.13 = (f32[192,768]{1,0:T(8,128)S(1)}, f32[192,768]{1,0:T(8,128)S(1)}, u32[]{:S(2)}, u32[]{:S(2)}) collective-permute-start(f32[192,768]{1,0:T(8,128)S(1)} %get-tuple-element.186.refs_2_), channel_id=1, source_target_pairs={{0,1},{1,0},{2,3},{3,2},{4,5},{5,4},{6,7},{7,6},{8,9},{9,8},{10,11... | collective-permute-start | bytes 1769480 | tf_op jit(solution)/shard_map/ppermute | solution.py:477
  71.9 13.5 %collective-permute-start.11 = (f32[96,1024]{1,0:T(8,128)S(1)}, f32[96,1024]{1,0:T(8,128)S(1)}, u32[]{:S(2)}, u32[]{:S(2)}) collective-permute-start(f32[96,1024]{1,0:T(8,128)S(1)} %get-tuple-element.180), channel_id=1, source_target_pairs={{0,4},{2,6},{4,0},{6,2},{8,12},{10,14},{12,8},{14,10},{16,20},{18,... | collective-permute-start | bytes 1179656 | tf_op jit(solution)/shard_map/ppermute | solution.py:480
  73.4 8.7 %collective-permute-start.10 = (f32[192,512]{1,0:T(8,128)S(1)}, f32[192,512]{1,0:T(8,128)S(1)}, u32[]{:S(2)}, u32[]{:S(2)}) collective-permute-start(f32[192,512]{1,0:T(8,128)S(1)} %get-tuple-element.178), channel_id=1, source_target_pairs={{0,8},{2,10},{4,12},{6,14},{8,0},{10,2},{12,4},{14,6},{16,24},{18,... | collective-permute-start | bytes 1179656 | tf_op jit(solution)/shard_map/ppermute | solution.py:480
  78.0 21.2 %collective-permute-start.15 = (f32[96,1024]{1,0:T(8,128)S(1)}, f32[96,1024]{1,0:T(8,128)S(1)}, u32[]{:S(2)}, u32[]{:S(2)}) collective-permute-start(f32[96,1024]{1,0:T(8,128)S(1)} %get-tuple-element.205), channel_id=1, source_target_pairs={{0,4},{2,6},{4,0},{6,2},{8,12},{10,14},{12,8},{14,10},{16,20},{18,... | collective-permute-start | bytes 1179656 | tf_op jit(solution)/shard_map/ppermute | solution.py:480
  78.6 8.3 %collective-permute-start.12 = (f32[384,1536]{1,0:T(8,128)S(1)}, f32[384,1536]{1,0:T(8,128)S(1)}, u32[]{:S(2)}, u32[]{:S(2)}) collective-permute-start(f32[384,1536]{1,0:T(8,128)S(1)} %get-tuple-element.183), channel_id=1, source_target_pairs={{0,2},{2,0},{4,6},{6,4},{8,10},{10,8},{12,14},{14,12},{16,18},{18,... | collective-permute-start | bytes 7077896 | tf_op jit(solution)/shard_map/ppermute | solution.py:480
  82.2 16.9 %collective-permute-start.14 = (f32[96,512]{1,0:T(8,128)S(1)}, f32[96,512]{1,0:T(8,128)S(1)}, u32[]{:S(2)}, u32[]{:S(2)}) collective-permute-start(f32[96,512]{1,0:T(8,128)S(1)} %get-tuple-element.203), channel_id=1, source_target_pairs={{0,16},{2,18},{4,20},{6,22},{8,24},{10,26},{12,28},{14,30},{16,0},... | collective-permute-start | bytes 589832 | tf_op jit(solution)/shard_map/ppermute | solution.py:480
  85.5 13.7 %collective-permute-start.16 = (f32[96,1024]{1,0:T(8,128)S(1)}, f32[96,1024]{1,0:T(8,128)S(1)}, u32[]{:S(2)}, u32[]{:S(2)}) collective-permute-start(f32[96,1024]{1,0:T(8,128)S(1)} %get-tuple-element.206), channel_id=1, source_target_pairs={{0,8},{2,10},{4,12},{6,14},{8,0},{10,2},{12,4},{14,6},{16,24},{18,... | collective-permute-start | bytes 1179656 | tf_op jit(solution)/shard_map/ppermute | solution.py:480
  86.9 17.5 %collective-permute-start.17 = (f32[96,1536]{1,0:T(8,128)S(1)}, f32[96,1536]{1,0:T(8,128)S(1)}, u32[]{:S(2)}, u32[]{:S(2)}) collective-permute-start(f32[96,1536]{1,0:T(8,128)S(1)} %get-tuple-element.208), channel_id=1, source_target_pairs={{0,4},{2,6},{4,0},{6,2},{8,12},{10,14},{12,8},{14,10},{16,20},{18,... | collective-permute-start | bytes 1769480 | tf_op jit(solution)/shard_map/ppermute | solution.py:480
  94.0 23.0 %collective-permute-start.20 = (f32[96,1536]{1,0:T(8,128)S(1)}, f32[96,1536]{1,0:T(8,128)S(1)}, u32[]{:S(2)}, u32[]{:S(2)}) collective-permute-start(f32[96,1536]{1,0:T(8,128)S(1)} %get-tuple-element.217), channel_id=1, source_target_pairs={{0,4},{2,6},{4,0},{6,2},{8,12},{10,14},{12,8},{14,10},{16,20},{18,... | collective-permute-start | bytes 1769480 | tf_op jit(solution)/shard_map/ppermute | solution.py:480
  99.2 12.6 %collective-permute-start.19 = (f32[48,1024]{1,0:T(8,128)S(1)}, f32[48,1024]{1,0:T(8,128)S(1)}, u32[]{:S(2)}, u32[]{:S(2)}) collective-permute-start(f32[48,1024]{1,0:T(8,128)S(1)} %get-tuple-element.215), channel_id=1, source_target_pairs={{0,16},{2,18},{4,20},{6,22},{8,24},{10,26},{12,28},{14,30},{16,0},... | collective-permute-start | bytes 589832 | tf_op jit(solution)/shard_map/ppermute | solution.py:480
  101.1 5.7 %collective-permute-start.18 = (f32[392,1536]{1,0:T(8,128)S(1)}, f32[392,1536]{1,0:T(8,128)S(1)}, u32[]{:S(2)}, u32[]{:S(2)}) collective-permute-start(f32[392,1536]{1,0:T(8,128)S(1)} %get-tuple-element.211), channel_id=1, source_target_pairs={{0,2},{2,0},{4,6},{6,4},{8,10},{10,8},{12,14},{14,12},{16,18},{18,... | collective-permute-start | bytes 7225352 | tf_op jit(solution)/shard_map/ppermute | solution.py:480
  104.5 14.4 %collective-permute-start.21 = (f32[96,1536]{1,0:T(8,128)S(1)}, f32[96,1536]{1,0:T(8,128)S(1)}, u32[]{:S(2)}, u32[]{:S(2)}) collective-permute-start(f32[96,1536]{1,0:T(8,128)S(1)} %get-tuple-element.218), channel_id=1, source_target_pairs={{0,8},{2,10},{4,12},{6,14},{8,0},{10,2},{12,4},{14,6},{16,24},{18,... | collective-permute-start | bytes 1769480 | tf_op jit(solution)/shard_map/ppermute | solution.py:480
  106.9 23.8 %collective-permute-start.22 = (f32[104,1536]{1,0:T(8,128)S(1)}, f32[104,1536]{1,0:T(8,128)S(1)}, u32[]{:S(2)}, u32[]{:S(2)}) collective-permute-start(f32[104,1536]{1,0:T(8,128)S(1)} %get-tuple-element.220), channel_id=1, source_target_pairs={{0,4},{2,6},{4,0},{6,2},{8,12},{10,14},{12,8},{14,10},{16,20},{18,... | collective-permute-start | bytes 1916936 | tf_op jit(solution)/shard_map/ppermute | solution.py:480
  108.5 33.3 %collective-permute-start.24 = (f32[96,1536]{1,0:T(8,128)S(1)}, f32[96,1536]{1,0:T(8,128)S(1)}, u32[]{:S(2)}, u32[]{:S(2)}) collective-permute-start(f32[96,1536]{1,0:T(8,128)S(1)} %get-tuple-element.225), channel_id=1, source_target_pairs={{0,4},{2,6},{4,0},{6,2},{8,12},{10,14},{12,8},{14,10},{16,20},{18,... | collective-permute-start | bytes 1769480 | tf_op jit(solution)/shard_map/ppermute | solution.py:480
  111.8 36.0 %collective-permute-start.28 = (f32[384,768]{1,0:T(8,128)S(1)}, f32[384,768]{1,0:T(8,128)S(1)}, u32[]{:S(2)}, u32[]{:S(2)}) collective-permute-start(f32[384,768]{1,0:T(8,128)S(1)} %get-tuple-element.233.refs_1_), channel_id=1, source_target_pairs={{0,1},{1,0},{2,3},{3,2},{4,5},{5,4},{6,7},{7,6},{8,9},{9,8},{10,11... | collective-permute-start | bytes 3538952 | tf_op jit(solution)/shard_map/ppermute | solution.py:477
  118.9 15.2 %collective-permute-start.23 = (f32[48,1536]{1,0:T(8,128)S(1)}, f32[48,1536]{1,0:T(8,128)S(1)}, u32[]{:S(2)}, u32[]{:S(2)}) collective-permute-start(f32[48,1536]{1,0:T(8,128)S(1)} %get-tuple-element.223), channel_id=1, source_target_pairs={{0,16},{2,18},{4,20},{6,22},{8,24},{10,26},{12,28},{14,30},{16,0},... | collective-permute-start | bytes 884744 | tf_op jit(solution)/shard_map/ppermute | solution.py:480
  130.8 11.3 %collective-permute-start.25 = (f32[56,1536]{1,0:T(8,128)S(1)}, f32[56,1536]{1,0:T(8,128)S(1)}, u32[]{:S(2)}, u32[]{:S(2)}) collective-permute-start(f32[56,1536]{1,0:T(8,128)S(1)} %get-tuple-element.226), channel_id=1, source_target_pairs={{0,8},{2,10},{4,12},{6,14},{8,0},{10,2},{12,4},{14,6},{16,24},{18,... | collective-permute-start | bytes 1032200 | tf_op jit(solution)/shard_map/ppermute | solution.py:480
  133.1 13.7 %collective-permute-start.26 = (f32[48,1536]{1,0:T(8,128)S(1)}, f32[48,1536]{1,0:T(8,128)S(1)}, u32[]{:S(2)}, u32[]{:S(2)}) collective-permute-start(f32[48,1536]{1,0:T(8,128)S(1)} %get-tuple-element.229), channel_id=1, source_target_pairs={{0,8},{2,10},{4,12},{6,14},{8,0},{10,2},{12,4},{14,6},{16,24},{18,... | collective-permute-start | bytes 884744 | tf_op jit(solution)/shard_map/ppermute | solution.py:480
  134.1 12.9 %collective-permute-start.27 = (f32[48,512]{1,0:T(8,128)S(1)}, f32[48,512]{1,0:T(8,128)S(1)}, u32[]{:S(2)}, u32[]{:S(2)}) collective-permute-start(f32[48,512]{1,0:T(8,128)S(1)} %get-tuple-element.231), channel_id=1, source_target_pairs={{0,4},{2,6},{4,0},{6,2},{8,12},{10,14},{12,8},{14,10},{16,20},{18,... | collective-permute-start | bytes 294920 | tf_op jit(solution)/shard_map/ppermute | solution.py:480
  142.2 7.1 %collective-permute-start.29 = (f32[8,896]{1,0:T(8,128)S(1)}, f32[8,896]{1,0:T(8,128)S(1)}, u32[]{:S(2)}, u32[]{:S(2)}) collective-permute-start(f32[8,896]{1,0:T(8,128)S(1)} %get-tuple-element.238.refs_1_), channel_id=1, source_target_pairs={{0,16},{2,18},{4,20},{6,22},{8,24},{10,26},{12,28},{14,30},{16,0},... | collective-permute-start | bytes 86024 | tf_op jit(solution)/shard_map/ppermute | solution.py:480
  144.8 12.7 %collective-permute-start.30 = (f32[48,1536]{1,0:T(8,128)S(1)}, f32[48,1536]{1,0:T(8,128)S(1)}, u32[]{:S(2)}, u32[]{:S(2)}) collective-permute-start(f32[48,1536]{1,0:T(8,128)S(1)} %get-tuple-element.241), channel_id=1, source_target_pairs={{0,16},{2,18},{4,20},{6,22},{8,24},{10,26},{12,28},{14,30},{16,0},... | collective-permute-start | bytes 884744 | tf_op jit(solution)/shard_map/ppermute | solution.py:480
  (16 other events, 120.2 us)
